TPU v7x, 32 devices: a whole 2x2x4 slice. The times are simulated.
32 devices in a mesh: ctx: 4 (over x, core), row: 2 (over y), batch: 4 (over z).
Axes of the slice: x: 2, y: 2, z: 4, core: 2. Of those that a mesh axis runs over, the one named last changes fastest.
Arguments:
- queries: bfloat16 [3072, 5120], P(('batch', 'ctx'), 'row'), parts along dimension 0
- keys: bfloat16 [3072, 5120], P(('batch', 'ctx'), 'row'), parts along dimension 0
- values: bfloat16 [3072, 5120], P(('batch', 'ctx'), 'row'), parts along dimension 0, may hold values from -6 to 6
- gain_q: float32 [5120], P('row'), may hold values from 1.2 to 2.4
- gain_k: float32 [5120], P('row'), may hold values from 1.2 to 2.4
- clip_ids: int32 [3072], P(('batch', 'ctx')), parts along dimension 0, may hold values from 0 to 3, never falling along the last dimension, each value on 1 to 480 neighbouring positions
- clip_grid: int32 [16, 2], P('batch'), parts along dimension 0, may hold values from 8 to 40
Outputs:
- attended: bfloat16 [3072, 5120], P(('batch', 'ctx'), 'row'), parts along dimension 0
There are 4 independent parts, one for each index of `batch`. A program takes and returns all parts, laid end to end along the dimension named above; an argument that names none is the same for every part. Nothing has to cross between parts.
Inputs may be any that keep to these rules, and one draw needn't show every extreme that they name: `clip_ids`: never falls along the tokens; each of the 4 clips has 1 to 480 tokens, and one has exactly 480.
All inputs are finite; a program needn't handle non-finite values.
Results may differ from a plain program's by a relative error of at most 0.012.
The roundings to bfloat16 on the way count: a program that leaves them out, or rounds other values in their place, can miss the bound.
Values may be sent and summed in bfloat16 or wider, within the bound.
No kernel may reach another device: no remote copies, remote signals or barrier semaphores. Data moves between devices by JAX's collectives and lax.ppermute only.
A program may use at most 64 MiB of HBM per device.

v0:
```python
import math

import jax
import jax.numpy as jnp
from jax import lax
from jax.sharding import PartitionSpec as P

HD = 128
D = 5120
CLIPS = 4


EPSILON = 1e-06
NEGATIVE = -1e30
ROTARY_BASE = 10000.0
block_limit = 1024


def lookup(lookup_table, positions):
    labels = jnp.arange(lookup_table.shape[0], dtype=jnp.int32)
    return jnp.sum(
        jnp.where(positions[:, None] == labels[None, :], lookup_table[None, :], 0), axis=1
    )


def spin(matrix, offsets, clip_of, clip_grid, head_size):
    row_count = matrix.shape[0]
    sixth_part = head_size // 6
    first_dims = head_size - 4 * sixth_part
    first_freqs = 1.0 / ROTARY_BASE ** (
        jnp.arange(0, first_dims, 2, dtype=jnp.float32) / first_dims
    )
    other_freqs = 1.0 / ROTARY_BASE ** (
        jnp.arange(0, 2 * sixth_part, 2, dtype=jnp.float32) / (2 * sixth_part)
    )
    heights = lookup(clip_grid[:, 0], clip_of)
    widths = lookup(clip_grid[:, 1], clip_of)
    frame_pos = offsets // (heights * widths)
    line_pos = offsets // widths % heights
    column_pos = offsets % widths
    angles = jnp.concatenate(
        [
            frame_pos.astype(jnp.float32)[:, None] * first_freqs[None, :],
            line_pos.astype(jnp.float32)[:, None] * other_freqs[None, :],
            column_pos.astype(jnp.float32)[:, None] * other_freqs[None, :],
        ],
        axis=1,
    )
    cosine = jnp.repeat(jnp.cos(angles), 2, axis=1)
    sine_table = jnp.repeat(jnp.sin(angles), 2, axis=1)
    feature = jnp.arange(head_size, dtype=jnp.int32)
    is_even = (feature % 2 == 0)[None, None, :]
    head_view = matrix.reshape(row_count, -1, head_size)
    partner = jnp.where(is_even, -jnp.roll(head_view, -1, axis=2), jnp.roll(head_view, 1, axis=2))
    turned = head_view * cosine[:, None, :] + partner * sine_table[:, None, :]
    return turned.reshape(row_count, -1)


def on_device(queries, keys, values, gain_q, gain_k, clip_ids, clip_grid):
    rows_here, width_here = queries.shape
    heads_here = width_here // HD
    score_scale = 1.0 / math.sqrt(HD)
    query_wide = queries.astype(jnp.float32)
    key_wide = keys.astype(jnp.float32)
    squares = lax.psum(
        (jnp.sum(query_wide * query_wide, axis=1), jnp.sum(key_wide * key_wide, axis=1)), "row"
    )
    query_scale = lax.rsqrt(squares[0] / D + EPSILON)
    key_scale = lax.rsqrt(squares[1] / D + EPSILON)
    labels = jnp.arange(CLIPS, dtype=jnp.int32)
    local_counts = jnp.sum((clip_ids[:, None] == labels[None, :]).astype(jnp.int32), axis=0)
    totals = lax.psum(local_counts, "ctx")
    starts = jnp.cumsum(totals) - totals
    first_row = lax.axis_index("ctx") * rows_here
    offsets = first_row + jnp.arange(rows_here, dtype=jnp.int32) - lookup(starts, clip_ids)
    query_rot = spin(
        query_wide * query_scale[:, None] * gain_q[None, :], offsets, clip_ids, clip_grid, HD
    ).astype(jnp.bfloat16)
    query_heads = query_rot.reshape(rows_here, heads_here, HD)
    key_send = spin(
        key_wide * key_scale[:, None] * gain_k[None, :], offsets, clip_ids, clip_grid, HD
    ).astype(jnp.bfloat16)
    initial = (
        jnp.full((heads_here, rows_here), NEGATIVE, jnp.float32),
        jnp.zeros((heads_here, rows_here), jnp.float32),
        jnp.zeros((rows_here, heads_here, HD), jnp.float32),
    )
    running = initial
    piece_start = jnp.int32(0)
    key_piece = lax.all_gather(key_send, "ctx", axis=0, tiled=True)
    value_piece = lax.all_gather(values, "ctx", axis=0, tiled=True)
    row_count = key_piece.shape[0]
    block_rows = min(row_count, block_limit)
    for block_first in range(0, row_count, block_rows):
        block_size = min(block_rows, row_count - block_first)
        fold_key_rows = key_piece[block_first : block_first + block_size]
        fold_value_rows = value_piece[block_first : block_first + block_size]
        key_index = piece_start + block_first + jnp.arange(fold_key_rows.shape[0], dtype=jnp.int32)
        key_key_clips = (
            jnp.sum((starts[None, :] <= key_index[:, None]).astype(jnp.int32), axis=1) - 1
        )
        peak_old, total_old, summed_old = running
        key_view = fold_key_rows.reshape(fold_key_rows.shape[0], heads_here, HD)
        value_view = fold_value_rows.reshape(fold_value_rows.shape[0], heads_here, HD)
        scores = (
            jnp.einsum("qhd,khd->hqk", query_heads, key_view, preferred_element_type=jnp.float32)
            * score_scale
        )
        same = clip_ids[:, None] == key_key_clips[None, :]
        masked = jnp.where(same[None, :, :], scores, NEGATIVE)
        peak_new = jnp.maximum(peak_old, jnp.max(masked, axis=2))
        weights = jnp.where(same[None, :, :], jnp.exp(masked - peak_new[:, :, None]), 0.0)
        factor = jnp.exp(peak_old - peak_new)
        total_new = total_old * factor + jnp.sum(weights, axis=2)
        summed = summed_old * jnp.transpose(factor)[:, :, None] + jnp.einsum(
            "hqk,khd->qhd",
            weights.astype(jnp.bfloat16),
            value_view,
            preferred_element_type=jnp.float32,
        )
        running = (peak_new, total_new, summed)
    attended = running[2] / jnp.transpose(running[1])[:, :, None]
    return attended.reshape(rows_here, width_here).astype(jnp.bfloat16)


def solution(mesh):
    in_specs = (
        P(("batch", "ctx"), "row"),
        P(("batch", "ctx"), "row"),
        P(("batch", "ctx"), "row"),
        P("row"),
        P("row"),
        P(("batch", "ctx")),
        P("batch", None),
    )
    out_specs = P(("batch", "ctx"), "row")
    return jax.shard_map(
        on_device, mesh=mesh, in_specs=in_specs, out_specs=out_specs, check_vma=False
    )
```

profile of v0, /device:TPU:0, one launch (start us, length us, event | category | flops | bytes accessed | tf_op | source)
XLA Modules:
  0.0 147.1 jit_solution(18207035335796790461)
XLA Ops:
  6.6 1.6 %fusion.6 = f32[192]{0:T(256)S(1)} fusion(bf16[192,2560]{1,0:T(8,128)(2,1)} %param.7), kind=kLoop, calls=%fused_computation.15 | loop fusion | flops 1474368 | bytes 983808 | tf_op jit(solution)/shard_map/reduce_sum | solution.py:66
  8.1 1.5 %fusion.8 = f32[192]{0:T(256)S(1)} fusion(bf16[192,2560]{1,0:T(8,128)(2,1)} %param.8), kind=kLoop, calls=%fused_computation.17 | loop fusion | flops 1474368 | bytes 983808 | tf_op jit(solution)/shard_map/reduce_sum | solution.py:66
  9.6 5.9 %all-reduce = (f32[192]{0:T(256)S(1)}, f32[192]{0:T(256)S(1)}) all-reduce(f32[192]{0:T(256)S(1)} %fusion.8, f32[192]{0:T(256)S(1)} %fusion.6), channel_id=1, replica_groups=mesh['ctx'=4,'row'=2,'batch'=4] {'row'}, use_global_device_ids=true, to_apply=%region_10.11 | all-reduce | flops 384 | bytes 3072 | tf_op jit(solution)/shard_map/psum | solution.py:65
  15.5 2.3 %fusion.7 = f32[192,2560]{1,0:T(8,128)} fusion(bf16[192,2560]{1,0:T(8,128)(2,1)S(1)} %copy-done.7, f32[2560]{0:T(1024)} %param.10, f32[192]{0:T(256)S(1)} %get-tuple-element.34), kind=kLoop, calls=%fused_computation.16 | loop fusion | flops 1474560 | bytes 2960128 | tf_op jit(solution)/shard_map/mul | solution.py:77
  17.7 1.6 %reshape.190 = f32[192,20,128]{2,1,0:T(8,128)S(1)} reshape(f32[192,2560]{1,0:T(8,128)} %fusion.7) | data formatting | bytes 3932160 | tf_op jit(solution)/shard_map/reshape | solution.py:53
  19.4 2.8 %fusion.35 = (f32[192,20,127]{2,1,0:T(8,128)}, f32[192,20,127]{2,1,0:T(8,128)}) fusion(f32[192,20,128]{2,1,0:T(8,128)S(1)} %reshape.190), kind=kLoop, calls=%fused_computation.79 | loop fusion | bytes 7802880 | tf_op jit(solution)/shard_map/jit(_roll_static)/slice | solution.py:54
  22.2 2.9 %fusion.36 = (f32[192,20,1]{2,1,0:T(8,128)}, f32[192,20,1]{2,1,0:T(8,128)}) fusion(f32[192,20,128]{2,1,0:T(8,128)S(1)} %reshape.190), kind=kLoop, calls=%fused_computation.80 | loop fusion | bytes 61440 | tf_op jit(solution)/shard_map/jit(_roll_static)/slice | solution.py:54
  25.1 1.5 %fusion.9 = f32[192,2560]{1,0:T(8,128)} fusion(bf16[192,2560]{1,0:T(8,128)(2,1)S(1)} %copy-done.8, f32[2560]{0:T(1024)S(1)} %copy-done.11, f32[192]{0:T(256)S(1)} %get-tuple-element.33), kind=kLoop, calls=%fused_computation.18 | loop fusion | flops 1474560 | bytes 2960128 | tf_op jit(solution)/shard_map/mul | solution.py:81
  26.7 1.6 %reshape.192 = f32[192,20,128]{2,1,0:T(8,128)S(1)} reshape(f32[192,2560]{1,0:T(8,128)} %fusion.9) | data formatting | bytes 3932160 | tf_op jit(solution)/shard_map/reshape | solution.py:53
  28.3 2.9 %fusion.37 = (f32[192,20,127]{2,1,0:T(8,128)}, f32[192,20,127]{2,1,0:T(8,128)}) fusion(f32[192,20,128]{2,1,0:T(8,128)S(1)} %reshape.192), kind=kLoop, calls=%fused_computation.81 | loop fusion | bytes 7802880 | tf_op jit(solution)/shard_map/jit(_roll_static)/slice | solution.py:54
  31.2 2.9 %fusion.38 = (f32[192,20,1]{2,1,0:T(8,128)}, f32[192,20,1]{2,1,0:T(8,128)}) fusion(f32[192,20,128]{2,1,0:T(8,128)S(1)} %reshape.192), kind=kLoop, calls=%fused_computation.82 | loop fusion | bytes 61440 | tf_op jit(solution)/shard_map/jit(_roll_static)/slice | solution.py:54
  34.2 5.5 %psum.21 = s32[4]{0:T(128)S(1)} all-reduce(s32[4]{0:T(128)S(1)} %convert_reduce_fusion.1), channel_id=1, replica_groups=mesh['ctx'=4,'row'=2,'batch'=4] {'ctx'}, use_global_device_ids=true, to_apply=%region_1.0 | all-reduce | flops 4 | bytes 32 | tf_op jit(solution)/shard_map/psum | solution.py:72
  41.1 3.2 %maximum_negate_fusion = f32[192,20,128]{2,1,0:T(8,128)S(1)} fusion(f32[192,20,1]{2,1,0:T(8,128)} %get-tuple-element.14, f32[192,20,127]{2,1,0:T(8,128)} %get-tuple-element.12), kind=kLoop, calls=%fused_computation.11 | loop fusion | flops 983040 | bytes 3932160 | tf_op jit(solution)/shard_map/neg | solution.py:54
  44.3 0.6 copy-done.2
  44.9 0.7 pad_maximum_fusion
  45.6 1.0 copy-done.5
  46.6 0.7 copy-done.6
  47.3 0.7 maximum_negate_fusion.1
  48.0 1.0 copy-done.3
  48.9 0.7 copy-done.4
  49.7 0.7 pad_maximum_fusion.1
  50.7 0.9 copy-done.9
  51.5 4.0 %fusion.22 = (bf16[24,20,8,128]{3,2,1,0:T(8,128)(2,1)S(1)}, bf16[192,2560]{1,0:T(8,128)(2,1)}) fusion(f32[24,8,20,128]{3,2,1,0:T(8,128)S(1)} %bitcast.93, f32[24,8,20,128]{3,2,1,0:T(8,128)S(1)} %bitcast.89, f32[24,8,20,128]{3,2,1,0:T(8,128)S(1)} %bitcast.88, f32[24,8,20,128]{3,2,1,0:T(8,128)S(1)} %bitcast.92, pred[2560]{0:T(1024)(128)(4,1)S(1)} %broadcast_bitcast_fusion, ...), kind=kLoop, calls=%fused_computation.33 | loop fusion | flops 7864320 | bytes 15753216
  55.7 0.5 all-gather.5.cloned.1.call-update
  56.5 32.8 %all-gather.3.cloned.1.call-done = bf16[768,2560]{1,0:T(8,128)(2,1)} async-done(((bf16[192,2560]{1,0:T(8,128)(2,1)}), bf16[768,2560]{1,0:T(8,128)(2,1)}) %all-gather.3.cloned.1.call-update) | async-done | bytes 3932176 | tf_op jit(solution)/shard_map/all_gather | solution.py:90
  89.3 6.3 %copy.27 = bf16[768,2560]{0,1:T(8,128)(2,1)} copy(bf16[768,2560]{1,0:T(8,128)(2,1)} %all-gather.3.cloned.1.call-done) | data formatting | bytes 7864320 | tf_op jit(solution)/shard_map/all_gather | solution.py:90
  95.6 4.4 %fusion = (f32[20,192]{1,0:T(8,128)S(1)}, f32[20,192,768]{2,1,0:T(8,128)S(1)}) fusion(pred[192,768]{1,0:T(8,128)(4,1)S(1)} %broadcast_compare_fusion, bf16[768,20,128]{0,2,1:T(8,128)(2,1)} %bitcast.87, bf16[24,20,8,128]{3,2,1,0:T(8,128)(2,1)S(1)} %get-tuple-element.10), kind=kOutput, calls=%fused_computation.2 | convolution fusion | flops 763818240 | bytes 16874496 | tf_op jit(solution)/shard_map/qhd,khd->hqk/dot_general | solution.py:106
  100.0 4.1 %fusion.1 = f32[20,192]{1,0:T(8,128)S(1)} fusion(f32[20,192,768]{2,1,0:T(8,128)S(1)} %get-tuple-element.32, f32[20,192]{1,0:T(8,128)S(1)} %get-tuple-element.23, pred[192,768]{1,0:T(8,128)(4,1)S(1)} %broadcast_compare_fusion), kind=kLoop, calls=%fused_computation.3 | loop fusion | flops 14741760 | bytes 11974656 | tf_op jit(solution)/shard_map/reduce_sum | solution.py:114
  104.4 19.5 %all-gather.5.cloned.1.call-done = bf16[768,2560]{1,0:T(8,128)(2,1)} async-done(((bf16[192,2560]{1,0:T(8,128)(2,1)}), bf16[768,2560]{1,0:T(8,128)(2,1)}) %all-gather.5.cloned.1.call-update) | async-done | bytes 3932176 | tf_op jit(solution)/shard_map/all_gather | solution.py:91
  123.9 6.3 %copy.30 = bf16[768,2560]{0,1:T(8,128)(2,1)} copy(bf16[768,2560]{1,0:T(8,128)(2,1)} %all-gather.5.cloned.1.call-done) | data formatting | bytes 7864320 | tf_op jit(solution)/shard_map/all_gather | solution.py:91
  130.2 8.9 %fusion.19 = bf16[20,24,8,128]{3,2,1,0:T(8,128)(2,1)S(1)} fusion(bf16[768,20,128]{0,2,1:T(8,128)(2,1)} %bitcast.94, f32[20,192,768]{2,1,0:T(8,128)} %copy-done, f32[20,192]{1,0:T(8,128)S(1)} %get-tuple-element.23, pred[192,768]{1,0:T(8,128)(4,1)S(1)} %broadcast_compare_fusion, f32[192,20]{0,1:T(8,128)S(1)} %bitcast_add_fusion.1, ...), kind=kOutput, calls=%fused_computation.32 | convolution fusion | flops 771194880 | bytes 16905216 | tf_op jit(solution)/shard_map/hqk,khd->qhd/dot_general | solution.py:115
  139.1 1.1 copy.66
  (52 shorter events, 2.7 us)
Async XLA Ops:
  6.5 8.9 %copy-start.7 = (bf16[192,2560]{1,0:T(8,128)(2,1)S(1)}, bf16[192,2560]{1,0:T(8,128)(2,1)}, u32[]{:S(2)}) copy-start(bf16[192,2560]{1,0:T(8,128)(2,1)} %param.7) | copy-start | bytes 2949124
  6.5 82.8 %all-gather.3.cloned.1.call-start = ((), (), s32[]{:S(2)}) async-start(), calls=%async_computation | async-start | bytes 4915200 | tf_op jit(solution)/shard_map/all_gather | solution.py:90
  22.2 2.9 %copy-start.8 = (bf16[192,2560]{1,0:T(8,128)(2,1)S(1)}, bf16[192,2560]{1,0:T(8,128)(2,1)}, u32[]{:S(2)}) copy-start(bf16[192,2560]{1,0:T(8,128)(2,1)} %param.8) | copy-start | bytes 2949124
  22.2 2.9 %copy-start.11 = (f32[2560]{0:T(1024)S(1)}, f32[2560]{0:T(1024)}, u32[]{:S(2)}) copy-start(f32[2560]{0:T(1024)} %param.11) | copy-start | bytes 30724
  31.2 2.9 %copy-start.12 = (s32[192]{0:T(256)S(1)}, s32[192]{0:T(256)}, u32[]{:S(2)}) copy-start(s32[192]{0:T(256)} %param.12) | copy-start | bytes 2308
  31.2 8.6 %copy-start.13 = (s32[4,2]{0,1:T(2,128)S(1)}, s32[4,2]{0,1:T(2,128)}, u32[]{:S(2)}) copy-start(s32[4,2]{0,1:T(2,128)} %param.13) | copy-start | bytes 100
  41.1 3.2 %copy-start.1 = (f32[192,20,127]{2,1,0:T(8,128)S(1)}, f32[192,20,127]{2,1,0:T(8,128)}, u32[]{:S(2)}) copy-start(f32[192,20,127]{2,1,0:T(8,128)} %get-tuple-element.13) | copy-start | bytes 5852164
  41.1 3.8 %copy-start.2 = (f32[192,20,1]{2,1,0:T(8,128)S(1)}, f32[192,20,1]{2,1,0:T(8,128)}, u32[]{:S(2)}) copy-start(f32[192,20,1]{2,1,0:T(8,128)} %get-tuple-element.15) | copy-start | bytes 46084
  44.9 1.7 %copy-start.5 = (f32[192,20,127]{2,1,0:T(8,128)S(1)}, f32[192,20,127]{2,1,0:T(8,128)}, u32[]{:S(2)}) copy-start(f32[192,20,127]{2,1,0:T(8,128)} %get-tuple-element.16) | copy-start | bytes 5852164
  44.9 2.4 %copy-start.6 = (f32[192,20,1]{2,1,0:T(8,128)S(1)}, f32[192,20,1]{2,1,0:T(8,128)}, u32[]{:S(2)}) copy-start(f32[192,20,1]{2,1,0:T(8,128)} %get-tuple-element.18) | copy-start | bytes 46084
  47.3 1.7 %copy-start.3 = (f32[192,20,127]{2,1,0:T(8,128)S(1)}, f32[192,20,127]{2,1,0:T(8,128)}, u32[]{:S(2)}) copy-start(f32[192,20,127]{2,1,0:T(8,128)} %get-tuple-element.17) | copy-start | bytes 5852164
  47.3 2.4 %copy-start.4 = (f32[192,20,1]{2,1,0:T(8,128)S(1)}, f32[192,20,1]{2,1,0:T(8,128)}, u32[]{:S(2)}) copy-start(f32[192,20,1]{2,1,0:T(8,128)} %get-tuple-element.19) | copy-start | bytes 46084
  50.3 1.2 copy-start.9
  50.3 1.2 copy-start.10
  55.5 68.4 %all-gather.5.cloned.1.call-start = ((), (), s32[]{:S(2)}) async-start(), calls=%async_computation.1 | async-start | bytes 4915200 | tf_op jit(solution)/shard_map/all_gather | solution.py:91
  99.9 4.4 %copy-start = (f32[20,192,768]{2,1,0:T(8,128)}, f32[20,192,768]{2,1,0:T(8,128)S(1)}, u32[]{:S(2)}) copy-start(f32[20,192,768]{2,1,0:T(8,128)S(1)} %get-tuple-element.32) | copy-start | bytes 35389444
Sparse Core Ops, SparseCore 0:
  55.6 33.6 all-gather.2
  90.9 32.9 all-gather.4
where the time goes:
time: 148 us; the launch traced here: 147 us
  waiting for transfers between devices  52.8 us (36%)
  local copies, waits for them, and re-layouts  34.4 us (23%)
  other arithmetic  21.4 us (14%)
  between operations  13.6 us (9%)
  matrix products  13.3 us (9%)
  blocking collectives  11.3 us (8%)
    all_gather x1, waiting for transfers between devices, on_device(): key_piece = lax.all_gather(key_send, 'ctx', axis=0, tiled=True)  32.8 us
    all_gather x1, waiting for transfers between devices, on_device(): value_piece = lax.all_gather(values, 'ctx', axis=0, tiled=True)  19.5 us
    slice x4, local copies, waits for them, and re-layouts, spin(): jnp.roll(head_view, -1, axis=2)  11.5 us
    dot_general x1, matrix products, on_device(): jnp.einsum('hqk,khd->qhd', weights.astype(jnp.bfloat16), value_view, pref...  8.9 us
    all_gather x1, local copies, waits for them, and re-layouts, on_device(): value_piece = lax.all_gather(values, 'ctx', axis=0, tiled=True)  6.31 us
    all_gather x1, local copies, waits for them, and re-layouts, on_device(): key_piece = lax.all_gather(key_send, 'ctx', axis=0, tiled=True)  6.26 us
    psum x1, blocking collectives, on_device(): lax.psum((jnp.sum(query_wide * query_wide, axis=1), jnp.sum(key_wide * ke...  5.86 us
    psum x1, blocking collectives, on_device(): totals = lax.psum(local_counts, 'ctx')  5.45 us
  transfers between devices with their start and end apart: 2, of which 2 were waited for; matrix products, arithmetic and copies ran while one was open for 10% of the time, Pallas kernels for 0%

commit v1 on v0

--- a/solution.py
+++ b/solution.py
@@ -1,19 +1,23 @@
+import functools
 import math
 
 import jax
 import jax.numpy as jnp
 from jax import lax
+from jax.experimental import pallas as pl
+from jax.experimental.pallas import tpu as pltpu
 from jax.sharding import PartitionSpec as P
 
 HD = 128
 D = 5120
 CLIPS = 4
-
-
 EPSILON = 1e-06
 NEGATIVE = -1e30
 ROTARY_BASE = 10000.0
 block_limit = 1024
+GROUPS = (4, 4, 4, 4, 2, 2)
+ACROSS = ((0, 2), (1, 3), (2, 0), (3, 1))
+BESIDE = ((0, 1), (1, 0), (2, 3), (3, 2))
 
 
 def lookup(lookup_table, positions):
@@ -21,6 +25,168 @@
     return jnp.sum(
         jnp.where(positions[:, None] == labels[None, :], lookup_table[None, :], 0), axis=1
     )
+
+
+def angles_of(offsets, clip_of, clip_grid):
+    sixth_part = HD // 6
+    first_dims = HD - 4 * sixth_part
+    first_freqs = 1.0 / ROTARY_BASE ** (
+        jnp.arange(0, first_dims, 2, dtype=jnp.float32) / first_dims
+    )
+    other_freqs = 1.0 / ROTARY_BASE ** (
+        jnp.arange(0, 2 * sixth_part, 2, dtype=jnp.float32) / (2 * sixth_part)
+    )
+    heights = lookup(clip_grid[:, 0], clip_of)
+    widths = lookup(clip_grid[:, 1], clip_of)
+    frame_pos = (offsets // (heights * widths)).astype(jnp.float32)[:, None]
+    line_pos = (offsets // widths % heights).astype(jnp.float32)[:, None]
+    column_pos = (offsets % widths).astype(jnp.float32)[:, None]
+    freqs = jnp.repeat(jnp.concatenate([first_freqs, other_freqs, other_freqs]), 2)[None, :]
+    feature = jnp.arange(HD, dtype=jnp.int32)[None, :]
+    position = jnp.where(
+        feature < first_dims,
+        frame_pos,
+        jnp.where(feature < first_dims + 2 * sixth_part, line_pos, column_pos),
+    )
+    return position * freqs
+
+
+def attend_kernel(
+    pieces, scale, q_ref, *refs
+):
+    k_refs, v_refs = refs[:pieces], refs[pieces : 2 * pieces]
+    (cq, sq, ck, sk, gq, gqs, gk, gks, swap, qc, kc, o_ref, bias, krot) = refs[2 * pieces :]
+    rows = q_ref.shape[0]
+
+    @pl.when(pl.program_id(0) == 0)
+    def _():
+        bias[...] = jnp.where(qc[...] == kc[...], 0.0, NEGATIVE).astype(jnp.float32)
+
+    def turn(x, gain, gain_s, cosine, sine):
+        other = jnp.dot(x, swap[...], preferred_element_type=jnp.float32)
+        return (
+            (x.astype(jnp.float32) * gain) * cosine + (other * gain_s) * sine
+        ).astype(jnp.bfloat16)
+
+    for i in range(pieces):
+        at = slice(i * rows, (i + 1) * rows)
+        krot[at, :] = turn(k_refs[i][...], gk[...], gks[...], ck[at, :], sk[at, :])
+    q = turn(q_ref[...], gq[...], gqs[...], cq[...], sq[...])
+    scores = (
+        lax.dot_general(q, krot[...], (((1,), (1,)), ((), ())), preferred_element_type=jnp.float32)
+        + bias[...]
+    )
+    peak = jnp.max(scores, axis=1, keepdims=True)
+    weights = jnp.exp2((scores - peak) * scale)
+    total = jnp.sum(weights, axis=1, keepdims=True)
+    weights = weights.astype(jnp.bfloat16)
+    out = jnp.zeros((rows, HD), jnp.float32)
+    for i in range(pieces):
+        at = slice(i * rows, (i + 1) * rows)
+        out += jnp.dot(weights[:, at], v_refs[i][...], preferred_element_type=jnp.float32)
+    o_ref[...] = (out / total).astype(o_ref.dtype)
+
+
+def attend(first, heads, q, near, far, tables, gains, swap, clips):
+    rows = q.shape[0]
+    cq, sq, ck, sk = tables
+    qc, kc = clips
+    tokens = ck.shape[0]
+    pieces = len(near[0]) + len(far)
+    whole = lambda a: pl.BlockSpec(a.shape, lambda h: (0,) * a.ndim)
+    wide = pl.BlockSpec((rows, HD), lambda h: (0, first + h))
+    k_spec = pl.BlockSpec((None, rows, HD), lambda h: (0, 0, h))
+    v_spec = pl.BlockSpec((None, rows, HD), lambda h: (1, 0, h))
+    gain_spec = pl.BlockSpec((1, HD), lambda h: (0, first + h))
+    kernel = functools.partial(attend_kernel, pieces, math.log2(math.e) / math.sqrt(HD))
+    return pl.pallas_call(
+        kernel,
+        grid=(heads,),
+        out_shape=jax.ShapeDtypeStruct((rows, heads * HD), jnp.bfloat16),
+        in_specs=[wide]
+        + [wide] * len(near[0])
+        + [k_spec] * len(far)
+        + [wide] * len(near[1])
+        + [v_spec] * len(far)
+        + [whole(a) for a in (cq, sq, ck, sk)]
+        + [gain_spec] * 4
+        + [whole(swap), whole(qc), whole(kc)],
+        out_specs=pl.BlockSpec((rows, HD), lambda h: (0, h)),
+        scratch_shapes=[
+            pltpu.VMEM((rows, tokens), jnp.float32),
+            pltpu.VMEM((tokens, HD), jnp.bfloat16),
+        ],
+        compiler_params=pltpu.CompilerParams(vmem_limit_bytes=24 * 1024 * 1024),
+        cost_estimate=pl.CostEstimate(
+            flops=4 * heads * rows * tokens * HD * 4,
+            bytes_accessed=heads * tokens * HD * 4 + tokens * HD * 8,
+            transcendentals=heads * rows * tokens,
+        ),
+    )(q, *near[0], *far, *near[1], *far, cq, sq, ck, sk, *gains, swap, qc, kc)
+
+
+def on_device(queries, keys, values, gain_q, gain_k, clip_ids, clip_grid):
+    rows, width = queries.shape
+    me = lax.axis_index("ctx")
+    tokens = 4 * rows
+
+    far, first = [], 0
+    for heads in GROUPS:
+        at = slice(first * HD, (first + heads) * HD)
+        far.append(lax.ppermute(jnp.stack([keys[:, at], values[:, at]]), "ctx", ACROSS))
+        first += heads
+    keys_beside = lax.ppermute(keys, "ctx", BESIDE)
+    values_beside = lax.ppermute(values, "ctx", BESIDE)
+
+    q32, k32 = queries.astype(jnp.float32), keys.astype(jnp.float32)
+    label = jnp.where(lax.axis_index("row") == 0, clip_ids, 0).astype(jnp.float32)
+    mine = jnp.stack([jnp.sum(q32 * q32, axis=1), jnp.sum(k32 * k32, axis=1), label])
+    slots = jnp.where(
+        jnp.arange(4)[None, :, None] == me, mine[:, None, :], 0.0
+    )
+    every = lax.psum(slots, ("ctx", "row"))
+    order = jnp.stack([me, me ^ 1, me ^ 2, me ^ 3])
+    pick = (order[:, None] == jnp.arange(4)[None, :])[None, :, :, None]
+    turned = jnp.sum(jnp.where(pick, every[:, None, :, :], 0.0), axis=2).reshape(3, tokens)
+    clip_of = turned[2].astype(jnp.int32)
+    labels = jnp.arange(CLIPS, dtype=jnp.int32)
+    starts = jnp.sum((clip_of[:, None] < labels[None, :]).astype(jnp.int32), axis=0)
+    index = (order[:, None] * rows + jnp.arange(rows)[None, :]).reshape(tokens)
+    offsets = index - lookup(starts, clip_of)
+    angles = angles_of(offsets, clip_of, clip_grid)
+    cosine, sine = jnp.cos(angles), jnp.sin(angles)
+    q_scale = lax.rsqrt(turned[0, :rows] / D + EPSILON)[:, None]
+    k_scale = lax.rsqrt(turned[1] / D + EPSILON)[:, None]
+    tables = (
+        cosine[:rows] * q_scale,
+        sine[:rows] * q_scale,
+        cosine * k_scale,
+        sine * k_scale,
+    )
+
+    def flip(gain):
+        return gain.reshape(-1, 2)[:, ::-1].reshape(1, width)
+
+    gains = (gain_q[None, :], flip(gain_q), gain_k[None, :], flip(gain_k))
+    at_row = jnp.arange(HD)[:, None]
+    at_column = jnp.arange(HD)[None, :]
+    swap = jnp.where(
+        at_row == (at_column ^ 1), jnp.where(at_column % 2 == 0, -1.0, 1.0), 0.0
+    ).astype(jnp.bfloat16)
+    clips = (clip_of[:rows, None], clip_of[None, :])
+
+    outs, first = [], 0
+    for heads, piece in zip(GROUPS, far):
+        passed = lax.ppermute(piece, "ctx", BESIDE)
+        outs.append(
+            attend(
+                first, heads, queries,
+                ((keys, keys_beside), (values, values_beside)),
+                (piece, passed), tables, gains, swap, clips,
+            )
+        )
+        first += heads
+    return jnp.concatenate(outs, axis=1)
 
 
 def spin(matrix, offsets, clip_of, clip_grid, head_size):
@@ -56,7 +222,7 @@
     return turned.reshape(row_count, -1)
 
 
-def on_device(queries, keys, values, gain_q, gain_k, clip_ids, clip_grid):
+def on_any(queries, keys, values, gain_q, gain_k, clip_ids, clip_grid):
     rows_here, width_here = queries.shape
     heads_here = width_here // HD
     score_scale = 1.0 / math.sqrt(HD)
@@ -135,5 +301,6 @@
     )
     out_specs = P(("batch", "ctx"), "row")
     return jax.shard_map(
-        on_device, mesh=mesh, in_specs=in_specs, out_specs=out_specs, check_vma=False
-    )
+        on_device if mesh.shape["ctx"] == 4 else on_any,
+        mesh=mesh, in_specs=in_specs, out_specs=out_specs, check_vma=False
+    )

time: 148 us -> 128 us (0.86)
  waiting for transfers between devices: 52.8 us -> 15.8 us
  Pallas kernels: 0 us -> 26.2 us
  blocking collectives: 11.3 us -> 31 us
  matrix products: 13.3 us -> 0 us
  between operations: 13.6 us -> 0.39 us
  other arithmetic: 21.4 us -> 9.12 us
  starting transfers between devices: 0.22 us -> 9.08 us
    all_gather x2 -> x0, waiting for transfers between devices: 52.3 us -> none  [the longest x1 32.8 us: on_device(): key_piece = lax.all_gather(key_send, 'ctx', axis=0, tiled=True)]
    pallas_call x0 -> x6, Pallas kernels: none -> 26.2 us  [attend(): pl.pallas_call(kernel, grid=(heads,), out_shape=jax.ShapeDtypeStruct((row...]
    psum x2 -> x1, blocking collectives: 11.3 us -> 31 us  [on_device(): every = lax.psum(slots, ('ctx', 'row'))]
    ppermute x0 -> x14, waiting for transfers between devices: none -> 15.8 us  [the longest x6 15.8 us: on_device(): lax.ppermute(jnp.stack([keys[:, at], values[:, at]]), 'ctx', ACROSS)]
    dot_general x2 -> x0, matrix products: 13.3 us -> none  [the longest x1 8.9 us: on_device(): jnp.einsum('hqk,khd->qhd', weights.astype(jnp.bfloat16), value_view, pref...]
    all_gather x2 -> x0, local copies, waits for them, and re-layouts: 12.6 us -> none  [the longest x1 6.31 us: on_device(): value_piece = lax.all_gather(values, 'ctx', axis=0, tiled=True)]
    rev x0 -> x2, local copies, waits for them, and re-layouts: none -> 12.4 us  [flip(): return gain.reshape(-1, 2)[:, ::-1].reshape(1, width)]
    slice x4 -> x0, local copies, waits for them, and re-layouts: 11.5 us -> none  [spin(): jnp.roll(head_view, -1, axis=2)]
  transfers between devices with their start and end apart: 2 -> 14, of which waited for: 2 -> 2; matrix products, arithmetic and copies ran while one was open for 10% -> 30% of each run, Pallas kernels for 0% -> 18%
where the time goes in v1:
time: 128 us; the launch traced here: 126 us
  local copies, waits for them, and re-layouts  34.2 us (27%)
  blocking collectives  31 us (24%)
  Pallas kernels  26.2 us (20%)
  waiting for transfers between devices  15.8 us (12%)
  other arithmetic  9.12 us (7%)
  starting transfers between devices  9.08 us (7%)
    psum x1, blocking collectives, on_device(): every = lax.psum(slots, ('ctx', 'row'))  31 us
    pallas_call x6, Pallas kernels, attend(): pl.pallas_call(kernel, grid=(heads,), out_shape=jax.ShapeDtypeStruct((row...  26.2 us
    ppermute x6, waiting for transfers between devices, on_device(): lax.ppermute(jnp.stack([keys[:, at], values[:, at]]), 'ctx', ACROSS)  15.8 us
    rev x2, local copies, waits for them, and re-layouts, flip(): return gain.reshape(-1, 2)[:, ::-1].reshape(1, width)  12.4 us
    reshape x4, local copies, waits for them, and re-layouts, flip(): return gain.reshape(-1, 2)[:, ::-1].reshape(1, width)  7.73 us
    ppermute x6, starting transfers between devices, on_device(): lax.ppermute(jnp.stack([keys[:, at], values[:, at]]), 'ctx', ACROSS)  7.4 us
    unnamed x45, local copies, waits for them, and re-layouts  4.59 us
    another operation x4, local copies, waits for them, and re-layouts, on_device(): jnp.stack([keys[:, at], values[:, at]])  3.64 us
  transfers between devices with their start and end apart: 14, of which 2 were waited for; matrix products, arithmetic and copies ran while one was open for 30% of the time, Pallas kernels for 18%

profile of v1, /device:TPU:0, one launch (start us, length us, event | category | flops | bytes accessed | tf_op | source)
XLA Modules:
  0.0 125.9 jit_solution(7649134188988042742)
XLA Ops:
  0.5 1.0 slice_bitcast_fusion.9
  1.5 1.0 slice_bitcast_fusion.8
  3.1 2.9 %collective-permute-start.12 = (bf16[2,192,256]{2,1,0:T(8,128)(2,1)}, bf16[2,192,256]{2,1,0:T(8,128)(2,1)}, u32[]{:S(2)}, u32[]{:S(2)}) collective-permute-start(bf16[2,192,256]{2,1,0:T(8,128)(2,1)} %pad_maximum_fusion.5), channel_id=1, source_target_pairs={{0,16},{8,24},{16,0},{24,8},{1,17},{9,25},{17,1},{25,9},{2,18},{10... | collective-permute-start | bytes 589832 | tf_op jit(solution)/shard_map/ppermute | solution.py:136
  6.8 0.8 slice_bitcast_fusion.1
  7.6 0.9 slice_bitcast_fusion
  8.5 0.8 pad_maximum_fusion.3
  9.3 2.0 %collective-permute-start.8 = (bf16[2,192,512]{2,1,0:T(8,128)(2,1)}, bf16[2,192,512]{2,1,0:T(8,128)(2,1)}, u32[]{:S(2)}, u32[]{:S(2)}) collective-permute-start(bf16[2,192,512]{2,1,0:T(8,128)(2,1)} %pad_maximum_fusion.3), channel_id=1, source_target_pairs={{0,16},{8,24},{16,0},{24,8},{1,17},{9,25},{17,1},{25,9},{2,18},{10... | collective-permute-start | bytes 1179656 | tf_op jit(solution)/shard_map/ppermute | solution.py:136
  12.2 31.0 %psum.7 = f32[3,4,192]{2,1,0:T(4,128)S(1)} all-reduce(f32[3,4,192]{2,1,0:T(4,128)S(1)} %broadcast_select_fusion), channel_id=1, replica_groups=mesh['ctx'=4,'row'=2,'batch'=4] {'ctx','row'}, use_global_device_ids=true, to_apply=%region_2.3 | all-reduce | flops 2304 | bytes 18432 | tf_op jit(solution)/shard_map/psum | solution.py:147
  44.6 2.7 %broadcast_multiply_fusion = (f32[768,128]{1,0:T(8,128)S(1)}, f32[768,128]{1,0:T(8,128)}, f32[768,128]{1,0:T(8,128)S(1)}, f32[768,128]{1,0:T(8,128)S(1)}) fusion(f32[768]{0:T(1024)S(1)} %rsqrt.23, f32[128]{0:T(128)S(1)} %mul.65, f32[768]{0:T(1024)S(1)} %get-tuple-element.30, f32[768]{0:T(1024)S(1)} %get-tuple-element.25, ...), kind=kLoop, calls=%fused_computation.17 | loop fusion | flops 491520 | bytes 1585920 | tf_op jit(solution)/shard_map/mul | solution.py:164
  48.3 1.3 %collective-permute-start.4 = (bf16[2,192,512]{2,1,0:T(8,128)(2,1)S(1)}, bf16[2,192,512]{2,1,0:T(8,128)(2,1)}, u32[]{:S(2)}, u32[]{:S(2)}) collective-permute-start(bf16[2,192,512]{2,1,0:T(8,128)(2,1)S(1)} %pad_maximum_fusion.1), channel_id=1, source_target_pairs={{0,16},{8,24},{16,0},{24,8},{1,17},{9,25},{17,1},{25,9},{2,18},{10... | collective-permute-start | bytes 1179656 | tf_op jit(solution)/shard_map/ppermute | solution.py:136
  49.6 0.8 pad_maximum_fusion
  50.4 0.8 collective-permute-start.1
  51.7 7.9 %collective-permute-done.6.refs_2_.refs_6_ = bf16[2,192,512]{2,1,0:T(8,128)(2,1)} collective-permute-done((bf16[2,192,512]{2,1,0:T(8,128)(2,1)S(1)}, bf16[2,192,512]{2,1,0:T(8,128)(2,1)}, u32[]{:S(2)}, u32[]{:S(2)}) %collective-permute-start.6) | collective-permute-done | bytes 393248 | tf_op jit(solution)/shard_map/ppermute | solution.py:136
  60.1 7.9 %collective-permute-done.4.refs_2_.refs_6_ = bf16[2,192,512]{2,1,0:T(8,128)(2,1)} collective-permute-done((bf16[2,192,512]{2,1,0:T(8,128)(2,1)S(1)}, bf16[2,192,512]{2,1,0:T(8,128)(2,1)}, u32[]{:S(2)}, u32[]{:S(2)}) %collective-permute-start.4) | collective-permute-done | bytes 393248 | tf_op jit(solution)/shard_map/ppermute | solution.py:136
  68.6 0.8 convert_element_type.76.refs_18_
  69.4 1.4 %reshape.246 = f32[1280,2]{1,0:T(8,128)} reshape(f32[2560]{0:T(1024)S(1)} %copy-done.15) | data formatting | bytes 20480 | tf_op jit(solution)/shard_map/reshape | solution.py:168
  70.8 0.7 broadcast_in_dim.202.refs_12_
  71.5 2.1 %reshape.248 = f32[1280,2]{1,0:T(8,128)} reshape(f32[2560]{0:T(1024)} %param.11) | data formatting | bytes 20480 | tf_op jit(solution)/shard_map/reshape | solution.py:168
  73.7 1.3 %broadcast_in_dim.203.refs_14_ = f32[1,2560]{1,0:T(1,128)} reshape(f32[2560]{0:T(1024)} %param.11) | data formatting | bytes 20480 | tf_op jit(solution)/shard_map/broadcast_in_dim | solution.py:170
  75.0 1.4 %copy.14.refs_17_ = s32[192,1]{1,0:T(8,128)} copy(s32[192,1]{0,1:T(1,128)} %slice_bitcast_fusion.12) | data formatting | bytes 1536 | tf_op jit(solution)/shard_map/broadcast_in_dim | solution.py:176
  76.3 6.2 %rev.6 = f32[1280,2]{1,0:T(8,128)} reverse(f32[1280,2]{1,0:T(8,128)} %reshape.246), dimensions={1} | reverse | bytes 20480 | tf_op jit(solution)/shard_map/rev | solution.py:168
  82.5 2.1 %reshape.247.refs_13_ = f32[1,2560]{1,0:T(1,128)} reshape(f32[1280,2]{1,0:T(8,128)} %rev.6) | data formatting | bytes 20480 | tf_op jit(solution)/shard_map/reshape | solution.py:168
  84.6 6.2 %rev.7 = f32[1280,2]{1,0:T(8,128)} reverse(f32[1280,2]{1,0:T(8,128)} %reshape.248), dimensions={1} | reverse | bytes 20480 | tf_op jit(solution)/shard_map/rev | solution.py:168
  90.8 2.1 %reshape.249.refs_15_ = f32[1,2560]{1,0:T(1,128)} reshape(f32[1280,2]{1,0:T(8,128)} %rev.7) | data formatting | bytes 20480 | tf_op jit(solution)/shard_map/reshape | solution.py:168
  94.8 1.0 copy-done.3
  95.8 0.9 copy-done.5
  98.8 5.0 %shard_map.75 = bf16[192,512]{1,0:T(8,128)(2,1)S(1)} custom-call(bf16[192,2560]{1,0:T(8,128)(2,1)S(1)} %copy-done.1, bf16[192,2560]{1,0:T(8,128)(2,1)S(1)} %copy-done, bf16[192,2560]{1,0:T(8,128)(2,1)} %collective-permute-done.refs_1_, bf16[2,192,512]{2,1,0:T(8,128)(2,1)} %collective-permute-done.6.refs_2_.refs_6_, ...), custom_call_target="tpu_custom_call" | custom-call | flops 1207959552 | bytes 2359296 | tf_op jit(solution)/shard_map/pallas_call | solution.py:102
  103.8 5.1 %shard_map.74 = bf16[192,512]{1,0:T(8,128)(2,1)S(1)} custom-call(bf16[192,2560]{1,0:T(8,128)(2,1)S(1)} %copy-done.1, bf16[192,2560]{1,0:T(8,128)(2,1)S(1)} %copy-done, bf16[192,2560]{1,0:T(8,128)(2,1)} %collective-permute-done.refs_1_, bf16[2,192,512]{2,1,0:T(8,128)(2,1)} %collective-permute-done.4.refs_2_.refs_6_, ...), custom_call_target="tpu_custom_call" | custom-call | flops 1207959552 | bytes 2359296 | tf_op jit(solution)/shard_map/pallas_call | solution.py:102
  108.9 5.0 %shard_map.73 = bf16[192,512]{1,0:T(8,128)(2,1)S(1)} custom-call(bf16[192,2560]{1,0:T(8,128)(2,1)S(1)} %copy-done.1, bf16[192,2560]{1,0:T(8,128)(2,1)S(1)} %copy-done, bf16[192,2560]{1,0:T(8,128)(2,1)} %collective-permute-done.refs_1_, bf16[2,192,512]{2,1,0:T(8,128)(2,1)} %collective-permute-done.1.refs_2_.refs_6_, ...), custom_call_target="tpu_custom_call" | custom-call | flops 1207959552 | bytes 2359296 | tf_op jit(solution)/shard_map/pallas_call | solution.py:102
  114.0 5.0 %shard_map.76 = bf16[192,512]{1,0:T(8,128)(2,1)S(1)} custom-call(bf16[192,2560]{1,0:T(8,128)(2,1)S(1)} %copy-done.1, bf16[192,2560]{1,0:T(8,128)(2,1)S(1)} %copy-done, bf16[192,2560]{1,0:T(8,128)(2,1)} %collective-permute-done.refs_1_, bf16[2,192,512]{2,1,0:T(8,128)(2,1)} %collective-permute-done.8.refs_2_.refs_6_, ...), custom_call_target="tpu_custom_call" | custom-call | flops 1207959552 | bytes 2359296 | tf_op jit(solution)/shard_map/pallas_call | solution.py:102
  119.0 3.0 %shard_map.77 = bf16[192,256]{1,0:T(8,128)(2,1)S(1)} custom-call(bf16[192,2560]{1,0:T(8,128)(2,1)S(1)} %copy-done.1, bf16[192,2560]{1,0:T(8,128)(2,1)S(1)} %copy-done, bf16[192,2560]{1,0:T(8,128)(2,1)} %collective-permute-done.refs_1_, bf16[2,192,256]{2,1,0:T(8,128)(2,1)} %collective-permute-done.10.refs_2_.refs_6_, ...), custom_call_target="tpu_custom_call" | custom-call | flops 603979776 | bytes 1572864 | tf_op jit(solution)/shard_map/pallas_call | solution.py:102
  122.0 3.2 %shard_map.78 = bf16[192,256]{1,0:T(8,128)(2,1)S(1)} custom-call(bf16[192,2560]{1,0:T(8,128)(2,1)S(1)} %copy-done.1, bf16[192,2560]{1,0:T(8,128)(2,1)S(1)} %copy-done, bf16[192,2560]{1,0:T(8,128)(2,1)} %collective-permute-done.refs_1_, bf16[2,192,256]{2,1,0:T(8,128)(2,1)} %collective-permute-done.12.refs_2_.refs_6_, ...), custom_call_target="tpu_custom_call" | custom-call | flops 603979776 | bytes 1572864 | tf_op jit(solution)/shard_map/pallas_call | solution.py:102
  (101 shorter events, 11.4 us)
Async XLA Ops:
  0.0 6.8 %copy-start = (bf16[192,2560]{1,0:T(8,128)(2,1)S(1)}, bf16[192,2560]{1,0:T(8,128)(2,1)}, u32[]{:S(2)}) copy-start(bf16[192,2560]{1,0:T(8,128)(2,1)} %refs_0_.11) | copy-start | bytes 2949124
  0.0 94.2 %collective-permute-start = (bf16[192,2560]{1,0:T(8,128)(2,1)}, bf16[192,2560]{1,0:T(8,128)(2,1)}, u32[]{:S(2)}, u32[]{:S(2)}) collective-permute-start(bf16[192,2560]{1,0:T(8,128)(2,1)} %refs_0_.11), channel_id=1, source_target_pairs={{0,8},{8,0},{16,24},{24,16},{1,9},{9,1},{17,25},{25,17},{2,10},{10... | collective-permute-start | bytes 2949128 | tf_op jit(solution)/shard_map/ppermute | solution.py:138
  0.5 94.2 %collective-permute-start.3 = (bf16[192,2560]{1,0:T(8,128)(2,1)}, bf16[192,2560]{1,0:T(8,128)(2,1)}, u32[]{:S(2)}, u32[]{:S(2)}) collective-permute-start(bf16[192,2560]{1,0:T(8,128)(2,1)} %refs_4_.11), channel_id=1, source_target_pairs={{0,8},{8,0},{16,24},{24,16},{1,9},{9,1},{17,25},{25,17},{2,10},{10... | collective-permute-start | bytes 2949128 | tf_op jit(solution)/shard_map/ppermute | solution.py:139
  3.1 44.3 %collective-permute-start.12 = (bf16[2,192,256]{2,1,0:T(8,128)(2,1)}, bf16[2,192,256]{2,1,0:T(8,128)(2,1)}, u32[]{:S(2)}, u32[]{:S(2)}) collective-permute-start(bf16[2,192,256]{2,1,0:T(8,128)(2,1)} %pad_maximum_fusion.5), channel_id=1, source_target_pairs={{0,16},{8,24},{16,0},{24,8},{1,17},{9,25},{17,1},{25,9},{2,18},{10... | collective-permute-start | bytes 589832 | tf_op jit(solution)/shard_map/ppermute | solution.py:136
  6.1 1.5 %copy-start.2 = (bf16[192,2560]{1,0:T(8,128)(2,1)S(1)}, bf16[192,2560]{1,0:T(8,128)(2,1)}, u32[]{:S(2)}) copy-start(bf16[192,2560]{1,0:T(8,128)(2,1)} %refs_4_.11) | copy-start | bytes 2949124
  6.8 41.5 %collective-permute-start.10 = (bf16[2,192,256]{2,1,0:T(8,128)(2,1)}, bf16[2,192,256]{2,1,0:T(8,128)(2,1)}, u32[]{:S(2)}, u32[]{:S(2)}) collective-permute-start(bf16[2,192,256]{2,1,0:T(8,128)(2,1)} %pad_maximum_fusion.4), channel_id=1, source_target_pairs={{0,16},{8,24},{16,0},{24,8},{1,17},{9,25},{17,1},{25,9},{2,18},{10... | collective-permute-start | bytes 589832 | tf_op jit(solution)/shard_map/ppermute | solution.py:136
  8.5 3.3 %copy-start.1 = (bf16[192,2560]{1,0:T(8,128)(2,1)S(1)}, bf16[192,2560]{1,0:T(8,128)(2,1)}, u32[]{:S(2)}) copy-start(bf16[192,2560]{1,0:T(8,128)(2,1)} %q_ref.11) | copy-start | bytes 2949124
  9.3 41.1 %collective-permute-start.8 = (bf16[2,192,512]{2,1,0:T(8,128)(2,1)}, bf16[2,192,512]{2,1,0:T(8,128)(2,1)}, u32[]{:S(2)}, u32[]{:S(2)}) collective-permute-start(bf16[2,192,512]{2,1,0:T(8,128)(2,1)} %pad_maximum_fusion.3), channel_id=1, source_target_pairs={{0,16},{8,24},{16,0},{24,8},{1,17},{9,25},{17,1},{25,9},{2,18},{10... | collective-permute-start | bytes 1179656 | tf_op jit(solution)/shard_map/ppermute | solution.py:136
  11.3 0.8 copy-start.18
  11.3 32.2 %copy-start.19 = (s32[4,2]{0,1:T(2,128)S(1)}, s32[4,2]{0,1:T(2,128)}, u32[]{:S(2)}) copy-start(s32[4,2]{0,1:T(2,128)} %param.13) | copy-start | bytes 100
  43.3 7.8 %copy-start.16 = (s32[1,4,192]{2,1,0:T(4,128)}, s32[1,4,192]{2,1,0:T(4,128)S(1)}, u32[]{:S(2)}) copy-start(s32[1,4,192]{2,1,0:T(4,128)S(1)} %get-tuple-element.29) | copy-start | bytes 9220
  44.6 2.8 %copy-start.13 = (bf16[1,192,512]{2,1,0:T(8,128)(2,1)S(1)}, bf16[1,192,512]{2,1,0:T(8,128)(2,1)}, u32[]{:S(2)}) copy-start(bf16[1,192,512]{2,1,0:T(8,128)(2,1)} %get-tuple-element.15) | copy-start | bytes 589828
  44.6 2.8 %copy-start.14 = (bf16[1,192,512]{2,1,0:T(8,128)(2,1)S(1)}, bf16[1,192,512]{2,1,0:T(8,128)(2,1)}, u32[]{:S(2)}) copy-start(bf16[1,192,512]{2,1,0:T(8,128)(2,1)} %get-tuple-element.19) | copy-start | bytes 589828
  47.2 0.9 copy-start.11
  47.2 1.0 copy-start.12
  47.2 2.4 %copy-start.9 = (bf16[1,192,512]{2,1,0:T(8,128)(2,1)S(1)}, bf16[1,192,512]{2,1,0:T(8,128)(2,1)}, u32[]{:S(2)}) copy-start(bf16[1,192,512]{2,1,0:T(8,128)(2,1)} %get-tuple-element.17) | copy-start | bytes 589828
  47.2 2.4 %copy-start.10 = (bf16[1,192,512]{2,1,0:T(8,128)(2,1)S(1)}, bf16[1,192,512]{2,1,0:T(8,128)(2,1)}, u32[]{:S(2)}) copy-start(bf16[1,192,512]{2,1,0:T(8,128)(2,1)} %get-tuple-element.21) | copy-start | bytes 589828
  47.4 21.9 %copy-start.15 = (f32[2560]{0:T(1024)S(1)}, f32[2560]{0:T(1024)}, u32[]{:S(2)}) copy-start(f32[2560]{0:T(1024)} %param.10) | copy-start | bytes 30724
  47.4 12.1 %collective-permute-start.6 = (bf16[2,192,512]{2,1,0:T(8,128)(2,1)S(1)}, bf16[2,192,512]{2,1,0:T(8,128)(2,1)}, u32[]{:S(2)}, u32[]{:S(2)}) collective-permute-start(bf16[2,192,512]{2,1,0:T(8,128)(2,1)S(1)} %pad_maximum_fusion.2), channel_id=1, source_target_pairs={{0,16},{8,24},{16,0},{24,8},{1,17},{9,25},{17,1},{25,9},{2,18},{10... | collective-permute-start | bytes 1179656 | tf_op jit(solution)/shard_map/ppermute | solution.py:136
  48.3 19.7 %collective-permute-start.4 = (bf16[2,192,512]{2,1,0:T(8,128)(2,1)S(1)}, bf16[2,192,512]{2,1,0:T(8,128)(2,1)}, u32[]{:S(2)}, u32[]{:S(2)}) collective-permute-start(bf16[2,192,512]{2,1,0:T(8,128)(2,1)S(1)} %pad_maximum_fusion.1), channel_id=1, source_target_pairs={{0,16},{8,24},{16,0},{24,8},{1,17},{9,25},{17,1},{25,9},{2,18},{10... | collective-permute-start | bytes 1179656 | tf_op jit(solution)/shard_map/ppermute | solution.py:136
  50.4 42.5 %collective-permute-start.1 = (bf16[2,192,512]{2,1,0:T(8,128)(2,1)}, bf16[2,192,512]{2,1,0:T(8,128)(2,1)}, u32[]{:S(2)}, u32[]{:S(2)}) collective-permute-start(bf16[2,192,512]{2,1,0:T(8,128)(2,1)} %pad_maximum_fusion), channel_id=1, source_target_pairs={{0,16},{8,24},{16,0},{24,8},{1,17},{9,25},{17,1},{25,9},{2,18},{10... | collective-permute-start | bytes 1179656 | tf_op jit(solution)/shard_map/ppermute | solution.py:136
  59.6 34.5 %collective-permute-start.7 = (bf16[2,192,512]{2,1,0:T(8,128)(2,1)}, bf16[2,192,512]{2,1,0:T(8,128)(2,1)}, u32[]{:S(2)}, u32[]{:S(2)}) collective-permute-start(bf16[2,192,512]{2,1,0:T(8,128)(2,1)} %collective-permute-done.6.refs_2_.refs_6_), channel_id=1, source_target_pairs={{0,8},{8,0},{16,24},{24,16},{1,9},{9,1},{17,25},{25,17},{2,10},{10... | collective-permute-start | bytes 1179656 | tf_op jit(solution)/shard_map/ppermute | solution.py:180
  68.0 35.8 %collective-permute-start.5 = (bf16[2,192,512]{2,1,0:T(8,128)(2,1)}, bf16[2,192,512]{2,1,0:T(8,128)(2,1)}, u32[]{:S(2)}, u32[]{:S(2)}) collective-permute-start(bf16[2,192,512]{2,1,0:T(8,128)(2,1)} %collective-permute-done.4.refs_2_.refs_6_), channel_id=1, source_target_pairs={{0,8},{8,0},{16,24},{24,16},{1,9},{9,1},{17,25},{25,17},{2,10},{10... | collective-permute-start | bytes 1179656 | tf_op jit(solution)/shard_map/ppermute | solution.py:180
  92.9 16.0 %collective-permute-start.2 = (bf16[2,192,512]{2,1,0:T(8,128)(2,1)}, bf16[2,192,512]{2,1,0:T(8,128)(2,1)S(1)}, u32[]{:S(2)}, u32[]{:S(2)}) collective-permute-start(bf16[2,192,512]{2,1,0:T(8,128)(2,1)} %collective-permute-done.1.refs_2_.refs_6_), channel_id=1, source_target_pairs={{0,8},{8,0},{16,24},{24,16},{1,9},{9,1},{17,25},{25,17},{2,10},{10... | collective-permute-start | bytes 1179656 | tf_op jit(solution)/shard_map/ppermute | solution.py:180
  94.1 27.9 %collective-permute-start.13 = (bf16[2,192,256]{2,1,0:T(8,128)(2,1)}, bf16[2,192,256]{2,1,0:T(8,128)(2,1)S(1)}, u32[]{:S(2)}, u32[]{:S(2)}) collective-permute-start(bf16[2,192,256]{2,1,0:T(8,128)(2,1)} %collective-permute-done.12.refs_2_.refs_6_), channel_id=1, source_target_pairs={{0,8},{8,0},{16,24},{24,16},{1,9},{9,1},{17,25},{25,17},{2,10},{10... | collective-permute-start | bytes 589832 | tf_op jit(solution)/shard_map/ppermute | solution.py:180
  94.2 24.8 %collective-permute-start.11 = (bf16[2,192,256]{2,1,0:T(8,128)(2,1)}, bf16[2,192,256]{2,1,0:T(8,128)(2,1)S(1)}, u32[]{:S(2)}, u32[]{:S(2)}) collective-permute-start(bf16[2,192,256]{2,1,0:T(8,128)(2,1)} %collective-permute-done.10.refs_2_.refs_6_), channel_id=1, source_target_pairs={{0,8},{8,0},{16,24},{24,16},{1,9},{9,1},{17,25},{25,17},{2,10},{10... | collective-permute-start | bytes 589832 | tf_op jit(solution)/shard_map/ppermute | solution.py:180
  94.7 19.3 %collective-permute-start.9 = (bf16[2,192,512]{2,1,0:T(8,128)(2,1)}, bf16[2,192,512]{2,1,0:T(8,128)(2,1)S(1)}, u32[]{:S(2)}, u32[]{:S(2)}) collective-permute-start(bf16[2,192,512]{2,1,0:T(8,128)(2,1)} %collective-permute-done.8.refs_2_.refs_6_), channel_id=1, source_target_pairs={{0,8},{8,0},{16,24},{24,16},{1,9},{9,1},{17,25},{25,17},{2,10},{10... | collective-permute-start | bytes 1179656 | tf_op jit(solution)/shard_map/ppermute | solution.py:180
  94.8 1.0 copy-start.3
  95.8 0.9 copy-start.5
  96.7 0.7 copy-start.6
  103.8 5.1 %copy-start.4 = (f32[768,128]{1,0:T(8,128)S(1)}, f32[768,128]{1,0:T(8,128)}, u32[]{:S(2)}) copy-start(f32[768,128]{1,0:T(8,128)} %get-tuple-element.23.refs_10_) | copy-start | bytes 1179652
  122.0 3.2 %copy-start.17 = (bf16[192,2560]{1,0:T(8,128)(2,1)}, bf16[192,2560]{1,0:T(8,128)(2,1)S(1)}, u32[]{:S(2)}) copy-start(bf16[192,2560]{1,0:T(8,128)(2,1)S(1)} %constant_dynamic-update-slice_fusion.1) | copy-start | bytes 2949124
  (2 other events, 1.4 us)

commit v2 on v0

--- a/solution.py
+++ b/solution.py
@@ -1,19 +1,23 @@
+import functools
 import math
 
 import jax
 import jax.numpy as jnp
 from jax import lax
+from jax.experimental import pallas as pl
+from jax.experimental.pallas import tpu as pltpu
 from jax.sharding import PartitionSpec as P
 
 HD = 128
 D = 5120
 CLIPS = 4
-
-
 EPSILON = 1e-06
 NEGATIVE = -1e30
 ROTARY_BASE = 10000.0
 block_limit = 1024
+GROUP_HEADS = 4
+ACROSS = ((0, 2), (1, 3), (2, 0), (3, 1))
+BESIDE = ((0, 1), (1, 0), (2, 3), (3, 2))
 
 
 def lookup(lookup_table, positions):
@@ -21,6 +25,185 @@
     return jnp.sum(
         jnp.where(positions[:, None] == labels[None, :], lookup_table[None, :], 0), axis=1
     )
+
+
+def angles_of(offsets, clip_of, clip_grid):
+    sixth_part = HD // 6
+    first_dims = HD - 4 * sixth_part
+    first_freqs = 1.0 / ROTARY_BASE ** (
+        jnp.arange(0, first_dims, 2, dtype=jnp.float32) / first_dims
+    )
+    other_freqs = 1.0 / ROTARY_BASE ** (
+        jnp.arange(0, 2 * sixth_part, 2, dtype=jnp.float32) / (2 * sixth_part)
+    )
+    heights = lookup(clip_grid[:, 0], clip_of)
+    widths = lookup(clip_grid[:, 1], clip_of)
+    frame_pos = (offsets // (heights * widths)).astype(jnp.float32)[:, None]
+    line_pos = (offsets // widths % heights).astype(jnp.float32)[:, None]
+    column_pos = (offsets % widths).astype(jnp.float32)[:, None]
+    freqs = jnp.repeat(jnp.concatenate([first_freqs, other_freqs, other_freqs]), 2)[None, :]
+    feature = jnp.arange(HD, dtype=jnp.int32)[None, :]
+    position = jnp.where(
+        feature < first_dims,
+        frame_pos,
+        jnp.where(feature < first_dims + 2 * sixth_part, line_pos, column_pos),
+    )
+    return position * freqs
+
+
+def turn(x, gain, gain_s, swap, cosine, sine):
+    other = jnp.dot(x, swap, preferred_element_type=jnp.float32)
+    return ((x.astype(jnp.float32) * gain) * cosine + (other * gain_s) * sine).astype(jnp.bfloat16)
+
+
+def flip(gain):
+    size = gain.shape[1]
+    even = lax.broadcasted_iota(jnp.int32, gain.shape, 1) % 2 == 0
+    return jnp.where(even, pltpu.roll(gain, size - 1, 1), pltpu.roll(gain, 1, 1))
+
+
+def signed_swap():
+    at_row = lax.broadcasted_iota(jnp.int32, (HD, HD), 0)
+    at_column = lax.broadcasted_iota(jnp.int32, (HD, HD), 1)
+    sign = jnp.where(at_column % 2 == 0, -1.0, 1.0)
+    return jnp.where(at_row == (at_column ^ 1), sign, 0.0).astype(jnp.bfloat16)
+
+
+def attend_kernel(heads, scale, q_ref, k0, k1, f0, f1, v0, v1, cq, sq, ck, sk, gq, gk, qc, kc, o_ref, bias):
+    rows = q_ref.shape[0]
+    swap = signed_swap()
+    bias[...] = jnp.where(qc[...] == kc[...], 0.0, NEGATIVE).astype(jnp.float32)
+    for h in range(heads):
+        at = slice(h * HD, (h + 1) * HD)
+        gain_k = gk[:, at]
+        flip_k = flip(gain_k)
+        pieces = (k0[:, at], k1[:, at], f0[0, :, at], f1[0, :, at])
+        keys = jnp.concatenate(
+            [
+                turn(x, gain_k, flip_k, swap, ck[i * rows : (i + 1) * rows], sk[i * rows : (i + 1) * rows])
+                for i, x in enumerate(pieces)
+            ],
+            axis=0,
+        )
+        gain_q = gq[:, at]
+        q = turn(q_ref[:, at], gain_q, flip(gain_q), swap, cq[...], sq[...])
+        scores = (
+            lax.dot_general(q, keys, (((1,), (1,)), ((), ())), preferred_element_type=jnp.float32)
+            + bias[...]
+        )
+        peak = jnp.max(scores, axis=1, keepdims=True)
+        weights = jnp.exp2((scores - peak) * scale)
+        total = jnp.sum(weights, axis=1, keepdims=True)
+        values = jnp.concatenate([v0[:, at], v1[:, at], f0[1, :, at], f1[1, :, at]], axis=0)
+        out = jnp.dot(weights.astype(jnp.bfloat16), values, preferred_element_type=jnp.float32)
+        o_ref[:, at] = (out / total).astype(o_ref.dtype)
+
+
+def attend(group, heads, q, near, far, tables, gains, clips):
+    rows = q.shape[0]
+    cq, sq, ck, sk = tables
+    qc, kc = clips
+    tokens = ck.shape[0]
+    whole = lambda a: pl.BlockSpec(a.shape, lambda i: (0,) * a.ndim)
+    wide = pl.BlockSpec((rows, heads * HD), lambda i: (0, group))
+    gain_spec = pl.BlockSpec((1, heads * HD), lambda i: (0, group))
+    kernel = functools.partial(attend_kernel, heads, math.log2(math.e) / math.sqrt(HD))
+    return pl.pallas_call(
+        kernel,
+        grid=(1,),
+        out_shape=jax.ShapeDtypeStruct((rows, heads * HD), jnp.bfloat16),
+        in_specs=[wide, wide, wide, whole(far[0]), whole(far[1]), wide, wide]
+        + [whole(a) for a in (cq, sq, ck, sk)]
+        + [gain_spec] * 2
+        + [whole(qc), whole(kc)],
+        out_specs=pl.BlockSpec((rows, heads * HD), lambda i: (0, 0)),
+        scratch_shapes=[pltpu.VMEM((rows, tokens), jnp.float32)],
+        compiler_params=pltpu.CompilerParams(vmem_limit_bytes=40 * 1024 * 1024),
+        cost_estimate=pl.CostEstimate(
+            flops=4 * heads * rows * tokens * HD * 4,
+            bytes_accessed=heads * tokens * HD * 4 + tokens * HD * 8,
+            transcendentals=heads * rows * tokens,
+        ),
+    )(q, near[0][0], near[0][1], *far, near[1][0], near[1][1], cq, sq, ck, sk, *gains, qc, kc)
+
+
+def deal_kernel(groups, k_ref, v_ref, *refs):
+    outs, sems = refs[:groups], refs[groups]
+    wide = outs[0].shape[2]
+    copies = []
+    for g in range(groups):
+        at = slice(g * wide, (g + 1) * wide)
+        for i, ref in enumerate((k_ref, v_ref)):
+            copies.append(pltpu.make_async_copy(ref.at[:, at], outs[g].at[i], sems.at[2 * g + i]))
+    for copy in copies:
+        copy.start()
+    for copy in copies:
+        copy.wait()
+
+
+def deal(keys, values, heads):
+    rows, width = keys.shape
+    groups = width // (heads * HD)
+    spec = pl.BlockSpec(memory_space=pl.ANY)
+    return pl.pallas_call(
+        functools.partial(deal_kernel, groups),
+        out_shape=[jax.ShapeDtypeStruct((2, rows, heads * HD), keys.dtype)] * groups,
+        in_specs=[spec, spec],
+        out_specs=[spec] * groups,
+        scratch_shapes=[pltpu.SemaphoreType.DMA((2 * groups,))],
+    )(keys, values)
+
+
+def on_device(queries, keys, values, gain_q, gain_k, clip_ids, clip_grid):
+    rows, width = queries.shape
+    me = lax.axis_index("ctx")
+    tokens = 4 * rows
+
+    q32, k32 = queries.astype(jnp.float32), keys.astype(jnp.float32)
+    label = jnp.where(lax.axis_index("row") == 0, clip_ids, 0).astype(jnp.float32)
+    mine = jnp.stack([jnp.sum(q32 * q32, axis=1), jnp.sum(k32 * k32, axis=1), label])
+    mine_across = lax.ppermute(mine, "ctx", ACROSS)
+    heads = GROUP_HEADS
+    sends = deal(keys, values, heads)
+    far = [lax.ppermute(piece, "ctx", ACROSS) for piece in sends]
+    keys_beside = lax.ppermute(keys, "ctx", BESIDE)
+    values_beside = lax.ppermute(values, "ctx", BESIDE)
+    pair = jnp.stack([mine, mine_across])
+    pair_beside = lax.ppermute(pair, "ctx", BESIDE)
+    turned = lax.psum(
+        jnp.stack([pair[0], pair_beside[0], pair[1], pair_beside[1]], axis=1), "row"
+    ).reshape(3, tokens)
+    order = jnp.stack([me, me ^ 1, me ^ 2, me ^ 3])
+    clip_of = turned[2].astype(jnp.int32)
+    labels = jnp.arange(CLIPS, dtype=jnp.int32)
+    starts = jnp.sum((clip_of[:, None] < labels[None, :]).astype(jnp.int32), axis=0)
+    index = (order[:, None] * rows + jnp.arange(rows)[None, :]).reshape(tokens)
+    offsets = index - lookup(starts, clip_of)
+    angles = angles_of(offsets, clip_of, clip_grid)
+    cosine, sine = jnp.cos(angles), jnp.sin(angles)
+    q_scale = lax.rsqrt(turned[0, :rows] / D + EPSILON)[:, None]
+    k_scale = lax.rsqrt(turned[1] / D + EPSILON)[:, None]
+    tables = (
+        cosine[:rows] * q_scale,
+        sine[:rows] * q_scale,
+        cosine * k_scale,
+        sine * k_scale,
+    )
+
+    gains = (gain_q[None, :], gain_k[None, :])
+    clips = (clip_of[:rows, None], clip_of[None, :])
+
+    outs = []
+    for group, piece in enumerate(far):
+        passed = lax.ppermute(piece, "ctx", BESIDE)
+        outs.append(
+            attend(
+                group, heads, queries,
+                ((keys, keys_beside), (values, values_beside)),
+                (piece, passed), tables, gains, clips,
+            )
+        )
+    return jnp.concatenate(outs, axis=1)
 
 
 def spin(matrix, offsets, clip_of, clip_grid, head_size):
@@ -56,7 +239,7 @@
     return turned.reshape(row_count, -1)
 
 
-def on_device(queries, keys, values, gain_q, gain_k, clip_ids, clip_grid):
+def on_any(queries, keys, values, gain_q, gain_k, clip_ids, clip_grid):
     rows_here, width_here = queries.shape
     heads_here = width_here // HD
     score_scale = 1.0 / math.sqrt(HD)
@@ -135,5 +318,6 @@
     )
     out_specs = P(("batch", "ctx"), "row")
     return jax.shard_map(
-        on_device, mesh=mesh, in_specs=in_specs, out_specs=out_specs, check_vma=False
-    )
+        on_device if mesh.shape["ctx"] == 4 else on_any,
+        mesh=mesh, in_specs=in_specs, out_specs=out_specs, check_vma=False
+    )

time: 148 us -> 134 us (0.905)
  Pallas kernels: 0 us -> 79.6 us
  local copies, waits for them, and re-layouts: 34.4 us -> 2.58 us
  waiting for transfers between devices: 52.8 us -> 28.2 us
  other arithmetic: 21.4 us -> 6.54 us
  matrix products: 13.3 us -> 0 us
  between operations: 13.6 us -> 0.31 us
  starting transfers between devices: 0.22 us -> 8.26 us
  blocking collectives: 11.3 us -> 8.3 us
    pallas_call x0 -> x6, Pallas kernels: none -> 79.6 us  [the longest x1 60.7 us: deal(): pl.pallas_call(functools.partial(deal_kernel, groups), out_shape=[jax.Sha...]
    all_gather x2 -> x0, waiting for transfers between devices: 52.3 us -> none  [the longest x1 32.8 us: on_device(): key_piece = lax.all_gather(key_send, 'ctx', axis=0, tiled=True)]
    ppermute x0 -> x14, waiting for transfers between devices: none -> 28.2 us  [the longest x5 27.4 us: on_device(): far = [lax.ppermute(piece, 'ctx', ACROSS) for piece in sends]]
    dot_general x2 -> x0, matrix products: 13.3 us -> none  [the longest x1 8.9 us: on_device(): jnp.einsum('hqk,khd->qhd', weights.astype(jnp.bfloat16), value_view, pref...]
    all_gather x2 -> x0, local copies, waits for them, and re-layouts: 12.6 us -> none  [the longest x1 6.31 us: on_device(): value_piece = lax.all_gather(values, 'ctx', axis=0, tiled=True)]
    slice x4 -> x0, local copies, waits for them, and re-layouts: 11.5 us -> none  [spin(): jnp.roll(head_view, -1, axis=2)]
    ppermute x0 -> x14, starting transfers between devices: none -> 8.26 us  [the longest x5 4.28 us: on_device(): far = [lax.ppermute(piece, 'ctx', ACROSS) for piece in sends]]
    reduce_sum x5 -> x2, other arithmetic: 7.33 us -> 1.77 us  [the longest x1 1.49 us: on_device(): jnp.sum(k32 * k32, axis=1)]
  transfers between devices with their start and end apart: 2 -> 14, of which waited for: 2 -> 5; matrix products, arithmetic and copies ran while one was open for 10% -> 6% of each run, Pallas kernels for 0% -> 57%
where the time goes in v2:
time: 134 us
  Pallas kernels  79.6 us (59%)
  waiting for transfers between devices  28.2 us (21%)
  blocking collectives  8.3 us (6%)
  starting transfers between devices  8.26 us (6%)
  other arithmetic  6.54 us (5%)
  local copies, waits for them, and re-layouts  2.58 us (2%)
    pallas_call x1, Pallas kernels, deal(): pl.pallas_call(functools.partial(deal_kernel, groups), out_shape=[jax.Sha...  60.7 us
    ppermute x5, waiting for transfers between devices, on_device(): far = [lax.ppermute(piece, 'ctx', ACROSS) for piece in sends]  27.4 us
    pallas_call x5, Pallas kernels, attend(): pl.pallas_call(kernel, grid=(1,), out_shape=jax.ShapeDtypeStruct((rows, h...  18.9 us
    psum x1, blocking collectives, on_device(): lax.psum(jnp.stack([pair[0], pair_beside[0], pair[1], pair_beside[1]], ax...  8.3 us
    ppermute x5, starting transfers between devices, on_device(): far = [lax.ppermute(piece, 'ctx', ACROSS) for piece in sends]  4.28 us
    mul x1, other arithmetic, on_device(): sine * k_scale  2.95 us
  transfers between devices with their start and end apart: 14, of which 5 were waited for; matrix products, arithmetic and copies ran while one was open for 6% of the time, Pallas kernels for 57%

profile of v2, /device:TPU:0, one launch (start us, length us, event | category | flops | bytes accessed | tf_op | source)
XLA Modules:
  0.0 133.8 jit_solution(4351694931720100698)
XLA Ops:
  0.0 0.5 collective-permute-start
  0.5 1.5 %multiply_reduce_fusion = f32[192]{0:T(256)S(1)} fusion(bf16[192,2560]{1,0:T(8,128)(2,1)} %k0.9), kind=kLoop, calls=%fused_computation | loop fusion | flops 1474368 | bytes 983808 | tf_op jit(solution)/shard_map/reduce_sum | solution.py:164
  2.0 0.3 multiply_reduce_fusion.1
  2.3 2.6 %collective-permute-start.4 = (f32[3,192]{1,0:T(4,128)S(1)}, f32[3,192]{1,0:T(4,128)S(1)}, u32[]{:S(2)}, u32[]{:S(2)}) collective-permute-start(f32[3,192]{1,0:T(4,128)S(1)} %get-tuple-element.31), channel_id=1, source_target_pairs={{0,16},{8,24},{16,0},{24,8},{1,17},{9,25},{17,1},{25,9},{2,18},{10... | collective-permute-start | bytes 6920 | tf_op jit(solution)/shard_map/ppermute | solution.py:165
  4.9 0.2 collective-permute-start.3
  5.1 60.7 %shard_map.73 = (bf16[2,192,512]{2,1,0:T(8,128)(2,1)}, bf16[2,192,512]{2,1,0:T(8,128)(2,1)}, bf16[2,192,512]{2,1,0:T(8,128)(2,1)}, bf16[2,192,512]{2,1,0:T(8,128)(2,1)}, bf16[2,192,512]{2,1,0:T(8,128)(2,1)}) custom-call(bf16[192,2560]{1,0:T(8,128)(2,1)} %k0.9, bf16[192,2560]{1,0:T(8,128)(2,1)} %v0.9), custom_call_target="tpu_custom_call" | custom-call | tf_op jit(solution)/shard_map/pallas_call | solution.py:148
  65.9 0.4 collective-permute-start.1
  66.3 1.7 %collective-permute-start.6 = (bf16[2,192,512]{2,1,0:T(8,128)(2,1)}, bf16[2,192,512]{2,1,0:T(8,128)(2,1)}, u32[]{:S(2)}, u32[]{:S(2)}) collective-permute-start(bf16[2,192,512]{2,1,0:T(8,128)(2,1)} %get-tuple-element.11), channel_id=1, source_target_pairs={{0,16},{8,24},{16,0},{24,8},{1,17},{9,25},{17,1},{25,9},{2,18},{10... | collective-permute-start | bytes 1179656 | tf_op jit(solution)/shard_map/ppermute | solution.py:168
  68.6 0.1 mul.65
  68.7 0.7 collective-permute-done.5
  69.4 0.3 collective-permute-start.8
  69.8 8.3 %psum.7 = f32[3,4,192]{2,1,0:T(4,128)S(1)} all-reduce(f32[3,4,192]{2,1,0:T(4,128)S(1)} %pad_maximum_fusion), channel_id=1, replica_groups=mesh['ctx'=4,'row'=2,'batch'=4] {'row'}, use_global_device_ids=true, to_apply=%region_2.3 | all-reduce | flops 2304 | bytes 18432 | tf_op jit(solution)/shard_map/psum | solution.py:173
  78.2 0.1 select_reduce_fusion.1
  78.4 0.3 fusion.2
  78.7 0.1 reshape.181
  78.9 1.5 %collective-permute-start.10 = (bf16[2,192,512]{2,1,0:T(8,128)(2,1)}, bf16[2,192,512]{2,1,0:T(8,128)(2,1)}, u32[]{:S(2)}, u32[]{:S(2)}) collective-permute-start(bf16[2,192,512]{2,1,0:T(8,128)(2,1)} %get-tuple-element.13), channel_id=1, source_target_pairs={{0,16},{8,24},{16,0},{24,8},{1,17},{9,25},{17,1},{25,9},{2,18},{10... | collective-permute-start | bytes 1179656 | tf_op jit(solution)/shard_map/ppermute | solution.py:168
  80.4 3.0 %broadcast_multiply_fusion = (f32[768,128]{1,0:T(8,128)S(1)}, f32[768,128]{1,0:T(8,128)}, f32[768,128]{1,0:T(8,128)}, f32[768,128]{1,0:T(8,128)}) fusion(f32[768]{0:T(1024)S(1)} %rsqrt.23, f32[128]{0:T(128)S(1)} %mul.65, f32[768]{0:T(1024)S(1)} %get-tuple-element.26, f32[768]{0:T(1024)S(1)} %get-tuple-element.21, pred[128]{0:T(512)(128)(4,1)S(1)} %get-tuple-element.36, ...), kind=kLoop, calls=%fused_computation.5 | loop fusion | flops 491520 | bytes 1585920 | tf_op jit(solution)/shard_map/mul | solution.py:190
  83.3 3.3 %collective-permute-done.6.f0 = bf16[2,192,512]{2,1,0:T(8,128)(2,1)} collective-permute-done((bf16[2,192,512]{2,1,0:T(8,128)(2,1)}, bf16[2,192,512]{2,1,0:T(8,128)(2,1)}, u32[]{:S(2)}, u32[]{:S(2)}) %collective-permute-start.6) | collective-permute-done | bytes 393248 | tf_op jit(solution)/shard_map/ppermute | solution.py:168
  86.6 0.3 collective-permute-start.12
  87.0 8.1 %collective-permute-done.8.f0 = bf16[2,192,512]{2,1,0:T(8,128)(2,1)} collective-permute-done((bf16[2,192,512]{2,1,0:T(8,128)(2,1)}, bf16[2,192,512]{2,1,0:T(8,128)(2,1)}, u32[]{:S(2)}, u32[]{:S(2)}) %collective-permute-start.8) | collective-permute-done | bytes 393248 | tf_op jit(solution)/shard_map/ppermute | solution.py:168
  95.0 8.4 %collective-permute-done.10.f0 = bf16[2,192,512]{2,1,0:T(8,128)(2,1)} collective-permute-done((bf16[2,192,512]{2,1,0:T(8,128)(2,1)}, bf16[2,192,512]{2,1,0:T(8,128)(2,1)}, u32[]{:S(2)}, u32[]{:S(2)}) %collective-permute-start.10) | collective-permute-done | bytes 393248 | tf_op jit(solution)/shard_map/ppermute | solution.py:168
  103.5 0.1 copy.22.qc
  103.7 7.6 %collective-permute-done.12.f0 = bf16[2,192,512]{2,1,0:T(8,128)(2,1)} collective-permute-done((bf16[2,192,512]{2,1,0:T(8,128)(2,1)}, bf16[2,192,512]{2,1,0:T(8,128)(2,1)}, u32[]{:S(2)}, u32[]{:S(2)}) %collective-permute-start.12) | collective-permute-done | bytes 393248 | tf_op jit(solution)/shard_map/ppermute | solution.py:168
  111.3 1.0 slice_multiply_fusion
  112.4 0.6 collective-permute-start.11
  113.0 1.0 copy-done.2
  114.0 3.8 %shard_map.74 = bf16[192,512]{1,0:T(8,128)(2,1)S(1)} custom-call(bf16[192,2560]{1,0:T(8,128)(2,1)S(1)} %copy-done.1, bf16[192,2560]{1,0:T(8,128)(2,1)S(1)} %copy-done, bf16[192,2560]{1,0:T(8,128)(2,1)S(1)} %collective-permute-done.k1, bf16[2,192,512]{2,1,0:T(8,128)(2,1)} %collective-permute-done.1.f0, bf16[2,192,512]{2,1,0:T(8,128)(2,1)} %collective-permute-done.2.f1, ...), custom_call_target="tpu_custom_call" | custom-call | flops 1207959552 | bytes 2359296 | tf_op jit(solution)/shard_map/pallas_call | solution.py:111
  117.8 3.7 %shard_map.75 = bf16[192,512]{1,0:T(8,128)(2,1)S(1)} custom-call(bf16[192,2560]{1,0:T(8,128)(2,1)S(1)} %copy-done.1, bf16[192,2560]{1,0:T(8,128)(2,1)S(1)} %copy-done, bf16[192,2560]{1,0:T(8,128)(2,1)S(1)} %collective-permute-done.k1, bf16[2,192,512]{2,1,0:T(8,128)(2,1)} %collective-permute-done.6.f0, bf16[2,192,512]{2,1,0:T(8,128)(2,1)} %collective-permute-done.7.f1, ...), custom_call_target="tpu_custom_call" | custom-call | flops 1207959552 | bytes 2359296 | tf_op jit(solution)/shard_map/pallas_call | solution.py:111
  121.6 3.7 %shard_map.76 = bf16[192,512]{1,0:T(8,128)(2,1)S(1)} custom-call(bf16[192,2560]{1,0:T(8,128)(2,1)S(1)} %copy-done.1, bf16[192,2560]{1,0:T(8,128)(2,1)S(1)} %copy-done, bf16[192,2560]{1,0:T(8,128)(2,1)S(1)} %collective-permute-done.k1, bf16[2,192,512]{2,1,0:T(8,128)(2,1)} %collective-permute-done.8.f0, bf16[2,192,512]{2,1,0:T(8,128)(2,1)S(1)} %collective-permute-done.9.f1, ...), custom_call_target="tpu_custom_call" | custom-call | flops 1207959552 | bytes 2359296 | tf_op jit(solution)/shard_map/pallas_call | solution.py:111
  125.3 3.7 %shard_map.77 = bf16[192,512]{1,0:T(8,128)(2,1)S(1)} custom-call(bf16[192,2560]{1,0:T(8,128)(2,1)S(1)} %copy-done.1, bf16[192,2560]{1,0:T(8,128)(2,1)S(1)} %copy-done, bf16[192,2560]{1,0:T(8,128)(2,1)S(1)} %collective-permute-done.k1, bf16[2,192,512]{2,1,0:T(8,128)(2,1)} %collective-permute-done.10.f0, bf16[2,192,512]{2,1,0:T(8,128)(2,1)S(1)} %collective-permute-done.11.f1, ...), custom_call_target="tpu_custom_call" | custom-call | flops 1207959552 | bytes 2359296 | tf_op jit(solution)/shard_map/pallas_call | solution.py:111
  129.1 4.0 %shard_map.78 = bf16[192,512]{1,0:T(8,128)(2,1)S(1)} custom-call(bf16[192,2560]{1,0:T(8,128)(2,1)S(1)} %copy-done.1, bf16[192,2560]{1,0:T(8,128)(2,1)S(1)} %copy-done, bf16[192,2560]{1,0:T(8,128)(2,1)S(1)} %collective-permute-done.k1, bf16[2,192,512]{2,1,0:T(8,128)(2,1)} %collective-permute-done.12.f0, bf16[2,192,512]{2,1,0:T(8,128)(2,1)S(1)} %collective-permute-done.13.f1, ...), custom_call_target="tpu_custom_call" | custom-call | flops 1207959552 | bytes 2359296 | tf_op jit(solution)/shard_map/pallas_call | solution.py:111
  133.1 0.7 constant_dynamic-update-slice_fusion
  (62 shorter events, 1.1 us)
Async XLA Ops:
  0.0 1.9 %copy-start.1 = (bf16[192,2560]{1,0:T(8,128)(2,1)S(1)}, bf16[192,2560]{1,0:T(8,128)(2,1)}, u32[]{:S(2)}) copy-start(bf16[192,2560]{1,0:T(8,128)(2,1)} %q_ref.9) | copy-start | bytes 2949124
  0.0 113.0 %collective-permute-start = (bf16[192,2560]{1,0:T(8,128)(2,1)}, bf16[192,2560]{1,0:T(8,128)(2,1)S(1)}, u32[]{:S(2)}, u32[]{:S(2)}) collective-permute-start(bf16[192,2560]{1,0:T(8,128)(2,1)} %k0.9), channel_id=1, source_target_pairs={{0,8},{8,0},{16,24},{24,16},{1,9},{9,1},{17,25},{25,17},{2,10},{10... | collective-permute-start | bytes 2949128 | tf_op jit(solution)/shard_map/ppermute | solution.py:169
  0.5 1.8 %copy-start.7 = (s32[192]{0:T(256)S(1)}, s32[192]{0:T(256)}, u32[]{:S(2)}) copy-start(s32[192]{0:T(256)} %param.12) | copy-start | bytes 2308
  2.3 65.7 %copy-start.8 = (s32[4,2]{0,1:T(2,128)S(1)}, s32[4,2]{0,1:T(2,128)}, u32[]{:S(2)}) copy-start(s32[4,2]{0,1:T(2,128)} %param.13) | copy-start | bytes 100
  2.3 66.2 %copy-start.5 = (f32[2560]{0:T(1024)S(1)}, f32[2560]{0:T(1024)}, u32[]{:S(2)}) copy-start(f32[2560]{0:T(1024)} %param.10) | copy-start | bytes 30724
  2.3 66.2 %copy-start.6 = (f32[2560]{0:T(1024)S(1)}, f32[2560]{0:T(1024)}, u32[]{:S(2)}) copy-start(f32[2560]{0:T(1024)} %param.11) | copy-start | bytes 30724
  2.3 65.9 %collective-permute-start.4 = (f32[3,192]{1,0:T(4,128)S(1)}, f32[3,192]{1,0:T(4,128)S(1)}, u32[]{:S(2)}, u32[]{:S(2)}) collective-permute-start(f32[3,192]{1,0:T(4,128)S(1)} %get-tuple-element.31), channel_id=1, source_target_pairs={{0,16},{8,24},{16,0},{24,8},{1,17},{9,25},{17,1},{25,9},{2,18},{10... | collective-permute-start | bytes 6920 | tf_op jit(solution)/shard_map/ppermute | solution.py:165
  4.9 108.0 %collective-permute-start.3 = (bf16[192,2560]{1,0:T(8,128)(2,1)}, bf16[192,2560]{1,0:T(8,128)(2,1)}, u32[]{:S(2)}, u32[]{:S(2)}) collective-permute-start(bf16[192,2560]{1,0:T(8,128)(2,1)} %v0.9), channel_id=1, source_target_pairs={{0,8},{8,0},{16,24},{24,16},{1,9},{9,1},{17,25},{25,17},{2,10},{10... | collective-permute-start | bytes 2949128 | tf_op jit(solution)/shard_map/ppermute | solution.py:170
  65.9 13.0 %collective-permute-start.1 = (bf16[2,192,512]{2,1,0:T(8,128)(2,1)}, bf16[2,192,512]{2,1,0:T(8,128)(2,1)}, u32[]{:S(2)}, u32[]{:S(2)}) collective-permute-start(bf16[2,192,512]{2,1,0:T(8,128)(2,1)} %get-tuple-element.10), channel_id=1, source_target_pairs={{0,16},{8,24},{16,0},{24,8},{1,17},{9,25},{17,1},{25,9},{2,18},{10... | collective-permute-start | bytes 1179656 | tf_op jit(solution)/shard_map/ppermute | solution.py:168
  66.3 20.3 %collective-permute-start.6 = (bf16[2,192,512]{2,1,0:T(8,128)(2,1)}, bf16[2,192,512]{2,1,0:T(8,128)(2,1)}, u32[]{:S(2)}, u32[]{:S(2)}) collective-permute-start(bf16[2,192,512]{2,1,0:T(8,128)(2,1)} %get-tuple-element.11), channel_id=1, source_target_pairs={{0,16},{8,24},{16,0},{24,8},{1,17},{9,25},{17,1},{25,9},{2,18},{10... | collective-permute-start | bytes 1179656 | tf_op jit(solution)/shard_map/ppermute | solution.py:168
  68.2 1.2 collective-permute-start.5
  69.4 25.6 %collective-permute-start.8 = (bf16[2,192,512]{2,1,0:T(8,128)(2,1)}, bf16[2,192,512]{2,1,0:T(8,128)(2,1)}, u32[]{:S(2)}, u32[]{:S(2)}) collective-permute-start(bf16[2,192,512]{2,1,0:T(8,128)(2,1)} %get-tuple-element.12), channel_id=1, source_target_pairs={{0,16},{8,24},{16,0},{24,8},{1,17},{9,25},{17,1},{25,9},{2,18},{10... | collective-permute-start | bytes 1179656 | tf_op jit(solution)/shard_map/ppermute | solution.py:168
  78.9 24.6 %collective-permute-start.10 = (bf16[2,192,512]{2,1,0:T(8,128)(2,1)}, bf16[2,192,512]{2,1,0:T(8,128)(2,1)}, u32[]{:S(2)}, u32[]{:S(2)}) collective-permute-start(bf16[2,192,512]{2,1,0:T(8,128)(2,1)} %get-tuple-element.13), channel_id=1, source_target_pairs={{0,16},{8,24},{16,0},{24,8},{1,17},{9,25},{17,1},{25,9},{2,18},{10... | collective-permute-start | bytes 1179656 | tf_op jit(solution)/shard_map/ppermute | solution.py:168
  80.4 32.7 %copy-start = (bf16[192,2560]{1,0:T(8,128)(2,1)S(1)}, bf16[192,2560]{1,0:T(8,128)(2,1)}, u32[]{:S(2)}) copy-start(bf16[192,2560]{1,0:T(8,128)(2,1)} %k0.9) | copy-start | bytes 2949124
  86.6 24.7 %collective-permute-start.12 = (bf16[2,192,512]{2,1,0:T(8,128)(2,1)}, bf16[2,192,512]{2,1,0:T(8,128)(2,1)}, u32[]{:S(2)}, u32[]{:S(2)}) collective-permute-start(bf16[2,192,512]{2,1,0:T(8,128)(2,1)} %get-tuple-element.14), channel_id=1, source_target_pairs={{0,16},{8,24},{16,0},{24,8},{1,17},{9,25},{17,1},{25,9},{2,18},{10... | collective-permute-start | bytes 1179656 | tf_op jit(solution)/shard_map/ppermute | solution.py:168
  95.0 17.3 %collective-permute-start.2 = (bf16[2,192,512]{2,1,0:T(8,128)(2,1)}, bf16[2,192,512]{2,1,0:T(8,128)(2,1)}, u32[]{:S(2)}, u32[]{:S(2)}) collective-permute-start(bf16[2,192,512]{2,1,0:T(8,128)(2,1)} %collective-permute-done.1.f0), channel_id=1, source_target_pairs={{0,8},{8,0},{16,24},{24,16},{1,9},{9,1},{17,25},{25,17},{2,10},{10... | collective-permute-start | bytes 1179656 | tf_op jit(solution)/shard_map/ppermute | solution.py:198
  103.5 14.4 %collective-permute-start.7 = (bf16[2,192,512]{2,1,0:T(8,128)(2,1)}, bf16[2,192,512]{2,1,0:T(8,128)(2,1)}, u32[]{:S(2)}, u32[]{:S(2)}) collective-permute-start(bf16[2,192,512]{2,1,0:T(8,128)(2,1)} %collective-permute-done.6.f0), channel_id=1, source_target_pairs={{0,8},{8,0},{16,24},{24,16},{1,9},{9,1},{17,25},{25,17},{2,10},{10... | collective-permute-start | bytes 1179656 | tf_op jit(solution)/shard_map/ppermute | solution.py:198
  111.3 10.3 %collective-permute-start.9 = (bf16[2,192,512]{2,1,0:T(8,128)(2,1)}, bf16[2,192,512]{2,1,0:T(8,128)(2,1)S(1)}, u32[]{:S(2)}, u32[]{:S(2)}) collective-permute-start(bf16[2,192,512]{2,1,0:T(8,128)(2,1)} %collective-permute-done.8.f0), channel_id=1, source_target_pairs={{0,8},{8,0},{16,24},{24,16},{1,9},{9,1},{17,25},{25,17},{2,10},{10... | collective-permute-start | bytes 1179656 | tf_op jit(solution)/shard_map/ppermute | solution.py:198
  112.4 12.9 %collective-permute-start.11 = (bf16[2,192,512]{2,1,0:T(8,128)(2,1)}, bf16[2,192,512]{2,1,0:T(8,128)(2,1)S(1)}, u32[]{:S(2)}, u32[]{:S(2)}) collective-permute-start(bf16[2,192,512]{2,1,0:T(8,128)(2,1)} %collective-permute-done.10.f0), channel_id=1, source_target_pairs={{0,8},{8,0},{16,24},{24,16},{1,9},{9,1},{17,25},{25,17},{2,10},{10... | collective-permute-start | bytes 1179656 | tf_op jit(solution)/shard_map/ppermute | solution.py:198
  112.9 16.1 %collective-permute-start.13 = (bf16[2,192,512]{2,1,0:T(8,128)(2,1)}, bf16[2,192,512]{2,1,0:T(8,128)(2,1)S(1)}, u32[]{:S(2)}, u32[]{:S(2)}) collective-permute-start(bf16[2,192,512]{2,1,0:T(8,128)(2,1)} %collective-permute-done.12.f0), channel_id=1, source_target_pairs={{0,8},{8,0},{16,24},{24,16},{1,9},{9,1},{17,25},{25,17},{2,10},{10... | collective-permute-start | bytes 1179656 | tf_op jit(solution)/shard_map/ppermute | solution.py:198
  113.0 1.0 copy-start.2
  114.0 3.8 %copy-start.3 = (f32[768,128]{1,0:T(8,128)S(1)}, f32[768,128]{1,0:T(8,128)}, u32[]{:S(2)}) copy-start(f32[768,128]{1,0:T(8,128)} %get-tuple-element.19.ck) | copy-start | bytes 1179652
  129.0 4.0 %copy-start.4 = (bf16[192,2560]{1,0:T(8,128)(2,1)}, bf16[192,2560]{1,0:T(8,128)(2,1)S(1)}, u32[]{:S(2)}) copy-start(bf16[192,2560]{1,0:T(8,128)(2,1)S(1)} %constant_dynamic-update-slice_fusion.1) | copy-start | bytes 2949124

commit v3 on v2

--- a/solution.py
+++ b/solution.py
@@ -127,30 +127,21 @@
     )(q, near[0][0], near[0][1], *far, near[1][0], near[1][1], cq, sq, ck, sk, *gains, qc, kc)
 
 
-def deal_kernel(groups, k_ref, v_ref, *refs):
-    outs, sems = refs[:groups], refs[groups]
+def deal_kernel(k_ref, v_ref, *outs):
     wide = outs[0].shape[2]
-    copies = []
-    for g in range(groups):
+    for g, out in enumerate(outs):
         at = slice(g * wide, (g + 1) * wide)
-        for i, ref in enumerate((k_ref, v_ref)):
-            copies.append(pltpu.make_async_copy(ref.at[:, at], outs[g].at[i], sems.at[2 * g + i]))
-    for copy in copies:
-        copy.start()
-    for copy in copies:
-        copy.wait()
+        out[0] = k_ref[:, at]
+        out[1] = v_ref[:, at]
 
 
 def deal(keys, values, heads):
     rows, width = keys.shape
     groups = width // (heads * HD)
-    spec = pl.BlockSpec(memory_space=pl.ANY)
     return pl.pallas_call(
-        functools.partial(deal_kernel, groups),
+        deal_kernel,
         out_shape=[jax.ShapeDtypeStruct((2, rows, heads * HD), keys.dtype)] * groups,
-        in_specs=[spec, spec],
-        out_specs=[spec] * groups,
-        scratch_shapes=[pltpu.SemaphoreType.DMA((2 * groups,))],
+        compiler_params=pltpu.CompilerParams(vmem_limit_bytes=24 * 1024 * 1024),
     )(keys, values)
 
 
@@ -195,6 +186,8 @@
 
     outs = []
     for group, piece in enumerate(far):
+        if group >= 2:
+            piece, outs[group - 2] = lax.optimization_barrier((piece, outs[group - 2]))
         passed = lax.ppermute(piece, "ctx", BESIDE)
         outs.append(
             attend(

time: 134 us -> 68.7 us (0.51)
  Pallas kernels: 79.6 us -> 20 us
  waiting for transfers between devices: 28.2 us -> 14.8 us
  local copies, waits for them, and re-layouts: 2.58 us -> 11 us
    pallas_call x1, Pallas kernels: 60.7 us -> 1.24 us  [deal(): pl.pallas_call(deal_kernel, out_shape=[jax.ShapeDtypeStruct((2, rows, hea...]
    ppermute x5, waiting for transfers between devices: 27.4 us -> 14.6 us  [on_device(): far = [lax.ppermute(piece, 'ctx', ACROSS) for piece in sends]]
    unnamed x22 -> x42, local copies, waits for them, and re-layouts: 1.1 us -> 6.39 us
    broadcast_in_dim x2, local copies, waits for them, and re-layouts: 0.12 us -> 2.02 us  [on_device(): clips = (clip_of[:rows, None], clip_of[None, :])]
  transfers between devices with their start and end apart: 14 -> 14, of which waited for: 5 -> 4; matrix products, arithmetic and copies ran while one was open for 6% -> 14% of each run, Pallas kernels for 57% -> 24%
where the time goes in v3:
time: 68.7 us; the launch traced here: 68.1 us
  Pallas kernels  20 us (29%)
  waiting for transfers between devices  14.8 us (22%)
  local copies, waits for them, and re-layouts  11 us (16%)
  starting transfers between devices  8.37 us (12%)
  blocking collectives  8.29 us (12%)
  other arithmetic  5.35 us (8%)
    pallas_call x5, Pallas kernels, attend(): pl.pallas_call(kernel, grid=(1,), out_shape=jax.ShapeDtypeStruct((rows, h...  18.7 us
    ppermute x5, waiting for transfers between devices, on_device(): far = [lax.ppermute(piece, 'ctx', ACROSS) for piece in sends]  14.6 us
    psum x1, blocking collectives, on_device(): lax.psum(jnp.stack([pair[0], pair_beside[0], pair[1], pair_beside[1]], ax...  8.29 us
    unnamed x42, local copies, waits for them, and re-layouts  6.39 us
    ppermute x5, starting transfers between devices, on_device(): far = [lax.ppermute(piece, 'ctx', ACROSS) for piece in sends]  4.41 us
    mul x1, other arithmetic, on_device(): sine * k_scale  2.63 us
    ppermute x1, starting transfers between devices, on_device(): mine_across = lax.ppermute(mine, 'ctx', ACROSS)  2.62 us
    broadcast_in_dim x2, local copies, waits for them, and re-layouts, on_device(): clips = (clip_of[:rows, None], clip_of[None, :])  2.02 us
  transfers between devices with their start and end apart: 14, of which 4 were waited for; matrix products, arithmetic and copies ran while one was open for 14% of the time, Pallas kernels for 24%

profile of v3, /device:TPU:0, one launch (start us, length us, event | category | flops | bytes accessed | tf_op | source)
XLA Modules:
  0.0 68.1 jit_solution(15919386613726634765)
XLA Ops:
  0.0 0.5 collective-permute-start.1
  0.5 1.6 %multiply_reduce_fusion = f32[192]{0:T(256)S(1)} fusion(bf16[192,2560]{1,0:T(8,128)(2,1)} %k0.9), kind=kLoop, calls=%fused_computation | loop fusion | flops 1474368 | bytes 983808 | tf_op jit(solution)/shard_map/reduce_sum | solution.py:155
  2.4 2.6 %collective-permute-start.5 = (f32[3,192]{1,0:T(4,128)S(1)}, f32[3,192]{1,0:T(4,128)S(1)}, u32[]{:S(2)}, u32[]{:S(2)}) collective-permute-start(f32[3,192]{1,0:T(4,128)S(1)} %get-tuple-element.43), channel_id=1, source_target_pairs={{0,16},{8,24},{16,0},{24,8},{1,17},{9,25},{17,1},{25,9},{2,18},{10... | collective-permute-start | bytes 6920 | tf_op jit(solution)/shard_map/ppermute | solution.py:156
  5.1 1.2 %copy-done.2 = bf16[192,2560]{1,0:T(8,128)(2,1)S(1)} copy-done((bf16[192,2560]{1,0:T(8,128)(2,1)S(1)}, bf16[192,2560]{1,0:T(8,128)(2,1)}, u32[]{:S(2)}) %copy-start.2) | copy-done | bytes 983064
  6.3 1.2 %shard_map.73 = (bf16[2,192,512]{2,1,0:T(8,128)(2,1)}, bf16[2,192,512]{2,1,0:T(8,128)(2,1)}, bf16[2,192,512]{2,1,0:T(8,128)(2,1)}, bf16[2,192,512]{2,1,0:T(8,128)(2,1)}, bf16[2,192,512]{2,1,0:T(8,128)(2,1)S(1)}) custom-call(bf16[192,2560]{1,0:T(8,128)(2,1)S(1)} %copy-done, bf16[192,2560]{1,0:T(8,128)(2,1)S(1)} %copy-done.2), custom_call_target="tpu_custom_call" | custom-call | tf_op jit(solution)/shard_map/pallas_call | solution.py:141
  7.6 0.8 %copy-done.11 = bf16[2,192,512]{2,1,0:T(8,128)(2,1)} copy-done((bf16[2,192,512]{2,1,0:T(8,128)(2,1)}, bf16[2,192,512]{2,1,0:T(8,128)(2,1)S(1)}, u32[]{:S(2)}) %copy-start.11) | copy-done | bytes 393240
  8.3 0.4 collective-permute-start
  8.7 1.7 %collective-permute-start.2 = (bf16[2,192,512]{2,1,0:T(8,128)(2,1)}, bf16[2,192,512]{2,1,0:T(8,128)(2,1)}, u32[]{:S(2)}, u32[]{:S(2)}) collective-permute-start(bf16[2,192,512]{2,1,0:T(8,128)(2,1)} %get-tuple-element.17), channel_id=1, source_target_pairs={{0,16},{8,24},{16,0},{24,8},{1,17},{9,25},{17,1},{25,9},{2,18},{10... | collective-permute-start | bytes 1179656 | tf_op jit(solution)/shard_map/ppermute | solution.py:159
  10.9 0.6 broadcast_in_dim.119.gk
  11.9 0.3 collective-permute-start.8
  12.2 8.3 %psum.7 = f32[3,4,192]{2,1,0:T(4,128)S(1)} all-reduce(f32[3,4,192]{2,1,0:T(4,128)S(1)} %pad_maximum_fusion), channel_id=1, replica_groups=mesh['ctx'=4,'row'=2,'batch'=4] {'row'}, use_global_device_ids=true, to_apply=%region_2.3 | all-reduce | flops 2304 | bytes 18432 | tf_op jit(solution)/shard_map/psum | solution.py:164
  21.3 2.6 %broadcast_multiply_fusion = (f32[768,128]{1,0:T(8,128)S(1)}, f32[768,128]{1,0:T(8,128)}, f32[768,128]{1,0:T(8,128)S(1)}, f32[768,128]{1,0:T(8,128)S(1)}) fusion(f32[768]{0:T(1024)S(1)} %rsqrt.23, f32[128]{0:T(128)S(1)} %mul.65, f32[768]{0:T(1024)S(1)} %get-tuple-element.38, f32[768]{0:T(1024)S(1)} %get-tuple-element.33, ...), kind=kLoop, calls=%fused_computation.5 | loop fusion | flops 491520 | bytes 1585920 | tf_op jit(solution)/shard_map/mul | solution.py:181
  23.9 5.1 %collective-permute-done.2.f0 = bf16[2,192,512]{2,1,0:T(8,128)(2,1)} collective-permute-done((bf16[2,192,512]{2,1,0:T(8,128)(2,1)}, bf16[2,192,512]{2,1,0:T(8,128)(2,1)}, u32[]{:S(2)}, u32[]{:S(2)}) %collective-permute-start.2) | collective-permute-done | bytes 393248 | tf_op jit(solution)/shard_map/ppermute | solution.py:159
  29.1 7.7 %collective-permute-done.8.f0 = bf16[2,192,512]{2,1,0:T(8,128)(2,1)} collective-permute-done((bf16[2,192,512]{2,1,0:T(8,128)(2,1)}, bf16[2,192,512]{2,1,0:T(8,128)(2,1)}, u32[]{:S(2)}, u32[]{:S(2)}) %collective-permute-start.8) | collective-permute-done | bytes 393248 | tf_op jit(solution)/shard_map/ppermute | solution.py:159
  36.9 0.3 collective-permute-start.7
  37.2 0.7 %copy-done.8 = bf16[2,192,512]{2,1,0:T(8,128)(2,1)} copy-done((bf16[2,192,512]{2,1,0:T(8,128)(2,1)}, bf16[2,192,512]{2,1,0:T(8,128)(2,1)S(1)}, u32[]{:S(2)}) %copy-start.8) | copy-done | bytes 393240
  37.9 0.6 slice_bitcast_fusion.2
  38.5 0.8 %convert_element_type.62.kc = s32[1,768]{1,0:T(1,128)S(1)} reshape(s32[1,4,192]{2,1,0:T(4,128)} %copy-done.13) | data formatting | bytes 6144 | tf_op jit(solution)/shard_map/convert_element_type | solution.py:168
  39.3 1.4 %copy.22.qc = s32[192,1]{1,0:T(8,128)} copy(s32[192,1]{0,1:T(1,128)} %slice_bitcast_fusion.2) | data formatting | bytes 1536 | tf_op jit(solution)/shard_map/broadcast_in_dim | solution.py:185
  40.7 1.0 %copy-done.4 = f32[768,128]{1,0:T(8,128)S(1)} copy-done((f32[768,128]{1,0:T(8,128)S(1)}, f32[768,128]{1,0:T(8,128)}, u32[]{:S(2)}) %copy-start.4) | copy-done | bytes 393240
  41.7 0.9 %copy-done.6 = s32[192,1]{1,0:T(8,128)S(1)} copy-done((s32[192,1]{1,0:T(8,128)S(1)}, s32[192,1]{1,0:T(8,128)}, u32[]{:S(2)}) %copy-start.6) | copy-done | bytes 792
  42.6 1.0 %copy-done.9 = bf16[2,192,512]{2,1,0:T(8,128)(2,1)S(1)} copy-done((bf16[2,192,512]{2,1,0:T(8,128)(2,1)S(1)}, bf16[2,192,512]{2,1,0:T(8,128)(2,1)}, u32[]{:S(2)}) %copy-start.9) | copy-done | bytes 393240
  43.6 0.7 %copy-done.10 = f32[1,2560]{1,0:T(1,128)S(1)} copy-done((f32[1,2560]{1,0:T(1,128)S(1)}, f32[1,2560]{1,0:T(1,128)}, u32[]{:S(2)}) %copy-start.10) | copy-done | bytes 10264
  44.3 3.7 %shard_map.74 = bf16[192,512]{1,0:T(8,128)(2,1)S(1)} custom-call(bf16[192,2560]{1,0:T(8,128)(2,1)S(1)} %copy-done.1, bf16[192,2560]{1,0:T(8,128)(2,1)S(1)} %copy-done, bf16[192,2560]{1,0:T(8,128)(2,1)} %collective-permute-done.1.k1, bf16[2,192,512]{2,1,0:T(8,128)(2,1)} %collective-permute-done.2.f0, bf16[2,192,512]{2,1,0:T(8,128)(2,1)S(1)} %copy-done.9, ...), custom_call_target="tpu_custom_call" | custom-call | flops 1207959552 | bytes 2359296 | tf_op jit(solution)/shard_map/pallas_call | solution.py:111
  48.1 0.6 collective-permute-start.11
  48.6 1.7 %collective-permute-start.10 = (bf16[2,192,512]{2,1,0:T(8,128)(2,1)S(1)}, bf16[2,192,512]{2,1,0:T(8,128)(2,1)S(1)}, u32[]{:S(2)}, u32[]{:S(2)}) collective-permute-start(bf16[2,192,512]{2,1,0:T(8,128)(2,1)S(1)} %copy-done.12), channel_id=1, source_target_pairs={{0,16},{8,24},{16,0},{24,8},{1,17},{9,25},{17,1},{25,9},{2,18},{10... | collective-permute-start | bytes 1179656 | tf_op jit(solution)/shard_map/ppermute | solution.py:159
  50.4 3.8 %shard_map.75 = bf16[192,512]{1,0:T(8,128)(2,1)S(1)} custom-call(bf16[192,2560]{1,0:T(8,128)(2,1)S(1)} %copy-done.1, bf16[192,2560]{1,0:T(8,128)(2,1)S(1)} %copy-done, bf16[192,2560]{1,0:T(8,128)(2,1)} %collective-permute-done.1.k1, bf16[2,192,512]{2,1,0:T(8,128)(2,1)} %collective-permute-done.8.f0, bf16[2,192,512]{2,1,0:T(8,128)(2,1)} %collective-permute-done.9.f1, ...), custom_call_target="tpu_custom_call" | custom-call | flops 1207959552 | bytes 2359296 | tf_op jit(solution)/shard_map/pallas_call | solution.py:111
  54.3 3.7 %shard_map.76 = bf16[192,512]{1,0:T(8,128)(2,1)S(1)} custom-call(bf16[192,2560]{1,0:T(8,128)(2,1)S(1)} %copy-done.1, bf16[192,2560]{1,0:T(8,128)(2,1)S(1)} %copy-done, bf16[192,2560]{1,0:T(8,128)(2,1)} %collective-permute-done.1.k1, bf16[2,192,512]{2,1,0:T(8,128)(2,1)} %collective-permute-done.f0, bf16[2,192,512]{2,1,0:T(8,128)(2,1)S(1)} %collective-permute-done.11.f1, ...), custom_call_target="tpu_custom_call" | custom-call | flops 1207959552 | bytes 2359296 | tf_op jit(solution)/shard_map/pallas_call | solution.py:111
  58.0 1.8 %collective-permute-done.10.f0 = bf16[2,192,512]{2,1,0:T(8,128)(2,1)S(1)} collective-permute-done((bf16[2,192,512]{2,1,0:T(8,128)(2,1)S(1)}, bf16[2,192,512]{2,1,0:T(8,128)(2,1)S(1)}, u32[]{:S(2)}, u32[]{:S(2)}) %collective-permute-start.10) | collective-permute-done | bytes 393248 | tf_op jit(solution)/shard_map/ppermute | solution.py:159
  59.8 3.7 %shard_map.77 = bf16[192,512]{1,0:T(8,128)(2,1)S(1)} custom-call(bf16[192,2560]{1,0:T(8,128)(2,1)S(1)} %copy-done.1, bf16[192,2560]{1,0:T(8,128)(2,1)S(1)} %copy-done, bf16[192,2560]{1,0:T(8,128)(2,1)} %collective-permute-done.1.k1, bf16[2,192,512]{2,1,0:T(8,128)(2,1)} %collective-permute-done.7.f0, bf16[2,192,512]{2,1,0:T(8,128)(2,1)S(1)} %collective-permute-done.12.f1, ...), custom_call_target="tpu_custom_call" | custom-call | flops 1207959552 | bytes 2359296 | tf_op jit(solution)/shard_map/pallas_call | solution.py:111
  63.5 3.9 %shard_map.78 = bf16[192,512]{1,0:T(8,128)(2,1)S(1)} custom-call(bf16[192,2560]{1,0:T(8,128)(2,1)S(1)} %copy-done.1, bf16[192,2560]{1,0:T(8,128)(2,1)S(1)} %copy-done, bf16[192,2560]{1,0:T(8,128)(2,1)} %collective-permute-done.1.k1, bf16[2,192,512]{2,1,0:T(8,128)(2,1)S(1)} %collective-permute-done.10.f0, ...), custom_call_target="tpu_custom_call" | custom-call | flops 1207959552 | bytes 2359296 | tf_op jit(solution)/shard_map/pallas_call | solution.py:111
  67.4 0.7 %constant_dynamic-update-slice_fusion = bf16[192,2560]{1,0:T(8,128)(2,1)} fusion(bf16[192,2560]{1,0:T(8,128)(2,1)} %copy-done.14, bf16[192,512]{1,0:T(8,128)(2,1)S(1)} %shard_map.78), kind=kLoop, calls=%fused_computation.16 | loop fusion | bytes 393216 | tf_op jit(solution)/shard_map/concatenate | solution.py:199
  (82 shorter events, 2.3 us)
Async XLA Ops:
  0.0 2.0 %copy-start.1 = (bf16[192,2560]{1,0:T(8,128)(2,1)S(1)}, bf16[192,2560]{1,0:T(8,128)(2,1)}, u32[]{:S(2)}) copy-start(bf16[192,2560]{1,0:T(8,128)(2,1)} %q_ref.9) | copy-start | bytes 2949124
  0.0 40.7 %collective-permute-start.1 = (bf16[192,2560]{1,0:T(8,128)(2,1)}, bf16[192,2560]{1,0:T(8,128)(2,1)}, u32[]{:S(2)}, u32[]{:S(2)}) collective-permute-start(bf16[192,2560]{1,0:T(8,128)(2,1)} %k0.9), channel_id=1, source_target_pairs={{0,8},{8,0},{16,24},{24,16},{1,9},{9,1},{17,25},{25,17},{2,10},{10... | collective-permute-start | bytes 2949128 | tf_op jit(solution)/shard_map/ppermute | solution.py:160
  0.5 1.9 %copy-start.17 = (s32[192]{0:T(256)S(1)}, s32[192]{0:T(256)}, u32[]{:S(2)}) copy-start(s32[192]{0:T(256)} %param.12) | copy-start | bytes 2308
  0.5 4.7 %copy-start = (bf16[192,2560]{1,0:T(8,128)(2,1)S(1)}, bf16[192,2560]{1,0:T(8,128)(2,1)}, u32[]{:S(2)}) copy-start(bf16[192,2560]{1,0:T(8,128)(2,1)} %k0.9) | copy-start | bytes 2949124
  2.3 8.1 %copy-start.18 = (s32[4,2]{0,1:T(2,128)S(1)}, s32[4,2]{0,1:T(2,128)}, u32[]{:S(2)}) copy-start(s32[4,2]{0,1:T(2,128)} %param.13) | copy-start | bytes 100
  2.4 8.2 %collective-permute-start.5 = (f32[3,192]{1,0:T(4,128)S(1)}, f32[3,192]{1,0:T(4,128)S(1)}, u32[]{:S(2)}, u32[]{:S(2)}) collective-permute-start(f32[3,192]{1,0:T(4,128)S(1)} %get-tuple-element.43), channel_id=1, source_target_pairs={{0,16},{8,24},{16,0},{24,8},{1,17},{9,25},{17,1},{25,9},{2,18},{10... | collective-permute-start | bytes 6920 | tf_op jit(solution)/shard_map/ppermute | solution.py:156
  5.0 35.7 %collective-permute-start.4 = (bf16[192,2560]{1,0:T(8,128)(2,1)}, bf16[192,2560]{1,0:T(8,128)(2,1)}, u32[]{:S(2)}, u32[]{:S(2)}) collective-permute-start(bf16[192,2560]{1,0:T(8,128)(2,1)} %v0.9), channel_id=1, source_target_pairs={{0,8},{8,0},{16,24},{24,16},{1,9},{9,1},{17,25},{25,17},{2,10},{10... | collective-permute-start | bytes 2949128 | tf_op jit(solution)/shard_map/ppermute | solution.py:161
  5.1 1.2 %copy-start.2 = (bf16[192,2560]{1,0:T(8,128)(2,1)S(1)}, bf16[192,2560]{1,0:T(8,128)(2,1)}, u32[]{:S(2)}) copy-start(bf16[192,2560]{1,0:T(8,128)(2,1)} %v0.9) | copy-start | bytes 2949124
  6.3 4.5 %copy-start.15 = (f32[2560]{0:T(1024)S(1)}, f32[2560]{0:T(1024)}, u32[]{:S(2)}) copy-start(f32[2560]{0:T(1024)} %param.10) | copy-start | bytes 30724
  6.3 4.5 %copy-start.16 = (f32[2560]{0:T(1024)S(1)}, f32[2560]{0:T(1024)}, u32[]{:S(2)}) copy-start(f32[2560]{0:T(1024)} %param.11) | copy-start | bytes 30724
  7.6 0.8 %copy-start.11 = (bf16[2,192,512]{2,1,0:T(8,128)(2,1)}, bf16[2,192,512]{2,1,0:T(8,128)(2,1)S(1)}, u32[]{:S(2)}) copy-start(bf16[2,192,512]{2,1,0:T(8,128)(2,1)S(1)} %get-tuple-element.22) | copy-start | bytes 1179652
  8.3 39.7 %collective-permute-start = (bf16[2,192,512]{2,1,0:T(8,128)(2,1)}, bf16[2,192,512]{2,1,0:T(8,128)(2,1)}, u32[]{:S(2)}, u32[]{:S(2)}) collective-permute-start(bf16[2,192,512]{2,1,0:T(8,128)(2,1)} %get-tuple-element.16), channel_id=1, source_target_pairs={{0,16},{8,24},{16,0},{24,8},{1,17},{9,25},{17,1},{25,9},{2,18},{10... | collective-permute-start | bytes 1179656 | tf_op jit(solution)/shard_map/ppermute | solution.py:159
  8.7 20.3 %collective-permute-start.2 = (bf16[2,192,512]{2,1,0:T(8,128)(2,1)}, bf16[2,192,512]{2,1,0:T(8,128)(2,1)}, u32[]{:S(2)}, u32[]{:S(2)}) collective-permute-start(bf16[2,192,512]{2,1,0:T(8,128)(2,1)} %get-tuple-element.17), channel_id=1, source_target_pairs={{0,16},{8,24},{16,0},{24,8},{1,17},{9,25},{17,1},{25,9},{2,18},{10... | collective-permute-start | bytes 1179656 | tf_op jit(solution)/shard_map/ppermute | solution.py:159
  10.6 1.2 %collective-permute-start.6 = (f32[2,3,192]{2,0,1:T(2,128)S(1)}, f32[2,3,192]{2,0,1:T(2,128)S(1)}, u32[]{:S(2)}, u32[]{:S(2)}) collective-permute-start(f32[2,3,192]{2,0,1:T(2,128)S(1)} %pad_maximum_fusion.1), channel_id=1, source_target_pairs={{0,8},{8,0},{16,24},{24,16},{1,9},{9,1},{17,25},{25,17},{2,10},{10... | collective-permute-start | bytes 13832 | tf_op jit(solution)/shard_map/ppermute | solution.py:163
  11.9 25.0 %collective-permute-start.8 = (bf16[2,192,512]{2,1,0:T(8,128)(2,1)}, bf16[2,192,512]{2,1,0:T(8,128)(2,1)}, u32[]{:S(2)}, u32[]{:S(2)}) collective-permute-start(bf16[2,192,512]{2,1,0:T(8,128)(2,1)} %get-tuple-element.20), channel_id=1, source_target_pairs={{0,16},{8,24},{16,0},{24,8},{1,17},{9,25},{17,1},{25,9},{2,18},{10... | collective-permute-start | bytes 1179656 | tf_op jit(solution)/shard_map/ppermute | solution.py:159
  20.5 17.4 %copy-start.13 = (s32[1,4,192]{2,1,0:T(4,128)}, s32[1,4,192]{2,1,0:T(4,128)S(1)}, u32[]{:S(2)}) copy-start(s32[1,4,192]{2,1,0:T(4,128)S(1)} %get-tuple-element.37) | copy-start | bytes 9220
  21.3 19.4 %copy-start.3 = (bf16[192,2560]{1,0:T(8,128)(2,1)S(1)}, bf16[192,2560]{1,0:T(8,128)(2,1)}, u32[]{:S(2)}) copy-start(bf16[192,2560]{1,0:T(8,128)(2,1)} %v0.9) | copy-start | bytes 2949124
  29.0 8.1 %collective-permute-start.3 = (bf16[2,192,512]{2,1,0:T(8,128)(2,1)}, bf16[2,192,512]{2,1,0:T(8,128)(2,1)S(1)}, u32[]{:S(2)}, u32[]{:S(2)}) collective-permute-start(bf16[2,192,512]{2,1,0:T(8,128)(2,1)} %collective-permute-done.2.f0), channel_id=1, source_target_pairs={{0,8},{8,0},{16,24},{24,16},{1,9},{9,1},{17,25},{25,17},{2,10},{10... | collective-permute-start | bytes 1179656 | tf_op jit(solution)/shard_map/ppermute | solution.py:191
  36.9 17.3 %collective-permute-start.7 = (bf16[2,192,512]{2,1,0:T(8,128)(2,1)}, bf16[2,192,512]{2,1,0:T(8,128)(2,1)}, u32[]{:S(2)}, u32[]{:S(2)}) collective-permute-start(bf16[2,192,512]{2,1,0:T(8,128)(2,1)} %get-tuple-element.19), channel_id=1, source_target_pairs={{0,16},{8,24},{16,0},{24,8},{1,17},{9,25},{17,1},{25,9},{2,18},{10... | collective-permute-start | bytes 1179656 | tf_op jit(solution)/shard_map/ppermute | solution.py:159
  37.2 0.7 %copy-start.8 = (bf16[2,192,512]{2,1,0:T(8,128)(2,1)}, bf16[2,192,512]{2,1,0:T(8,128)(2,1)S(1)}, u32[]{:S(2)}) copy-start(bf16[2,192,512]{2,1,0:T(8,128)(2,1)S(1)} %collective-permute-done.3.f1) | copy-start | bytes 1179652
  37.9 12.5 %collective-permute-start.9 = (bf16[2,192,512]{2,1,0:T(8,128)(2,1)}, bf16[2,192,512]{2,1,0:T(8,128)(2,1)}, u32[]{:S(2)}, u32[]{:S(2)}) collective-permute-start(bf16[2,192,512]{2,1,0:T(8,128)(2,1)} %collective-permute-done.8.f0), channel_id=1, source_target_pairs={{0,8},{8,0},{16,24},{24,16},{1,9},{9,1},{17,25},{25,17},{2,10},{10... | collective-permute-start | bytes 1179656 | tf_op jit(solution)/shard_map/ppermute | solution.py:191
  40.7 1.0 %copy-start.4 = (f32[768,128]{1,0:T(8,128)S(1)}, f32[768,128]{1,0:T(8,128)}, u32[]{:S(2)}) copy-start(f32[768,128]{1,0:T(8,128)} %get-tuple-element.31.ck) | copy-start | bytes 1179652
  41.7 0.9 %copy-start.6 = (s32[192,1]{1,0:T(8,128)S(1)}, s32[192,1]{1,0:T(8,128)}, u32[]{:S(2)}) copy-start(s32[192,1]{1,0:T(8,128)} %copy.22.qc) | copy-start | bytes 2308
  42.6 1.0 %copy-start.9 = (bf16[2,192,512]{2,1,0:T(8,128)(2,1)S(1)}, bf16[2,192,512]{2,1,0:T(8,128)(2,1)}, u32[]{:S(2)}) copy-start(bf16[2,192,512]{2,1,0:T(8,128)(2,1)} %copy-done.8) | copy-start | bytes 1179652
  44.3 4.3 %copy-start.12 = (bf16[2,192,512]{2,1,0:T(8,128)(2,1)S(1)}, bf16[2,192,512]{2,1,0:T(8,128)(2,1)}, u32[]{:S(2)}) copy-start(bf16[2,192,512]{2,1,0:T(8,128)(2,1)} %copy-done.11) | copy-start | bytes 1179652
  44.3 6.1 %copy-start.5 = (f32[768,128]{1,0:T(8,128)S(1)}, f32[768,128]{1,0:T(8,128)}, u32[]{:S(2)}) copy-start(f32[768,128]{1,0:T(8,128)} %get-tuple-element.31.ck) | copy-start | bytes 1179652
  44.3 6.1 %copy-start.7 = (s32[192,1]{1,0:T(8,128)S(1)}, s32[192,1]{1,0:T(8,128)}, u32[]{:S(2)}) copy-start(s32[192,1]{1,0:T(8,128)} %copy.22.qc) | copy-start | bytes 2308
  48.1 6.2 %collective-permute-start.11 = (bf16[2,192,512]{2,1,0:T(8,128)(2,1)}, bf16[2,192,512]{2,1,0:T(8,128)(2,1)S(1)}, u32[]{:S(2)}, u32[]{:S(2)}) collective-permute-start(bf16[2,192,512]{2,1,0:T(8,128)(2,1)} %collective-permute-done.f0), channel_id=1, source_target_pairs={{0,8},{8,0},{16,24},{24,16},{1,9},{9,1},{17,25},{25,17},{2,10},{10... | collective-permute-start | bytes 1179656 | tf_op jit(solution)/shard_map/ppermute | solution.py:191
  48.6 11.1 %collective-permute-start.10 = (bf16[2,192,512]{2,1,0:T(8,128)(2,1)S(1)}, bf16[2,192,512]{2,1,0:T(8,128)(2,1)S(1)}, u32[]{:S(2)}, u32[]{:S(2)}) collective-permute-start(bf16[2,192,512]{2,1,0:T(8,128)(2,1)S(1)} %copy-done.12), channel_id=1, source_target_pairs={{0,16},{8,24},{16,0},{24,8},{1,17},{9,25},{17,1},{25,9},{2,18},{10... | collective-permute-start | bytes 1179656 | tf_op jit(solution)/shard_map/ppermute | solution.py:159
  54.2 5.6 %collective-permute-start.12 = (bf16[2,192,512]{2,1,0:T(8,128)(2,1)}, bf16[2,192,512]{2,1,0:T(8,128)(2,1)S(1)}, u32[]{:S(2)}, u32[]{:S(2)}) collective-permute-start(bf16[2,192,512]{2,1,0:T(8,128)(2,1)} %collective-permute-done.7.f0), channel_id=1, source_target_pairs={{0,8},{8,0},{16,24},{24,16},{1,9},{9,1},{17,25},{25,17},{2,10},{10... | collective-permute-start | bytes 1179656 | tf_op jit(solution)/shard_map/ppermute | solution.py:191
  59.7 3.8 %collective-permute-start.13 = (bf16[2,192,512]{2,1,0:T(8,128)(2,1)S(1)}, bf16[2,192,512]{2,1,0:T(8,128)(2,1)S(1)}, u32[]{:S(2)}, u32[]{:S(2)}) collective-permute-start(bf16[2,192,512]{2,1,0:T(8,128)(2,1)S(1)} %collective-permute-done.10.f0), channel_id=1, source_target_pairs={{0,8},{8,0},{16,24},{24,16},{1,9},{9,1},{17,25},{25,17},{2,10},{10... | collective-permute-start | bytes 1179656 | tf_op jit(solution)/shard_map/ppermute | solution.py:191
  63.5 3.9 %copy-start.14 = (bf16[192,2560]{1,0:T(8,128)(2,1)}, bf16[192,2560]{1,0:T(8,128)(2,1)S(1)}, u32[]{:S(2)}) copy-start(bf16[192,2560]{1,0:T(8,128)(2,1)S(1)} %constant_dynamic-update-slice_fusion.1) | copy-start | bytes 2949124
  (1 other events, 0.7 us)

commit v4 on v0

--- a/solution.py
+++ b/solution.py
@@ -1,25 +1,514 @@
+import functools
 import math
 
 import jax
 import jax.numpy as jnp
 from jax import lax
+from jax.experimental import pallas as pl
+from jax.experimental.pallas import tpu as pltpu
 from jax.sharding import PartitionSpec as P
 
 HD = 128
 D = 5120
 CLIPS = 4
-
-
 EPSILON = 1e-06
 NEGATIVE = -1e30
 ROTARY_BASE = 10000.0
 block_limit = 1024
 
+ROWS = 192
+CHIP = 2 * ROWS
+MOST = 480
+NEAR = 96
+REST = CHIP - NEAR
+HALF = 5
+WIDE = HALF * HD
+FIRST_ROWS = 1600
+SECOND_ROWS = 1600
+BACK_ROWS = 640
+ACROSS = ((0, 2), (1, 3), (2, 0), (3, 1))
+BESIDE = ((0, 1), (1, 0), (2, 3), (3, 2))
+INNER = ((1, 2), (2, 1))
+OUTWARD = ((1, 0), (2, 3))
+OTHER_ROW = ((0, 1), (1, 0))
+SCORE_SCALE = math.log2(math.e) / math.sqrt(HD)
+VMEM = 24 * 1024 * 1024
+
+
+def plan(start, side):
+    first = start // 16 * 16
+    last = (start + MOST + 15) // 16 * 16
+    below, above = CHIP - first, last - CHIP
+    mine = jnp.where(side == 0, below, above)
+    theirs = jnp.where(side == 0, above, below)
+    most = jnp.maximum(mine, theirs)
+    lent = sum((most > limit).astype(jnp.int32) for limit in (256, 272, 288, 320, 352))
+    return first, mine, theirs, HALF - lent, (mine > theirs).astype(jnp.int32)
+
+
+def sixteen(offset):
+    return pl.multiple_of(offset, 16)
+
+
+def deal_kernel(me_ref, q_ref, k_ref, v_ref, out, near, sums):
+    me = me_ref[0]
+    half = out.shape[2]
+    at = pl.ds(pl.multiple_of((1 - lax.rem(me, 2)) * half, 128), half)
+    rows = pl.ds(sixteen((1 - me // 2) * NEAR), NEAR)
+    for i, ref in enumerate((q_ref, k_ref, v_ref)):
+        out[i] = ref[:, at]
+    for i, ref in enumerate((k_ref, v_ref)):
+        near[i] = ref[rows, :]
+    for i, ref in enumerate((q_ref, k_ref)):
+        lanes = jnp.zeros((ROWS, HD), jnp.float32)
+        for column in range(0, ref.shape[1], HD):
+            x = ref[:, column : column + HD].astype(jnp.float32)
+            lanes += x * x
+        sums[i : i + 1, :] = jnp.sum(jnp.transpose(lanes), axis=0, keepdims=True)
+
+
+def pack_kernel(me_ref, q_ref, k_ref, v_ref, mate, ids, mate_ids, first_out, second_out, chip, buffer):
+    me = me_ref[0]
+    side, core = me // 2, lax.rem(me, 2)
+    here, there = ids[...], mate_ids[...]
+    edge = jnp.where(
+        side == 0,
+        jnp.maximum(jnp.max(here), jnp.max(there)),
+        jnp.minimum(jnp.min(here), jnp.min(there)),
+    )
+    count = (
+        jnp.sum(jnp.where(here == edge, 1.0, 0.0)) + jnp.sum(jnp.where(there == edge, 1.0, 0.0))
+    ).astype(jnp.int32)
+    start = jnp.where(side == 0, CHIP - count, count - NEAR)
+    first, mine, _, kept, major = plan(start, side)
+    for i, ref in enumerate((q_ref, k_ref, v_ref)):
+        chip[i, pl.ds(sixteen(core * ROWS), ROWS), :] = ref[...]
+        chip[i, pl.ds(sixteen((1 - core) * ROWS), ROWS), :] = mate[i]
+        chip[i, CHIP:, :] = jnp.zeros((NEAR, ref.shape[1]), ref.dtype)
+    buffer[...] = jnp.zeros_like(buffer)
+    near_at = jnp.where(side == 0, REST, 0)
+    rest_at = jnp.where(side == 0, first, NEAR)
+    rest = mine - NEAR
+
+    def put(offset, which, head, row, length):
+        at = slice(head * HD, (head + 1) * HD)
+
+        def step(i, carry):
+            buffer[pl.ds(sixteen(offset + i * NEAR), NEAR), :] = chip[
+                which, pl.ds(sixteen(row + i * NEAR), NEAR), at
+            ]
+            return carry
+
+        lax.fori_loop(0, (length + NEAR - 1) // NEAR, step, 0)
+
+    offset = jnp.int32(0)
+    for i in range(HALF):
+        head = HALF + i
+        lend = jnp.logical_and(i >= kept, major == 0)
+        send = jnp.logical_or(i < kept, major == 0)
+        put(offset, 0, head, near_at, jnp.where(lend, NEAR, 0))
+        offset += jnp.where(lend, NEAR, 0)
+        put(offset, 0, head, rest_at, jnp.where(lend, rest, 0))
+        offset += jnp.where(lend, rest, 0)
+        length = jnp.where(send, rest, 0)
+        for which in (1, 2):
+            put(offset, which, head, rest_at, length)
+            offset += length
+    for head in range(HALF):
+        for which in (1, 2):
+            put(offset, which, head, rest_at, rest)
+            offset += rest
+    first_out[...] = buffer[:FIRST_ROWS, :]
+    second_out[...] = buffer[FIRST_ROWS : FIRST_ROWS + SECOND_ROWS, :]
+
+
+def turn(x, gain, gain_s, swap, cosine, sine):
+    other = jnp.dot(x, swap, preferred_element_type=jnp.float32)
+    return ((x.astype(jnp.float32) * gain) * cosine + (other * gain_s) * sine).astype(jnp.bfloat16)
+
+
+def flip(gain):
+    size = gain.shape[1]
+    even = lax.broadcasted_iota(jnp.int32, gain.shape, 1) % 2 == 0
+    return jnp.where(even, pltpu.roll(gain, size - 1, 1), pltpu.roll(gain, 1, 1))
+
+
+def signed_swap():
+    at_row = lax.broadcasted_iota(jnp.int32, (HD, HD), 0)
+    at_column = lax.broadcasted_iota(jnp.int32, (HD, HD), 1)
+    sign = jnp.where(at_column % 2 == 0, -1.0, 1.0)
+    return jnp.where(at_row == (at_column ^ 1), sign, 0.0).astype(jnp.bfloat16)
+
+
+def softmax_product(scores, values):
+    peak = jnp.max(scores, axis=0, keepdims=True)
+    weights = jnp.exp2((scores - peak) * SCORE_SCALE)
+    total = jnp.sum(weights, axis=0, keepdims=True)
+    out = lax.dot_general(
+        values, weights.astype(jnp.bfloat16), (((0,), (0,)), ((), ())),
+        preferred_element_type=jnp.float32,
+    )
+    return jnp.transpose(out / total).astype(jnp.bfloat16)
+
+
+def columns_of(row):
+    return jnp.transpose(jnp.broadcast_to(row, (HD, row.shape[1])))
+
+
+def spread_scales(sums):
+    return [columns_of(lax.rsqrt(sums[i : i + 1, :] / D + EPSILON)) for i in range(2)]
+
+
+def turn_kernel(me_ref, q_ref, k_ref, v_ref, mate, cosine, sine, sums, gq, gk, out, table):
+    core = lax.rem(me_ref[0], 2)
+    swap = signed_swap()
+    for i, scale in enumerate(spread_scales(sums)):
+        table[2 * i] = cosine[...] * scale
+        table[2 * i + 1] = sine[...] * scale
+    for here, rows in ((True, core), (False, 1 - core)):
+        rows = pl.ds(sixteen(rows * ROWS), ROWS)
+        out[2, rows, :] = v_ref[...] if here else mate[2]
+        for i, (ref, gains) in enumerate(((q_ref, gq), (k_ref, gk))):
+            cos_here, sin_here = table[2 * i, rows, :], table[2 * i + 1, rows, :]
+            for h in range(out.shape[2] // HD):
+                at = slice(h * HD, (h + 1) * HD)
+                gain = gains[:, at]
+                x = ref[:, at] if here else mate[i, :, at]
+                out[i, rows, at] = turn(x, gain, flip(gain), swap, cos_here, sin_here)
+
+
+def attend_kernel(flexible, info, *refs):
+    (local, near_here, near_passed, cosine, sine, sums, gq, gk, ids) = refs[:9]
+    refs = refs[9:]
+    if flexible:
+        first_in, own_out, mate_out, back = refs[:4]
+        refs = refs[4:]
+    else:
+        first_in, second_in, own_out, mate_out = refs[:4]
+        refs = refs[4:]
+    near, stream, bias, scales, table, keys, values, result = refs[:8]
+    core, side, theirs, kept, major = info[0], info[1], info[2], info[3], info[4]
+    edge, first = info[5].astype(jnp.float32), info[7]
+    inner = side != core
+    rest = theirs - NEAR
+
+    @pl.when(inner)
+    def _():
+        near[...] = near_here[...]
+
+    @pl.when(jnp.logical_not(inner))
+    def _():
+        near[...] = near_passed[...]
+
+    stream[:FIRST_ROWS, :] = first_in[...]
+    if flexible:
+        stream[FIRST_ROWS:, :] = jnp.zeros((stream.shape[0] - FIRST_ROWS, HD), stream.dtype)
+    else:
+        stream[FIRST_ROWS : FIRST_ROWS + SECOND_ROWS, :] = second_in[...]
+        stream[FIRST_ROWS + SECOND_ROWS :, :] = jnp.zeros((REST, HD), stream.dtype)
+
+    near_rows = pl.ds(sixteen(jnp.where(side == 0, 0, REST)), NEAR)
+    rest_rows = pl.ds(sixteen(jnp.where(side == 0, NEAR, first)), REST)
+    for i, scale in enumerate(spread_scales(sums)):
+        if i == 1 or flexible:
+            scales[:CHIP, :] = scale
+            scales[CHIP:, :] = jnp.ones((REST, HD), jnp.float32)
+            for j, ref in enumerate((cosine, sine)):
+                table[2 * i + j, :NEAR, :] = ref[:NEAR, :] * scales[near_rows, :]
+                table[2 * i + j, NEAR:, :] = ref[NEAR:, :] * scales[rest_rows, :]
+
+    clip_of = columns_of(ids[...])
+    for t in range(0, CHIP, HD):
+        bias[:, t : t + HD] = jnp.where(clip_of == ids[:, t : t + HD], 0.0, NEGATIVE)
+    if flexible:
+        bias[:, CHIP:] = jnp.where(clip_of == edge, 0.0, NEGATIVE)
+
+    swap = signed_swap()
+    if flexible:
+        base = jnp.int32(0)
+    else:
+        base = 2 * rest * kept + jnp.where(major == 1, (HALF - kept) * (2 * rest + theirs), 0)
+    bases = []
+    for h in range(HALF):
+        at = slice(h * HD, (h + 1) * HD)
+        gain = gk[:, at]
+        key_at = base
+        bases.append(base)
+        if flexible:
+            lend = jnp.logical_and(h >= kept, major == 1)
+            took = jnp.logical_or(h < kept, major == 1)
+            key_at = base + jnp.where(lend, theirs, 0)
+            base += jnp.where(took, 2 * rest, 0) + jnp.where(lend, theirs, 0)
+        else:
+            base += 2 * rest
+        far = jnp.concatenate([near[0, :, at], stream[pl.ds(sixteen(key_at), REST), :]], axis=0)
+        keys[h, :CHIP, :] = local[1, :, at]
+        keys[h, CHIP:, :] = turn(far, gain, flip(gain), swap, table[2], table[3])
+        values[h, :CHIP, :] = local[2, :, at]
+        values[h, CHIP : CHIP + NEAR, :] = near[1, :, at]
+        values[h, CHIP + NEAR :, :] = stream[pl.ds(sixteen(key_at + rest), REST), :]
+        for t in range(0, CHIP, HD):
+            scores = lax.dot_general(
+                keys[h], local[0, t : t + HD, at], (((1,), (1,)), ((), ())),
+                preferred_element_type=jnp.float32,
+            ) + bias[:, t : t + HD]
+            result[t : t + HD, at] = softmax_product(scores, values[h])
+    own_out[...] = result[pl.ds(sixteen(core * ROWS), ROWS), :]
+    mate_out[...] = result[pl.ds(sixteen((1 - core) * ROWS), ROWS), :]
+    if flexible:
+        back_rows = refs[8]
+        back_rows[...] = jnp.zeros_like(back_rows)
+        for h in range(HALF):
+            at = slice(h * HD, (h + 1) * HD)
+
+            @pl.when(jnp.logical_and(h >= kept, major == 1))
+            def _():
+                gain = gq[:, at]
+                x = stream[pl.ds(sixteen(bases[h]), 2 * HD), :]
+                far_q = turn(
+                    x, gain, flip(gain), swap, table[0, : 2 * HD, :], table[1, : 2 * HD, :]
+                )
+
+                def answer(t):
+                    scores = lax.dot_general(
+                        keys[h], far_q[t : t + HD], (((1,), (1,)), ((), ())),
+                        preferred_element_type=jnp.float32,
+                    ) + bias[:, CHIP:]
+                    back_rows[pl.ds(sixteen((h - kept) * theirs + t), HD), :] = softmax_product(
+                        scores, values[h]
+                    )
+
+                answer(0)
+                pl.when(theirs > HD)(lambda: answer(HD))
+
+        back[...] = back_rows[:BACK_ROWS, :]
+
+
+def join_kernel(
+    info, flex_here, fixed_here, flex_there, fixed_there, back_here, back_there, ids, out, rows, lines
+):
+    core, side = info[0], info[1]
+    mine = info[6]
+    kept, major, first = info[3], info[4], info[7]
+    edge = info[5].astype(jnp.float32)
+    half = 2 * WIDE
+    inside = jnp.transpose(jnp.broadcast_to(ids[...], (HD, ROWS))) == edge
+    for here, flex, fixed, back in (
+        (True, flex_here, fixed_here, back_here),
+        (False, flex_there, fixed_there, back_there),
+    ):
+        column = pl.multiple_of((core if here else 1 - core) * half, 128)
+        out[:, pl.ds(column, WIDE)] = fixed[...]
+        out[:, pl.ds(pl.multiple_of(column + WIDE, 128), WIDE)] = flex[...]
+
+        @pl.when(jnp.logical_and(major == 0, kept < HALF))
+        def _():
+            rows[:BACK_ROWS, :] = back[...]
+            rows[BACK_ROWS:, :] = jnp.zeros((REST, HD), rows.dtype)
+            for h in range(HALF):
+
+                @pl.when(h >= kept)
+                def _():
+                    base = (h - kept) * mine
+                    near_at = jnp.where(side == 0, REST, 0)
+                    rest_at = jnp.where(side == 0, first, NEAR)
+                    lines[pl.ds(sixteen(rest_at), REST), :] = rows[
+                        pl.ds(sixteen(base + NEAR), REST), :
+                    ]
+                    lines[pl.ds(sixteen(near_at), NEAR), :] = rows[pl.ds(sixteen(base), NEAR), :]
+                    at = slice(h * HD, (h + 1) * HD)
+                    place = pl.ds(pl.multiple_of(column + WIDE + h * HD, 128), HD)
+                    out[:, place] = jnp.where(
+                        inside, lines[pl.ds(sixteen(core * ROWS), ROWS), :], flex[:, at]
+                    )
+
 
 def lookup(lookup_table, positions):
     labels = jnp.arange(lookup_table.shape[0], dtype=jnp.int32)
     return jnp.sum(
         jnp.where(positions[:, None] == labels[None, :], lookup_table[None, :], 0), axis=1
+    )
+
+
+def angles_of(offsets, clip_of, clip_grid):
+    sixth_part = HD // 6
+    first_dims = HD - 4 * sixth_part
+    first_freqs = 1.0 / ROTARY_BASE ** (
+        jnp.arange(0, first_dims, 2, dtype=jnp.float32) / first_dims
+    )
+    other_freqs = 1.0 / ROTARY_BASE ** (
+        jnp.arange(0, 2 * sixth_part, 2, dtype=jnp.float32) / (2 * sixth_part)
+    )
+    heights = lookup(clip_grid[:, 0], clip_of)
+    widths = lookup(clip_grid[:, 1], clip_of)
+    frame_pos = (offsets // (heights * widths)).astype(jnp.float32)[:, None]
+    line_pos = (offsets // widths % heights).astype(jnp.float32)[:, None]
+    column_pos = (offsets % widths).astype(jnp.float32)[:, None]
+    freqs = jnp.repeat(jnp.concatenate([first_freqs, other_freqs, other_freqs]), 2)[None, :]
+    feature = jnp.arange(HD, dtype=jnp.int32)[None, :]
+    position = jnp.where(
+        feature < first_dims,
+        frame_pos,
+        jnp.where(feature < first_dims + 2 * sixth_part, line_pos, column_pos),
+    )
+    return position * freqs
+
+
+def whole(a):
+    return pl.BlockSpec(a.shape, lambda i, s: (0,) * len(a.shape))
+
+
+def call(kernel, out_shape, in_specs, out_specs, scratch, scalars, *operands):
+    return pl.pallas_call(
+        kernel,
+        out_shape=out_shape,
+        grid_spec=pltpu.PrefetchScalarGridSpec(
+            num_scalar_prefetch=1,
+            grid=(1,),
+            in_specs=in_specs,
+            out_specs=out_specs,
+            scratch_shapes=scratch,
+        ),
+        compiler_params=pltpu.CompilerParams(vmem_limit_bytes=VMEM),
+        cost_estimate=pl.CostEstimate(flops=0, bytes_accessed=0, transcendentals=0),
+    )(scalars, *operands)
+
+
+def attend(flexible, info, streams, local, near, near_passed, waves, sums, gains, ids):
+    group = 1 if flexible else 0
+    bf16, f32 = jnp.bfloat16, jnp.float32
+    here = pl.BlockSpec((3, CHIP, WIDE), lambda i, s: (0, 0, group))
+    nears = pl.BlockSpec((2, NEAR, WIDE), lambda i, s: (0, 0, 2 * s[0] + group))
+    gain = pl.BlockSpec((1, WIDE), lambda i, s: (0, 2 * s[0] + group))
+    far = pl.BlockSpec((CHIP, HD), lambda i, s: (1, 0))
+    shapes = [jax.ShapeDtypeStruct((ROWS, WIDE), bf16)] * 2
+    stream_rows = FIRST_ROWS + (0 if flexible else SECOND_ROWS) + REST
+    scratch = [
+        pltpu.VMEM((2, NEAR, WIDE), bf16),
+        pltpu.VMEM((stream_rows, HD), bf16),
+        pltpu.VMEM((2 * CHIP, CHIP + (HD if flexible else 0)), f32),
+        pltpu.VMEM((CHIP + REST, HD), f32),
+        pltpu.VMEM((4, CHIP, HD), f32),
+        pltpu.VMEM((HALF, 2 * CHIP, HD), bf16),
+        pltpu.VMEM((HALF, 2 * CHIP, HD), bf16),
+        pltpu.VMEM((CHIP, WIDE), bf16),
+    ]
+    if flexible:
+        shapes = shapes + [jax.ShapeDtypeStruct((BACK_ROWS, HD), bf16)]
+        scratch = scratch + [pltpu.VMEM((BACK_ROWS + 2 * HD, HD), bf16)]
+    operands = (local, near, near_passed, *waves, sums, *gains, ids, *streams)
+    in_specs = [here, nears, nears, far, far, whole(sums), gain, gain, whole(ids)]
+    in_specs += [whole(s) for s in streams]
+    return call(
+        functools.partial(attend_kernel, flexible), shapes, in_specs, [whole(s) for s in shapes],
+        scratch, info, *operands,
+    )
+
+
+def on_device(queries, keys, values, gain_q, gain_k, clip_ids, clip_grid):
+    width = queries.shape[1]
+    half = width // 2
+    bf16, f32 = jnp.bfloat16, jnp.float32
+    me = lax.axis_index("ctx").astype(jnp.int32)
+    side, core = me // 2, me % 2
+    at_me = me[None]
+
+    clip_row = clip_ids.astype(f32)[None, :]
+    mate_row = lax.ppermute(clip_row, "ctx", BESIDE)
+
+    deal_shapes = [
+        jax.ShapeDtypeStruct((3, ROWS, half), bf16),
+        jax.ShapeDtypeStruct((2, NEAR, width), bf16),
+        jax.ShapeDtypeStruct((2, ROWS), f32),
+    ]
+    dealt, near_send, sums = call(
+        deal_kernel, deal_shapes, [whole(queries)] * 3, [whole(s) for s in deal_shapes], [],
+        at_me, queries, keys, values,
+    )
+    mate = lax.ppermute(dealt, "ctx", BESIDE)
+    near = lax.ppermute(near_send, "ctx", INNER)
+    own_spec = pl.BlockSpec((ROWS, half), lambda i, s: (0, s[0] % 2))
+    stream_shapes = [
+        jax.ShapeDtypeStruct((FIRST_ROWS, HD), bf16),
+        jax.ShapeDtypeStruct((SECOND_ROWS, HD), bf16),
+    ]
+    first_send, second_send = call(
+        pack_kernel, stream_shapes,
+        [own_spec] * 3 + [whole(mate), whole(clip_row), whole(mate_row)],
+        [whole(s) for s in stream_shapes],
+        [
+            pltpu.VMEM((3, CHIP + NEAR, half), bf16),
+            pltpu.VMEM((FIRST_ROWS + SECOND_ROWS + NEAR, HD), bf16),
+        ],
+        at_me, queries, keys, values, mate, clip_row, mate_row,
+    )
+
+    sums = sums + lax.ppermute(sums, "row", OTHER_ROW)
+    mate_sums = lax.ppermute(sums, "ctx", BESIDE)
+
+    def by_core(here, there):
+        return jnp.where(
+            core == 0, jnp.concatenate([here, there], 1), jnp.concatenate([there, here], 1)
+        )
+
+    chip_sums = by_core(sums, mate_sums)
+    far_sums = lax.ppermute(chip_sums, "ctx", ACROSS)
+    first_send, chip_sums = lax.optimization_barrier((first_send, chip_sums))
+    first_stream = lax.ppermute(first_send, "ctx", ACROSS)
+    second_stream = lax.ppermute(second_send, "ctx", ACROSS)
+    chip_ids = by_core(clip_row, mate_row)[0].astype(jnp.int32)
+    chip_ids, _ = lax.optimization_barrier((chip_ids, first_send))
+    edge = jnp.where(side == 0, chip_ids[CHIP - 1], chip_ids[0])
+    count = jnp.sum((chip_ids == edge).astype(jnp.int32))
+    start = jnp.where(side == 0, CHIP - count, count - NEAR)
+    first, mine, theirs, kept, major = plan(start, side)
+    info = jnp.stack([core, side, theirs, kept, major, edge, mine, first])
+
+    slots = jnp.arange(CHIP, dtype=jnp.int32)
+    near_tokens = jnp.where(side == 0, CHIP, REST) + slots[:NEAR]
+    rest_tokens = jnp.where(side == 0, CHIP + NEAR, first) + slots[:REST]
+    rest_end = jnp.where(side == 0, start + MOST, REST)
+    rest_valid = (rest_tokens >= start) & (rest_tokens < rest_end)
+    far_tokens = jnp.concatenate([near_tokens, rest_tokens])
+    far_valid = jnp.concatenate([jnp.ones((NEAR,), bool), rest_valid])
+    labels = jnp.arange(CLIPS, dtype=jnp.int32)
+    below = jnp.sum((chip_ids[:, None] < labels[None, :]).astype(jnp.int32), axis=0)
+    local_offsets = jnp.where(
+        (side == 1) & (chip_ids == edge), CHIP - start + slots, slots - lookup(below, chip_ids)
+    )
+    far_offsets = jnp.maximum(far_tokens - start, 0)
+    offsets = jnp.concatenate([local_offsets, far_offsets])
+    clip_of = jnp.concatenate([chip_ids, jnp.broadcast_to(edge, (CHIP,))])
+    angles = angles_of(offsets, clip_of, clip_grid)
+    waves = (jnp.cos(angles), jnp.sin(angles))
+    gains = (gain_q[None, :], gain_k[None, :])
+    mask_ids = jnp.concatenate([chip_ids, jnp.where(far_valid, edge, -1)]).astype(f32)[None, :]
+
+    wave_spec = pl.BlockSpec((CHIP, HD), lambda i, s: (0, 0))
+    gain_spec = pl.BlockSpec((1, half), lambda i, s: (0, s[0] % 2))
+    local_shape = jax.ShapeDtypeStruct((3, CHIP, half), bf16)
+    local = call(
+        turn_kernel, local_shape,
+        [own_spec] * 3 + [whole(mate), wave_spec, wave_spec, whole(chip_sums), gain_spec, gain_spec],
+        whole(local_shape), [pltpu.VMEM((4, CHIP, HD), f32)],
+        at_me, queries, keys, values, mate, *waves, chip_sums, *gains,
+    )
+    near, _ = lax.optimization_barrier((near, second_send))
+    near_passed = lax.ppermute(near, "ctx", OUTWARD)
+
+    common = (local, near, near_passed, waves, far_sums, gains, mask_ids)
+    flex_here, flex_send, back_send = attend(True, info, (first_stream,), *common)
+    back_here = lax.ppermute(back_send, "ctx", ACROSS)
+    flex_there = lax.ppermute(flex_send, "ctx", BESIDE)
+    fixed_here, fixed_send = attend(False, info, (first_stream, second_stream), *common)
+    fixed_there = lax.ppermute(fixed_send, "ctx", BESIDE)
+    back_there = lax.ppermute(back_here, "ctx", BESIDE)
+    out_shape = jax.ShapeDtypeStruct((ROWS, width), bf16)
+    operands = (flex_here, fixed_here, flex_there, fixed_there, back_here, back_there, clip_row)
+    return call(
+        join_kernel, out_shape, [whole(a) for a in operands], whole(out_shape),
+        [pltpu.VMEM((BACK_ROWS + REST, HD), bf16), pltpu.VMEM((2 * REST, HD), bf16)],
+        info, *operands,
     )
 
 
@@ -56,7 +545,7 @@
     return turned.reshape(row_count, -1)
 
 
-def on_device(queries, keys, values, gain_q, gain_k, clip_ids, clip_grid):
+def on_any(queries, keys, values, gain_q, gain_k, clip_ids, clip_grid):
     rows_here, width_here = queries.shape
     heads_here = width_here // HD
     score_scale = 1.0 / math.sqrt(HD)
@@ -134,6 +623,8 @@
         P("batch", None),
     )
     out_specs = P(("batch", "ctx"), "row")
+    pair_of_chips = mesh.shape["ctx"] == 4 and mesh.shape["row"] == 2
     return jax.shard_map(
-        on_device, mesh=mesh, in_specs=in_specs, out_specs=out_specs, check_vma=False
-    )
+        on_device if pair_of_chips else on_any,
+        mesh=mesh, in_specs=in_specs, out_specs=out_specs, check_vma=False,
+    )

time: 148 us -> 55.4 us (0.37)
  waiting for transfers between devices: 52.8 us -> 4.33 us
  local copies, waits for them, and re-layouts: 34.4 us -> 5.56 us
  Pallas kernels: 0 us -> 26 us
  other arithmetic: 21.4 us -> 4.95 us
  matrix products: 13.3 us -> 0 us
  starting transfers between devices: 0.22 us -> 11.9 us
  blocking collectives: 11.3 us -> 0 us
  between operations: 13.6 us -> 2.5 us
    all_gather x2 -> x0, waiting for transfers between devices: 52.3 us -> none  [the longest x1 32.8 us: on_device(): key_piece = lax.all_gather(key_send, 'ctx', axis=0, tiled=True)]
    pallas_call x0 -> x6, Pallas kernels: none -> 26 us  [call(): pl.pallas_call(kernel, out_shape=out_shape, grid_spec=pltpu.PrefetchScala...]
    dot_general x2 -> x0, matrix products: 13.3 us -> none  [the longest x1 8.9 us: on_device(): jnp.einsum('hqk,khd->qhd', weights.astype(jnp.bfloat16), value_view, pref...]
    all_gather x2 -> x0, local copies, waits for them, and re-layouts: 12.6 us -> none  [the longest x1 6.31 us: on_device(): value_piece = lax.all_gather(values, 'ctx', axis=0, tiled=True)]
    ppermute x0 -> x13, starting transfers between devices: none -> 11.9 us  [the longest x1 2.52 us: on_device(): sums = sums + lax.ppermute(sums, 'row', OTHER_ROW)]
    psum x2 -> x0, blocking collectives: 11.3 us -> none  [the longest x1 5.86 us: on_device(): lax.psum((jnp.sum(query_wide * query_wide, axis=1), jnp.sum(key_wide * ke...]
    slice x4 -> x1, local copies, waits for them, and re-layouts: 11.5 us -> 0.58 us  [on_device(): edge = jnp.where(side == 0, chip_ids[CHIP - 1], chip_ids[0])]
    reduce_sum x5 -> x2, other arithmetic: 7.33 us -> 0.75 us  [the longest x1 0.63 us: on_device(): count = jnp.sum((chip_ids == edge).astype(jnp.int32))]
  transfers between devices with their start and end apart: 2 -> 13, of which waited for: 2 -> 6; matrix products, arithmetic and copies ran while one was open for 10% -> 11% of each run, Pallas kernels for 0% -> 41%
where the time goes in v4:
time: 55.4 us; the launch traced here: 55.2 us
  Pallas kernels  26 us (47%)
  starting transfers between devices  11.9 us (21%)
  local copies, waits for them, and re-layouts  5.56 us (10%)
  other arithmetic  4.95 us (9%)
  waiting for transfers between devices  4.33 us (8%)
  between operations  2.5 us (5%)
    pallas_call x6, Pallas kernels, call(): pl.pallas_call(kernel, out_shape=out_shape, grid_spec=pltpu.PrefetchScala...  26 us
    unnamed x22, local copies, waits for them, and re-layouts  4.63 us
    sin x1, other arithmetic, on_device(): waves = (jnp.cos(angles), jnp.sin(angles))  2.72 us
    ppermute x1, starting transfers between devices, on_device(): sums = sums + lax.ppermute(sums, 'row', OTHER_ROW)  2.52 us
    ppermute x1, waiting for transfers between devices, on_device(): first_stream = lax.ppermute(first_send, 'ctx', ACROSS)  2.26 us
    ppermute x1, starting transfers between devices, on_device(): mate_sums = lax.ppermute(sums, 'ctx', BESIDE)  1.98 us
    ppermute x1, starting transfers between devices, on_device(): near = lax.ppermute(near_send, 'ctx', INNER)  1.63 us
    ppermute x1, starting transfers between devices, on_device(): near_passed = lax.ppermute(near, 'ctx', OUTWARD)  1.29 us
  transfers between devices with their start and end apart: 13, of which 6 were waited for; matrix products, arithmetic and copies ran while one was open for 11% of the time, Pallas kernels for 41%

profile of v4, /device:TPU:0, one launch (start us, length us, event | category | flops | bytes accessed | tf_op | source)
XLA Modules:
  0.0 55.2 jit_solution(16228864320705204497)
XLA Ops:
  0.0 1.2 %copy-done = bf16[192,2560]{1,0:T(8,128)(2,1)S(1)} copy-done((bf16[192,2560]{1,0:T(8,128)(2,1)S(1)}, bf16[192,2560]{1,0:T(8,128)(2,1)}, u32[]{:S(2)}) %copy-start) | copy-done | bytes 983064
  1.2 1.2 %copy-done.2 = bf16[192,2560]{1,0:T(8,128)(2,1)S(1)} copy-done((bf16[192,2560]{1,0:T(8,128)(2,1)S(1)}, bf16[192,2560]{1,0:T(8,128)(2,1)}, u32[]{:S(2)}) %copy-start.2) | copy-done | bytes 983064
  2.4 1.2 %copy-done.4 = bf16[192,2560]{1,0:T(8,128)(2,1)S(1)} copy-done((bf16[192,2560]{1,0:T(8,128)(2,1)S(1)}, bf16[192,2560]{1,0:T(8,128)(2,1)}, u32[]{:S(2)}) %copy-start.4) | copy-done | bytes 983064
  3.6 1.9 %shard_map.73 = (bf16[3,192,1280]{2,1,0:T(8,128)(2,1)}, bf16[2,96,2560]{2,1,0:T(8,128)(2,1)}, f32[2,192]{1,0:T(2,128)S(1)}) custom-call(s32[1]{0:T(128)} %bitcast.4.me_ref, bf16[192,2560]{1,0:T(8,128)(2,1)S(1)} %copy-done, bf16[192,2560]{1,0:T(8,128)(2,1)S(1)} %copy-done.2, bf16[192,2560]{1,0:T(8,128)(2,1)S(1)} %copy-done.4), custom_call_target="tpu_custom_call" | custom-call | tf_op jit(solution)/shard_map/pallas_call | solution.py:362
  5.5 0.5 collective-permute-start.1
  6.0 2.5 %collective-permute-start.2 = (f32[2,192]{1,0:T(2,128)S(1)}, f32[2,192]{1,0:T(2,128)S(1)}, u32[]{:S(2)}, u32[]{:S(2)}) collective-permute-start(f32[2,192]{1,0:T(2,128)S(1)} %get-tuple-element.21), channel_id=1, source_target_pairs={{0,4},{4,0},{1,5},{5,1},{2,6},{6,2},{3,7},{7,3},{8,12},{12,8},{9,1... | collective-permute-start | bytes 4616 | tf_op jit(solution)/shard_map/ppermute | solution.py:446
  8.5 0.7 %convert_element_type.59 = f32[192]{0:T(256)S(1)} convert(s32[192]{0:T(256)} %param.12) | non-fusion elementwise | flops 192 | bytes 1536 | tf_op jit(solution)/shard_map/convert_element_type | solution.py:416
  9.2 0.2 collective-permute-start
  9.4 1.6 %collective-permute-start.4 = (bf16[2,96,2560]{2,1,0:T(8,128)(2,1)}, bf16[2,96,2560]{2,1,0:T(8,128)(2,1)}, u32[]{:S(2)}, u32[]{:S(2)}) collective-permute-start(bf16[2,96,2560]{2,1,0:T(8,128)(2,1)} %get-tuple-element.25), channel_id=1, source_target_pairs={{8,16},{16,8},{9,17},{17,9},{10,18},{18,10},{11,19},{19,11},{12,20... | collective-permute-start | bytes 2949128 | tf_op jit(solution)/shard_map/ppermute | solution.py:429
  11.3 0.1 mul.28
  11.5 2.0 %collective-permute-start.3 = (f32[2,192]{1,0:T(2,128)S(1)}, f32[2,192]{1,0:T(2,128)S(1)}, u32[]{:S(2)}, u32[]{:S(2)}) collective-permute-start(f32[2,192]{1,0:T(2,128)S(1)} %add.79), channel_id=1, source_target_pairs={{0,8},{8,0},{16,24},{24,16},{1,9},{9,1},{17,25},{25,17},{2,10},{10... | collective-permute-start | bytes 4616 | tf_op jit(solution)/shard_map/ppermute | solution.py:447
  13.6 0.7 %collective-permute-done.3 = f32[2,192]{1,0:T(2,128)S(1)} collective-permute-done((f32[2,192]{1,0:T(2,128)S(1)}, f32[2,192]{1,0:T(2,128)S(1)}, u32[]{:S(2)}, u32[]{:S(2)}) %collective-permute-start.3) | collective-permute-done | bytes 1568 | tf_op jit(solution)/shard_map/ppermute | solution.py:447
  14.4 0.6 %collective-permute-start.6 = (f32[2,384]{1,0:T(2,128)S(1)}, f32[2,384]{1,0:T(2,128)S(1)}, u32[]{:S(2)}, u32[]{:S(2)}) collective-permute-start(f32[2,384]{1,0:T(2,128)S(1)} %maximum_select_fusion.sums), channel_id=1, source_target_pairs={{0,16},{8,24},{16,0},{24,8},{1,17},{9,25},{17,1},{25,9},{2,18},{10... | collective-permute-start | bytes 9224 | tf_op jit(solution)/shard_map/ppermute | solution.py:455
  15.1 3.5 %shard_map.74 = (bf16[1600,128]{1,0:T(8,128)(2,1)}, bf16[1600,128]{1,0:T(8,128)(2,1)}) custom-call(s32[1]{0:T(128)} %bitcast.4.me_ref, bf16[192,2560]{1,0:T(8,128)(2,1)S(1)} %copy-done.1, bf16[192,2560]{1,0:T(8,128)(2,1)S(1)} %copy-done.3, bf16[192,2560]{1,0:T(8,128)(2,1)S(1)} %copy-done.5, bf16[3,192,1280]{2,1,0:T(8,128)(2,1)} %collective-permute-done.1.mate, ...), custom_call_target="tpu_custom_call" | custom-call | tf_op jit(solution)/shard_map/pallas_call | solution.py:362
  18.6 0.6 %fusion.10 = (s32[1]{0:T(128)}, s32[1]{0:T(128)}) fusion(s32[384]{0:T(512)S(1)} %fusion.8), kind=kLoop, calls=%fused_computation.47 | loop fusion | bytes 16 | tf_op jit(solution)/shard_map/slice | solution.py:461
  20.3 0.6 %convert_reduce_fusion.1 = (s32[]{:T(128)}, pred[384]{0:T(512)(128)(4,1)S(1)}) fusion(s32[384]{0:T(512)S(1)} %fusion.8, s32[]{:T(128)} %select_n.139), kind=kLoop, calls=%fused_computation.35 | loop fusion | flops 1151 | bytes 1928 | tf_op jit(solution)/shard_map/reduce_sum | solution.py:462
  22.1 1.2 %collective-permute-start.7 = (bf16[1600,128]{1,0:T(8,128)(2,1)}, bf16[1600,128]{1,0:T(8,128)(2,1)}, u32[]{:S(2)}, u32[]{:S(2)}) collective-permute-start(bf16[1600,128]{1,0:T(8,128)(2,1)} %get-tuple-element.22), channel_id=1, source_target_pairs={{0,16},{8,24},{16,0},{24,8},{1,17},{9,25},{17,1},{25,9},{2,18},{10... | collective-permute-start | bytes 1228808 | tf_op jit(solution)/shard_map/ppermute | solution.py:457
  23.3 0.9 %collective-permute-start.8 = (bf16[1600,128]{1,0:T(8,128)(2,1)}, bf16[1600,128]{1,0:T(8,128)(2,1)}, u32[]{:S(2)}, u32[]{:S(2)}) collective-permute-start(bf16[1600,128]{1,0:T(8,128)(2,1)} %get-tuple-element.26), channel_id=1, source_target_pairs={{0,16},{8,24},{16,0},{24,8},{1,17},{9,25},{17,1},{25,9},{2,18},{10... | collective-permute-start | bytes 1228808 | tf_op jit(solution)/shard_map/ppermute | solution.py:458
  24.4 1.3 %collective-permute-start.5 = (bf16[2,96,2560]{2,1,0:T(8,128)(2,1)}, bf16[2,96,2560]{2,1,0:T(8,128)(2,1)}, u32[]{:S(2)}, u32[]{:S(2)}) collective-permute-start(bf16[2,96,2560]{2,1,0:T(8,128)(2,1)} %collective-permute-done.4.refs_1_), channel_id=1, source_target_pairs={{8,0},{16,24},{9,1},{17,25},{10,2},{18,26},{11,3},{19,27},{12,4},{... | collective-permute-start | bytes 2949128 | tf_op jit(solution)/shard_map/ppermute | solution.py:497
  25.9 0.3 fusion.2
  26.1 2.7 %fusion = (f32[768,128]{1,0:T(8,128)S(1)}, f32[768,128]{1,0:T(8,128)}) fusion(f32[128]{0:T(128)S(1)} %mul.28, f32[768]{0:T(1024)S(1)} %get-tuple-element.43, f32[768]{0:T(1024)S(1)} %get-tuple-element.42, f32[768]{0:T(1024)S(1)} %get-tuple-element.41, pred[128]{0:T(512)(128)(4,1)S(1)} %get-tuple-element.50, pred[128]{0:T(512)(128)(4,1)S(1)} %get-tuple-element.51), kind=kLoop, calls=%fused_computation.1 | loop fusion | flops 294912 | bytes 796416 | tf_op jit(solution)/shard_map/sin | solution.py:483
  29.0 1.0 %copy-done.6 = f32[768,128]{1,0:T(8,128)S(1)} copy-done((f32[768,128]{1,0:T(8,128)S(1)}, f32[768,128]{1,0:T(8,128)}, u32[]{:S(2)}) %copy-start.6) | copy-done | bytes 393240
  30.0 2.9 %shard_map.75.refs_0_ = bf16[3,384,1280]{2,1,0:T(8,128)(2,1)S(1)} custom-call(s32[1]{0:T(128)} %bitcast.4.me_ref, bf16[192,2560]{1,0:T(8,128)(2,1)S(1)} %copy-done.1, bf16[192,2560]{1,0:T(8,128)(2,1)S(1)} %copy-done.3, bf16[192,2560]{1,0:T(8,128)(2,1)S(1)} %copy-done.5, bf16[3,192,1280]{2,1,0:T(8,128)(2,1)} %collective-permute-done.1.mate, ...), custom_call_target="tpu_custom_call" | custom-call | tf_op jit(solution)/shard_map/pallas_call | solution.py:362
  32.9 2.3 %collective-permute-done.7.refs_9_ = bf16[1600,128]{1,0:T(8,128)(2,1)} collective-permute-done((bf16[1600,128]{1,0:T(8,128)(2,1)}, bf16[1600,128]{1,0:T(8,128)(2,1)}, u32[]{:S(2)}, u32[]{:S(2)}) %collective-permute-start.7) | collective-permute-done | bytes 409632 | tf_op jit(solution)/shard_map/ppermute | solution.py:457
  35.1 10.2 %shard_map.76 = (bf16[192,640]{1,0:T(8,128)(2,1)S(1)}, bf16[192,640]{1,0:T(8,128)(2,1)S(1)}, bf16[640,128]{1,0:T(8,128)(2,1)S(1)}) custom-call(s32[8]{0:T(128)S(1)} %stack.39.info, bf16[3,384,1280]{2,1,0:T(8,128)(2,1)S(1)} %shard_map.75.refs_0_, bf16[2,96,2560]{2,1,0:T(8,128)(2,1)} %collective-permute-done.4.refs_1_, ...), custom_call_target="tpu_custom_call" | custom-call | tf_op jit(solution)/shard_map/pallas_call | solution.py:362
  45.5 5.8 %shard_map.77 = (bf16[192,640]{1,0:T(8,128)(2,1)S(1)}, bf16[192,640]{1,0:T(8,128)(2,1)S(1)}) custom-call(s32[8]{0:T(128)S(1)} %stack.39.info, bf16[3,384,1280]{2,1,0:T(8,128)(2,1)S(1)} %shard_map.75.refs_0_, bf16[2,96,2560]{2,1,0:T(8,128)(2,1)} %collective-permute-done.4.refs_1_, bf16[2,96,2560]{2,1,0:T(8,128)(2,1)} %collective-permute-done.5.refs_2_, ...), custom_call_target="tpu_custom_call" | custom-call | tf_op jit(solution)/shard_map/pallas_call | solution.py:362
  51.3 0.5 collective-permute-start.10
  52.0 0.4 collective-permute-start.12
  52.4 0.6 %collective-permute-done.10.fixed_there = bf16[192,640]{1,0:T(8,128)(2,1)S(1)} collective-permute-done((bf16[192,640]{1,0:T(8,128)(2,1)S(1)}, bf16[192,640]{1,0:T(8,128)(2,1)S(1)}, u32[]{:S(2)}, u32[]{:S(2)}) %collective-permute-start.10) | collective-permute-done | bytes 245792 | tf_op jit(solution)/shard_map/ppermute | solution.py:504
  53.0 0.4 collective-permute-done.9.flex_there
  53.4 0.2 collective-permute-done.12.back_there
  53.6 1.6 %shard_map.78 = bf16[192,2560]{1,0:T(8,128)(2,1)} custom-call(s32[8]{0:T(128)S(1)} %stack.39.info, bf16[192,640]{1,0:T(8,128)(2,1)S(1)} %get-tuple-element.28.flex_here, bf16[192,640]{1,0:T(8,128)(2,1)S(1)} %get-tuple-element.29.fixed_here, bf16[192,640]{1,0:T(8,128)(2,1)S(1)} %collective-permute-done.9.flex_there, ...), custom_call_target="tpu_custom_call" | custom-call | tf_op jit(solution)/shard_map/pallas_call | solution.py:362
  (53 shorter events, 1.1 us)
Async XLA Ops:
  0.0 1.2 %copy-start = (bf16[192,2560]{1,0:T(8,128)(2,1)S(1)}, bf16[192,2560]{1,0:T(8,128)(2,1)}, u32[]{:S(2)}) copy-start(bf16[192,2560]{1,0:T(8,128)(2,1)} %q_ref.5) | copy-start | bytes 2949124
  1.2 1.2 %copy-start.2 = (bf16[192,2560]{1,0:T(8,128)(2,1)S(1)}, bf16[192,2560]{1,0:T(8,128)(2,1)}, u32[]{:S(2)}) copy-start(bf16[192,2560]{1,0:T(8,128)(2,1)} %k_ref.5) | copy-start | bytes 2949124
  2.4 1.2 %copy-start.4 = (bf16[192,2560]{1,0:T(8,128)(2,1)S(1)}, bf16[192,2560]{1,0:T(8,128)(2,1)}, u32[]{:S(2)}) copy-start(bf16[192,2560]{1,0:T(8,128)(2,1)} %v_ref.5) | copy-start | bytes 2949124
  3.6 7.5 %copy-start.10 = (s32[4,2]{0,1:T(2,128)S(1)}, s32[4,2]{0,1:T(2,128)}, u32[]{:S(2)}) copy-start(s32[4,2]{0,1:T(2,128)} %param.13) | copy-start | bytes 100
  3.6 7.8 %copy-start.8 = (f32[2560]{0:T(1024)S(1)}, f32[2560]{0:T(1024)}, u32[]{:S(2)}) copy-start(f32[2560]{0:T(1024)} %param.10) | copy-start | bytes 30724
  3.6 7.8 %copy-start.9 = (f32[2560]{0:T(1024)S(1)}, f32[2560]{0:T(1024)}, u32[]{:S(2)}) copy-start(f32[2560]{0:T(1024)} %param.11) | copy-start | bytes 30724
  3.6 11.4 %copy-start.1 = (bf16[192,2560]{1,0:T(8,128)(2,1)S(1)}, bf16[192,2560]{1,0:T(8,128)(2,1)}, u32[]{:S(2)}) copy-start(bf16[192,2560]{1,0:T(8,128)(2,1)} %q_ref.5) | copy-start | bytes 2949124
  3.6 11.4 %copy-start.3 = (bf16[192,2560]{1,0:T(8,128)(2,1)S(1)}, bf16[192,2560]{1,0:T(8,128)(2,1)}, u32[]{:S(2)}) copy-start(bf16[192,2560]{1,0:T(8,128)(2,1)} %k_ref.5) | copy-start | bytes 2949124
  3.6 11.4 %copy-start.5 = (bf16[192,2560]{1,0:T(8,128)(2,1)S(1)}, bf16[192,2560]{1,0:T(8,128)(2,1)}, u32[]{:S(2)}) copy-start(bf16[192,2560]{1,0:T(8,128)(2,1)} %v_ref.5) | copy-start | bytes 2949124
  5.5 9.5 %collective-permute-start.1 = (bf16[3,192,1280]{2,1,0:T(8,128)(2,1)}, bf16[3,192,1280]{2,1,0:T(8,128)(2,1)}, u32[]{:S(2)}, u32[]{:S(2)}) collective-permute-start(bf16[3,192,1280]{2,1,0:T(8,128)(2,1)} %get-tuple-element.19), channel_id=1, source_target_pairs={{0,8},{8,0},{16,24},{24,16},{1,9},{9,1},{17,25},{25,17},{2,10},{10... | collective-permute-start | bytes 4423688 | tf_op jit(solution)/shard_map/ppermute | solution.py:428
  6.0 5.5 %collective-permute-start.2 = (f32[2,192]{1,0:T(2,128)S(1)}, f32[2,192]{1,0:T(2,128)S(1)}, u32[]{:S(2)}, u32[]{:S(2)}) collective-permute-start(f32[2,192]{1,0:T(2,128)S(1)} %get-tuple-element.21), channel_id=1, source_target_pairs={{0,4},{4,0},{1,5},{5,1},{2,6},{6,2},{3,7},{7,3},{8,12},{12,8},{9,1... | collective-permute-start | bytes 4616 | tf_op jit(solution)/shard_map/ppermute | solution.py:446
  9.2 4.3 %collective-permute-start = (f32[1,192]{1,0:T(1,128)S(1)}, f32[1,192]{1,0:T(1,128)S(1)}, u32[]{:S(2)}, u32[]{:S(2)}) collective-permute-start(f32[1,192]{1,0:T(1,128)S(1)} %bitcast.17), channel_id=1, source_target_pairs={{0,8},{8,0},{16,24},{24,16},{1,9},{9,1},{17,25},{25,17},{2,10},{10... | collective-permute-start | bytes 2312 | tf_op jit(solution)/shard_map/ppermute | solution.py:417
  9.4 14.9 %collective-permute-start.4 = (bf16[2,96,2560]{2,1,0:T(8,128)(2,1)}, bf16[2,96,2560]{2,1,0:T(8,128)(2,1)}, u32[]{:S(2)}, u32[]{:S(2)}) collective-permute-start(bf16[2,96,2560]{2,1,0:T(8,128)(2,1)} %get-tuple-element.25), channel_id=1, source_target_pairs={{8,16},{16,8},{9,17},{17,9},{10,18},{18,10},{11,19},{19,11},{12,20... | collective-permute-start | bytes 2949128 | tf_op jit(solution)/shard_map/ppermute | solution.py:429
  11.5 2.8 %collective-permute-start.3 = (f32[2,192]{1,0:T(2,128)S(1)}, f32[2,192]{1,0:T(2,128)S(1)}, u32[]{:S(2)}, u32[]{:S(2)}) collective-permute-start(f32[2,192]{1,0:T(2,128)S(1)} %add.79), channel_id=1, source_target_pairs={{0,8},{8,0},{16,24},{24,16},{1,9},{9,1},{17,25},{25,17},{2,10},{10... | collective-permute-start | bytes 4616 | tf_op jit(solution)/shard_map/ppermute | solution.py:447
  14.4 18.5 %collective-permute-start.6 = (f32[2,384]{1,0:T(2,128)S(1)}, f32[2,384]{1,0:T(2,128)S(1)}, u32[]{:S(2)}, u32[]{:S(2)}) collective-permute-start(f32[2,384]{1,0:T(2,128)S(1)} %maximum_select_fusion.sums), channel_id=1, source_target_pairs={{0,16},{8,24},{16,0},{24,8},{1,17},{9,25},{17,1},{25,9},{2,18},{10... | collective-permute-start | bytes 9224 | tf_op jit(solution)/shard_map/ppermute | solution.py:455
  22.1 13.1 %collective-permute-start.7 = (bf16[1600,128]{1,0:T(8,128)(2,1)}, bf16[1600,128]{1,0:T(8,128)(2,1)}, u32[]{:S(2)}, u32[]{:S(2)}) collective-permute-start(bf16[1600,128]{1,0:T(8,128)(2,1)} %get-tuple-element.22), channel_id=1, source_target_pairs={{0,16},{8,24},{16,0},{24,8},{1,17},{9,25},{17,1},{25,9},{2,18},{10... | collective-permute-start | bytes 1228808 | tf_op jit(solution)/shard_map/ppermute | solution.py:457
  23.3 22.2 %collective-permute-start.8 = (bf16[1600,128]{1,0:T(8,128)(2,1)}, bf16[1600,128]{1,0:T(8,128)(2,1)}, u32[]{:S(2)}, u32[]{:S(2)}) collective-permute-start(bf16[1600,128]{1,0:T(8,128)(2,1)} %get-tuple-element.26), channel_id=1, source_target_pairs={{0,16},{8,24},{16,0},{24,8},{1,17},{9,25},{17,1},{25,9},{2,18},{10... | collective-permute-start | bytes 1228808 | tf_op jit(solution)/shard_map/ppermute | solution.py:458
  24.4 10.8 %collective-permute-start.5 = (bf16[2,96,2560]{2,1,0:T(8,128)(2,1)}, bf16[2,96,2560]{2,1,0:T(8,128)(2,1)}, u32[]{:S(2)}, u32[]{:S(2)}) collective-permute-start(bf16[2,96,2560]{2,1,0:T(8,128)(2,1)} %collective-permute-done.4.refs_1_), channel_id=1, source_target_pairs={{8,0},{16,24},{9,1},{17,25},{10,2},{18,26},{11,3},{19,27},{12,4},{... | collective-permute-start | bytes 2949128 | tf_op jit(solution)/shard_map/ppermute | solution.py:497
  29.0 1.0 %copy-start.6 = (f32[768,128]{1,0:T(8,128)S(1)}, f32[768,128]{1,0:T(8,128)}, u32[]{:S(2)}) copy-start(f32[768,128]{1,0:T(8,128)} %get-tuple-element.40.cosine.refs_3_) | copy-start | bytes 1179652
  30.0 5.2 %copy-start.7 = (f32[768,128]{1,0:T(8,128)S(1)}, f32[768,128]{1,0:T(8,128)}, u32[]{:S(2)}) copy-start(f32[768,128]{1,0:T(8,128)} %get-tuple-element.40.cosine.refs_3_) | copy-start | bytes 1179652
  45.4 6.6 %collective-permute-start.11 = (bf16[640,128]{1,0:T(8,128)(2,1)S(1)}, bf16[640,128]{1,0:T(8,128)(2,1)S(1)}, u32[]{:S(2)}, u32[]{:S(2)}) collective-permute-start(bf16[640,128]{1,0:T(8,128)(2,1)S(1)} %get-tuple-element.32), channel_id=1, source_target_pairs={{0,16},{8,24},{16,0},{24,8},{1,17},{9,25},{17,1},{25,9},{2,18},{10... | collective-permute-start | bytes 491528 | tf_op jit(solution)/shard_map/ppermute | solution.py:501
  51.3 1.7 %collective-permute-start.10 = (bf16[192,640]{1,0:T(8,128)(2,1)S(1)}, bf16[192,640]{1,0:T(8,128)(2,1)S(1)}, u32[]{:S(2)}, u32[]{:S(2)}) collective-permute-start(bf16[192,640]{1,0:T(8,128)(2,1)S(1)} %get-tuple-element.31), channel_id=1, source_target_pairs={{0,8},{8,0},{16,24},{24,16},{1,9},{9,1},{17,25},{25,17},{2,10},{10... | collective-permute-start | bytes 737288 | tf_op jit(solution)/shard_map/ppermute | solution.py:504
  51.8 1.5 %collective-permute-start.9 = (bf16[192,640]{1,0:T(8,128)(2,1)S(1)}, bf16[192,640]{1,0:T(8,128)(2,1)S(1)}, u32[]{:S(2)}, u32[]{:S(2)}) collective-permute-start(bf16[192,640]{1,0:T(8,128)(2,1)S(1)} %get-tuple-element.30), channel_id=1, source_target_pairs={{0,8},{8,0},{16,24},{24,16},{1,9},{9,1},{17,25},{25,17},{2,10},{10... | collective-permute-start | bytes 737288 | tf_op jit(solution)/shard_map/ppermute | solution.py:502
  52.0 1.6 %collective-permute-start.12 = (bf16[640,128]{1,0:T(8,128)(2,1)S(1)}, bf16[640,128]{1,0:T(8,128)(2,1)S(1)}, u32[]{:S(2)}, u32[]{:S(2)}) collective-permute-start(bf16[640,128]{1,0:T(8,128)(2,1)S(1)} %collective-permute-done.11.back_here), channel_id=1, source_target_pairs={{0,8},{8,0},{16,24},{24,16},{1,9},{9,1},{17,25},{25,17},{2,10},{10... | collective-permute-start | bytes 491528 | tf_op jit(solution)/shard_map/ppermute | solution.py:505

commit v5 on v4

v5 whole, which is shorter than its diff:
```python
import functools
import math

import jax
import jax.numpy as jnp
from jax import lax
from jax.experimental import pallas as pl
from jax.experimental.pallas import tpu as pltpu
from jax.sharding import PartitionSpec as P

HD = 128
D = 5120
CLIPS = 4
EPSILON = 1e-06
NEGATIVE = -1e30
ROTARY_BASE = 10000.0
block_limit = 1024

ROWS = 192
CHIP = 2 * ROWS
MOST = 480
NEAR = 96
REST = CHIP - NEAR
HALF = 5
WIDE = HALF * HD
TILE = 192
SHORT = 640
FIRST_ROWS = 1600
SECOND_ROWS = 1600
SUM_ROWS = 32
STREAM_ROWS = FIRST_ROWS + SECOND_ROWS
BACK_ROWS = 640
ACROSS = ((0, 2), (1, 3), (2, 0), (3, 1))
BESIDE = ((0, 1), (1, 0), (2, 3), (3, 2))
STRAIGHT = ((1, 3), (2, 0))
SLANTED = ((1, 2), (2, 1))
OTHER_ROW = ((0, 1), (1, 0))
OPPOSITE = tuple((2 * a + r, 2 * b + 1 - r) for a, b in BESIDE for r in (0, 1))
SCORE_SCALE = math.log2(math.e) / math.sqrt(HD)
VMEM = 24 * 1024 * 1024
ALL_VMEM = 60 * 1024 * 1024


def plan(start, side):
    first = start // 16 * 16
    last = (start + MOST + 15) // 16 * 16
    below, above = CHIP - first, last - CHIP
    mine = jnp.where(side == 0, below, above)
    theirs = jnp.where(side == 0, above, below)
    most = jnp.maximum(mine, theirs)
    lent = sum((most > limit).astype(jnp.int32) for limit in (256, 272, 288, 320, 352))
    return first, mine, theirs, HALF - lent, (mine > theirs).astype(jnp.int32)


def sixteen(offset):
    return pl.multiple_of(offset, 16)


def deal_kernel(me_ref, q_ref, k_ref, v_ref, ids, out, near_own, near_other, sums):
    me = me_ref[0]
    core = lax.rem(me, 2)
    half = out.shape[2]
    at = pl.ds(pl.multiple_of((1 - core) * half, 128), half)
    own = pl.ds(pl.multiple_of(core * half, 128), half)
    rows = pl.ds(sixteen((1 - me // 2) * NEAR), NEAR)
    for i, ref in enumerate((k_ref, v_ref)):
        near_own[i] = ref[rows, own]
        near_other[i] = ref[rows, at]
    for i, ref in enumerate((q_ref, k_ref, v_ref)):
        out[i] = ref[:, at]
    for i, ref in enumerate((q_ref, k_ref)):
        lanes = jnp.zeros((ROWS, HD), jnp.float32)
        for column in range(0, ref.shape[1], HD):
            x = ref[:, column : column + HD].astype(jnp.float32)
            lanes += x * x
        sums[i : i + 1, :] = jnp.sum(jnp.transpose(lanes), axis=0, keepdims=True)
    sums[2:3, :] = ids[...].astype(jnp.float32)


def side_by_side(core, here, there, out):
    for ref, at in ((here, 0), (there, 1)):

        @pl.when(core == at)
        def _():
            out[:, :ROWS] = ref

        @pl.when(core != at)
        def _():
            out[:, ROWS:] = ref


def pack_kernel(
    me_ref, q_ref, k_ref, v_ref, mate, sums, mate_sums, row_sums, mate_row_sums,
    first_out, second_out, totals, info, chip, buffer,
):
    me = me_ref[0]
    side, core = me // 2, lax.rem(me, 2)
    here, there = sums[2:3, :], mate_sums[2:3, :]
    edge = jnp.where(
        side == 0,
        jnp.maximum(jnp.max(here), jnp.max(there)),
        jnp.minimum(jnp.min(here), jnp.min(there)),
    )
    count = (
        jnp.sum(jnp.where(here == edge, 1.0, 0.0)) + jnp.sum(jnp.where(there == edge, 1.0, 0.0))
    ).astype(jnp.int32)
    start = jnp.where(side == 0, CHIP - count, count - NEAR)
    first, mine, theirs, kept, major = plan(start, side)
    known = (core, side, theirs, kept, major, edge.astype(jnp.int32), mine, first, start)
    for i, value in enumerate(known):
        info[i] = value
    half = chip.shape[2]
    columns = pl.ds(pl.multiple_of(core * half, 128), half)
    for i, ref in enumerate((q_ref, k_ref, v_ref)):
        chip[i, pl.ds(sixteen(core * ROWS), ROWS), :] = ref[:, columns]
        chip[i, pl.ds(sixteen((1 - core) * ROWS), ROWS), :] = mate[i]
        chip[i, CHIP:, :] = jnp.zeros((NEAR, half), ref.dtype)
    buffer[...] = jnp.zeros_like(buffer)
    near_at = jnp.where(side == 0, REST, 0)
    rest_at = jnp.where(side == 0, first, NEAR)
    rest = mine - NEAR

    def put(offset, which, head, row, length):
        at = slice(head * HD, (head + 1) * HD)

        def step(i, carry):
            buffer[pl.ds(sixteen(offset + i * NEAR), NEAR), :] = chip[
                which, pl.ds(sixteen(row + i * NEAR), NEAR), at
            ]
            return carry

        lax.fori_loop(0, (length + NEAR - 1) // NEAR, step, 0)

    offset = jnp.int32(0)
    for i in range(HALF):
        head = HALF + i
        lend = jnp.logical_and(i >= kept, major == 0)
        send = jnp.logical_or(i < kept, major == 0)
        put(offset, 0, head, near_at, jnp.where(lend, NEAR, 0))
        offset += jnp.where(lend, NEAR, 0)
        put(offset, 0, head, rest_at, jnp.where(lend, rest, 0))
        offset += jnp.where(lend, rest, 0)
        length = jnp.where(send, rest, 0)
        for which in (1, 2):
            put(offset, which, head, rest_at, length)
            offset += length
    for head in range(HALF):
        for which in (1, 2):
            put(offset, which, head, rest_at, rest)
            offset += rest
    side_by_side(
        core, sums[:2, :] + row_sums[:2, :], mate_sums[:2, :] + mate_row_sums[:2, :], totals
    )
    parts = []
    for i in range(2):
        left = totals[i : i + 1, :]
        for _ in range(3):
            part = left.astype(jnp.bfloat16)
            left = left - part.astype(jnp.float32)
            parts += [part[:, t : t + HD] for t in range(0, CHIP, HD)]
    parts += [jnp.zeros_like(parts[0])] * (SUM_ROWS - len(parts))
    first_out[:FIRST_ROWS, :] = buffer[:FIRST_ROWS, :]
    first_out[FIRST_ROWS:, :] = jnp.concatenate(parts, axis=0)
    second_out[...] = buffer[FIRST_ROWS:STREAM_ROWS, :]


def turn(x, gain, gain_s, swap, cosine, sine):
    other = jnp.dot(x, swap, preferred_element_type=jnp.float32)
    return ((x.astype(jnp.float32) * gain) * cosine + (other * gain_s) * sine).astype(jnp.bfloat16)


def flip(gain):
    size = gain.shape[1]
    even = lax.broadcasted_iota(jnp.int32, gain.shape, 1) % 2 == 0
    return jnp.where(even, pltpu.roll(gain, size - 1, 1), pltpu.roll(gain, 1, 1))


def signed_swap():
    at_row = lax.broadcasted_iota(jnp.int32, (HD, HD), 0)
    at_column = lax.broadcasted_iota(jnp.int32, (HD, HD), 1)
    sign = jnp.where(at_column % 2 == 0, -1.0, 1.0)
    return jnp.where(at_row == (at_column ^ 1), sign, 0.0).astype(jnp.bfloat16)


def attention(q, keys, bias, values):
    scores = lax.dot_general(
        q, keys, (((1,), (1,)), ((), ())), preferred_element_type=jnp.float32
    ) + bias
    peak = jnp.max(scores, axis=1, keepdims=True)
    weights = jnp.exp2((scores - peak) * SCORE_SCALE).astype(jnp.bfloat16)
    columns = jnp.concatenate([values, jnp.ones_like(values)], axis=1)
    sums = jnp.dot(weights, columns, preferred_element_type=jnp.float32)
    return (sums[:, :HD] / sums[:, HD:]).astype(jnp.bfloat16)


def columns_of(row):
    return jnp.transpose(jnp.broadcast_to(row, (HD, row.shape[1])))


def waves_kernel(info, grid, sums, mate_sums, freqs, cosine, sine, ids, chip_ids):
    core, side, first, start = info[0], info[1], info[7], info[8]
    edge_label = info[5]
    edge = edge_label.astype(jnp.float32)
    side_by_side(core, sums[2:3, :], mate_sums[2:3, :], chip_ids)
    here = chip_ids[...]
    slot = lax.broadcasted_iota(jnp.int32, (1, CHIP), 1)
    rest_start = jnp.where(side == 0, CHIP, first - NEAR)
    rest_end = jnp.where(side == 0, start + MOST, REST)
    token = slot + jnp.where(slot < NEAR, jnp.where(side == 0, CHIP, REST), rest_start)
    valid = jnp.logical_or(
        slot < NEAR, jnp.logical_and(token >= start, token < rest_end)
    )
    ids[:, :CHIP] = here
    ids[:, CHIP:] = jnp.where(valid, edge, -1.0)
    place = slot.astype(jnp.float32)
    offset, height, line_size = place, jnp.zeros_like(place), jnp.zeros_like(place)
    for label in range(CLIPS):
        same = here == float(label)
        below = jnp.sum(jnp.where(here < float(label), 1.0, 0.0), axis=1, keepdims=True)
        offset = offset - jnp.where(same, below, 0.0)
        height = height + jnp.where(same, grid[label, 0].astype(jnp.float32), 0.0)
        line_size = line_size + jnp.where(same, grid[label, 1].astype(jnp.float32), 0.0)
    carried = jnp.logical_and(here == edge, side == 1)
    offset = jnp.where(carried, place + (CHIP - start).astype(jnp.float32), offset)
    far_offset = jnp.maximum(token - start, 0).astype(jnp.float32)
    ones = jnp.ones_like(place)
    offset = jnp.concatenate([offset, far_offset], axis=1)
    height = jnp.concatenate([height, ones * grid[edge_label, 0].astype(jnp.float32)], axis=1)
    line_size = jnp.concatenate([line_size, ones * grid[edge_label, 1].astype(jnp.float32)], axis=1)
    frame = jnp.floor((offset + 0.5) / (height * line_size))
    offset = offset - frame * (height * line_size)
    line = jnp.floor((offset + 0.5) / line_size)
    column = offset - line * line_size
    sixth_part = HD // 6
    first_dims = HD - 4 * sixth_part
    feature = lax.broadcasted_iota(jnp.int32, (1, HD), 1)
    angles = freqs[...] * jnp.where(
        feature < first_dims,
        columns_of(frame),
        jnp.where(feature < first_dims + 2 * sixth_part, columns_of(line), columns_of(column)),
    )
    cosine[...] = jnp.cos(angles)
    sine[...] = jnp.sin(angles)


def turn_kernel(info, q_ref, k_ref, v_ref, mate, cosine, sine, totals, gq, gk, out, table):
    core = info[0]
    half = out.shape[2]
    columns = pl.ds(pl.multiple_of(core * half, 128), half)
    swap = signed_swap()
    for i in range(2):
        scale = columns_of(lax.rsqrt(totals[i : i + 1, :] / D + EPSILON))
        for j, ref in enumerate((cosine, sine)):
            table[2 * i + j] = ref[:CHIP, :] * scale
    for here, rows in ((True, core), (False, 1 - core)):
        rows = pl.ds(sixteen(rows * ROWS), ROWS)
        out[2, rows, :] = v_ref[:, columns] if here else mate[2]
        for i, (ref, gains) in enumerate(((q_ref, gq), (k_ref, gk))):
            cos_here, sin_here = table[2 * i, rows, :], table[2 * i + 1, rows, :]
            for h in range(half // HD):
                at = slice(h * HD, (h + 1) * HD)
                place = pl.ds(pl.multiple_of(core * half + h * HD, 128), HD)
                gain = gains[:, place]
                x = ref[:, place] if here else mate[i, :, at]
                out[i, rows, at] = turn(x, gain, flip(gain), swap, cos_here, sin_here)


def attend_kernel(flexible, head, count, info, *refs):
    local, near_straight, near_slanted, gq, gk, ids = refs[:6]
    streams = 1 if flexible else 2
    refs = refs[6:]
    if flexible:
        (cosine, sine), refs = refs[:2], refs[2:]
    else:
        table, refs = refs[0], refs[1:]
    arrived, refs = refs[:streams], refs[streams:]
    own_out, mate_out, refs = refs[0], refs[1], refs[2:]
    if flexible:
        back, table, refs = refs[0], refs[1], refs[2:]
    near, stream, bias, keys, values, result, sems = refs[:7]
    core, side, theirs, kept, major = info[0], info[1], info[2], info[3], info[4]
    edge = info[5].astype(jnp.float32)
    inner = side != core
    rest = theirs - NEAR
    near_columns = slice(head * HD, (head + count) * HD)
    sizes = (FIRST_ROWS, SECOND_ROWS)[:streams]
    copies, filled = [], 0
    for i, (ref, size) in enumerate(zip(arrived, sizes)):
        copies.append(
            pltpu.make_async_copy(
                ref.at[:size, :], stream.at[filled : filled + size, :], sems.at[1 + i]
            )
        )
        filled += size
    near_copies = [
        pltpu.make_async_copy(ref.at[:, :, near_columns], near, sems.at[0])
        for ref in (near_slanted, near_straight)
    ]
    for copy in copies:
        copy.start()
    pl.when(inner)(near_copies[0].start)
    pl.when(jnp.logical_not(inner))(near_copies[1].start)
    stream[filled:, :] = jnp.zeros((REST, HD), stream.dtype)

    columns = pl.ds(pl.multiple_of((2 * HALF * core + head) * HD, 128), count * HD)
    gq, gk = gq[:, columns], gk[:, columns]
    clip_of = columns_of(ids[:, :CHIP])
    for t in range(0, 2 * CHIP, HD):
        bias[:, t : t + HD] = jnp.where(clip_of == ids[:, t : t + HD], 0.0, NEGATIVE)
    for h in range(count):
        here = slice((head + h) * HD, (head + h + 1) * HD)
        keys[h, :CHIP, :] = local[1, :, here]
        values[h, :CHIP, :] = local[2, :, here]
    if flexible:
        back_rows, asked, scales, extra = refs[7:11]
        first = info[7]
        sum_copy = pltpu.make_async_copy(arrived[0].at[FIRST_ROWS:, :], extra, sems.at[4])
        sum_copy.start()
        near_rows = pl.ds(sixteen(jnp.where(side == 0, 0, REST)), NEAR)
        rest_rows = pl.ds(sixteen(jnp.where(side == 0, NEAR, first)), REST)
        scales[CHIP:, :] = jnp.ones((REST, HD), jnp.float32)
        back_rows[...] = jnp.zeros_like(back_rows)
        sum_copy.wait()
        parts = extra[...].astype(jnp.float32)
        for i, waves in enumerate((asked, table)):
            for j in range(3):
                total = sum(parts[9 * i + 3 * p + j : 9 * i + 3 * p + j + 1, :] for p in range(3))
                scales[j * HD : (j + 1) * HD, :] = columns_of(lax.rsqrt(total / D + EPSILON))
            for j, ref in enumerate((cosine, sine)):
                waves[j, :NEAR, :] = ref[CHIP : CHIP + NEAR, :] * scales[near_rows, :]
                waves[j, NEAR:, :] = ref[CHIP + NEAR :, :] * scales[rest_rows, :]
    near_copies[0].wait()
    for copy in copies:
        copy.wait()

    swap = signed_swap()
    if flexible:
        base = jnp.int32(0)
    else:
        base = 2 * rest * kept + jnp.where(major == 1, (HALF - kept) * (2 * rest + theirs), 0)
        base += 2 * rest * head
    bases = []
    for h in range(count):
        at = slice(h * HD, (h + 1) * HD)
        gain = gk[:, at]
        key_at = base
        bases.append(base)
        if flexible:
            lend = jnp.logical_and(h >= kept, major == 1)
            took = jnp.logical_or(h < kept, major == 1)
            key_at = base + jnp.where(lend, theirs, 0)
            base += jnp.where(took, 2 * rest, 0) + jnp.where(lend, theirs, 0)
        else:
            base += 2 * rest
        far = jnp.concatenate([near[0, :, at], stream[pl.ds(sixteen(key_at), REST), :]], axis=0)
        keys[h, CHIP:, :] = turn(far, gain, flip(gain), swap, table[0], table[1])
        values[h, CHIP : CHIP + NEAR, :] = near[1, :, at]
        values[h, CHIP + NEAR :, :] = stream[pl.ds(sixteen(key_at + rest), REST), :]

    def answer_here(seen):
        for h in range(count):
            at = slice(h * HD, (h + 1) * HD)
            here = slice((head + h) * HD, (head + h + 1) * HD)
            for t in range(0, CHIP, TILE):
                rows = slice(t, t + TILE)
                result[rows, at] = attention(
                    local[0, rows, here], keys[h, :seen, :], bias[rows, :seen], values[h, :seen, :]
                )

    short = theirs <= SHORT - CHIP
    pl.when(short)(lambda: answer_here(SHORT))
    pl.when(jnp.logical_not(short))(lambda: answer_here(2 * CHIP))
    own_out[...] = result[pl.ds(sixteen(core * ROWS), ROWS), :]
    mate_out[...] = result[pl.ds(sixteen((1 - core) * ROWS), ROWS), :]
    if flexible:
        far_bias = jnp.where(ids[:, :SHORT] == edge, 0.0, NEGATIVE)

        def answer_there(t):
            for h in range(HALF):
                at = slice(h * HD, (h + 1) * HD)
                gain = gq[:, at]
                x = stream[pl.ds(sixteen(bases[h] + t), HD), :]
                far_q = turn(
                    x, gain, flip(gain), swap, asked[0, t : t + HD, :], asked[1, t : t + HD, :]
                )
                place = jnp.where(h >= kept, (h - kept) * theirs + t, BACK_ROWS + HD)
                back_rows[pl.ds(sixteen(place), HD), :] = attention(
                    far_q, keys[h, :SHORT, :], far_bias, values[h, :SHORT, :]
                )

        lending = jnp.logical_and(kept < HALF, major == 1)
        pl.when(jnp.logical_and(lending, theirs > HD))(lambda: answer_there(HD))
        pl.when(lending)(lambda: answer_there(0))
        back[...] = back_rows[:BACK_ROWS, :]


def join_kernel(
    info, flex_here, fixed_here, flex_there, fixed_there, back_here, back_there, ids, out, rows, lines
):
    core, side = info[0], info[1]
    mine = info[6]
    kept, major, first = info[3], info[4], info[7]
    edge = info[5].astype(jnp.float32)
    half = 2 * WIDE
    inside = columns_of(ids[...].astype(jnp.float32)) == edge
    for here, flex, fixed, back in (
        (True, flex_here, fixed_here, back_here),
        (False, flex_there, fixed_there, back_there),
    ):
        column = pl.multiple_of((core if here else 1 - core) * half, 128)
        out[:, pl.ds(column, WIDE)] = fixed[...]
        out[:, pl.ds(pl.multiple_of(column + WIDE, 128), WIDE)] = flex[...]

        @pl.when(jnp.logical_and(major == 0, kept < HALF))
        def _():
            rows[:BACK_ROWS, :] = back[...]
            rows[BACK_ROWS:, :] = jnp.zeros((REST, HD), rows.dtype)
            for h in range(HALF):

                @pl.when(h >= kept)
                def _():
                    base = (h - kept) * mine
                    near_at = jnp.where(side == 0, REST, 0)
                    rest_at = jnp.where(side == 0, first, NEAR)
                    lines[pl.ds(sixteen(rest_at), REST), :] = rows[
                        pl.ds(sixteen(base + NEAR), REST), :
                    ]
                    lines[pl.ds(sixteen(near_at), NEAR), :] = rows[pl.ds(sixteen(base), NEAR), :]
                    at = slice(h * HD, (h + 1) * HD)
                    place = pl.ds(pl.multiple_of(column + WIDE + h * HD, 128), HD)
                    out[:, place] = jnp.where(
                        inside, lines[pl.ds(sixteen(core * ROWS), ROWS), :], flex[:, at]
                    )


def frequencies():
    sixth_part = HD // 6
    first_dims = HD - 4 * sixth_part
    first_freqs = 1.0 / ROTARY_BASE ** (
        jnp.arange(0, first_dims, 2, dtype=jnp.float32) / first_dims
    )
    other_freqs = 1.0 / ROTARY_BASE ** (
        jnp.arange(0, 2 * sixth_part, 2, dtype=jnp.float32) / (2 * sixth_part)
    )
    return jnp.repeat(jnp.concatenate([first_freqs, other_freqs, other_freqs]), 2)[None, :]


def whole(a):
    return pl.BlockSpec(a.shape, lambda i, s: (0,) * len(a.shape))


def held():
    return pl.BlockSpec(memory_space=pltpu.VMEM)


def call(kernel, out_shape, in_specs, out_specs, scratch, scalars, *operands, limit=VMEM):
    return pl.pallas_call(
        kernel,
        out_shape=out_shape,
        grid_spec=pltpu.PrefetchScalarGridSpec(
            num_scalar_prefetch=1,
            grid=(1,),
            in_specs=in_specs,
            out_specs=out_specs,
            scratch_shapes=scratch,
        ),
        compiler_params=pltpu.CompilerParams(vmem_limit_bytes=limit),
        cost_estimate=pl.CostEstimate(flops=0, bytes_accessed=0, transcendentals=0),
    )(scalars, *operands)


def attend(flexible, head, count, info, streams, waves, local, near_straight, near_slanted, gains, ids):
    bf16, f32 = jnp.bfloat16, jnp.float32
    there = pl.BlockSpec(memory_space=pl.ANY)
    shapes = [jax.ShapeDtypeStruct((ROWS, count * HD), bf16)] * 2
    stream_rows = sum((FIRST_ROWS, SECOND_ROWS)[: len(streams)]) + REST
    scratch = [
        pltpu.VMEM((2, NEAR, count * HD), bf16),
        pltpu.VMEM((stream_rows, HD), bf16),
        pltpu.VMEM((CHIP, 2 * CHIP), f32),
        pltpu.VMEM((count, 2 * CHIP, HD), bf16),
        pltpu.VMEM((count, 2 * CHIP, HD), bf16),
        pltpu.VMEM((CHIP, count * HD), bf16),
        pltpu.SemaphoreType.DMA((5,)),
    ]
    if flexible:
        far_waves = jax.ShapeDtypeStruct((2, CHIP, HD), f32)
        shapes = shapes + [jax.ShapeDtypeStruct((BACK_ROWS, HD), bf16), far_waves]
        scratch = scratch + [
            pltpu.VMEM((BACK_ROWS + 2 * HD, HD), bf16),
            pltpu.VMEM((2, CHIP, HD), f32),
            pltpu.VMEM((CHIP + REST, HD), f32),
            pltpu.VMEM((SUM_ROWS, HD), bf16),
        ]
    operands = (local, near_straight, near_slanted, *gains, ids, *waves, *streams)
    in_specs = [held(), there, there] + [held()] * (3 + len(waves)) + [there] * len(streams)
    return call(
        functools.partial(attend_kernel, flexible, head, count), shapes,
        in_specs, [held()] * len(shapes), scratch, info, *operands,
    )


def on_device(queries, keys, values, gain_q, gain_k, clip_ids, clip_grid):
    width = queries.shape[1]
    half = width // 2
    bf16, f32 = jnp.bfloat16, jnp.float32
    me = lax.axis_index("ctx").astype(jnp.int32)
    side, core = me // 2, me % 2
    at_me = me[None]

    clip_row = clip_ids[None, :]

    near_shape = jax.ShapeDtypeStruct((2, NEAR, half), bf16)
    deal_shapes = [
        jax.ShapeDtypeStruct((3, ROWS, half), bf16),
        near_shape,
        near_shape,
        jax.ShapeDtypeStruct((3, ROWS), f32),
    ]
    dealt, near_own, near_other, sums = call(
        deal_kernel, deal_shapes, [whole(queries)] * 3 + [whole(clip_row)],
        [whole(s) for s in deal_shapes], [], at_me, queries, keys, values, clip_row, limit=ALL_VMEM,
    )
    near_straight = lax.ppermute(near_own, "ctx", STRAIGHT)
    near_slanted = lax.ppermute(near_other, "ctx", SLANTED)
    mate = lax.ppermute(dealt, "ctx", BESIDE)
    mate_sums = lax.ppermute(sums, "ctx", BESIDE)
    row_sums = lax.ppermute(sums, "row", OTHER_ROW)
    mate_row_sums = lax.ppermute(sums, ("ctx", "row"), OPPOSITE)
    stream_shapes = [
        jax.ShapeDtypeStruct((FIRST_ROWS + SUM_ROWS, HD), bf16),
        jax.ShapeDtypeStruct((SECOND_ROWS, HD), bf16),
        jax.ShapeDtypeStruct((2, CHIP), f32),
    ]
    first_send, second_send, totals, info = call(
        pack_kernel, stream_shapes + [jax.ShapeDtypeStruct((9,), jnp.int32)],
        [held()] * 8, [whole(shape) for shape in stream_shapes[:2]] + [held()] + [pl.BlockSpec(memory_space=pltpu.SMEM)],
        [
            pltpu.VMEM((3, CHIP + NEAR, half), bf16),
            pltpu.VMEM((STREAM_ROWS + NEAR, HD), bf16),
        ],
        at_me, queries, keys, values, mate, sums, mate_sums, row_sums, mate_row_sums,
    )

    first_stream = lax.ppermute(first_send, "ctx", ACROSS)
    second_stream = lax.ppermute(second_send, "ctx", ACROSS)
    near_straight, near_slanted, sums, _ = lax.optimization_barrier(
        (near_straight, near_slanted, sums, first_send)
    )
    wave_shape = jax.ShapeDtypeStruct((2 * CHIP, HD), f32)
    cosine, sine, mask_ids = call(
        waves_kernel, [wave_shape, wave_shape, jax.ShapeDtypeStruct((1, 2 * CHIP), f32)],
        [pl.BlockSpec(memory_space=pltpu.SMEM)] + [held()] * 3, [held()] * 3,
        [pltpu.VMEM((1, CHIP), f32)], info, clip_grid, sums, mate_sums, frequencies(),
    )
    gains = (gain_q[None, :], gain_k[None, :])
    local_shape = jax.ShapeDtypeStruct((3, CHIP, half), bf16)
    local = call(
        turn_kernel, local_shape, [held()] * 9, held(), [pltpu.VMEM((4, CHIP, HD), f32)],
        info, queries, keys, values, mate, cosine, sine, totals, *gains,
    )
    common = (local, near_straight, near_slanted, gains, mask_ids)
    flex_here, flex_send, back_send, far_waves = attend(
        True, HALF, HALF, info, (first_stream,), (cosine, sine), *common
    )
    back_here = lax.ppermute(back_send, "ctx", ACROSS)
    flex_there = lax.ppermute(flex_send, "ctx", BESIDE)
    fixed_here, fixed_send = attend(
        False, 0, HALF, info, (first_stream, second_stream), (far_waves,), *common
    )
    fixed_there = lax.ppermute(fixed_send, "ctx", BESIDE)
    back_here, _ = lax.optimization_barrier((back_here, fixed_send))
    back_there = lax.ppermute(back_here, "ctx", BESIDE)
    out_shape = jax.ShapeDtypeStruct((ROWS, width), bf16)
    operands = (
        flex_here, fixed_here, flex_there, fixed_there, back_here, back_there, clip_row
    )
    return call(
        join_kernel, out_shape, [held()] * len(operands), whole(out_shape),
        [pltpu.VMEM((BACK_ROWS + REST, HD), bf16), pltpu.VMEM((2 * REST, HD), bf16)],
        info, *operands,
    )


def lookup(lookup_table, positions):
    labels = jnp.arange(lookup_table.shape[0], dtype=jnp.int32)
    return jnp.sum(
        jnp.where(positions[:, None] == labels[None, :], lookup_table[None, :], 0), axis=1
    )


def spin(matrix, offsets, clip_of, clip_grid, head_size):
    row_count = matrix.shape[0]
    sixth_part = head_size // 6
    first_dims = head_size - 4 * sixth_part
    first_freqs = 1.0 / ROTARY_BASE ** (
        jnp.arange(0, first_dims, 2, dtype=jnp.float32) / first_dims
    )
    other_freqs = 1.0 / ROTARY_BASE ** (
        jnp.arange(0, 2 * sixth_part, 2, dtype=jnp.float32) / (2 * sixth_part)
    )
    heights = lookup(clip_grid[:, 0], clip_of)
    widths = lookup(clip_grid[:, 1], clip_of)
    frame_pos = offsets // (heights * widths)
    line_pos = offsets // widths % heights
    column_pos = offsets % widths
    angles = jnp.concatenate(
        [
            frame_pos.astype(jnp.float32)[:, None] * first_freqs[None, :],
            line_pos.astype(jnp.float32)[:, None] * other_freqs[None, :],
            column_pos.astype(jnp.float32)[:, None] * other_freqs[None, :],
        ],
        axis=1,
    )
    cosine = jnp.repeat(jnp.cos(angles), 2, axis=1)
    sine_table = jnp.repeat(jnp.sin(angles), 2, axis=1)
    feature = jnp.arange(head_size, dtype=jnp.int32)
    is_even = (feature % 2 == 0)[None, None, :]
    head_view = matrix.reshape(row_count, -1, head_size)
    partner = jnp.where(is_even, -jnp.roll(head_view, -1, axis=2), jnp.roll(head_view, 1, axis=2))
    turned = head_view * cosine[:, None, :] + partner * sine_table[:, None, :]
    return turned.reshape(row_count, -1)


def on_any(queries, keys, values, gain_q, gain_k, clip_ids, clip_grid):
    rows_here, width_here = queries.shape
    heads_here = width_here // HD
    score_scale = 1.0 / math.sqrt(HD)
    query_wide = queries.astype(jnp.float32)
    key_wide = keys.astype(jnp.float32)
    squares = lax.psum(
        (jnp.sum(query_wide * query_wide, axis=1), jnp.sum(key_wide * key_wide, axis=1)), "row"
    )
    query_scale = lax.rsqrt(squares[0] / D + EPSILON)
    key_scale = lax.rsqrt(squares[1] / D + EPSILON)
    labels = jnp.arange(CLIPS, dtype=jnp.int32)
    local_counts = jnp.sum((clip_ids[:, None] == labels[None, :]).astype(jnp.int32), axis=0)
    totals = lax.psum(local_counts, "ctx")
    starts = jnp.cumsum(totals) - totals
    first_row = lax.axis_index("ctx") * rows_here
    offsets = first_row + jnp.arange(rows_here, dtype=jnp.int32) - lookup(starts, clip_ids)
    query_rot = spin(
        query_wide * query_scale[:, None] * gain_q[None, :], offsets, clip_ids, clip_grid, HD
    ).astype(jnp.bfloat16)
    query_heads = query_rot.reshape(rows_here, heads_here, HD)
    key_send = spin(
        key_wide * key_scale[:, None] * gain_k[None, :], offsets, clip_ids, clip_grid, HD
    ).astype(jnp.bfloat16)
    initial = (
        jnp.full((heads_here, rows_here), NEGATIVE, jnp.float32),
        jnp.zeros((heads_here, rows_here), jnp.float32),
        jnp.zeros((rows_here, heads_here, HD), jnp.float32),
    )
    running = initial
    piece_start = jnp.int32(0)
    key_piece = lax.all_gather(key_send, "ctx", axis=0, tiled=True)
    value_piece = lax.all_gather(values, "ctx", axis=0, tiled=True)
    row_count = key_piece.shape[0]
    block_rows = min(row_count, block_limit)
    for block_first in range(0, row_count, block_rows):
        block_size = min(block_rows, row_count - block_first)
        fold_key_rows = key_piece[block_first : block_first + block_size]
        fold_value_rows = value_piece[block_first : block_first + block_size]
        key_index = piece_start + block_first + jnp.arange(fold_key_rows.shape[0], dtype=jnp.int32)
        key_key_clips = (
            jnp.sum((starts[None, :] <= key_index[:, None]).astype(jnp.int32), axis=1) - 1
        )
        peak_old, total_old, summed_old = running
        key_view = fold_key_rows.reshape(fold_key_rows.shape[0], heads_here, HD)
        value_view = fold_value_rows.reshape(fold_value_rows.shape[0], heads_here, HD)
        scores = (
            jnp.einsum("qhd,khd->hqk", query_heads, key_view, preferred_element_type=jnp.float32)
            * score_scale
        )
        same = clip_ids[:, None] == key_key_clips[None, :]
        masked = jnp.where(same[None, :, :], scores, NEGATIVE)
        peak_new = jnp.maximum(peak_old, jnp.max(masked, axis=2))
        weights = jnp.where(same[None, :, :], jnp.exp(masked - peak_new[:, :, None]), 0.0)
        factor = jnp.exp(peak_old - peak_new)
        total_new = total_old * factor + jnp.sum(weights, axis=2)
        summed = summed_old * jnp.transpose(factor)[:, :, None] + jnp.einsum(
            "hqk,khd->qhd",
            weights.astype(jnp.bfloat16),
            value_view,
            preferred_element_type=jnp.float32,
        )
        running = (peak_new, total_new, summed)
    attended = running[2] / jnp.transpose(running[1])[:, :, None]
    return attended.reshape(rows_here, width_here).astype(jnp.bfloat16)


def solution(mesh):
    in_specs = (
        P(("batch", "ctx"), "row"),
        P(("batch", "ctx"), "row"),
        P(("batch", "ctx"), "row"),
        P("row"),
        P("row"),
        P(("batch", "ctx")),
        P("batch", None),
    )
    out_specs = P(("batch", "ctx"), "row")
    pair_of_chips = mesh.shape["ctx"] == 4 and mesh.shape["row"] == 2
    return jax.shard_map(
        on_device if pair_of_chips else on_any,
        mesh=mesh, in_specs=in_specs, out_specs=out_specs, check_vma=False,
    )
```

time: 55.4 us -> 50.1 us (0.904); the launches traced: 55.2 us -> 49.2 us
  other arithmetic: 4.95 us -> 0.1 us
  Pallas kernels: 26 us -> 21.2 us
  starting transfers between devices: 11.9 us -> 16.2 us
  waiting for transfers between devices: 4.33 us -> 8.43 us
  local copies, waits for them, and re-layouts: 5.56 us -> 3.15 us
  between operations: 2.5 us -> 0.17 us
    pallas_call x6 -> x7, Pallas kernels: 26 us -> 21.2 us  [call(): pl.pallas_call(kernel, out_shape=out_shape, grid_spec=pltpu.PrefetchScala...]
    ppermute x1, starting transfers between devices: 0.07 us -> 3.97 us  [on_device(): back_here = lax.ppermute(back_send, 'ctx', ACROSS)]
    ppermute x5 -> x4, waiting for transfers between devices: 0.01 us -> 3.03 us  [the longest x1 1.7 us: on_device(): row_sums = lax.ppermute(sums, 'row', OTHER_ROW)]
    sin x1 -> x0, other arithmetic: 2.72 us -> none  [on_device(): waves = (jnp.cos(angles), jnp.sin(angles))]
    ppermute x5 -> x4, starting transfers between devices: 6.31 us -> 8.4 us  [the longest x1 5.3 us: on_device(): mate_row_sums = lax.ppermute(sums, ('ctx', 'row'), OPPOSITE)]
    unnamed x22 -> x25, local copies, waits for them, and re-layouts: 4.63 us -> 2.91 us
    ppermute x1, waiting for transfers between devices: 2.26 us -> 3.88 us  [on_device(): first_stream = lax.ppermute(first_send, 'ctx', ACROSS)]
    ppermute x1, starting transfers between devices: 1.98 us -> 0.58 us  [on_device(): mate_sums = lax.ppermute(sums, 'ctx', BESIDE)]
  transfers between devices with their start and end apart: 13 -> 12, of which waited for: 6 -> 6; matrix products, arithmetic and copies ran while one was open for 11% -> 1% of each run, Pallas kernels for 41% -> 31%
where the time goes in v5:
time: 50.1 us; the launch traced here: 49.2 us
  Pallas kernels  21.2 us (42%)
  starting transfers between devices  16.2 us (32%)
  waiting for transfers between devices  8.43 us (17%)
  local copies, waits for them, and re-layouts  3.15 us (6%)
    pallas_call x7, Pallas kernels, call(): pl.pallas_call(kernel, out_shape=out_shape, grid_spec=pltpu.PrefetchScala...  21.2 us
    ppermute x1, starting transfers between devices, on_device(): mate_row_sums = lax.ppermute(sums, ('ctx', 'row'), OPPOSITE)  5.3 us
    ppermute x1, starting transfers between devices, on_device(): back_here = lax.ppermute(back_send, 'ctx', ACROSS)  3.97 us
    ppermute x1, waiting for transfers between devices, on_device(): first_stream = lax.ppermute(first_send, 'ctx', ACROSS)  3.88 us
    unnamed x25, local copies, waits for them, and re-layouts  2.91 us
    ppermute x1, waiting for transfers between devices, on_device(): row_sums = lax.ppermute(sums, 'row', OTHER_ROW)  1.7 us
    ppermute x1, starting transfers between devices, on_device(): near_slanted = lax.ppermute(near_other, 'ctx', SLANTED)  1.48 us
    ppermute x1, starting transfers between devices, on_device(): near_straight = lax.ppermute(near_own, 'ctx', STRAIGHT)  1.41 us
  transfers between devices with their start and end apart: 12, of which 6 were waited for; matrix products, arithmetic and copies ran while one was open for 1% of the time, Pallas kernels for 31%

profile of v5, /device:TPU:0, one launch (start us, length us, event | category | flops | bytes accessed | tf_op | source)
XLA Modules:
  0.0 49.2 jit_solution(5570154691043986370)
XLA Ops:
  0.0 3.8 %shard_map.73 = (bf16[3,192,1280]{2,1,0:T(8,128)(2,1)}, bf16[2,96,1280]{2,1,0:T(8,128)(2,1)}, bf16[2,96,1280]{2,1,0:T(8,128)(2,1)}, f32[3,192]{1,0:T(4,128)}) custom-call(s32[1]{0:T(128)} %bitcast.me_ref, bf16[192,2560]{1,0:T(8,128)(2,1)} %q_ref.5, bf16[192,2560]{1,0:T(8,128)(2,1)} %k_ref.5, bf16[192,2560]{1,0:T(8,128)(2,1)} %v_ref.5, s32[1,192]{1,0:T(1,128)} %bitcast.2), custom_call_target="tpu_custom_call" | custom-call | tf_op jit(solution)/shard_map/pallas_call | solution.py:457
  3.8 0.5 collective-permute-start
  4.3 1.4 %collective-permute-start.4 = (bf16[2,96,1280]{2,1,0:T(8,128)(2,1)}, bf16[2,96,1280]{2,1,0:T(8,128)(2,1)S(1)}, u32[]{:S(2)}, u32[]{:S(2)}) collective-permute-start(bf16[2,96,1280]{2,1,0:T(8,128)(2,1)} %get-tuple-element.29), channel_id=1, source_target_pairs={{8,24},{16,0},{9,25},{17,1},{10,26},{18,2},{11,27},{19,3},{12,28},... | collective-permute-start | bytes 1474568 | tf_op jit(solution)/shard_map/ppermute | solution.py:524
  5.7 1.5 %collective-permute-start.5 = (bf16[2,96,1280]{2,1,0:T(8,128)(2,1)}, bf16[2,96,1280]{2,1,0:T(8,128)(2,1)}, u32[]{:S(2)}, u32[]{:S(2)}) collective-permute-start(bf16[2,96,1280]{2,1,0:T(8,128)(2,1)} %get-tuple-element.30), channel_id=1, source_target_pairs={{8,16},{16,8},{9,17},{17,9},{10,18},{18,10},{11,19},{19,11},{12,20... | collective-permute-start | bytes 1474568 | tf_op jit(solution)/shard_map/ppermute | solution.py:525
  7.2 5.3 %collective-permute-start.3 = (f32[3,192]{1,0:T(4,128)}, f32[3,192]{1,0:T(4,128)S(1)}, u32[]{:S(2)}, u32[]{:S(2)}) collective-permute-start(f32[3,192]{1,0:T(4,128)} %get-tuple-element.32.sums), channel_id=1, source_target_pairs={{0,12},{4,8},{8,4},{12,0},{16,28},{20,24},{24,20},{28,16},{1,13},{... | collective-permute-start | bytes 6920 | tf_op jit(solution)/shard_map/ppermute | solution.py:529
  12.5 0.2 collective-permute-start.2
  12.7 1.3 %collective-permute-done.3.mate_row_sums = f32[3,192]{1,0:T(4,128)S(1)} collective-permute-done((f32[3,192]{1,0:T(4,128)}, f32[3,192]{1,0:T(4,128)S(1)}, u32[]{:S(2)}, u32[]{:S(2)}) %collective-permute-start.3) | collective-permute-done | bytes 2336 | tf_op jit(solution)/shard_map/ppermute | solution.py:529
  14.0 0.6 %collective-permute-start.1 = (f32[3,192]{1,0:T(4,128)}, f32[3,192]{1,0:T(4,128)S(1)}, u32[]{:S(2)}, u32[]{:S(2)}) collective-permute-start(f32[3,192]{1,0:T(4,128)} %get-tuple-element.32.sums), channel_id=1, source_target_pairs={{0,8},{8,0},{16,24},{24,16},{1,9},{9,1},{17,25},{25,17},{2,10},{10... | collective-permute-start | bytes 6920 | tf_op jit(solution)/shard_map/ppermute | solution.py:527
  14.6 1.7 %collective-permute-done.2.row_sums = f32[3,192]{1,0:T(4,128)S(1)} collective-permute-done((f32[3,192]{1,0:T(4,128)}, f32[3,192]{1,0:T(4,128)S(1)}, u32[]{:S(2)}, u32[]{:S(2)}) %collective-permute-start.2) | collective-permute-done | bytes 2336 | tf_op jit(solution)/shard_map/ppermute | solution.py:528
  16.3 0.7 %copy-done.5 = f32[3,192]{1,0:T(4,128)S(1)} copy-done((f32[3,192]{1,0:T(4,128)S(1)}, f32[3,192]{1,0:T(4,128)}, u32[]{:S(2)}) %copy-start.5) | copy-done | bytes 2328
  17.0 1.7 %shard_map.74 = (bf16[1632,128]{1,0:T(8,128)(2,1)}, bf16[1600,128]{1,0:T(8,128)(2,1)S(1)}, f32[2,384]{1,0:T(2,128)S(1)}, s32[9]{0:T(128)S(1)}) custom-call(s32[1]{0:T(128)} %bitcast.me_ref, bf16[192,2560]{1,0:T(8,128)(2,1)S(1)} %copy-done, bf16[192,2560]{1,0:T(8,128)(2,1)S(1)} %copy-done.1, bf16[192,2560]{1,0:T(8,128)(2,1)S(1)} %copy-done.2, ...), custom_call_target="tpu_custom_call" | custom-call | tf_op jit(solution)/shard_map/pallas_call | solution.py:457
  18.7 0.7 %copy-done.8 = bf16[1600,128]{1,0:T(8,128)(2,1)} copy-done((bf16[1600,128]{1,0:T(8,128)(2,1)}, bf16[1600,128]{1,0:T(8,128)(2,1)S(1)}, u32[]{:S(2)}) %copy-start.8) | copy-done | bytes 409624
  19.5 1.2 %collective-permute-start.6 = (bf16[1632,128]{1,0:T(8,128)(2,1)}, bf16[1632,128]{1,0:T(8,128)(2,1)}, u32[]{:S(2)}, u32[]{:S(2)}) collective-permute-start(bf16[1632,128]{1,0:T(8,128)(2,1)} %get-tuple-element.31), channel_id=1, source_target_pairs={{0,16},{8,24},{16,0},{24,8},{1,17},{9,25},{17,1},{25,9},{2,18},{10... | collective-permute-start | bytes 1253384 | tf_op jit(solution)/shard_map/ppermute | solution.py:545
  20.7 0.1 copy.9.grid
  20.9 0.8 %collective-permute-start.7 = (bf16[1600,128]{1,0:T(8,128)(2,1)}, bf16[1600,128]{1,0:T(8,128)(2,1)}, u32[]{:S(2)}, u32[]{:S(2)}) collective-permute-start(bf16[1600,128]{1,0:T(8,128)(2,1)} %copy-done.8), channel_id=1, source_target_pairs={{0,16},{8,24},{16,0},{24,8},{1,17},{9,25},{17,1},{25,9},{2,18},{10... | collective-permute-start | bytes 1228808 | tf_op jit(solution)/shard_map/ppermute | solution.py:546
  21.7 0.1 pad_maximum_fusion
  21.8 0.1 broadcast_in_dim.17
  21.9 0.2 broadcast_in_dim_reshape.3.freqs
  22.1 2.9 %shard_map.75 = (f32[768,128]{1,0:T(8,128)S(1)}, f32[768,128]{1,0:T(8,128)S(1)}, f32[1,768]{1,0:T(1,128)S(1)}) custom-call(s32[9]{0:T(128)S(1)} %get-tuple-element.28.info, s32[4,2]{1,0:T(4,128)S(1)} %copy.9.grid, f32[3,192]{1,0:T(4,128)S(1)} %copy-done.6, f32[3,192]{1,0:T(4,128)S(1)} %collective-permute-done.1.mate_sums, ...), custom_call_target="tpu_custom_call" | custom-call | tf_op jit(solution)/shard_map/pallas_call | solution.py:457
  25.0 1.4 %copy-done.4 = bf16[3,192,1280]{2,1,0:T(8,128)(2,1)S(1)} copy-done((bf16[3,192,1280]{2,1,0:T(8,128)(2,1)S(1)}, bf16[3,192,1280]{2,1,0:T(8,128)(2,1)}, u32[]{:S(2)}) %copy-start.4) | copy-done | bytes 1474584
  26.3 2.1 %shard_map.76.refs_0_ = bf16[3,384,1280]{2,1,0:T(8,128)(2,1)S(1)} custom-call(s32[9]{0:T(128)S(1)} %get-tuple-element.28.info, bf16[192,2560]{1,0:T(8,128)(2,1)S(1)} %copy-done, bf16[192,2560]{1,0:T(8,128)(2,1)S(1)} %copy-done.1, bf16[192,2560]{1,0:T(8,128)(2,1)S(1)} %copy-done.2, bf16[3,192,1280]{2,1,0:T(8,128)(2,1)S(1)} %copy-done.4, ...), custom_call_target="tpu_custom_call" | custom-call | tf_op jit(solution)/shard_map/pallas_call | solution.py:457
  28.5 3.9 %collective-permute-done.6.refs_8_.refs_7_ = bf16[1632,128]{1,0:T(8,128)(2,1)} collective-permute-done((bf16[1632,128]{1,0:T(8,128)(2,1)}, bf16[1632,128]{1,0:T(8,128)(2,1)}, u32[]{:S(2)}, u32[]{:S(2)}) %collective-permute-start.6) | collective-permute-done | bytes 417824 | tf_op jit(solution)/shard_map/ppermute | solution.py:545
  32.3 4.4 %shard_map.77 = (bf16[192,640]{1,0:T(8,128)(2,1)S(1)}, bf16[192,640]{1,0:T(8,128)(2,1)S(1)}, bf16[640,128]{1,0:T(8,128)(2,1)S(1)}, f32[2,384,128]{2,1,0:T(8,128)S(1)}) custom-call(s32[9]{0:T(128)S(1)} %get-tuple-element.28.info, bf16[3,384,1280]{2,1,0:T(8,128)(2,1)S(1)} %shard_map.76.refs_0_, bf16[2,96,1280]{2,1,0:T(8,128)(2,1)S(1)} %collective-permute-done.4.refs_1_, ...), custom_call_target="tpu_custom_call" | custom-call | tf_op jit(solution)/shard_map/pallas_call | solution.py:457
  36.8 4.0 %collective-permute-start.10 = (bf16[640,128]{1,0:T(8,128)(2,1)S(1)}, bf16[640,128]{1,0:T(8,128)(2,1)S(1)}, u32[]{:S(2)}, u32[]{:S(2)}) collective-permute-start(bf16[640,128]{1,0:T(8,128)(2,1)S(1)} %get-tuple-element.45), channel_id=1, source_target_pairs={{0,16},{8,24},{16,0},{24,8},{1,17},{9,25},{17,1},{25,9},{2,18},{10... | collective-permute-start | bytes 491528 | tf_op jit(solution)/shard_map/ppermute | solution.py:566
  40.8 4.3 %shard_map.78 = (bf16[192,640]{1,0:T(8,128)(2,1)S(1)}, bf16[192,640]{1,0:T(8,128)(2,1)S(1)}) custom-call(s32[9]{0:T(128)S(1)} %get-tuple-element.28.info, bf16[3,384,1280]{2,1,0:T(8,128)(2,1)S(1)} %shard_map.76.refs_0_, bf16[2,96,1280]{2,1,0:T(8,128)(2,1)S(1)} %collective-permute-done.4.refs_1_, bf16[2,96,1280]{2,1,0:T(8,128)(2,1)} %collective-permute-done.5.refs_2_, ...), custom_call_target="tpu_custom_call" | custom-call | tf_op jit(solution)/shard_map/pallas_call | solution.py:457
  45.1 0.1 collective-permute-start.9
  45.1 0.5 %collective-permute-start.8 = (bf16[192,640]{1,0:T(8,128)(2,1)S(1)}, bf16[192,640]{1,0:T(8,128)(2,1)S(1)}, u32[]{:S(2)}, u32[]{:S(2)}) collective-permute-start(bf16[192,640]{1,0:T(8,128)(2,1)S(1)} %get-tuple-element.43), channel_id=1, source_target_pairs={{0,8},{8,0},{16,24},{24,16},{1,9},{9,1},{17,25},{25,17},{2,10},{10... | collective-permute-start | bytes 737288 | tf_op jit(solution)/shard_map/ppermute | solution.py:567
  45.6 0.1 collective-permute-start.11
  45.7 0.9 %collective-permute-done.9.fixed_there = bf16[192,640]{1,0:T(8,128)(2,1)S(1)} collective-permute-done((bf16[192,640]{1,0:T(8,128)(2,1)S(1)}, bf16[192,640]{1,0:T(8,128)(2,1)S(1)}, u32[]{:S(2)}, u32[]{:S(2)}) %collective-permute-start.9) | collective-permute-done | bytes 245792 | tf_op jit(solution)/shard_map/ppermute | solution.py:571
  46.6 0.4 collective-permute-done.8.flex_there
  47.0 0.2 collective-permute-done.11.back_there
  47.2 1.9 %shard_map.79 = bf16[192,2560]{1,0:T(8,128)(2,1)} custom-call(s32[9]{0:T(128)S(1)} %get-tuple-element.28.info, bf16[192,640]{1,0:T(8,128)(2,1)S(1)} %get-tuple-element.39.flex_here, bf16[192,640]{1,0:T(8,128)(2,1)S(1)} %get-tuple-element.42.fixed_here, bf16[192,640]{1,0:T(8,128)(2,1)S(1)} %collective-permute-done.8.flex_there, ...), custom_call_target="tpu_custom_call" | custom-call | tf_op jit(solution)/shard_map/pallas_call | solution.py:457
  (31 shorter events, 0.1 us)
Async XLA Ops:
  0.0 16.3 %copy-start = (bf16[192,2560]{1,0:T(8,128)(2,1)S(1)}, bf16[192,2560]{1,0:T(8,128)(2,1)}, u32[]{:S(2)}) copy-start(bf16[192,2560]{1,0:T(8,128)(2,1)} %q_ref.5) | copy-start | bytes 2949124
  0.0 16.3 %copy-start.1 = (bf16[192,2560]{1,0:T(8,128)(2,1)S(1)}, bf16[192,2560]{1,0:T(8,128)(2,1)}, u32[]{:S(2)}) copy-start(bf16[192,2560]{1,0:T(8,128)(2,1)} %k_ref.5) | copy-start | bytes 2949124
  0.0 16.3 %copy-start.2 = (bf16[192,2560]{1,0:T(8,128)(2,1)S(1)}, bf16[192,2560]{1,0:T(8,128)(2,1)}, u32[]{:S(2)}) copy-start(bf16[192,2560]{1,0:T(8,128)(2,1)} %v_ref.5) | copy-start | bytes 2949124
  3.8 12.5 %collective-permute-start = (bf16[3,192,1280]{2,1,0:T(8,128)(2,1)}, bf16[3,192,1280]{2,1,0:T(8,128)(2,1)S(1)}, u32[]{:S(2)}, u32[]{:S(2)}) collective-permute-start(bf16[3,192,1280]{2,1,0:T(8,128)(2,1)} %get-tuple-element.26), channel_id=1, source_target_pairs={{0,8},{8,0},{16,24},{24,16},{1,9},{9,1},{17,25},{25,17},{2,10},{10... | collective-permute-start | bytes 4423688 | tf_op jit(solution)/shard_map/ppermute | solution.py:526
  4.3 17.8 %copy-start.6 = (f32[3,192]{1,0:T(4,128)S(1)}, f32[3,192]{1,0:T(4,128)}, u32[]{:S(2)}) copy-start(f32[3,192]{1,0:T(4,128)} %get-tuple-element.32.sums) | copy-start | bytes 6916
  4.3 17.8 %collective-permute-start.4 = (bf16[2,96,1280]{2,1,0:T(8,128)(2,1)}, bf16[2,96,1280]{2,1,0:T(8,128)(2,1)S(1)}, u32[]{:S(2)}, u32[]{:S(2)}) collective-permute-start(bf16[2,96,1280]{2,1,0:T(8,128)(2,1)} %get-tuple-element.29), channel_id=1, source_target_pairs={{8,24},{16,0},{9,25},{17,1},{10,26},{18,2},{11,27},{19,3},{12,28},... | collective-permute-start | bytes 1474568 | tf_op jit(solution)/shard_map/ppermute | solution.py:524
  5.7 16.3 %collective-permute-start.5 = (bf16[2,96,1280]{2,1,0:T(8,128)(2,1)}, bf16[2,96,1280]{2,1,0:T(8,128)(2,1)}, u32[]{:S(2)}, u32[]{:S(2)}) collective-permute-start(bf16[2,96,1280]{2,1,0:T(8,128)(2,1)} %get-tuple-element.30), channel_id=1, source_target_pairs={{8,16},{16,8},{9,17},{17,9},{10,18},{18,10},{11,19},{19,11},{12,20... | collective-permute-start | bytes 1474568 | tf_op jit(solution)/shard_map/ppermute | solution.py:525
  7.2 13.5 %copy-start.11 = (s32[4,2]{0,1:T(2,128)S(1)}, s32[4,2]{0,1:T(2,128)}, u32[]{:S(2)}) copy-start(s32[4,2]{0,1:T(2,128)} %param.13) | copy-start | bytes 100
  7.2 6.8 %collective-permute-start.3 = (f32[3,192]{1,0:T(4,128)}, f32[3,192]{1,0:T(4,128)S(1)}, u32[]{:S(2)}, u32[]{:S(2)}) collective-permute-start(f32[3,192]{1,0:T(4,128)} %get-tuple-element.32.sums), channel_id=1, source_target_pairs={{0,12},{4,8},{8,4},{12,0},{16,28},{20,24},{24,20},{28,16},{1,13},{... | collective-permute-start | bytes 6920 | tf_op jit(solution)/shard_map/ppermute | solution.py:529
  12.5 3.8 %collective-permute-start.2 = (f32[3,192]{1,0:T(4,128)}, f32[3,192]{1,0:T(4,128)S(1)}, u32[]{:S(2)}, u32[]{:S(2)}) collective-permute-start(f32[3,192]{1,0:T(4,128)} %get-tuple-element.32.sums), channel_id=1, source_target_pairs={{0,4},{4,0},{1,5},{5,1},{2,6},{6,2},{3,7},{7,3},{8,12},{12,8},{9,1... | collective-permute-start | bytes 6920 | tf_op jit(solution)/shard_map/ppermute | solution.py:528
  14.0 2.3 %collective-permute-start.1 = (f32[3,192]{1,0:T(4,128)}, f32[3,192]{1,0:T(4,128)S(1)}, u32[]{:S(2)}, u32[]{:S(2)}) collective-permute-start(f32[3,192]{1,0:T(4,128)} %get-tuple-element.32.sums), channel_id=1, source_target_pairs={{0,8},{8,0},{16,24},{24,16},{1,9},{9,1},{17,25},{25,17},{2,10},{10... | collective-permute-start | bytes 6920 | tf_op jit(solution)/shard_map/ppermute | solution.py:527
  16.3 0.7 %copy-start.5 = (f32[3,192]{1,0:T(4,128)S(1)}, f32[3,192]{1,0:T(4,128)}, u32[]{:S(2)}) copy-start(f32[3,192]{1,0:T(4,128)} %get-tuple-element.32.sums) | copy-start | bytes 6916
  17.0 1.7 %copy-start.3 = (bf16[3,192,1280]{2,1,0:T(8,128)(2,1)}, bf16[3,192,1280]{2,1,0:T(8,128)(2,1)S(1)}, u32[]{:S(2)}) copy-start(bf16[3,192,1280]{2,1,0:T(8,128)(2,1)S(1)} %collective-permute-done.mate) | copy-start | bytes 4423684
  17.0 3.8 %copy-start.9 = (f32[2560]{0:T(1024)S(1)}, f32[2560]{0:T(1024)}, u32[]{:S(2)}) copy-start(f32[2560]{0:T(1024)} %param.10) | copy-start | bytes 30724
  17.0 3.8 %copy-start.10 = (f32[2560]{0:T(1024)S(1)}, f32[2560]{0:T(1024)}, u32[]{:S(2)}) copy-start(f32[2560]{0:T(1024)} %param.11) | copy-start | bytes 30724
  18.7 0.8 %copy-start.8 = (bf16[1600,128]{1,0:T(8,128)(2,1)}, bf16[1600,128]{1,0:T(8,128)(2,1)S(1)}, u32[]{:S(2)}) copy-start(bf16[1600,128]{1,0:T(8,128)(2,1)S(1)} %get-tuple-element.41) | copy-start | bytes 1228804
  19.5 12.9 %collective-permute-start.6 = (bf16[1632,128]{1,0:T(8,128)(2,1)}, bf16[1632,128]{1,0:T(8,128)(2,1)}, u32[]{:S(2)}, u32[]{:S(2)}) collective-permute-start(bf16[1632,128]{1,0:T(8,128)(2,1)} %get-tuple-element.31), channel_id=1, source_target_pairs={{0,16},{8,24},{16,0},{24,8},{1,17},{9,25},{17,1},{25,9},{2,18},{10... | collective-permute-start | bytes 1253384 | tf_op jit(solution)/shard_map/ppermute | solution.py:545
  20.9 19.9 %collective-permute-start.7 = (bf16[1600,128]{1,0:T(8,128)(2,1)}, bf16[1600,128]{1,0:T(8,128)(2,1)}, u32[]{:S(2)}, u32[]{:S(2)}) collective-permute-start(bf16[1600,128]{1,0:T(8,128)(2,1)} %copy-done.8), channel_id=1, source_target_pairs={{0,16},{8,24},{16,0},{24,8},{1,17},{9,25},{17,1},{25,9},{2,18},{10... | collective-permute-start | bytes 1228808 | tf_op jit(solution)/shard_map/ppermute | solution.py:546
  25.0 1.4 %copy-start.4 = (bf16[3,192,1280]{2,1,0:T(8,128)(2,1)S(1)}, bf16[3,192,1280]{2,1,0:T(8,128)(2,1)}, u32[]{:S(2)}) copy-start(bf16[3,192,1280]{2,1,0:T(8,128)(2,1)} %copy-done.3) | copy-start | bytes 4423684
  36.8 8.9 %collective-permute-start.10 = (bf16[640,128]{1,0:T(8,128)(2,1)S(1)}, bf16[640,128]{1,0:T(8,128)(2,1)S(1)}, u32[]{:S(2)}, u32[]{:S(2)}) collective-permute-start(bf16[640,128]{1,0:T(8,128)(2,1)S(1)} %get-tuple-element.45), channel_id=1, source_target_pairs={{0,16},{8,24},{16,0},{24,8},{1,17},{9,25},{17,1},{25,9},{2,18},{10... | collective-permute-start | bytes 491528 | tf_op jit(solution)/shard_map/ppermute | solution.py:566
  40.8 6.5 %copy-start.7 = (s32[192]{0:T(256)S(1)}, s32[192]{0:T(256)}, u32[]{:S(2)}) copy-start(s32[192]{0:T(256)} %param.12) | copy-start | bytes 2308
  45.1 1.6 %collective-permute-start.9 = (bf16[192,640]{1,0:T(8,128)(2,1)S(1)}, bf16[192,640]{1,0:T(8,128)(2,1)S(1)}, u32[]{:S(2)}, u32[]{:S(2)}) collective-permute-start(bf16[192,640]{1,0:T(8,128)(2,1)S(1)} %get-tuple-element.44), channel_id=1, source_target_pairs={{0,8},{8,0},{16,24},{24,16},{1,9},{9,1},{17,25},{25,17},{2,10},{10... | collective-permute-start | bytes 737288 | tf_op jit(solution)/shard_map/ppermute | solution.py:571
  45.1 1.9 %collective-permute-start.8 = (bf16[192,640]{1,0:T(8,128)(2,1)S(1)}, bf16[192,640]{1,0:T(8,128)(2,1)S(1)}, u32[]{:S(2)}, u32[]{:S(2)}) collective-permute-start(bf16[192,640]{1,0:T(8,128)(2,1)S(1)} %get-tuple-element.43), channel_id=1, source_target_pairs={{0,8},{8,0},{16,24},{24,16},{1,9},{9,1},{17,25},{25,17},{2,10},{10... | collective-permute-start | bytes 737288 | tf_op jit(solution)/shard_map/ppermute | solution.py:567
  45.6 1.6 %collective-permute-start.11 = (bf16[640,128]{1,0:T(8,128)(2,1)S(1)}, bf16[640,128]{1,0:T(8,128)(2,1)S(1)}, u32[]{:S(2)}, u32[]{:S(2)}) collective-permute-start(bf16[640,128]{1,0:T(8,128)(2,1)S(1)} %collective-permute-done.10.back_here), channel_id=1, source_target_pairs={{0,8},{8,0},{16,24},{24,16},{1,9},{9,1},{17,25},{25,17},{2,10},{10... | collective-permute-start | bytes 491528 | tf_op jit(solution)/shard_map/ppermute | solution.py:573

commit v6 on v5

--- a/solution.py
+++ b/solution.py
@@ -52,17 +52,29 @@
     return first, mine, theirs, HALF - lent, (mine > theirs).astype(jnp.int32)
 
 
+def position():
+    me = lax.axis_index("ctx")
+    return me // 2, lax.rem(me, 2)
+
+
+def known(info):
+    row = info[...]
+    lane = lax.broadcasted_iota(jnp.int32, row.shape, 1)
+    start = jnp.sum(jnp.where(lane == 0, row, 0.0)).astype(jnp.int32)
+    side, core = position()
+    return side, core, start, row[:, 1:2], plan(start, side)
+
+
 def sixteen(offset):
     return pl.multiple_of(offset, 16)
 
 
-def deal_kernel(me_ref, q_ref, k_ref, v_ref, ids, out, near_own, near_other, sums):
-    me = me_ref[0]
-    core = lax.rem(me, 2)
+def deal_kernel(q_ref, k_ref, v_ref, ids, out, near_own, near_other, sums):
+    side, core = position()
     half = out.shape[2]
     at = pl.ds(pl.multiple_of((1 - core) * half, 128), half)
     own = pl.ds(pl.multiple_of(core * half, 128), half)
-    rows = pl.ds(sixteen((1 - me // 2) * NEAR), NEAR)
+    rows = pl.ds(sixteen((1 - side) * NEAR), NEAR)
     for i, ref in enumerate((k_ref, v_ref)):
         near_own[i] = ref[rows, own]
         near_other[i] = ref[rows, at]
@@ -90,11 +102,10 @@
 
 
 def pack_kernel(
-    me_ref, q_ref, k_ref, v_ref, mate, sums, mate_sums, row_sums, mate_row_sums,
+    q_ref, k_ref, v_ref, mate, sums, mate_sums, row_sums, mate_row_sums,
     first_out, second_out, totals, info, chip, buffer,
 ):
-    me = me_ref[0]
-    side, core = me // 2, lax.rem(me, 2)
+    side, core = position()
     here, there = sums[2:3, :], mate_sums[2:3, :]
     edge = jnp.where(
         side == 0,
@@ -105,10 +116,9 @@
         jnp.sum(jnp.where(here == edge, 1.0, 0.0)) + jnp.sum(jnp.where(there == edge, 1.0, 0.0))
     ).astype(jnp.int32)
     start = jnp.where(side == 0, CHIP - count, count - NEAR)
-    first, mine, theirs, kept, major = plan(start, side)
-    known = (core, side, theirs, kept, major, edge.astype(jnp.int32), mine, first, start)
-    for i, value in enumerate(known):
-        info[i] = value
+    first, mine, _, kept, major = plan(start, side)
+    lane = lax.broadcasted_iota(jnp.int32, info.shape, 1)
+    info[...] = jnp.where(lane == 0, start.astype(jnp.float32), edge)
     half = chip.shape[2]
     columns = pl.ds(pl.multiple_of(core * half, 128), half)
     for i, ref in enumerate((q_ref, k_ref, v_ref)):
@@ -197,10 +207,8 @@
     return jnp.transpose(jnp.broadcast_to(row, (HD, row.shape[1])))
 
 
-def waves_kernel(info, grid, sums, mate_sums, freqs, cosine, sine, ids, chip_ids):
-    core, side, first, start = info[0], info[1], info[7], info[8]
-    edge_label = info[5]
-    edge = edge_label.astype(jnp.float32)
+def waves_kernel(grid, info, sums, mate_sums, freqs, cosine, sine, ids, chip_ids):
+    side, core, start, edge, (first, *_) = known(info)
     side_by_side(core, sums[2:3, :], mate_sums[2:3, :], chip_ids)
     here = chip_ids[...]
     slot = lax.broadcasted_iota(jnp.int32, (1, CHIP), 1)
@@ -225,8 +233,12 @@
     far_offset = jnp.maximum(token - start, 0).astype(jnp.float32)
     ones = jnp.ones_like(place)
     offset = jnp.concatenate([offset, far_offset], axis=1)
-    height = jnp.concatenate([height, ones * grid[edge_label, 0].astype(jnp.float32)], axis=1)
-    line_size = jnp.concatenate([line_size, ones * grid[edge_label, 1].astype(jnp.float32)], axis=1)
+    far_sizes = []
+    for axis in range(2):
+        sizes = [jnp.where(edge == float(c), grid[c, axis].astype(jnp.float32), 0.0) for c in range(CLIPS)]
+        far_sizes.append(ones * sum(sizes))
+    height = jnp.concatenate([height, far_sizes[0]], axis=1)
+    line_size = jnp.concatenate([line_size, far_sizes[1]], axis=1)
     frame = jnp.floor((offset + 0.5) / (height * line_size))
     offset = offset - frame * (height * line_size)
     line = jnp.floor((offset + 0.5) / line_size)
@@ -243,8 +255,8 @@
     sine[...] = jnp.sin(angles)
 
 
-def turn_kernel(info, q_ref, k_ref, v_ref, mate, cosine, sine, totals, gq, gk, out, table):
-    core = info[0]
+def turn_kernel(q_ref, k_ref, v_ref, mate, cosine, sine, totals, gq, gk, out, table):
+    _, core = position()
     half = out.shape[2]
     columns = pl.ds(pl.multiple_of(core * half, 128), half)
     swap = signed_swap()
@@ -278,8 +290,7 @@
     if flexible:
         back, table, refs = refs[0], refs[1], refs[2:]
     near, stream, bias, keys, values, result, sems = refs[:7]
-    core, side, theirs, kept, major = info[0], info[1], info[2], info[3], info[4]
-    edge = info[5].astype(jnp.float32)
+    side, core, _, edge, (first, _, theirs, kept, major) = known(info)
     inner = side != core
     rest = theirs - NEAR
     near_columns = slice(head * HD, (head + count) * HD)
@@ -313,7 +324,6 @@
         values[h, :CHIP, :] = local[2, :, here]
     if flexible:
         back_rows, asked, scales, extra = refs[7:11]
-        first = info[7]
         sum_copy = pltpu.make_async_copy(arrived[0].at[FIRST_ROWS:, :], extra, sems.at[4])
         sum_copy.start()
         near_rows = pl.ds(sixteen(jnp.where(side == 0, 0, REST)), NEAR)
@@ -357,7 +367,17 @@
         values[h, CHIP : CHIP + NEAR, :] = near[1, :, at]
         values[h, CHIP + NEAR :, :] = stream[pl.ds(sixteen(key_at + rest), REST), :]
 
-    def answer_here(seen):
+    def far_answer(h, t):
+        at = slice(h * HD, (h + 1) * HD)
+        gain = gq[:, at]
+        x = stream[pl.ds(sixteen(bases[h] + t), HD), :]
+        far_q = turn(x, gain, flip(gain), swap, asked[0, t : t + HD, :], asked[1, t : t + HD, :])
+        place = jnp.where(h >= kept, (h - kept) * theirs + t, BACK_ROWS + HD)
+        back_rows[pl.ds(sixteen(place), HD), :] = attention(
+            far_q, keys[h, :SHORT, :], far_bias, values[h, :SHORT, :]
+        )
+
+    def answers(seen, lent):
         for h in range(count):
             at = slice(h * HD, (h + 1) * HD)
             here = slice((head + h) * HD, (head + h + 1) * HD)
@@ -366,41 +386,34 @@
                 result[rows, at] = attention(
                     local[0, rows, here], keys[h, :seen, :], bias[rows, :seen], values[h, :seen, :]
                 )
+            if lent:
+                far_answer(h, 0)
 
     short = theirs <= SHORT - CHIP
-    pl.when(short)(lambda: answer_here(SHORT))
-    pl.when(jnp.logical_not(short))(lambda: answer_here(2 * CHIP))
+    if flexible:
+        far_bias = jnp.where(ids[:, :SHORT] == edge, 0.0, NEGATIVE)
+        lending = jnp.logical_and(kept < HALF, major == 1)
+
+        @pl.when(jnp.logical_and(lending, theirs > HD))
+        def _():
+            for h in range(count):
+                far_answer(h, HD)
+
+        pl.when(lending)(lambda: answers(SHORT, True))
+        pl.when(jnp.logical_and(short, jnp.logical_not(lending)))(lambda: answers(SHORT, False))
+    else:
+        pl.when(short)(lambda: answers(SHORT, False))
+    pl.when(jnp.logical_not(short))(lambda: answers(2 * CHIP, False))
     own_out[...] = result[pl.ds(sixteen(core * ROWS), ROWS), :]
     mate_out[...] = result[pl.ds(sixteen((1 - core) * ROWS), ROWS), :]
     if flexible:
-        far_bias = jnp.where(ids[:, :SHORT] == edge, 0.0, NEGATIVE)
-
-        def answer_there(t):
-            for h in range(HALF):
-                at = slice(h * HD, (h + 1) * HD)
-                gain = gq[:, at]
-                x = stream[pl.ds(sixteen(bases[h] + t), HD), :]
-                far_q = turn(
-                    x, gain, flip(gain), swap, asked[0, t : t + HD, :], asked[1, t : t + HD, :]
-                )
-                place = jnp.where(h >= kept, (h - kept) * theirs + t, BACK_ROWS + HD)
-                back_rows[pl.ds(sixteen(place), HD), :] = attention(
-                    far_q, keys[h, :SHORT, :], far_bias, values[h, :SHORT, :]
-                )
-
-        lending = jnp.logical_and(kept < HALF, major == 1)
-        pl.when(jnp.logical_and(lending, theirs > HD))(lambda: answer_there(HD))
-        pl.when(lending)(lambda: answer_there(0))
         back[...] = back_rows[:BACK_ROWS, :]
 
 
 def join_kernel(
     info, flex_here, fixed_here, flex_there, fixed_there, back_here, back_there, ids, out, rows, lines
 ):
-    core, side = info[0], info[1]
-    mine = info[6]
-    kept, major, first = info[3], info[4], info[7]
-    edge = info[5].astype(jnp.float32)
+    side, core, _, edge, (first, mine, _, kept, major) = known(info)
     half = 2 * WIDE
     inside = columns_of(ids[...].astype(jnp.float32)) == edge
     for here, flex, fixed, back in (
@@ -446,27 +459,24 @@
 
 
 def whole(a):
-    return pl.BlockSpec(a.shape, lambda i, s: (0,) * len(a.shape))
+    return pl.BlockSpec(a.shape, lambda i: (0,) * len(a.shape))
 
 
 def held():
     return pl.BlockSpec(memory_space=pltpu.VMEM)
 
 
-def call(kernel, out_shape, in_specs, out_specs, scratch, scalars, *operands, limit=VMEM):
+def call(kernel, out_shape, in_specs, out_specs, scratch, *operands, limit=VMEM):
     return pl.pallas_call(
         kernel,
+        grid=(1,),
         out_shape=out_shape,
-        grid_spec=pltpu.PrefetchScalarGridSpec(
-            num_scalar_prefetch=1,
-            grid=(1,),
-            in_specs=in_specs,
-            out_specs=out_specs,
-            scratch_shapes=scratch,
-        ),
+        in_specs=in_specs,
+        out_specs=out_specs,
+        scratch_shapes=scratch,
         compiler_params=pltpu.CompilerParams(vmem_limit_bytes=limit),
         cost_estimate=pl.CostEstimate(flops=0, bytes_accessed=0, transcendentals=0),
-    )(scalars, *operands)
+    )(*operands)
 
 
 def attend(flexible, head, count, info, streams, waves, local, near_straight, near_slanted, gains, ids):
@@ -493,7 +503,7 @@
             pltpu.VMEM((SUM_ROWS, HD), bf16),
         ]
     operands = (local, near_straight, near_slanted, *gains, ids, *waves, *streams)
-    in_specs = [held(), there, there] + [held()] * (3 + len(waves)) + [there] * len(streams)
+    in_specs = [held(), held(), there, there] + [held()] * (3 + len(waves)) + [there] * len(streams)
     return call(
         functools.partial(attend_kernel, flexible, head, count), shapes,
         in_specs, [held()] * len(shapes), scratch, info, *operands,
@@ -504,9 +514,6 @@
     width = queries.shape[1]
     half = width // 2
     bf16, f32 = jnp.bfloat16, jnp.float32
-    me = lax.axis_index("ctx").astype(jnp.int32)
-    side, core = me // 2, me % 2
-    at_me = me[None]
 
     clip_row = clip_ids[None, :]
 
@@ -519,7 +526,7 @@
     ]
     dealt, near_own, near_other, sums = call(
         deal_kernel, deal_shapes, [whole(queries)] * 3 + [whole(clip_row)],
-        [whole(s) for s in deal_shapes], [], at_me, queries, keys, values, clip_row, limit=ALL_VMEM,
+        [whole(s) for s in deal_shapes], [], queries, keys, values, clip_row, limit=ALL_VMEM,
     )
     near_straight = lax.ppermute(near_own, "ctx", STRAIGHT)
     near_slanted = lax.ppermute(near_other, "ctx", SLANTED)
@@ -533,13 +540,13 @@
         jax.ShapeDtypeStruct((2, CHIP), f32),
     ]
     first_send, second_send, totals, info = call(
-        pack_kernel, stream_shapes + [jax.ShapeDtypeStruct((9,), jnp.int32)],
-        [held()] * 8, [whole(shape) for shape in stream_shapes[:2]] + [held()] + [pl.BlockSpec(memory_space=pltpu.SMEM)],
+        pack_kernel, stream_shapes + [jax.ShapeDtypeStruct((1, HD), f32)],
+        [held()] * 8, [whole(shape) for shape in stream_shapes[:2]] + [held()] * 2,
         [
             pltpu.VMEM((3, CHIP + NEAR, half), bf16),
             pltpu.VMEM((STREAM_ROWS + NEAR, HD), bf16),
         ],
-        at_me, queries, keys, values, mate, sums, mate_sums, row_sums, mate_row_sums,
+        queries, keys, values, mate, sums, mate_sums, row_sums, mate_row_sums,
     )
 
     first_stream = lax.ppermute(first_send, "ctx", ACROSS)
@@ -550,24 +557,25 @@
     wave_shape = jax.ShapeDtypeStruct((2 * CHIP, HD), f32)
     cosine, sine, mask_ids = call(
         waves_kernel, [wave_shape, wave_shape, jax.ShapeDtypeStruct((1, 2 * CHIP), f32)],
-        [pl.BlockSpec(memory_space=pltpu.SMEM)] + [held()] * 3, [held()] * 3,
-        [pltpu.VMEM((1, CHIP), f32)], info, clip_grid, sums, mate_sums, frequencies(),
+        [pl.BlockSpec(memory_space=pltpu.SMEM)] + [held()] * 4, [held()] * 3,
+        [pltpu.VMEM((1, CHIP), f32)], clip_grid, info, sums, mate_sums, frequencies(),
     )
     gains = (gain_q[None, :], gain_k[None, :])
     local_shape = jax.ShapeDtypeStruct((3, CHIP, half), bf16)
     local = call(
         turn_kernel, local_shape, [held()] * 9, held(), [pltpu.VMEM((4, CHIP, HD), f32)],
-        info, queries, keys, values, mate, cosine, sine, totals, *gains,
+        queries, keys, values, mate, cosine, sine, totals, *gains,
     )
     common = (local, near_straight, near_slanted, gains, mask_ids)
     flex_here, flex_send, back_send, far_waves = attend(
         True, HALF, HALF, info, (first_stream,), (cosine, sine), *common
     )
     back_here = lax.ppermute(back_send, "ctx", ACROSS)
-    flex_there = lax.ppermute(flex_send, "ctx", BESIDE)
     fixed_here, fixed_send = attend(
         False, 0, HALF, info, (first_stream, second_stream), (far_waves,), *common
     )
+    flex_send, fixed_send = lax.optimization_barrier((flex_send, fixed_send))
+    flex_there = lax.ppermute(flex_send, "ctx", BESIDE)
     fixed_there = lax.ppermute(fixed_send, "ctx", BESIDE)
     back_here, _ = lax.optimization_barrier((back_here, fixed_send))
     back_there = lax.ppermute(back_here, "ctx", BESIDE)
@@ -576,7 +584,7 @@
         flex_here, fixed_here, flex_there, fixed_there, back_here, back_there, clip_row
     )
     return call(
-        join_kernel, out_shape, [held()] * len(operands), whole(out_shape),
+        join_kernel, out_shape, [held()] * 8, whole(out_shape),
         [pltpu.VMEM((BACK_ROWS + REST, HD), bf16), pltpu.VMEM((2 * REST, HD), bf16)],
         info, *operands,
     )

time: 50.1 us -> 49.5 us (0.988); the launches traced: 49.2 us -> 49.2 us
  Pallas kernels: 21.2 us -> 18.8 us
  starting transfers between devices: 16.2 us -> 17.6 us
  waiting for transfers between devices: 8.43 us -> 9.37 us
    pallas_call x7, Pallas kernels: 21.2 us -> 18.8 us  [call(): pl.pallas_call(kernel, grid=(1,), out_shape=out_shape, in_specs=in_specs,...]
    ppermute x1, starting transfers between devices: 3.97 us -> 5.44 us  [on_device(): back_here = lax.ppermute(back_send, 'ctx', ACROSS)]
    ppermute x1, waiting for transfers between devices: 3.88 us -> 4.83 us  [on_device(): first_stream = lax.ppermute(first_send, 'ctx', ACROSS)]
    ppermute x1, waiting for transfers between devices: 0.35 us -> 0.92 us  [on_device(): flex_there = lax.ppermute(flex_send, 'ctx', BESIDE)]
    ppermute x1, waiting for transfers between devices: 0.92 us -> 0.35 us  [on_device(): fixed_there = lax.ppermute(fixed_send, 'ctx', BESIDE)]
  transfers between devices with their start and end apart: 12 -> 12, of which waited for: 6 -> 6; matrix products, arithmetic and copies ran while one was open for 1% -> 1% of each run, Pallas kernels for 31% -> 28%
where the time goes in v6:
time: 49.5 us; the launch traced here: 49.2 us
  Pallas kernels  18.8 us (38%)
  starting transfers between devices  17.6 us (36%)
  waiting for transfers between devices  9.37 us (19%)
  local copies, waits for them, and re-layouts  3.16 us (6%)
    pallas_call x7, Pallas kernels, call(): pl.pallas_call(kernel, grid=(1,), out_shape=out_shape, in_specs=in_specs,...  18.8 us
    ppermute x1, starting transfers between devices, on_device(): back_here = lax.ppermute(back_send, 'ctx', ACROSS)  5.44 us
    ppermute x1, starting transfers between devices, on_device(): mate_row_sums = lax.ppermute(sums, ('ctx', 'row'), OPPOSITE)  5.3 us
    ppermute x1, waiting for transfers between devices, on_device(): first_stream = lax.ppermute(first_send, 'ctx', ACROSS)  4.83 us
    unnamed x25, local copies, waits for them, and re-layouts  2.91 us
    ppermute x1, waiting for transfers between devices, on_device(): row_sums = lax.ppermute(sums, 'row', OTHER_ROW)  1.7 us
    ppermute x1, starting transfers between devices, on_device(): near_slanted = lax.ppermute(near_other, 'ctx', SLANTED)  1.48 us
    ppermute x1, starting transfers between devices, on_device(): near_straight = lax.ppermute(near_own, 'ctx', STRAIGHT)  1.41 us
  transfers between devices with their start and end apart: 12, of which 6 were waited for; matrix products, arithmetic and copies ran while one was open for 1% of the time, Pallas kernels for 28%

profile of v6, /device:TPU:0, one launch (start us, length us, event | category | flops | bytes accessed | tf_op | source)
XLA Modules:
  0.0 49.2 jit_solution(3504823858517221694)
XLA Ops:
  0.0 3.8 %shard_map.73 = (bf16[3,192,1280]{2,1,0:T(8,128)(2,1)}, bf16[2,96,1280]{2,1,0:T(8,128)(2,1)}, bf16[2,96,1280]{2,1,0:T(8,128)(2,1)}, f32[3,192]{1,0:T(4,128)}) custom-call(bf16[192,2560]{1,0:T(8,128)(2,1)} %q_ref.5, bf16[192,2560]{1,0:T(8,128)(2,1)} %k_ref.5, bf16[192,2560]{1,0:T(8,128)(2,1)} %v_ref.5, s32[1,192]{1,0:T(1,128)} %bitcast.1), custom_call_target="tpu_custom_call" | custom-call | tf_op jit(solution)/shard_map/pallas_call | solution.py:470
  3.8 0.5 collective-permute-start
  4.3 1.4 %collective-permute-start.4 = (bf16[2,96,1280]{2,1,0:T(8,128)(2,1)}, bf16[2,96,1280]{2,1,0:T(8,128)(2,1)S(1)}, u32[]{:S(2)}, u32[]{:S(2)}) collective-permute-start(bf16[2,96,1280]{2,1,0:T(8,128)(2,1)} %get-tuple-element.31), channel_id=1, source_target_pairs={{8,24},{16,0},{9,25},{17,1},{10,26},{18,2},{11,27},{19,3},{12,28},... | collective-permute-start | bytes 1474568 | tf_op jit(solution)/shard_map/ppermute | solution.py:531
  5.7 1.5 %collective-permute-start.5 = (bf16[2,96,1280]{2,1,0:T(8,128)(2,1)}, bf16[2,96,1280]{2,1,0:T(8,128)(2,1)}, u32[]{:S(2)}, u32[]{:S(2)}) collective-permute-start(bf16[2,96,1280]{2,1,0:T(8,128)(2,1)} %get-tuple-element.32), channel_id=1, source_target_pairs={{8,16},{16,8},{9,17},{17,9},{10,18},{18,10},{11,19},{19,11},{12,20... | collective-permute-start | bytes 1474568 | tf_op jit(solution)/shard_map/ppermute | solution.py:532
  7.2 5.3 %collective-permute-start.3 = (f32[3,192]{1,0:T(4,128)}, f32[3,192]{1,0:T(4,128)S(1)}, u32[]{:S(2)}, u32[]{:S(2)}) collective-permute-start(f32[3,192]{1,0:T(4,128)} %get-tuple-element.34.sums), channel_id=1, source_target_pairs={{0,12},{4,8},{8,4},{12,0},{16,28},{20,24},{24,20},{28,16},{1,13},{... | collective-permute-start | bytes 6920 | tf_op jit(solution)/shard_map/ppermute | solution.py:536
  12.5 0.2 collective-permute-start.2
  12.7 1.3 %collective-permute-done.3.mate_row_sums = f32[3,192]{1,0:T(4,128)S(1)} collective-permute-done((f32[3,192]{1,0:T(4,128)}, f32[3,192]{1,0:T(4,128)S(1)}, u32[]{:S(2)}, u32[]{:S(2)}) %collective-permute-start.3) | collective-permute-done | bytes 2336 | tf_op jit(solution)/shard_map/ppermute | solution.py:536
  14.0 0.6 %collective-permute-start.1 = (f32[3,192]{1,0:T(4,128)}, f32[3,192]{1,0:T(4,128)S(1)}, u32[]{:S(2)}, u32[]{:S(2)}) collective-permute-start(f32[3,192]{1,0:T(4,128)} %get-tuple-element.34.sums), channel_id=1, source_target_pairs={{0,8},{8,0},{16,24},{24,16},{1,9},{9,1},{17,25},{25,17},{2,10},{10... | collective-permute-start | bytes 6920 | tf_op jit(solution)/shard_map/ppermute | solution.py:534
  14.6 1.7 %collective-permute-done.2.row_sums = f32[3,192]{1,0:T(4,128)S(1)} collective-permute-done((f32[3,192]{1,0:T(4,128)}, f32[3,192]{1,0:T(4,128)S(1)}, u32[]{:S(2)}, u32[]{:S(2)}) %collective-permute-start.2) | collective-permute-done | bytes 2336 | tf_op jit(solution)/shard_map/ppermute | solution.py:535
  16.3 0.7 %copy-done.5 = f32[3,192]{1,0:T(4,128)S(1)} copy-done((f32[3,192]{1,0:T(4,128)S(1)}, f32[3,192]{1,0:T(4,128)}, u32[]{:S(2)}) %copy-start.5) | copy-done | bytes 2328
  17.0 1.8 %shard_map.74 = (bf16[1632,128]{1,0:T(8,128)(2,1)}, bf16[1600,128]{1,0:T(8,128)(2,1)S(1)}, f32[2,384]{1,0:T(2,128)S(1)}, f32[1,128]{1,0:T(1,128)S(1)}) custom-call(bf16[192,2560]{1,0:T(8,128)(2,1)S(1)} %copy-done, bf16[192,2560]{1,0:T(8,128)(2,1)S(1)} %copy-done.1, bf16[192,2560]{1,0:T(8,128)(2,1)S(1)} %copy-done.2, ...), custom_call_target="tpu_custom_call" | custom-call | tf_op jit(solution)/shard_map/pallas_call | solution.py:470
  18.8 0.8 %copy-done.8 = bf16[1600,128]{1,0:T(8,128)(2,1)} copy-done((bf16[1600,128]{1,0:T(8,128)(2,1)}, bf16[1600,128]{1,0:T(8,128)(2,1)S(1)}, u32[]{:S(2)}) %copy-start.8) | copy-done | bytes 409624
  19.6 1.2 %collective-permute-start.6 = (bf16[1632,128]{1,0:T(8,128)(2,1)}, bf16[1632,128]{1,0:T(8,128)(2,1)}, u32[]{:S(2)}, u32[]{:S(2)}) collective-permute-start(bf16[1632,128]{1,0:T(8,128)(2,1)} %get-tuple-element.33), channel_id=1, source_target_pairs={{0,16},{8,24},{16,0},{24,8},{1,17},{9,25},{17,1},{25,9},{2,18},{10... | collective-permute-start | bytes 1253384 | tf_op jit(solution)/shard_map/ppermute | solution.py:552
  20.8 0.1 copy.9.grid
  20.9 0.9 %collective-permute-start.7 = (bf16[1600,128]{1,0:T(8,128)(2,1)}, bf16[1600,128]{1,0:T(8,128)(2,1)}, u32[]{:S(2)}, u32[]{:S(2)}) collective-permute-start(bf16[1600,128]{1,0:T(8,128)(2,1)} %copy-done.8), channel_id=1, source_target_pairs={{0,16},{8,24},{16,0},{24,8},{1,17},{9,25},{17,1},{25,9},{2,18},{10... | collective-permute-start | bytes 1228808 | tf_op jit(solution)/shard_map/ppermute | solution.py:553
  21.8 0.1 pad_maximum_fusion
  21.9 0.1 broadcast_in_dim.13
  22.0 0.2 broadcast_in_dim_reshape.3.freqs
  22.2 2.5 %shard_map.75 = (f32[768,128]{1,0:T(8,128)S(1)}, f32[768,128]{1,0:T(8,128)S(1)}, f32[1,768]{1,0:T(1,128)S(1)}) custom-call(s32[4,2]{1,0:T(4,128)S(1)} %copy.9.grid, f32[1,128]{1,0:T(1,128)S(1)} %get-tuple-element.30.info, f32[3,192]{1,0:T(4,128)S(1)} %copy-done.6, f32[3,192]{1,0:T(4,128)S(1)} %collective-permute-done.1.mate_sums, ...), custom_call_target="tpu_custom_call" | custom-call | tf_op jit(solution)/shard_map/pallas_call | solution.py:470
  24.7 1.4 %copy-done.4 = bf16[3,192,1280]{2,1,0:T(8,128)(2,1)S(1)} copy-done((bf16[3,192,1280]{2,1,0:T(8,128)(2,1)S(1)}, bf16[3,192,1280]{2,1,0:T(8,128)(2,1)}, u32[]{:S(2)}) %copy-start.4) | copy-done | bytes 1474584
  26.1 1.5 %shard_map.76.refs_0_ = bf16[3,384,1280]{2,1,0:T(8,128)(2,1)S(1)} custom-call(bf16[192,2560]{1,0:T(8,128)(2,1)S(1)} %copy-done, bf16[192,2560]{1,0:T(8,128)(2,1)S(1)} %copy-done.1, bf16[192,2560]{1,0:T(8,128)(2,1)S(1)} %copy-done.2, bf16[3,192,1280]{2,1,0:T(8,128)(2,1)S(1)} %copy-done.4, f32[768,128]{1,0:T(8,128)S(1)} %get-tuple-element.35.cosine.refs_6_, ...), custom_call_target="tpu_custom_call" | custom-call | tf_op jit(solution)/shard_map/pallas_call | solution.py:470
  27.6 4.8 %collective-permute-done.6.refs_8_.refs_7_ = bf16[1632,128]{1,0:T(8,128)(2,1)} collective-permute-done((bf16[1632,128]{1,0:T(8,128)(2,1)}, bf16[1632,128]{1,0:T(8,128)(2,1)}, u32[]{:S(2)}, u32[]{:S(2)}) %collective-permute-start.6) | collective-permute-done | bytes 417824 | tf_op jit(solution)/shard_map/ppermute | solution.py:552
  32.4 4.0 %shard_map.77 = (bf16[192,640]{1,0:T(8,128)(2,1)S(1)}, bf16[192,640]{1,0:T(8,128)(2,1)S(1)}, bf16[640,128]{1,0:T(8,128)(2,1)S(1)}, f32[2,384,128]{2,1,0:T(8,128)S(1)}) custom-call(f32[1,128]{1,0:T(1,128)S(1)} %get-tuple-element.30.info, bf16[3,384,1280]{2,1,0:T(8,128)(2,1)S(1)} %shard_map.76.refs_0_, ...), custom_call_target="tpu_custom_call" | custom-call | tf_op jit(solution)/shard_map/pallas_call | solution.py:470
  36.4 5.4 %collective-permute-start.10 = (bf16[640,128]{1,0:T(8,128)(2,1)S(1)}, bf16[640,128]{1,0:T(8,128)(2,1)S(1)}, u32[]{:S(2)}, u32[]{:S(2)}) collective-permute-start(bf16[640,128]{1,0:T(8,128)(2,1)S(1)} %get-tuple-element.49), channel_id=1, source_target_pairs={{0,16},{8,24},{16,0},{24,8},{1,17},{9,25},{17,1},{25,9},{2,18},{10... | collective-permute-start | bytes 491528 | tf_op jit(solution)/shard_map/ppermute | solution.py:573
  41.9 3.8 %shard_map.78 = (bf16[192,640]{1,0:T(8,128)(2,1)S(1)}, bf16[192,640]{1,0:T(8,128)(2,1)S(1)}) custom-call(f32[1,128]{1,0:T(1,128)S(1)} %get-tuple-element.30.info, bf16[3,384,1280]{2,1,0:T(8,128)(2,1)S(1)} %shard_map.76.refs_0_, bf16[2,96,1280]{2,1,0:T(8,128)(2,1)S(1)} %collective-permute-done.4.refs_1_, bf16[2,96,1280]{2,1,0:T(8,128)(2,1)} %collective-permute-done.5.refs_2_, ...), custom_call_target="tpu_custom_call" | custom-call | tf_op jit(solution)/shard_map/pallas_call | solution.py:470
  45.7 0.1 collective-permute-start.8
  45.8 0.5 %collective-permute-start.9 = (bf16[192,640]{1,0:T(8,128)(2,1)S(1)}, bf16[192,640]{1,0:T(8,128)(2,1)S(1)}, u32[]{:S(2)}, u32[]{:S(2)}) collective-permute-start(bf16[192,640]{1,0:T(8,128)(2,1)S(1)} %get-tuple-element.48), channel_id=1, source_target_pairs={{0,8},{8,0},{16,24},{24,16},{1,9},{9,1},{17,25},{25,17},{2,10},{10... | collective-permute-start | bytes 737288 | tf_op jit(solution)/shard_map/ppermute | solution.py:579
  46.3 0.1 collective-permute-start.11
  46.4 0.9 %collective-permute-done.8.flex_there = bf16[192,640]{1,0:T(8,128)(2,1)S(1)} collective-permute-done((bf16[192,640]{1,0:T(8,128)(2,1)S(1)}, bf16[192,640]{1,0:T(8,128)(2,1)S(1)}, u32[]{:S(2)}, u32[]{:S(2)}) %collective-permute-start.8) | collective-permute-done | bytes 245792 | tf_op jit(solution)/shard_map/ppermute | solution.py:578
  47.3 0.4 collective-permute-done.9.fixed_there
  47.6 0.2 collective-permute-done.11.back_there
  47.9 1.4 %shard_map.79 = bf16[192,2560]{1,0:T(8,128)(2,1)} custom-call(f32[1,128]{1,0:T(1,128)S(1)} %get-tuple-element.30.info, bf16[192,640]{1,0:T(8,128)(2,1)S(1)} %get-tuple-element.41.flex_here, bf16[192,640]{1,0:T(8,128)(2,1)S(1)} %get-tuple-element.44.fixed_here, bf16[192,640]{1,0:T(8,128)(2,1)S(1)} %collective-permute-done.8.flex_there, ...), custom_call_target="tpu_custom_call" | custom-call | tf_op jit(solution)/shard_map/pallas_call | solution.py:470
  (31 shorter events, 0.1 us)
Async XLA Ops:
  0.0 16.3 %copy-start = (bf16[192,2560]{1,0:T(8,128)(2,1)S(1)}, bf16[192,2560]{1,0:T(8,128)(2,1)}, u32[]{:S(2)}) copy-start(bf16[192,2560]{1,0:T(8,128)(2,1)} %q_ref.5) | copy-start | bytes 2949124
  0.0 16.3 %copy-start.1 = (bf16[192,2560]{1,0:T(8,128)(2,1)S(1)}, bf16[192,2560]{1,0:T(8,128)(2,1)}, u32[]{:S(2)}) copy-start(bf16[192,2560]{1,0:T(8,128)(2,1)} %k_ref.5) | copy-start | bytes 2949124
  0.0 16.3 %copy-start.2 = (bf16[192,2560]{1,0:T(8,128)(2,1)S(1)}, bf16[192,2560]{1,0:T(8,128)(2,1)}, u32[]{:S(2)}) copy-start(bf16[192,2560]{1,0:T(8,128)(2,1)} %v_ref.5) | copy-start | bytes 2949124
  3.8 12.5 %collective-permute-start = (bf16[3,192,1280]{2,1,0:T(8,128)(2,1)}, bf16[3,192,1280]{2,1,0:T(8,128)(2,1)S(1)}, u32[]{:S(2)}, u32[]{:S(2)}) collective-permute-start(bf16[3,192,1280]{2,1,0:T(8,128)(2,1)} %get-tuple-element.28), channel_id=1, source_target_pairs={{0,8},{8,0},{16,24},{24,16},{1,9},{9,1},{17,25},{25,17},{2,10},{10... | collective-permute-start | bytes 4423688 | tf_op jit(solution)/shard_map/ppermute | solution.py:533
  4.3 17.9 %copy-start.6 = (f32[3,192]{1,0:T(4,128)S(1)}, f32[3,192]{1,0:T(4,128)}, u32[]{:S(2)}) copy-start(f32[3,192]{1,0:T(4,128)} %get-tuple-element.34.sums) | copy-start | bytes 6916
  4.3 17.9 %collective-permute-start.4 = (bf16[2,96,1280]{2,1,0:T(8,128)(2,1)}, bf16[2,96,1280]{2,1,0:T(8,128)(2,1)S(1)}, u32[]{:S(2)}, u32[]{:S(2)}) collective-permute-start(bf16[2,96,1280]{2,1,0:T(8,128)(2,1)} %get-tuple-element.31), channel_id=1, source_target_pairs={{8,24},{16,0},{9,25},{17,1},{10,26},{18,2},{11,27},{19,3},{12,28},... | collective-permute-start | bytes 1474568 | tf_op jit(solution)/shard_map/ppermute | solution.py:531
  5.7 16.5 %collective-permute-start.5 = (bf16[2,96,1280]{2,1,0:T(8,128)(2,1)}, bf16[2,96,1280]{2,1,0:T(8,128)(2,1)}, u32[]{:S(2)}, u32[]{:S(2)}) collective-permute-start(bf16[2,96,1280]{2,1,0:T(8,128)(2,1)} %get-tuple-element.32), channel_id=1, source_target_pairs={{8,16},{16,8},{9,17},{17,9},{10,18},{18,10},{11,19},{19,11},{12,20... | collective-permute-start | bytes 1474568 | tf_op jit(solution)/shard_map/ppermute | solution.py:532
  7.2 13.6 %copy-start.11 = (s32[4,2]{0,1:T(2,128)S(1)}, s32[4,2]{0,1:T(2,128)}, u32[]{:S(2)}) copy-start(s32[4,2]{0,1:T(2,128)} %param.13) | copy-start | bytes 100
  7.2 6.8 %collective-permute-start.3 = (f32[3,192]{1,0:T(4,128)}, f32[3,192]{1,0:T(4,128)S(1)}, u32[]{:S(2)}, u32[]{:S(2)}) collective-permute-start(f32[3,192]{1,0:T(4,128)} %get-tuple-element.34.sums), channel_id=1, source_target_pairs={{0,12},{4,8},{8,4},{12,0},{16,28},{20,24},{24,20},{28,16},{1,13},{... | collective-permute-start | bytes 6920 | tf_op jit(solution)/shard_map/ppermute | solution.py:536
  12.5 3.8 %collective-permute-start.2 = (f32[3,192]{1,0:T(4,128)}, f32[3,192]{1,0:T(4,128)S(1)}, u32[]{:S(2)}, u32[]{:S(2)}) collective-permute-start(f32[3,192]{1,0:T(4,128)} %get-tuple-element.34.sums), channel_id=1, source_target_pairs={{0,4},{4,0},{1,5},{5,1},{2,6},{6,2},{3,7},{7,3},{8,12},{12,8},{9,1... | collective-permute-start | bytes 6920 | tf_op jit(solution)/shard_map/ppermute | solution.py:535
  14.0 2.3 %collective-permute-start.1 = (f32[3,192]{1,0:T(4,128)}, f32[3,192]{1,0:T(4,128)S(1)}, u32[]{:S(2)}, u32[]{:S(2)}) collective-permute-start(f32[3,192]{1,0:T(4,128)} %get-tuple-element.34.sums), channel_id=1, source_target_pairs={{0,8},{8,0},{16,24},{24,16},{1,9},{9,1},{17,25},{25,17},{2,10},{10... | collective-permute-start | bytes 6920 | tf_op jit(solution)/shard_map/ppermute | solution.py:534
  16.3 0.7 %copy-start.5 = (f32[3,192]{1,0:T(4,128)S(1)}, f32[3,192]{1,0:T(4,128)}, u32[]{:S(2)}) copy-start(f32[3,192]{1,0:T(4,128)} %get-tuple-element.34.sums) | copy-start | bytes 6916
  17.0 1.8 %copy-start.3 = (bf16[3,192,1280]{2,1,0:T(8,128)(2,1)}, bf16[3,192,1280]{2,1,0:T(8,128)(2,1)S(1)}, u32[]{:S(2)}) copy-start(bf16[3,192,1280]{2,1,0:T(8,128)(2,1)S(1)} %collective-permute-done.mate) | copy-start | bytes 4423684
  17.0 3.9 %copy-start.9 = (f32[2560]{0:T(1024)S(1)}, f32[2560]{0:T(1024)}, u32[]{:S(2)}) copy-start(f32[2560]{0:T(1024)} %param.10) | copy-start | bytes 30724
  17.0 3.9 %copy-start.10 = (f32[2560]{0:T(1024)S(1)}, f32[2560]{0:T(1024)}, u32[]{:S(2)}) copy-start(f32[2560]{0:T(1024)} %param.11) | copy-start | bytes 30724
  18.8 0.8 %copy-start.8 = (bf16[1600,128]{1,0:T(8,128)(2,1)}, bf16[1600,128]{1,0:T(8,128)(2,1)S(1)}, u32[]{:S(2)}) copy-start(bf16[1600,128]{1,0:T(8,128)(2,1)S(1)} %get-tuple-element.43) | copy-start | bytes 1228804
  19.6 12.9 %collective-permute-start.6 = (bf16[1632,128]{1,0:T(8,128)(2,1)}, bf16[1632,128]{1,0:T(8,128)(2,1)}, u32[]{:S(2)}, u32[]{:S(2)}) collective-permute-start(bf16[1632,128]{1,0:T(8,128)(2,1)} %get-tuple-element.33), channel_id=1, source_target_pairs={{0,16},{8,24},{16,0},{24,8},{1,17},{9,25},{17,1},{25,9},{2,18},{10... | collective-permute-start | bytes 1253384 | tf_op jit(solution)/shard_map/ppermute | solution.py:552
  20.9 20.9 %collective-permute-start.7 = (bf16[1600,128]{1,0:T(8,128)(2,1)}, bf16[1600,128]{1,0:T(8,128)(2,1)}, u32[]{:S(2)}, u32[]{:S(2)}) collective-permute-start(bf16[1600,128]{1,0:T(8,128)(2,1)} %copy-done.8), channel_id=1, source_target_pairs={{0,16},{8,24},{16,0},{24,8},{1,17},{9,25},{17,1},{25,9},{2,18},{10... | collective-permute-start | bytes 1228808 | tf_op jit(solution)/shard_map/ppermute | solution.py:553
  24.7 1.4 %copy-start.4 = (bf16[3,192,1280]{2,1,0:T(8,128)(2,1)S(1)}, bf16[3,192,1280]{2,1,0:T(8,128)(2,1)}, u32[]{:S(2)}) copy-start(bf16[3,192,1280]{2,1,0:T(8,128)(2,1)} %copy-done.3) | copy-start | bytes 4423684
  36.4 9.8 %collective-permute-start.10 = (bf16[640,128]{1,0:T(8,128)(2,1)S(1)}, bf16[640,128]{1,0:T(8,128)(2,1)S(1)}, u32[]{:S(2)}, u32[]{:S(2)}) collective-permute-start(bf16[640,128]{1,0:T(8,128)(2,1)S(1)} %get-tuple-element.49), channel_id=1, source_target_pairs={{0,16},{8,24},{16,0},{24,8},{1,17},{9,25},{17,1},{25,9},{2,18},{10... | collective-permute-start | bytes 491528 | tf_op jit(solution)/shard_map/ppermute | solution.py:573
  41.9 6.0 %copy-start.7 = (s32[192]{0:T(256)S(1)}, s32[192]{0:T(256)}, u32[]{:S(2)}) copy-start(s32[192]{0:T(256)} %param.12) | copy-start | bytes 2308
  45.7 1.6 %collective-permute-start.8 = (bf16[192,640]{1,0:T(8,128)(2,1)S(1)}, bf16[192,640]{1,0:T(8,128)(2,1)S(1)}, u32[]{:S(2)}, u32[]{:S(2)}) collective-permute-start(bf16[192,640]{1,0:T(8,128)(2,1)S(1)} %get-tuple-element.47), channel_id=1, source_target_pairs={{0,8},{8,0},{16,24},{24,16},{1,9},{9,1},{17,25},{25,17},{2,10},{10... | collective-permute-start | bytes 737288 | tf_op jit(solution)/shard_map/ppermute | solution.py:578
  45.8 1.9 %collective-permute-start.9 = (bf16[192,640]{1,0:T(8,128)(2,1)S(1)}, bf16[192,640]{1,0:T(8,128)(2,1)S(1)}, u32[]{:S(2)}, u32[]{:S(2)}) collective-permute-start(bf16[192,640]{1,0:T(8,128)(2,1)S(1)} %get-tuple-element.48), channel_id=1, source_target_pairs={{0,8},{8,0},{16,24},{24,16},{1,9},{9,1},{17,25},{25,17},{2,10},{10... | collective-permute-start | bytes 737288 | tf_op jit(solution)/shard_map/ppermute | solution.py:579
  46.3 1.6 %collective-permute-start.11 = (bf16[640,128]{1,0:T(8,128)(2,1)S(1)}, bf16[640,128]{1,0:T(8,128)(2,1)S(1)}, u32[]{:S(2)}, u32[]{:S(2)}) collective-permute-start(bf16[640,128]{1,0:T(8,128)(2,1)S(1)} %collective-permute-done.10.back_here), channel_id=1, source_target_pairs={{0,8},{8,0},{16,24},{24,16},{1,9},{9,1},{17,25},{25,17},{2,10},{10... | collective-permute-start | bytes 491528 | tf_op jit(solution)/shard_map/ppermute | solution.py:581

commit v7 on v6

--- a/solution.py
+++ b/solution.py
@@ -367,13 +367,13 @@
         values[h, CHIP : CHIP + NEAR, :] = near[1, :, at]
         values[h, CHIP + NEAR :, :] = stream[pl.ds(sixteen(key_at + rest), REST), :]
 
-    def far_answer(h, t):
+    def far_answer(h, size):
         at = slice(h * HD, (h + 1) * HD)
         gain = gq[:, at]
-        x = stream[pl.ds(sixteen(bases[h] + t), HD), :]
-        far_q = turn(x, gain, flip(gain), swap, asked[0, t : t + HD, :], asked[1, t : t + HD, :])
-        place = jnp.where(h >= kept, (h - kept) * theirs + t, BACK_ROWS + HD)
-        back_rows[pl.ds(sixteen(place), HD), :] = attention(
+        x = stream[pl.ds(sixteen(bases[h]), size), :]
+        far_q = turn(x, gain, flip(gain), swap, asked[0, :size, :], asked[1, :size, :])
+        place = jnp.where(h >= kept, (h - kept) * theirs, BACK_ROWS + HD)
+        back_rows[pl.ds(sixteen(place), size), :] = attention(
             far_q, keys[h, :SHORT, :], far_bias, values[h, :SHORT, :]
         )
 
@@ -386,24 +386,21 @@
                 result[rows, at] = attention(
                     local[0, rows, here], keys[h, :seen, :], bias[rows, :seen], values[h, :seen, :]
                 )
-            if lent:
-                far_answer(h, 0)
+            if lent == HD or (lent and h > 0):
+                far_answer(h, lent)
 
     short = theirs <= SHORT - CHIP
     if flexible:
         far_bias = jnp.where(ids[:, :SHORT] == edge, 0.0, NEGATIVE)
         lending = jnp.logical_and(kept < HALF, major == 1)
 
-        @pl.when(jnp.logical_and(lending, theirs > HD))
-        def _():
-            for h in range(count):
-                far_answer(h, HD)
-
-        pl.when(lending)(lambda: answers(SHORT, True))
-        pl.when(jnp.logical_and(short, jnp.logical_not(lending)))(lambda: answers(SHORT, False))
+        wide = theirs > HD
+        pl.when(jnp.logical_and(lending, wide))(lambda: answers(SHORT, 2 * HD))
+        pl.when(jnp.logical_and(lending, jnp.logical_not(wide)))(lambda: answers(SHORT, HD))
+        pl.when(jnp.logical_and(short, jnp.logical_not(lending)))(lambda: answers(SHORT, 0))
     else:
-        pl.when(short)(lambda: answers(SHORT, False))
-    pl.when(jnp.logical_not(short))(lambda: answers(2 * CHIP, False))
+        pl.when(short)(lambda: answers(SHORT, 0))
+    pl.when(jnp.logical_not(short))(lambda: answers(2 * CHIP, 0))
     own_out[...] = result[pl.ds(sixteen(core * ROWS), ROWS), :]
     mate_out[...] = result[pl.ds(sixteen((1 - core) * ROWS), ROWS), :]
     if flexible:
@@ -497,7 +494,7 @@
         far_waves = jax.ShapeDtypeStruct((2, CHIP, HD), f32)
         shapes = shapes + [jax.ShapeDtypeStruct((BACK_ROWS, HD), bf16), far_waves]
         scratch = scratch + [
-            pltpu.VMEM((BACK_ROWS + 2 * HD, HD), bf16),
+            pltpu.VMEM((BACK_ROWS + 3 * HD, HD), bf16),
             pltpu.VMEM((2, CHIP, HD), f32),
             pltpu.VMEM((CHIP + REST, HD), f32),
             pltpu.VMEM((SUM_ROWS, HD), bf16),

time: 49.5 us -> 49.1 us (level)
  starting transfers between devices: 17.6 us -> 12.3 us
  Pallas kernels: 18.8 us -> 22 us
  waiting for transfers between devices: 9.37 us -> 11.1 us
    ppermute x1, starting transfers between devices: 5.44 us -> 0.07 us  [on_device(): back_here = lax.ppermute(back_send, 'ctx', ACROSS)]
    pallas_call x7, Pallas kernels: 18.8 us -> 22 us  [call(): pl.pallas_call(kernel, grid=(1,), out_shape=out_shape, in_specs=in_specs,...]
    ppermute x1, waiting for transfers between devices: 0.01 us -> 1.73 us  [on_device(): second_stream = lax.ppermute(second_send, 'ctx', ACROSS)]
  transfers between devices with their start and end apart: 12 -> 12, of which waited for: 6 -> 7; matrix products, arithmetic and copies ran while one was open for 1% -> 1% of each run, Pallas kernels for 28% -> 35%
where the time goes in v7:
time: 49.1 us; the launch traced here: 48.8 us
  Pallas kernels  22 us (45%)
  starting transfers between devices  12.3 us (25%)
  waiting for transfers between devices  11.1 us (23%)
  local copies, waits for them, and re-layouts  3.16 us (6%)
    pallas_call x7, Pallas kernels, call(): pl.pallas_call(kernel, grid=(1,), out_shape=out_shape, in_specs=in_specs,...  22 us
    ppermute x1, starting transfers between devices, on_device(): mate_row_sums = lax.ppermute(sums, ('ctx', 'row'), OPPOSITE)  5.3 us
    ppermute x1, waiting for transfers between devices, on_device(): first_stream = lax.ppermute(first_send, 'ctx', ACROSS)  4.83 us
    unnamed x25, local copies, waits for them, and re-layouts  2.91 us
    ppermute x1, waiting for transfers between devices, on_device(): second_stream = lax.ppermute(second_send, 'ctx', ACROSS)  1.73 us
    ppermute x1, waiting for transfers between devices, on_device(): row_sums = lax.ppermute(sums, 'row', OTHER_ROW)  1.7 us
    ppermute x1, starting transfers between devices, on_device(): near_slanted = lax.ppermute(near_other, 'ctx', SLANTED)  1.48 us
    ppermute x1, starting transfers between devices, on_device(): near_straight = lax.ppermute(near_own, 'ctx', STRAIGHT)  1.41 us
  transfers between devices with their start and end apart: 12, of which 7 were waited for; matrix products, arithmetic and copies ran while one was open for 1% of the time, Pallas kernels for 35%

profile of v7, /device:TPU:0, one launch (start us, length us, event | category | flops | bytes accessed | tf_op | source)
XLA Modules:
  0.0 48.8 jit_solution(7473731256140157785)
XLA Ops:
  0.0 3.8 %shard_map.73 = (bf16[3,192,1280]{2,1,0:T(8,128)(2,1)}, bf16[2,96,1280]{2,1,0:T(8,128)(2,1)}, bf16[2,96,1280]{2,1,0:T(8,128)(2,1)}, f32[3,192]{1,0:T(4,128)}) custom-call(bf16[192,2560]{1,0:T(8,128)(2,1)} %q_ref.5, bf16[192,2560]{1,0:T(8,128)(2,1)} %k_ref.5, bf16[192,2560]{1,0:T(8,128)(2,1)} %v_ref.5, s32[1,192]{1,0:T(1,128)} %bitcast.1), custom_call_target="tpu_custom_call" | custom-call | tf_op jit(solution)/shard_map/pallas_call | solution.py:467
  3.8 0.5 collective-permute-start
  4.3 1.4 %collective-permute-start.4 = (bf16[2,96,1280]{2,1,0:T(8,128)(2,1)}, bf16[2,96,1280]{2,1,0:T(8,128)(2,1)S(1)}, u32[]{:S(2)}, u32[]{:S(2)}) collective-permute-start(bf16[2,96,1280]{2,1,0:T(8,128)(2,1)} %get-tuple-element.31), channel_id=1, source_target_pairs={{8,24},{16,0},{9,25},{17,1},{10,26},{18,2},{11,27},{19,3},{12,28},... | collective-permute-start | bytes 1474568 | tf_op jit(solution)/shard_map/ppermute | solution.py:528
  5.7 1.5 %collective-permute-start.5 = (bf16[2,96,1280]{2,1,0:T(8,128)(2,1)}, bf16[2,96,1280]{2,1,0:T(8,128)(2,1)}, u32[]{:S(2)}, u32[]{:S(2)}) collective-permute-start(bf16[2,96,1280]{2,1,0:T(8,128)(2,1)} %get-tuple-element.32), channel_id=1, source_target_pairs={{8,16},{16,8},{9,17},{17,9},{10,18},{18,10},{11,19},{19,11},{12,20... | collective-permute-start | bytes 1474568 | tf_op jit(solution)/shard_map/ppermute | solution.py:529
  7.2 5.3 %collective-permute-start.3 = (f32[3,192]{1,0:T(4,128)}, f32[3,192]{1,0:T(4,128)S(1)}, u32[]{:S(2)}, u32[]{:S(2)}) collective-permute-start(f32[3,192]{1,0:T(4,128)} %get-tuple-element.34.sums), channel_id=1, source_target_pairs={{0,12},{4,8},{8,4},{12,0},{16,28},{20,24},{24,20},{28,16},{1,13},{... | collective-permute-start | bytes 6920 | tf_op jit(solution)/shard_map/ppermute | solution.py:533
  12.5 0.2 collective-permute-start.2
  12.7 1.3 %collective-permute-done.3.mate_row_sums = f32[3,192]{1,0:T(4,128)S(1)} collective-permute-done((f32[3,192]{1,0:T(4,128)}, f32[3,192]{1,0:T(4,128)S(1)}, u32[]{:S(2)}, u32[]{:S(2)}) %collective-permute-start.3) | collective-permute-done | bytes 2336 | tf_op jit(solution)/shard_map/ppermute | solution.py:533
  14.0 0.6 %collective-permute-start.1 = (f32[3,192]{1,0:T(4,128)}, f32[3,192]{1,0:T(4,128)S(1)}, u32[]{:S(2)}, u32[]{:S(2)}) collective-permute-start(f32[3,192]{1,0:T(4,128)} %get-tuple-element.34.sums), channel_id=1, source_target_pairs={{0,8},{8,0},{16,24},{24,16},{1,9},{9,1},{17,25},{25,17},{2,10},{10... | collective-permute-start | bytes 6920 | tf_op jit(solution)/shard_map/ppermute | solution.py:531
  14.6 1.7 %collective-permute-done.2.row_sums = f32[3,192]{1,0:T(4,128)S(1)} collective-permute-done((f32[3,192]{1,0:T(4,128)}, f32[3,192]{1,0:T(4,128)S(1)}, u32[]{:S(2)}, u32[]{:S(2)}) %collective-permute-start.2) | collective-permute-done | bytes 2336 | tf_op jit(solution)/shard_map/ppermute | solution.py:532
  16.3 0.7 %copy-done.5 = f32[3,192]{1,0:T(4,128)S(1)} copy-done((f32[3,192]{1,0:T(4,128)S(1)}, f32[3,192]{1,0:T(4,128)}, u32[]{:S(2)}) %copy-start.5) | copy-done | bytes 2328
  17.0 2.0 %shard_map.74 = (bf16[1632,128]{1,0:T(8,128)(2,1)}, bf16[1600,128]{1,0:T(8,128)(2,1)S(1)}, f32[2,384]{1,0:T(2,128)S(1)}, f32[1,128]{1,0:T(1,128)S(1)}) custom-call(bf16[192,2560]{1,0:T(8,128)(2,1)S(1)} %copy-done, bf16[192,2560]{1,0:T(8,128)(2,1)S(1)} %copy-done.1, bf16[192,2560]{1,0:T(8,128)(2,1)S(1)} %copy-done.2, ...), custom_call_target="tpu_custom_call" | custom-call | tf_op jit(solution)/shard_map/pallas_call | solution.py:467
  19.0 0.8 %copy-done.8 = bf16[1600,128]{1,0:T(8,128)(2,1)} copy-done((bf16[1600,128]{1,0:T(8,128)(2,1)}, bf16[1600,128]{1,0:T(8,128)(2,1)S(1)}, u32[]{:S(2)}) %copy-start.8) | copy-done | bytes 409624
  19.7 0.8 %collective-permute-start.6 = (bf16[1632,128]{1,0:T(8,128)(2,1)}, bf16[1632,128]{1,0:T(8,128)(2,1)}, u32[]{:S(2)}, u32[]{:S(2)}) collective-permute-start(bf16[1632,128]{1,0:T(8,128)(2,1)} %get-tuple-element.33), channel_id=1, source_target_pairs={{0,16},{8,24},{16,0},{24,8},{1,17},{9,25},{17,1},{25,9},{2,18},{10... | collective-permute-start | bytes 1253384 | tf_op jit(solution)/shard_map/ppermute | solution.py:549
  20.6 0.1 copy.9.grid
  20.7 1.3 %collective-permute-start.7 = (bf16[1600,128]{1,0:T(8,128)(2,1)}, bf16[1600,128]{1,0:T(8,128)(2,1)}, u32[]{:S(2)}, u32[]{:S(2)}) collective-permute-start(bf16[1600,128]{1,0:T(8,128)(2,1)} %copy-done.8), channel_id=1, source_target_pairs={{0,16},{8,24},{16,0},{24,8},{1,17},{9,25},{17,1},{25,9},{2,18},{10... | collective-permute-start | bytes 1228808 | tf_op jit(solution)/shard_map/ppermute | solution.py:550
  22.0 0.1 pad_maximum_fusion
  22.1 0.1 broadcast_in_dim.13
  22.1 0.2 broadcast_in_dim_reshape.3.freqs
  22.3 2.5 %shard_map.75 = (f32[768,128]{1,0:T(8,128)S(1)}, f32[768,128]{1,0:T(8,128)S(1)}, f32[1,768]{1,0:T(1,128)S(1)}) custom-call(s32[4,2]{1,0:T(4,128)S(1)} %copy.9.grid, f32[1,128]{1,0:T(1,128)S(1)} %get-tuple-element.30.info, f32[3,192]{1,0:T(4,128)S(1)} %copy-done.6, f32[3,192]{1,0:T(4,128)S(1)} %collective-permute-done.1.mate_sums, ...), custom_call_target="tpu_custom_call" | custom-call | tf_op jit(solution)/shard_map/pallas_call | solution.py:467
  24.9 1.4 %copy-done.4 = bf16[3,192,1280]{2,1,0:T(8,128)(2,1)S(1)} copy-done((bf16[3,192,1280]{2,1,0:T(8,128)(2,1)S(1)}, bf16[3,192,1280]{2,1,0:T(8,128)(2,1)}, u32[]{:S(2)}) %copy-start.4) | copy-done | bytes 1474584
  26.3 1.5 %shard_map.76.refs_0_ = bf16[3,384,1280]{2,1,0:T(8,128)(2,1)S(1)} custom-call(bf16[192,2560]{1,0:T(8,128)(2,1)S(1)} %copy-done, bf16[192,2560]{1,0:T(8,128)(2,1)S(1)} %copy-done.1, bf16[192,2560]{1,0:T(8,128)(2,1)S(1)} %copy-done.2, bf16[3,192,1280]{2,1,0:T(8,128)(2,1)S(1)} %copy-done.4, f32[768,128]{1,0:T(8,128)S(1)} %get-tuple-element.35.cosine.refs_6_, ...), custom_call_target="tpu_custom_call" | custom-call | tf_op jit(solution)/shard_map/pallas_call | solution.py:467
  27.8 4.8 %collective-permute-done.6.refs_8_.refs_7_ = bf16[1632,128]{1,0:T(8,128)(2,1)} collective-permute-done((bf16[1632,128]{1,0:T(8,128)(2,1)}, bf16[1632,128]{1,0:T(8,128)(2,1)}, u32[]{:S(2)}, u32[]{:S(2)}) %collective-permute-start.6) | collective-permute-done | bytes 417824 | tf_op jit(solution)/shard_map/ppermute | solution.py:549
  32.6 6.4 %shard_map.77 = (bf16[192,640]{1,0:T(8,128)(2,1)S(1)}, bf16[192,640]{1,0:T(8,128)(2,1)S(1)}, bf16[640,128]{1,0:T(8,128)(2,1)S(1)}, f32[2,384,128]{2,1,0:T(8,128)S(1)}) custom-call(f32[1,128]{1,0:T(1,128)S(1)} %get-tuple-element.30.info, bf16[3,384,1280]{2,1,0:T(8,128)(2,1)S(1)} %shard_map.76.refs_0_, ...), custom_call_target="tpu_custom_call" | custom-call | tf_op jit(solution)/shard_map/pallas_call | solution.py:467
  39.0 0.1 collective-permute-start.10
  39.1 1.7 %collective-permute-done.7.refs_8_ = bf16[1600,128]{1,0:T(8,128)(2,1)} collective-permute-done((bf16[1600,128]{1,0:T(8,128)(2,1)}, bf16[1600,128]{1,0:T(8,128)(2,1)}, u32[]{:S(2)}, u32[]{:S(2)}) %collective-permute-start.7) | collective-permute-done | bytes 409632 | tf_op jit(solution)/shard_map/ppermute | solution.py:550
  40.8 4.7 %shard_map.78 = (bf16[192,640]{1,0:T(8,128)(2,1)S(1)}, bf16[192,640]{1,0:T(8,128)(2,1)S(1)}) custom-call(f32[1,128]{1,0:T(1,128)S(1)} %get-tuple-element.30.info, bf16[3,384,1280]{2,1,0:T(8,128)(2,1)S(1)} %shard_map.76.refs_0_, bf16[2,96,1280]{2,1,0:T(8,128)(2,1)S(1)} %collective-permute-done.4.refs_1_, bf16[2,96,1280]{2,1,0:T(8,128)(2,1)} %collective-permute-done.5.refs_2_, ...), custom_call_target="tpu_custom_call" | custom-call | tf_op jit(solution)/shard_map/pallas_call | solution.py:467
  45.5 0.5 %collective-permute-start.9 = (bf16[192,640]{1,0:T(8,128)(2,1)S(1)}, bf16[192,640]{1,0:T(8,128)(2,1)S(1)}, u32[]{:S(2)}, u32[]{:S(2)}) collective-permute-start(bf16[192,640]{1,0:T(8,128)(2,1)S(1)} %get-tuple-element.48), channel_id=1, source_target_pairs={{0,8},{8,0},{16,24},{24,16},{1,9},{9,1},{17,25},{25,17},{2,10},{10... | collective-permute-start | bytes 737288 | tf_op jit(solution)/shard_map/ppermute | solution.py:576
  46.0 0.1 collective-permute-start.11
  46.1 0.9 %collective-permute-done.8.flex_there = bf16[192,640]{1,0:T(8,128)(2,1)S(1)} collective-permute-done((bf16[192,640]{1,0:T(8,128)(2,1)S(1)}, bf16[192,640]{1,0:T(8,128)(2,1)S(1)}, u32[]{:S(2)}, u32[]{:S(2)}) %collective-permute-start.8) | collective-permute-done | bytes 245792 | tf_op jit(solution)/shard_map/ppermute | solution.py:575
  47.0 0.4 collective-permute-done.9.fixed_there
  47.4 0.2 collective-permute-done.11.back_there
  47.6 1.1 %shard_map.79 = bf16[192,2560]{1,0:T(8,128)(2,1)} custom-call(f32[1,128]{1,0:T(1,128)S(1)} %get-tuple-element.30.info, bf16[192,640]{1,0:T(8,128)(2,1)S(1)} %get-tuple-element.41.flex_here, bf16[192,640]{1,0:T(8,128)(2,1)S(1)} %get-tuple-element.44.fixed_here, bf16[192,640]{1,0:T(8,128)(2,1)S(1)} %collective-permute-done.8.flex_there, ...), custom_call_target="tpu_custom_call" | custom-call | tf_op jit(solution)/shard_map/pallas_call | solution.py:467
  (31 shorter events, 0.2 us)
Async XLA Ops:
  0.0 16.3 %copy-start = (bf16[192,2560]{1,0:T(8,128)(2,1)S(1)}, bf16[192,2560]{1,0:T(8,128)(2,1)}, u32[]{:S(2)}) copy-start(bf16[192,2560]{1,0:T(8,128)(2,1)} %q_ref.5) | copy-start | bytes 2949124
  0.0 16.3 %copy-start.1 = (bf16[192,2560]{1,0:T(8,128)(2,1)S(1)}, bf16[192,2560]{1,0:T(8,128)(2,1)}, u32[]{:S(2)}) copy-start(bf16[192,2560]{1,0:T(8,128)(2,1)} %k_ref.5) | copy-start | bytes 2949124
  0.0 16.3 %copy-start.2 = (bf16[192,2560]{1,0:T(8,128)(2,1)S(1)}, bf16[192,2560]{1,0:T(8,128)(2,1)}, u32[]{:S(2)}) copy-start(bf16[192,2560]{1,0:T(8,128)(2,1)} %v_ref.5) | copy-start | bytes 2949124
  3.8 12.5 %collective-permute-start = (bf16[3,192,1280]{2,1,0:T(8,128)(2,1)}, bf16[3,192,1280]{2,1,0:T(8,128)(2,1)S(1)}, u32[]{:S(2)}, u32[]{:S(2)}) collective-permute-start(bf16[3,192,1280]{2,1,0:T(8,128)(2,1)} %get-tuple-element.28), channel_id=1, source_target_pairs={{0,8},{8,0},{16,24},{24,16},{1,9},{9,1},{17,25},{25,17},{2,10},{10... | collective-permute-start | bytes 4423688 | tf_op jit(solution)/shard_map/ppermute | solution.py:530
  4.3 18.1 %copy-start.6 = (f32[3,192]{1,0:T(4,128)S(1)}, f32[3,192]{1,0:T(4,128)}, u32[]{:S(2)}) copy-start(f32[3,192]{1,0:T(4,128)} %get-tuple-element.34.sums) | copy-start | bytes 6916
  4.3 18.0 %collective-permute-start.4 = (bf16[2,96,1280]{2,1,0:T(8,128)(2,1)}, bf16[2,96,1280]{2,1,0:T(8,128)(2,1)S(1)}, u32[]{:S(2)}, u32[]{:S(2)}) collective-permute-start(bf16[2,96,1280]{2,1,0:T(8,128)(2,1)} %get-tuple-element.31), channel_id=1, source_target_pairs={{8,24},{16,0},{9,25},{17,1},{10,26},{18,2},{11,27},{19,3},{12,28},... | collective-permute-start | bytes 1474568 | tf_op jit(solution)/shard_map/ppermute | solution.py:528
  5.7 16.6 %collective-permute-start.5 = (bf16[2,96,1280]{2,1,0:T(8,128)(2,1)}, bf16[2,96,1280]{2,1,0:T(8,128)(2,1)}, u32[]{:S(2)}, u32[]{:S(2)}) collective-permute-start(bf16[2,96,1280]{2,1,0:T(8,128)(2,1)} %get-tuple-element.32), channel_id=1, source_target_pairs={{8,16},{16,8},{9,17},{17,9},{10,18},{18,10},{11,19},{19,11},{12,20... | collective-permute-start | bytes 1474568 | tf_op jit(solution)/shard_map/ppermute | solution.py:529
  7.2 13.4 %copy-start.11 = (s32[4,2]{0,1:T(2,128)S(1)}, s32[4,2]{0,1:T(2,128)}, u32[]{:S(2)}) copy-start(s32[4,2]{0,1:T(2,128)} %param.13) | copy-start | bytes 100
  7.2 6.8 %collective-permute-start.3 = (f32[3,192]{1,0:T(4,128)}, f32[3,192]{1,0:T(4,128)S(1)}, u32[]{:S(2)}, u32[]{:S(2)}) collective-permute-start(f32[3,192]{1,0:T(4,128)} %get-tuple-element.34.sums), channel_id=1, source_target_pairs={{0,12},{4,8},{8,4},{12,0},{16,28},{20,24},{24,20},{28,16},{1,13},{... | collective-permute-start | bytes 6920 | tf_op jit(solution)/shard_map/ppermute | solution.py:533
  12.5 3.8 %collective-permute-start.2 = (f32[3,192]{1,0:T(4,128)}, f32[3,192]{1,0:T(4,128)S(1)}, u32[]{:S(2)}, u32[]{:S(2)}) collective-permute-start(f32[3,192]{1,0:T(4,128)} %get-tuple-element.34.sums), channel_id=1, source_target_pairs={{0,4},{4,0},{1,5},{5,1},{2,6},{6,2},{3,7},{7,3},{8,12},{12,8},{9,1... | collective-permute-start | bytes 6920 | tf_op jit(solution)/shard_map/ppermute | solution.py:532
  14.0 2.3 %collective-permute-start.1 = (f32[3,192]{1,0:T(4,128)}, f32[3,192]{1,0:T(4,128)S(1)}, u32[]{:S(2)}, u32[]{:S(2)}) collective-permute-start(f32[3,192]{1,0:T(4,128)} %get-tuple-element.34.sums), channel_id=1, source_target_pairs={{0,8},{8,0},{16,24},{24,16},{1,9},{9,1},{17,25},{25,17},{2,10},{10... | collective-permute-start | bytes 6920 | tf_op jit(solution)/shard_map/ppermute | solution.py:531
  16.3 0.7 %copy-start.5 = (f32[3,192]{1,0:T(4,128)S(1)}, f32[3,192]{1,0:T(4,128)}, u32[]{:S(2)}) copy-start(f32[3,192]{1,0:T(4,128)} %get-tuple-element.34.sums) | copy-start | bytes 6916
  17.0 2.0 %copy-start.3 = (bf16[3,192,1280]{2,1,0:T(8,128)(2,1)}, bf16[3,192,1280]{2,1,0:T(8,128)(2,1)S(1)}, u32[]{:S(2)}) copy-start(bf16[3,192,1280]{2,1,0:T(8,128)(2,1)S(1)} %collective-permute-done.mate) | copy-start | bytes 4423684
  17.0 3.7 %copy-start.9 = (f32[2560]{0:T(1024)S(1)}, f32[2560]{0:T(1024)}, u32[]{:S(2)}) copy-start(f32[2560]{0:T(1024)} %param.10) | copy-start | bytes 30724
  17.0 3.7 %copy-start.10 = (f32[2560]{0:T(1024)S(1)}, f32[2560]{0:T(1024)}, u32[]{:S(2)}) copy-start(f32[2560]{0:T(1024)} %param.11) | copy-start | bytes 30724
  19.0 0.8 %copy-start.8 = (bf16[1600,128]{1,0:T(8,128)(2,1)}, bf16[1600,128]{1,0:T(8,128)(2,1)S(1)}, u32[]{:S(2)}) copy-start(bf16[1600,128]{1,0:T(8,128)(2,1)S(1)} %get-tuple-element.43) | copy-start | bytes 1228804
  19.7 12.9 %collective-permute-start.6 = (bf16[1632,128]{1,0:T(8,128)(2,1)}, bf16[1632,128]{1,0:T(8,128)(2,1)}, u32[]{:S(2)}, u32[]{:S(2)}) collective-permute-start(bf16[1632,128]{1,0:T(8,128)(2,1)} %get-tuple-element.33), channel_id=1, source_target_pairs={{0,16},{8,24},{16,0},{24,8},{1,17},{9,25},{17,1},{25,9},{2,18},{10... | collective-permute-start | bytes 1253384 | tf_op jit(solution)/shard_map/ppermute | solution.py:549
  20.7 20.1 %collective-permute-start.7 = (bf16[1600,128]{1,0:T(8,128)(2,1)}, bf16[1600,128]{1,0:T(8,128)(2,1)}, u32[]{:S(2)}, u32[]{:S(2)}) collective-permute-start(bf16[1600,128]{1,0:T(8,128)(2,1)} %copy-done.8), channel_id=1, source_target_pairs={{0,16},{8,24},{16,0},{24,8},{1,17},{9,25},{17,1},{25,9},{2,18},{10... | collective-permute-start | bytes 1228808 | tf_op jit(solution)/shard_map/ppermute | solution.py:550
  24.9 1.4 %copy-start.4 = (bf16[3,192,1280]{2,1,0:T(8,128)(2,1)S(1)}, bf16[3,192,1280]{2,1,0:T(8,128)(2,1)}, u32[]{:S(2)}) copy-start(bf16[3,192,1280]{2,1,0:T(8,128)(2,1)} %copy-done.3) | copy-start | bytes 4423684
  39.0 7.1 %collective-permute-start.10 = (bf16[640,128]{1,0:T(8,128)(2,1)S(1)}, bf16[640,128]{1,0:T(8,128)(2,1)S(1)}, u32[]{:S(2)}, u32[]{:S(2)}) collective-permute-start(bf16[640,128]{1,0:T(8,128)(2,1)S(1)} %get-tuple-element.49), channel_id=1, source_target_pairs={{0,16},{8,24},{16,0},{24,8},{1,17},{9,25},{17,1},{25,9},{2,18},{10... | collective-permute-start | bytes 491528 | tf_op jit(solution)/shard_map/ppermute | solution.py:570
  40.8 6.8 %copy-start.7 = (s32[192]{0:T(256)S(1)}, s32[192]{0:T(256)}, u32[]{:S(2)}) copy-start(s32[192]{0:T(256)} %param.12) | copy-start | bytes 2308
  45.5 1.6 %collective-permute-start.8 = (bf16[192,640]{1,0:T(8,128)(2,1)S(1)}, bf16[192,640]{1,0:T(8,128)(2,1)S(1)}, u32[]{:S(2)}, u32[]{:S(2)}) collective-permute-start(bf16[192,640]{1,0:T(8,128)(2,1)S(1)} %get-tuple-element.47), channel_id=1, source_target_pairs={{0,8},{8,0},{16,24},{24,16},{1,9},{9,1},{17,25},{25,17},{2,10},{10... | collective-permute-start | bytes 737288 | tf_op jit(solution)/shard_map/ppermute | solution.py:575
  45.5 1.9 %collective-permute-start.9 = (bf16[192,640]{1,0:T(8,128)(2,1)S(1)}, bf16[192,640]{1,0:T(8,128)(2,1)S(1)}, u32[]{:S(2)}, u32[]{:S(2)}) collective-permute-start(bf16[192,640]{1,0:T(8,128)(2,1)S(1)} %get-tuple-element.48), channel_id=1, source_target_pairs={{0,8},{8,0},{16,24},{24,16},{1,9},{9,1},{17,25},{25,17},{2,10},{10... | collective-permute-start | bytes 737288 | tf_op jit(solution)/shard_map/ppermute | solution.py:576
  46.0 1.6 %collective-permute-start.11 = (bf16[640,128]{1,0:T(8,128)(2,1)S(1)}, bf16[640,128]{1,0:T(8,128)(2,1)S(1)}, u32[]{:S(2)}, u32[]{:S(2)}) collective-permute-start(bf16[640,128]{1,0:T(8,128)(2,1)S(1)} %collective-permute-done.10.back_here), channel_id=1, source_target_pairs={{0,8},{8,0},{16,24},{24,16},{1,9},{9,1},{17,25},{25,17},{2,10},{10... | collective-permute-start | bytes 491528 | tf_op jit(solution)/shard_map/ppermute | solution.py:578

commit v8 on v7

--- a/solution.py
+++ b/solution.py
@@ -277,6 +277,28 @@
                 out[i, rows, at] = turn(x, gain, flip(gain), swap, cos_here, sin_here)
 
 
+def local_kernel(local, ids, partial, peaks, bias):
+    clip_of = columns_of(ids[:, :CHIP])
+    for t in range(0, CHIP, HD):
+        bias[:, t : t + HD] = jnp.where(clip_of == ids[:, t : t + HD], 0.0, NEGATIVE)
+    for h in range(HALF):
+        at = slice(h * HD, (h + 1) * HD)
+        values = local[2, :, at]
+        columns = jnp.concatenate([values, jnp.ones_like(values)], axis=1)
+        for t in range(0, CHIP, TILE):
+            rows = slice(t, t + TILE)
+            scores = lax.dot_general(
+                local[0, rows, at], local[1, :, at], (((1,), (1,)), ((), ())),
+                preferred_element_type=jnp.float32,
+            ) + bias[rows, :]
+            peak = jnp.max(scores, axis=1, keepdims=True)
+            weights = jnp.exp2((scores - peak) * SCORE_SCALE).astype(jnp.bfloat16)
+            partial[rows, 2 * h * HD : 2 * (h + 1) * HD] = jnp.dot(
+                weights, columns, preferred_element_type=jnp.float32
+            )
+            peaks[rows, at] = jnp.broadcast_to(peak, (TILE, HD))
+
+
 def attend_kernel(flexible, head, count, info, *refs):
     local, near_straight, near_slanted, gq, gk, ids = refs[:6]
     streams = 1 if flexible else 2
@@ -284,7 +306,7 @@
     if flexible:
         (cosine, sine), refs = refs[:2], refs[2:]
     else:
-        table, refs = refs[0], refs[1:]
+        (table, partial, peaks), refs = refs[:3], refs[3:]
     arrived, refs = refs[:streams], refs[streams:]
     own_out, mate_out, refs = refs[0], refs[1], refs[2:]
     if flexible:
@@ -316,9 +338,9 @@
     columns = pl.ds(pl.multiple_of((2 * HALF * core + head) * HD, 128), count * HD)
     gq, gk = gq[:, columns], gk[:, columns]
     clip_of = columns_of(ids[:, :CHIP])
-    for t in range(0, 2 * CHIP, HD):
+    for t in range(0 if flexible else CHIP, 2 * CHIP, HD):
         bias[:, t : t + HD] = jnp.where(clip_of == ids[:, t : t + HD], 0.0, NEGATIVE)
-    for h in range(count):
+    for h in range(count if flexible else 0):
         here = slice((head + h) * HD, (head + h + 1) * HD)
         keys[h, :CHIP, :] = local[1, :, here]
         values[h, :CHIP, :] = local[2, :, here]
@@ -389,6 +411,27 @@
             if lent == HD or (lent and h > 0):
                 far_answer(h, lent)
 
+    def merged(seen):
+        for h in range(count):
+            at = slice(h * HD, (h + 1) * HD)
+            here = slice((head + h) * HD, (head + h + 1) * HD)
+            far = values[h, CHIP:seen, :]
+            columns = jnp.concatenate([far, jnp.ones_like(far)], axis=1)
+            for t in range(0, CHIP, TILE):
+                rows = slice(t, t + TILE)
+                scores = lax.dot_general(
+                    local[0, rows, here], keys[h, CHIP:seen, :], (((1,), (1,)), ((), ())),
+                    preferred_element_type=jnp.float32,
+                ) + bias[rows, CHIP:seen]
+                before = peaks[rows, h * HD : h * HD + 1]
+                peak = jnp.maximum(before, jnp.max(scores, axis=1, keepdims=True))
+                weights = jnp.exp2((scores - peak) * SCORE_SCALE).astype(jnp.bfloat16)
+                sums = jnp.dot(weights, columns, preferred_element_type=jnp.float32)
+                sums += jnp.exp2((before - peak) * SCORE_SCALE) * partial[
+                    rows, 2 * h * HD : 2 * (h + 1) * HD
+                ]
+                result[rows, at] = (sums[:, :HD] / sums[:, HD:]).astype(jnp.bfloat16)
+
     short = theirs <= SHORT - CHIP
     if flexible:
         far_bias = jnp.where(ids[:, :SHORT] == edge, 0.0, NEGATIVE)
@@ -398,9 +441,10 @@
         pl.when(jnp.logical_and(lending, wide))(lambda: answers(SHORT, 2 * HD))
         pl.when(jnp.logical_and(lending, jnp.logical_not(wide)))(lambda: answers(SHORT, HD))
         pl.when(jnp.logical_and(short, jnp.logical_not(lending)))(lambda: answers(SHORT, 0))
+        pl.when(jnp.logical_not(short))(lambda: answers(2 * CHIP, 0))
     else:
-        pl.when(short)(lambda: answers(SHORT, 0))
-    pl.when(jnp.logical_not(short))(lambda: answers(2 * CHIP, 0))
+        pl.when(short)(lambda: merged(SHORT))
+        pl.when(jnp.logical_not(short))(lambda: merged(2 * CHIP))
     own_out[...] = result[pl.ds(sixteen(core * ROWS), ROWS), :]
     mate_out[...] = result[pl.ds(sixteen((1 - core) * ROWS), ROWS), :]
     if flexible:
@@ -564,12 +608,22 @@
         queries, keys, values, mate, cosine, sine, totals, *gains,
     )
     common = (local, near_straight, near_slanted, gains, mask_ids)
+    partial, peaks = call(
+        local_kernel,
+        [
+            jax.ShapeDtypeStruct((CHIP, 2 * WIDE), f32),
+            jax.ShapeDtypeStruct((CHIP, WIDE), f32),
+        ],
+        [held()] * 2, [held()] * 2, [pltpu.VMEM((CHIP, CHIP), f32)], local, mask_ids,
+    )
+    first_stream, partial = lax.optimization_barrier((first_stream, partial))
     flex_here, flex_send, back_send, far_waves = attend(
         True, HALF, HALF, info, (first_stream,), (cosine, sine), *common
     )
     back_here = lax.ppermute(back_send, "ctx", ACROSS)
     fixed_here, fixed_send = attend(
-        False, 0, HALF, info, (first_stream, second_stream), (far_waves,), *common
+        False, 0, HALF, info, (first_stream, second_stream),
+        (far_waves, partial, peaks), *common
     )
     flex_send, fixed_send = lax.optimization_barrier((flex_send, fixed_send))
     flex_there = lax.ppermute(flex_send, "ctx", BESIDE)

time: 49.1 us -> 48.3 us (0.984)
  waiting for transfers between devices: 11.1 us -> 7.48 us
  starting transfers between devices: 12.3 us -> 15.5 us
    ppermute x1, starting transfers between devices: 0.07 us -> 3.33 us  [on_device(): back_here = lax.ppermute(back_send, 'ctx', ACROSS)]
    ppermute x1, waiting for transfers between devices: 4.83 us -> 2.66 us  [on_device(): first_stream = lax.ppermute(first_send, 'ctx', ACROSS)]
    ppermute x1, waiting for transfers between devices: 1.73 us -> 0.28 us  [on_device(): second_stream = lax.ppermute(second_send, 'ctx', ACROSS)]
    pallas_call x7 -> x8, Pallas kernels: 22 us -> 21.9 us  [call(): pl.pallas_call(kernel, grid=(1,), out_shape=out_shape, in_specs=in_specs,...]
where the time goes in v8:
time: 48.3 us
  Pallas kernels  21.9 us (45%)
  starting transfers between devices  15.5 us (32%)
  waiting for transfers between devices  7.48 us (15%)
  local copies, waits for them, and re-layouts  3.16 us (7%)
    pallas_call x8, Pallas kernels, call(): pl.pallas_call(kernel, grid=(1,), out_shape=out_shape, in_specs=in_specs,...  21.9 us
    ppermute x1, starting transfers between devices, on_device(): mate_row_sums = lax.ppermute(sums, ('ctx', 'row'), OPPOSITE)  5.3 us
    ppermute x1, starting transfers between devices, on_device(): back_here = lax.ppermute(back_send, 'ctx', ACROSS)  3.33 us
    unnamed x25, local copies, waits for them, and re-layouts  2.92 us
    ppermute x1, waiting for transfers between devices, on_device(): first_stream = lax.ppermute(first_send, 'ctx', ACROSS)  2.66 us
    ppermute x1, waiting for transfers between devices, on_device(): row_sums = lax.ppermute(sums, 'row', OTHER_ROW)  1.7 us
    ppermute x1, starting transfers between devices, on_device(): near_slanted = lax.ppermute(near_other, 'ctx', SLANTED)  1.48 us
    ppermute x1, starting transfers between devices, on_device(): near_straight = lax.ppermute(near_own, 'ctx', STRAIGHT)  1.41 us
  transfers between devices with their start and end apart: 12, of which 7 were waited for; matrix products, arithmetic and copies ran while one was open for 1% of the time, Pallas kernels for 35%

profile of v8, /device:TPU:0, one launch (start us, length us, event | category | flops | bytes accessed | tf_op | source)
XLA Modules:
  0.0 48.3 jit_solution(14174140715917859178)
XLA Ops:
  0.0 3.8 %shard_map.73 = (bf16[3,192,1280]{2,1,0:T(8,128)(2,1)}, bf16[2,96,1280]{2,1,0:T(8,128)(2,1)}, bf16[2,96,1280]{2,1,0:T(8,128)(2,1)}, f32[3,192]{1,0:T(4,128)}) custom-call(bf16[192,2560]{1,0:T(8,128)(2,1)} %q_ref.5, bf16[192,2560]{1,0:T(8,128)(2,1)} %k_ref.5, bf16[192,2560]{1,0:T(8,128)(2,1)} %v_ref.5, s32[1,192]{1,0:T(1,128)} %bitcast.1), custom_call_target="tpu_custom_call" | custom-call | tf_op jit(solution)/shard_map/pallas_call | solution.py:511
  3.8 0.5 collective-permute-start
  4.3 1.4 %collective-permute-start.4 = (bf16[2,96,1280]{2,1,0:T(8,128)(2,1)}, bf16[2,96,1280]{2,1,0:T(8,128)(2,1)S(1)}, u32[]{:S(2)}, u32[]{:S(2)}) collective-permute-start(bf16[2,96,1280]{2,1,0:T(8,128)(2,1)} %get-tuple-element.35), channel_id=1, source_target_pairs={{8,24},{16,0},{9,25},{17,1},{10,26},{18,2},{11,27},{19,3},{12,28},... | collective-permute-start | bytes 1474568 | tf_op jit(solution)/shard_map/ppermute | solution.py:572
  5.7 1.5 %collective-permute-start.5 = (bf16[2,96,1280]{2,1,0:T(8,128)(2,1)}, bf16[2,96,1280]{2,1,0:T(8,128)(2,1)}, u32[]{:S(2)}, u32[]{:S(2)}) collective-permute-start(bf16[2,96,1280]{2,1,0:T(8,128)(2,1)} %get-tuple-element.36), channel_id=1, source_target_pairs={{8,16},{16,8},{9,17},{17,9},{10,18},{18,10},{11,19},{19,11},{12,20... | collective-permute-start | bytes 1474568 | tf_op jit(solution)/shard_map/ppermute | solution.py:573
  7.2 5.3 %collective-permute-start.3 = (f32[3,192]{1,0:T(4,128)}, f32[3,192]{1,0:T(4,128)S(1)}, u32[]{:S(2)}, u32[]{:S(2)}) collective-permute-start(f32[3,192]{1,0:T(4,128)} %get-tuple-element.38.sums), channel_id=1, source_target_pairs={{0,12},{4,8},{8,4},{12,0},{16,28},{20,24},{24,20},{28,16},{1,13},{... | collective-permute-start | bytes 6920 | tf_op jit(solution)/shard_map/ppermute | solution.py:577
  12.5 0.2 collective-permute-start.2
  12.7 1.3 %collective-permute-done.3.mate_row_sums = f32[3,192]{1,0:T(4,128)S(1)} collective-permute-done((f32[3,192]{1,0:T(4,128)}, f32[3,192]{1,0:T(4,128)S(1)}, u32[]{:S(2)}, u32[]{:S(2)}) %collective-permute-start.3) | collective-permute-done | bytes 2336 | tf_op jit(solution)/shard_map/ppermute | solution.py:577
  14.0 0.6 %collective-permute-start.1 = (f32[3,192]{1,0:T(4,128)}, f32[3,192]{1,0:T(4,128)S(1)}, u32[]{:S(2)}, u32[]{:S(2)}) collective-permute-start(f32[3,192]{1,0:T(4,128)} %get-tuple-element.38.sums), channel_id=1, source_target_pairs={{0,8},{8,0},{16,24},{24,16},{1,9},{9,1},{17,25},{25,17},{2,10},{10... | collective-permute-start | bytes 6920 | tf_op jit(solution)/shard_map/ppermute | solution.py:575
  14.6 1.7 %collective-permute-done.2.row_sums = f32[3,192]{1,0:T(4,128)S(1)} collective-permute-done((f32[3,192]{1,0:T(4,128)}, f32[3,192]{1,0:T(4,128)S(1)}, u32[]{:S(2)}, u32[]{:S(2)}) %collective-permute-start.2) | collective-permute-done | bytes 2336 | tf_op jit(solution)/shard_map/ppermute | solution.py:576
  16.3 0.7 %copy-done.5 = f32[3,192]{1,0:T(4,128)S(1)} copy-done((f32[3,192]{1,0:T(4,128)S(1)}, f32[3,192]{1,0:T(4,128)}, u32[]{:S(2)}) %copy-start.5) | copy-done | bytes 2328
  17.0 2.0 %shard_map.74 = (bf16[1632,128]{1,0:T(8,128)(2,1)}, bf16[1600,128]{1,0:T(8,128)(2,1)S(1)}, f32[2,384]{1,0:T(2,128)S(1)}, f32[1,128]{1,0:T(1,128)S(1)}) custom-call(bf16[192,2560]{1,0:T(8,128)(2,1)S(1)} %copy-done, bf16[192,2560]{1,0:T(8,128)(2,1)S(1)} %copy-done.1, bf16[192,2560]{1,0:T(8,128)(2,1)S(1)} %copy-done.2, ...), custom_call_target="tpu_custom_call" | custom-call | tf_op jit(solution)/shard_map/pallas_call | solution.py:511
  19.0 0.7 %copy-done.8 = bf16[1600,128]{1,0:T(8,128)(2,1)} copy-done((bf16[1600,128]{1,0:T(8,128)(2,1)}, bf16[1600,128]{1,0:T(8,128)(2,1)S(1)}, u32[]{:S(2)}) %copy-start.8) | copy-done | bytes 409624
  19.8 0.9 %collective-permute-start.6 = (bf16[1632,128]{1,0:T(8,128)(2,1)}, bf16[1632,128]{1,0:T(8,128)(2,1)}, u32[]{:S(2)}, u32[]{:S(2)}) collective-permute-start(bf16[1632,128]{1,0:T(8,128)(2,1)} %get-tuple-element.37), channel_id=1, source_target_pairs={{0,16},{8,24},{16,0},{24,8},{1,17},{9,25},{17,1},{25,9},{2,18},{10... | collective-permute-start | bytes 1253384 | tf_op jit(solution)/shard_map/ppermute | solution.py:593
  20.7 0.1 copy.9.grid
  20.8 1.2 %collective-permute-start.7 = (bf16[1600,128]{1,0:T(8,128)(2,1)}, bf16[1600,128]{1,0:T(8,128)(2,1)}, u32[]{:S(2)}, u32[]{:S(2)}) collective-permute-start(bf16[1600,128]{1,0:T(8,128)(2,1)} %copy-done.8), channel_id=1, source_target_pairs={{0,16},{8,24},{16,0},{24,8},{1,17},{9,25},{17,1},{25,9},{2,18},{10... | collective-permute-start | bytes 1228808 | tf_op jit(solution)/shard_map/ppermute | solution.py:594
  22.0 0.1 pad_maximum_fusion
  22.2 0.2 broadcast_in_dim_reshape.3.freqs
  22.4 2.5 %shard_map.75 = (f32[768,128]{1,0:T(8,128)S(1)}, f32[768,128]{1,0:T(8,128)S(1)}, f32[1,768]{1,0:T(1,128)S(1)}) custom-call(s32[4,2]{1,0:T(4,128)S(1)} %copy.9.grid, f32[1,128]{1,0:T(1,128)S(1)} %get-tuple-element.34.info, f32[3,192]{1,0:T(4,128)S(1)} %copy-done.6, f32[3,192]{1,0:T(4,128)S(1)} %collective-permute-done.1.mate_sums, ...), custom_call_target="tpu_custom_call" | custom-call | tf_op jit(solution)/shard_map/pallas_call | solution.py:511
  24.9 1.4 %copy-done.4 = bf16[3,192,1280]{2,1,0:T(8,128)(2,1)S(1)} copy-done((bf16[3,192,1280]{2,1,0:T(8,128)(2,1)S(1)}, bf16[3,192,1280]{2,1,0:T(8,128)(2,1)}, u32[]{:S(2)}) %copy-start.4) | copy-done | bytes 1474584
  26.3 1.5 %shard_map.76.local.refs_0_ = bf16[3,384,1280]{2,1,0:T(8,128)(2,1)S(1)} custom-call(bf16[192,2560]{1,0:T(8,128)(2,1)S(1)} %copy-done, bf16[192,2560]{1,0:T(8,128)(2,1)S(1)} %copy-done.1, bf16[192,2560]{1,0:T(8,128)(2,1)S(1)} %copy-done.2, bf16[3,192,1280]{2,1,0:T(8,128)(2,1)S(1)} %copy-done.4, f32[768,128]{1,0:T(8,128)S(1)} %get-tuple-element.39.cosine.refs_6_, ...), custom_call_target="tpu_custom_call" | custom-call | tf_op jit(solution)/shard_map/pallas_call | solution.py:511
  27.8 2.2 %shard_map.77 = (f32[384,1280]{1,0:T(8,128)S(1)}, f32[384,640]{1,0:T(8,128)S(1)}) custom-call(bf16[3,384,1280]{2,1,0:T(8,128)(2,1)S(1)} %shard_map.76.local.refs_0_, f32[1,768]{1,0:T(1,128)S(1)} %get-tuple-element.44.ids.refs_5_), custom_call_target="tpu_custom_call" | custom-call | tf_op jit(solution)/shard_map/pallas_call | solution.py:511
  30.0 2.7 %collective-permute-done.6.refs_8_.refs_9_ = bf16[1632,128]{1,0:T(8,128)(2,1)} collective-permute-done((bf16[1632,128]{1,0:T(8,128)(2,1)}, bf16[1632,128]{1,0:T(8,128)(2,1)}, u32[]{:S(2)}, u32[]{:S(2)}) %collective-permute-start.6) | collective-permute-done | bytes 417824 | tf_op jit(solution)/shard_map/ppermute | solution.py:593
  32.7 4.2 %shard_map.78 = (bf16[192,640]{1,0:T(8,128)(2,1)S(1)}, bf16[192,640]{1,0:T(8,128)(2,1)S(1)}, bf16[640,128]{1,0:T(8,128)(2,1)S(1)}, f32[2,384,128]{2,1,0:T(8,128)S(1)}) custom-call(f32[1,128]{1,0:T(1,128)S(1)} %get-tuple-element.34.info, bf16[3,384,1280]{2,1,0:T(8,128)(2,1)S(1)} %shard_map.76.local.refs_0_, ...), custom_call_target="tpu_custom_call" | custom-call | tf_op jit(solution)/shard_map/pallas_call | solution.py:511
  36.9 3.3 %collective-permute-start.10 = (bf16[640,128]{1,0:T(8,128)(2,1)S(1)}, bf16[640,128]{1,0:T(8,128)(2,1)S(1)}, u32[]{:S(2)}, u32[]{:S(2)}) collective-permute-start(bf16[640,128]{1,0:T(8,128)(2,1)S(1)} %get-tuple-element.57), channel_id=1, source_target_pairs={{0,16},{8,24},{16,0},{24,8},{1,17},{9,25},{17,1},{25,9},{2,18},{10... | collective-permute-start | bytes 491528 | tf_op jit(solution)/shard_map/ppermute | solution.py:623
  40.2 0.3 collective-permute-done.7.refs_10_
  40.5 4.3 %shard_map.79 = (bf16[192,640]{1,0:T(8,128)(2,1)S(1)}, bf16[192,640]{1,0:T(8,128)(2,1)S(1)}) custom-call(f32[1,128]{1,0:T(1,128)S(1)} %get-tuple-element.34.info, bf16[3,384,1280]{2,1,0:T(8,128)(2,1)S(1)} %shard_map.76.local.refs_0_, bf16[2,96,1280]{2,1,0:T(8,128)(2,1)S(1)} %collective-permute-done.4.refs_1_, ...), custom_call_target="tpu_custom_call" | custom-call | tf_op jit(solution)/shard_map/pallas_call | solution.py:511
  44.9 0.5 %collective-permute-start.9 = (bf16[192,640]{1,0:T(8,128)(2,1)S(1)}, bf16[192,640]{1,0:T(8,128)(2,1)S(1)}, u32[]{:S(2)}, u32[]{:S(2)}) collective-permute-start(bf16[192,640]{1,0:T(8,128)(2,1)S(1)} %get-tuple-element.56), channel_id=1, source_target_pairs={{0,8},{8,0},{16,24},{24,16},{1,9},{9,1},{17,25},{25,17},{2,10},{10... | collective-permute-start | bytes 737288 | tf_op jit(solution)/shard_map/ppermute | solution.py:630
  45.4 0.1 collective-permute-start.11
  45.5 0.9 %collective-permute-done.8.flex_there = bf16[192,640]{1,0:T(8,128)(2,1)S(1)} collective-permute-done((bf16[192,640]{1,0:T(8,128)(2,1)S(1)}, bf16[192,640]{1,0:T(8,128)(2,1)S(1)}, u32[]{:S(2)}, u32[]{:S(2)}) %collective-permute-start.8) | collective-permute-done | bytes 245792 | tf_op jit(solution)/shard_map/ppermute | solution.py:629
  46.4 0.4 collective-permute-done.9.fixed_there
  46.8 0.2 collective-permute-done.11.back_there
  47.0 1.3 %shard_map.80 = bf16[192,2560]{1,0:T(8,128)(2,1)} custom-call(f32[1,128]{1,0:T(1,128)S(1)} %get-tuple-element.34.info, bf16[192,640]{1,0:T(8,128)(2,1)S(1)} %get-tuple-element.47.flex_here, bf16[192,640]{1,0:T(8,128)(2,1)S(1)} %get-tuple-element.52.fixed_here, bf16[192,640]{1,0:T(8,128)(2,1)S(1)} %collective-permute-done.8.flex_there, ...), custom_call_target="tpu_custom_call" | custom-call | tf_op jit(solution)/shard_map/pallas_call | solution.py:511
  (32 shorter events, 0.2 us)
Async XLA Ops:
  0.0 16.3 %copy-start.2 = (bf16[192,2560]{1,0:T(8,128)(2,1)S(1)}, bf16[192,2560]{1,0:T(8,128)(2,1)}, u32[]{:S(2)}) copy-start(bf16[192,2560]{1,0:T(8,128)(2,1)} %v_ref.5) | copy-start | bytes 2949124
  0.0 16.3 %copy-start.1 = (bf16[192,2560]{1,0:T(8,128)(2,1)S(1)}, bf16[192,2560]{1,0:T(8,128)(2,1)}, u32[]{:S(2)}) copy-start(bf16[192,2560]{1,0:T(8,128)(2,1)} %k_ref.5) | copy-start | bytes 2949124
  0.0 16.3 %copy-start = (bf16[192,2560]{1,0:T(8,128)(2,1)S(1)}, bf16[192,2560]{1,0:T(8,128)(2,1)}, u32[]{:S(2)}) copy-start(bf16[192,2560]{1,0:T(8,128)(2,1)} %q_ref.5) | copy-start | bytes 2949124
  3.8 12.5 %collective-permute-start = (bf16[3,192,1280]{2,1,0:T(8,128)(2,1)}, bf16[3,192,1280]{2,1,0:T(8,128)(2,1)S(1)}, u32[]{:S(2)}, u32[]{:S(2)}) collective-permute-start(bf16[3,192,1280]{2,1,0:T(8,128)(2,1)} %get-tuple-element.32), channel_id=1, source_target_pairs={{0,8},{8,0},{16,24},{24,16},{1,9},{9,1},{17,25},{25,17},{2,10},{10... | collective-permute-start | bytes 4423688 | tf_op jit(solution)/shard_map/ppermute | solution.py:574
  4.3 18.1 %copy-start.6 = (f32[3,192]{1,0:T(4,128)S(1)}, f32[3,192]{1,0:T(4,128)}, u32[]{:S(2)}) copy-start(f32[3,192]{1,0:T(4,128)} %get-tuple-element.38.sums) | copy-start | bytes 6916
  4.3 18.1 %collective-permute-start.4 = (bf16[2,96,1280]{2,1,0:T(8,128)(2,1)}, bf16[2,96,1280]{2,1,0:T(8,128)(2,1)S(1)}, u32[]{:S(2)}, u32[]{:S(2)}) collective-permute-start(bf16[2,96,1280]{2,1,0:T(8,128)(2,1)} %get-tuple-element.35), channel_id=1, source_target_pairs={{8,24},{16,0},{9,25},{17,1},{10,26},{18,2},{11,27},{19,3},{12,28},... | collective-permute-start | bytes 1474568 | tf_op jit(solution)/shard_map/ppermute | solution.py:572
  5.7 16.7 %collective-permute-start.5 = (bf16[2,96,1280]{2,1,0:T(8,128)(2,1)}, bf16[2,96,1280]{2,1,0:T(8,128)(2,1)}, u32[]{:S(2)}, u32[]{:S(2)}) collective-permute-start(bf16[2,96,1280]{2,1,0:T(8,128)(2,1)} %get-tuple-element.36), channel_id=1, source_target_pairs={{8,16},{16,8},{9,17},{17,9},{10,18},{18,10},{11,19},{19,11},{12,20... | collective-permute-start | bytes 1474568 | tf_op jit(solution)/shard_map/ppermute | solution.py:573
  7.2 13.5 %copy-start.11 = (s32[4,2]{0,1:T(2,128)S(1)}, s32[4,2]{0,1:T(2,128)}, u32[]{:S(2)}) copy-start(s32[4,2]{0,1:T(2,128)} %param.13) | copy-start | bytes 100
  7.2 6.8 %collective-permute-start.3 = (f32[3,192]{1,0:T(4,128)}, f32[3,192]{1,0:T(4,128)S(1)}, u32[]{:S(2)}, u32[]{:S(2)}) collective-permute-start(f32[3,192]{1,0:T(4,128)} %get-tuple-element.38.sums), channel_id=1, source_target_pairs={{0,12},{4,8},{8,4},{12,0},{16,28},{20,24},{24,20},{28,16},{1,13},{... | collective-permute-start | bytes 6920 | tf_op jit(solution)/shard_map/ppermute | solution.py:577
  12.5 3.8 %collective-permute-start.2 = (f32[3,192]{1,0:T(4,128)}, f32[3,192]{1,0:T(4,128)S(1)}, u32[]{:S(2)}, u32[]{:S(2)}) collective-permute-start(f32[3,192]{1,0:T(4,128)} %get-tuple-element.38.sums), channel_id=1, source_target_pairs={{0,4},{4,0},{1,5},{5,1},{2,6},{6,2},{3,7},{7,3},{8,12},{12,8},{9,1... | collective-permute-start | bytes 6920 | tf_op jit(solution)/shard_map/ppermute | solution.py:576
  14.0 2.3 %collective-permute-start.1 = (f32[3,192]{1,0:T(4,128)}, f32[3,192]{1,0:T(4,128)S(1)}, u32[]{:S(2)}, u32[]{:S(2)}) collective-permute-start(f32[3,192]{1,0:T(4,128)} %get-tuple-element.38.sums), channel_id=1, source_target_pairs={{0,8},{8,0},{16,24},{24,16},{1,9},{9,1},{17,25},{25,17},{2,10},{10... | collective-permute-start | bytes 6920 | tf_op jit(solution)/shard_map/ppermute | solution.py:575
  16.3 0.7 %copy-start.5 = (f32[3,192]{1,0:T(4,128)S(1)}, f32[3,192]{1,0:T(4,128)}, u32[]{:S(2)}) copy-start(f32[3,192]{1,0:T(4,128)} %get-tuple-element.38.sums) | copy-start | bytes 6916
  17.0 2.0 %copy-start.3 = (bf16[3,192,1280]{2,1,0:T(8,128)(2,1)}, bf16[3,192,1280]{2,1,0:T(8,128)(2,1)S(1)}, u32[]{:S(2)}) copy-start(bf16[3,192,1280]{2,1,0:T(8,128)(2,1)S(1)} %collective-permute-done.mate) | copy-start | bytes 4423684
  17.0 3.8 %copy-start.9 = (f32[2560]{0:T(1024)S(1)}, f32[2560]{0:T(1024)}, u32[]{:S(2)}) copy-start(f32[2560]{0:T(1024)} %param.10) | copy-start | bytes 30724
  17.0 3.8 %copy-start.10 = (f32[2560]{0:T(1024)S(1)}, f32[2560]{0:T(1024)}, u32[]{:S(2)}) copy-start(f32[2560]{0:T(1024)} %param.11) | copy-start | bytes 30724
  19.0 0.7 %copy-start.8 = (bf16[1600,128]{1,0:T(8,128)(2,1)}, bf16[1600,128]{1,0:T(8,128)(2,1)S(1)}, u32[]{:S(2)}) copy-start(bf16[1600,128]{1,0:T(8,128)(2,1)S(1)} %get-tuple-element.51) | copy-start | bytes 1228804
  19.8 12.9 %collective-permute-start.6 = (bf16[1632,128]{1,0:T(8,128)(2,1)}, bf16[1632,128]{1,0:T(8,128)(2,1)}, u32[]{:S(2)}, u32[]{:S(2)}) collective-permute-start(bf16[1632,128]{1,0:T(8,128)(2,1)} %get-tuple-element.37), channel_id=1, source_target_pairs={{0,16},{8,24},{16,0},{24,8},{1,17},{9,25},{17,1},{25,9},{2,18},{10... | collective-permute-start | bytes 1253384 | tf_op jit(solution)/shard_map/ppermute | solution.py:593
  20.8 19.7 %collective-permute-start.7 = (bf16[1600,128]{1,0:T(8,128)(2,1)}, bf16[1600,128]{1,0:T(8,128)(2,1)}, u32[]{:S(2)}, u32[]{:S(2)}) collective-permute-start(bf16[1600,128]{1,0:T(8,128)(2,1)} %copy-done.8), channel_id=1, source_target_pairs={{0,16},{8,24},{16,0},{24,8},{1,17},{9,25},{17,1},{25,9},{2,18},{10... | collective-permute-start | bytes 1228808 | tf_op jit(solution)/shard_map/ppermute | solution.py:594
  24.9 1.4 %copy-start.4 = (bf16[3,192,1280]{2,1,0:T(8,128)(2,1)S(1)}, bf16[3,192,1280]{2,1,0:T(8,128)(2,1)}, u32[]{:S(2)}) copy-start(bf16[3,192,1280]{2,1,0:T(8,128)(2,1)} %copy-done.3) | copy-start | bytes 4423684
  36.9 8.5 %collective-permute-start.10 = (bf16[640,128]{1,0:T(8,128)(2,1)S(1)}, bf16[640,128]{1,0:T(8,128)(2,1)S(1)}, u32[]{:S(2)}, u32[]{:S(2)}) collective-permute-start(bf16[640,128]{1,0:T(8,128)(2,1)S(1)} %get-tuple-element.57), channel_id=1, source_target_pairs={{0,16},{8,24},{16,0},{24,8},{1,17},{9,25},{17,1},{25,9},{2,18},{10... | collective-permute-start | bytes 491528 | tf_op jit(solution)/shard_map/ppermute | solution.py:623
  40.5 6.5 %copy-start.7 = (s32[192]{0:T(256)S(1)}, s32[192]{0:T(256)}, u32[]{:S(2)}) copy-start(s32[192]{0:T(256)} %param.12) | copy-start | bytes 2308
  44.8 1.6 %collective-permute-start.8 = (bf16[192,640]{1,0:T(8,128)(2,1)S(1)}, bf16[192,640]{1,0:T(8,128)(2,1)S(1)}, u32[]{:S(2)}, u32[]{:S(2)}) collective-permute-start(bf16[192,640]{1,0:T(8,128)(2,1)S(1)} %get-tuple-element.55), channel_id=1, source_target_pairs={{0,8},{8,0},{16,24},{24,16},{1,9},{9,1},{17,25},{25,17},{2,10},{10... | collective-permute-start | bytes 737288 | tf_op jit(solution)/shard_map/ppermute | solution.py:629
  44.9 1.9 %collective-permute-start.9 = (bf16[192,640]{1,0:T(8,128)(2,1)S(1)}, bf16[192,640]{1,0:T(8,128)(2,1)S(1)}, u32[]{:S(2)}, u32[]{:S(2)}) collective-permute-start(bf16[192,640]{1,0:T(8,128)(2,1)S(1)} %get-tuple-element.56), channel_id=1, source_target_pairs={{0,8},{8,0},{16,24},{24,16},{1,9},{9,1},{17,25},{25,17},{2,10},{10... | collective-permute-start | bytes 737288 | tf_op jit(solution)/shard_map/ppermute | solution.py:630
  45.4 1.6 %collective-permute-start.11 = (bf16[640,128]{1,0:T(8,128)(2,1)S(1)}, bf16[640,128]{1,0:T(8,128)(2,1)S(1)}, u32[]{:S(2)}, u32[]{:S(2)}) collective-permute-start(bf16[640,128]{1,0:T(8,128)(2,1)S(1)} %collective-permute-done.10.back_here), channel_id=1, source_target_pairs={{0,8},{8,0},{16,24},{24,16},{1,9},{9,1},{17,25},{25,17},{2,10},{10... | collective-permute-start | bytes 491528 | tf_op jit(solution)/shard_map/ppermute | solution.py:632

commit v9 on v8

--- a/solution.py
+++ b/solution.py
@@ -417,8 +417,8 @@
             here = slice((head + h) * HD, (head + h + 1) * HD)
             far = values[h, CHIP:seen, :]
             columns = jnp.concatenate([far, jnp.ones_like(far)], axis=1)
-            for t in range(0, CHIP, TILE):
-                rows = slice(t, t + TILE)
+            for t in range(0, CHIP, HD):
+                rows = slice(t, t + HD)
                 scores = lax.dot_general(
                     local[0, rows, here], keys[h, CHIP:seen, :], (((1,), (1,)), ((), ())),
                     preferred_element_type=jnp.float32,

time: 48.3 us -> 48.1 us (level)
  transfers between devices with their start and end apart: 12 -> 12, of which waited for: 7 -> 6; matrix products, arithmetic and copies ran while one was open for 1% -> 1% of each run, Pallas kernels for 35% -> 34%
where the time goes in v9:
time: 48.1 us
  Pallas kernels  21.6 us (45%)
  starting transfers between devices  15.8 us (33%)
  waiting for transfers between devices  7.2 us (15%)
  local copies, waits for them, and re-layouts  3.16 us (7%)
    pallas_call x8, Pallas kernels, call(): pl.pallas_call(kernel, grid=(1,), out_shape=out_shape, in_specs=in_specs,...  21.6 us
    ppermute x1, starting transfers between devices, on_device(): mate_row_sums = lax.ppermute(sums, ('ctx', 'row'), OPPOSITE)  5.3 us
    ppermute x1, starting transfers between devices, on_device(): back_here = lax.ppermute(back_send, 'ctx', ACROSS)  3.67 us
    unnamed x25, local copies, waits for them, and re-layouts  2.92 us
    ppermute x1, waiting for transfers between devices, on_device(): first_stream = lax.ppermute(first_send, 'ctx', ACROSS)  2.66 us
    ppermute x1, waiting for transfers between devices, on_device(): row_sums = lax.ppermute(sums, 'row', OTHER_ROW)  1.7 us
    ppermute x1, starting transfers between devices, on_device(): near_slanted = lax.ppermute(near_other, 'ctx', SLANTED)  1.48 us
    ppermute x1, starting transfers between devices, on_device(): near_straight = lax.ppermute(near_own, 'ctx', STRAIGHT)  1.41 us
  transfers between devices with their start and end apart: 12, of which 6 were waited for; matrix products, arithmetic and copies ran while one was open for 1% of the time, Pallas kernels for 34%

profile of v9, /device:TPU:0, one launch (start us, length us, event | category | flops | bytes accessed | tf_op | source)
XLA Modules:
  0.0 48.1 jit_solution(17986576538877546468)
XLA Ops:
  0.0 3.8 %shard_map.73 = (bf16[3,192,1280]{2,1,0:T(8,128)(2,1)}, bf16[2,96,1280]{2,1,0:T(8,128)(2,1)}, bf16[2,96,1280]{2,1,0:T(8,128)(2,1)}, f32[3,192]{1,0:T(4,128)}) custom-call(bf16[192,2560]{1,0:T(8,128)(2,1)} %q_ref.5, bf16[192,2560]{1,0:T(8,128)(2,1)} %k_ref.5, bf16[192,2560]{1,0:T(8,128)(2,1)} %v_ref.5, s32[1,192]{1,0:T(1,128)} %bitcast.1), custom_call_target="tpu_custom_call" | custom-call | tf_op jit(solution)/shard_map/pallas_call | solution.py:511
  3.8 0.5 collective-permute-start
  4.3 1.4 %collective-permute-start.4 = (bf16[2,96,1280]{2,1,0:T(8,128)(2,1)}, bf16[2,96,1280]{2,1,0:T(8,128)(2,1)S(1)}, u32[]{:S(2)}, u32[]{:S(2)}) collective-permute-start(bf16[2,96,1280]{2,1,0:T(8,128)(2,1)} %get-tuple-element.35), channel_id=1, source_target_pairs={{8,24},{16,0},{9,25},{17,1},{10,26},{18,2},{11,27},{19,3},{12,28},... | collective-permute-start | bytes 1474568 | tf_op jit(solution)/shard_map/ppermute | solution.py:572
  5.7 1.5 %collective-permute-start.5 = (bf16[2,96,1280]{2,1,0:T(8,128)(2,1)}, bf16[2,96,1280]{2,1,0:T(8,128)(2,1)}, u32[]{:S(2)}, u32[]{:S(2)}) collective-permute-start(bf16[2,96,1280]{2,1,0:T(8,128)(2,1)} %get-tuple-element.36), channel_id=1, source_target_pairs={{8,16},{16,8},{9,17},{17,9},{10,18},{18,10},{11,19},{19,11},{12,20... | collective-permute-start | bytes 1474568 | tf_op jit(solution)/shard_map/ppermute | solution.py:573
  7.2 5.3 %collective-permute-start.3 = (f32[3,192]{1,0:T(4,128)}, f32[3,192]{1,0:T(4,128)S(1)}, u32[]{:S(2)}, u32[]{:S(2)}) collective-permute-start(f32[3,192]{1,0:T(4,128)} %get-tuple-element.38.sums), channel_id=1, source_target_pairs={{0,12},{4,8},{8,4},{12,0},{16,28},{20,24},{24,20},{28,16},{1,13},{... | collective-permute-start | bytes 6920 | tf_op jit(solution)/shard_map/ppermute | solution.py:577
  12.5 0.2 collective-permute-start.2
  12.7 1.3 %collective-permute-done.3.mate_row_sums = f32[3,192]{1,0:T(4,128)S(1)} collective-permute-done((f32[3,192]{1,0:T(4,128)}, f32[3,192]{1,0:T(4,128)S(1)}, u32[]{:S(2)}, u32[]{:S(2)}) %collective-permute-start.3) | collective-permute-done | bytes 2336 | tf_op jit(solution)/shard_map/ppermute | solution.py:577
  14.0 0.6 %collective-permute-start.1 = (f32[3,192]{1,0:T(4,128)}, f32[3,192]{1,0:T(4,128)S(1)}, u32[]{:S(2)}, u32[]{:S(2)}) collective-permute-start(f32[3,192]{1,0:T(4,128)} %get-tuple-element.38.sums), channel_id=1, source_target_pairs={{0,8},{8,0},{16,24},{24,16},{1,9},{9,1},{17,25},{25,17},{2,10},{10... | collective-permute-start | bytes 6920 | tf_op jit(solution)/shard_map/ppermute | solution.py:575
  14.6 1.7 %collective-permute-done.2.row_sums = f32[3,192]{1,0:T(4,128)S(1)} collective-permute-done((f32[3,192]{1,0:T(4,128)}, f32[3,192]{1,0:T(4,128)S(1)}, u32[]{:S(2)}, u32[]{:S(2)}) %collective-permute-start.2) | collective-permute-done | bytes 2336 | tf_op jit(solution)/shard_map/ppermute | solution.py:576
  16.3 0.7 %copy-done.5 = f32[3,192]{1,0:T(4,128)S(1)} copy-done((f32[3,192]{1,0:T(4,128)S(1)}, f32[3,192]{1,0:T(4,128)}, u32[]{:S(2)}) %copy-start.5) | copy-done | bytes 2328
  17.0 1.8 %shard_map.74 = (bf16[1632,128]{1,0:T(8,128)(2,1)}, bf16[1600,128]{1,0:T(8,128)(2,1)S(1)}, f32[2,384]{1,0:T(2,128)S(1)}, f32[1,128]{1,0:T(1,128)S(1)}) custom-call(bf16[192,2560]{1,0:T(8,128)(2,1)S(1)} %copy-done, bf16[192,2560]{1,0:T(8,128)(2,1)S(1)} %copy-done.1, bf16[192,2560]{1,0:T(8,128)(2,1)S(1)} %copy-done.2, ...), custom_call_target="tpu_custom_call" | custom-call | tf_op jit(solution)/shard_map/pallas_call | solution.py:511
  18.8 0.7 %copy-done.8 = bf16[1600,128]{1,0:T(8,128)(2,1)} copy-done((bf16[1600,128]{1,0:T(8,128)(2,1)}, bf16[1600,128]{1,0:T(8,128)(2,1)S(1)}, u32[]{:S(2)}) %copy-start.8) | copy-done | bytes 409624
  19.6 1.2 %collective-permute-start.6 = (bf16[1632,128]{1,0:T(8,128)(2,1)}, bf16[1632,128]{1,0:T(8,128)(2,1)}, u32[]{:S(2)}, u32[]{:S(2)}) collective-permute-start(bf16[1632,128]{1,0:T(8,128)(2,1)} %get-tuple-element.37), channel_id=1, source_target_pairs={{0,16},{8,24},{16,0},{24,8},{1,17},{9,25},{17,1},{25,9},{2,18},{10... | collective-permute-start | bytes 1253384 | tf_op jit(solution)/shard_map/ppermute | solution.py:593
  20.8 0.1 copy.9.grid
  20.9 0.9 %collective-permute-start.7 = (bf16[1600,128]{1,0:T(8,128)(2,1)}, bf16[1600,128]{1,0:T(8,128)(2,1)}, u32[]{:S(2)}, u32[]{:S(2)}) collective-permute-start(bf16[1600,128]{1,0:T(8,128)(2,1)} %copy-done.8), channel_id=1, source_target_pairs={{0,16},{8,24},{16,0},{24,8},{1,17},{9,25},{17,1},{25,9},{2,18},{10... | collective-permute-start | bytes 1228808 | tf_op jit(solution)/shard_map/ppermute | solution.py:594
  21.8 0.1 pad_maximum_fusion
  21.9 0.1 broadcast_in_dim.13
  22.0 0.2 broadcast_in_dim_reshape.3.freqs
  22.2 2.5 %shard_map.75 = (f32[768,128]{1,0:T(8,128)S(1)}, f32[768,128]{1,0:T(8,128)S(1)}, f32[1,768]{1,0:T(1,128)S(1)}) custom-call(s32[4,2]{1,0:T(4,128)S(1)} %copy.9.grid, f32[1,128]{1,0:T(1,128)S(1)} %get-tuple-element.34.info, f32[3,192]{1,0:T(4,128)S(1)} %copy-done.6, f32[3,192]{1,0:T(4,128)S(1)} %collective-permute-done.1.mate_sums, ...), custom_call_target="tpu_custom_call" | custom-call | tf_op jit(solution)/shard_map/pallas_call | solution.py:511
  24.7 1.4 %copy-done.4 = bf16[3,192,1280]{2,1,0:T(8,128)(2,1)S(1)} copy-done((bf16[3,192,1280]{2,1,0:T(8,128)(2,1)S(1)}, bf16[3,192,1280]{2,1,0:T(8,128)(2,1)}, u32[]{:S(2)}) %copy-start.4) | copy-done | bytes 1474584
  26.1 1.5 %shard_map.76.local.refs_0_ = bf16[3,384,1280]{2,1,0:T(8,128)(2,1)S(1)} custom-call(bf16[192,2560]{1,0:T(8,128)(2,1)S(1)} %copy-done, bf16[192,2560]{1,0:T(8,128)(2,1)S(1)} %copy-done.1, bf16[192,2560]{1,0:T(8,128)(2,1)S(1)} %copy-done.2, bf16[3,192,1280]{2,1,0:T(8,128)(2,1)S(1)} %copy-done.4, f32[768,128]{1,0:T(8,128)S(1)} %get-tuple-element.39.cosine.refs_6_, ...), custom_call_target="tpu_custom_call" | custom-call | tf_op jit(solution)/shard_map/pallas_call | solution.py:511
  27.6 2.2 %shard_map.77 = (f32[384,1280]{1,0:T(8,128)S(1)}, f32[384,640]{1,0:T(8,128)S(1)}) custom-call(bf16[3,384,1280]{2,1,0:T(8,128)(2,1)S(1)} %shard_map.76.local.refs_0_, f32[1,768]{1,0:T(1,128)S(1)} %get-tuple-element.44.ids.refs_5_), custom_call_target="tpu_custom_call" | custom-call | tf_op jit(solution)/shard_map/pallas_call | solution.py:511
  29.8 2.7 %collective-permute-done.6.refs_8_.refs_9_ = bf16[1632,128]{1,0:T(8,128)(2,1)} collective-permute-done((bf16[1632,128]{1,0:T(8,128)(2,1)}, bf16[1632,128]{1,0:T(8,128)(2,1)}, u32[]{:S(2)}, u32[]{:S(2)}) %collective-permute-start.6) | collective-permute-done | bytes 417824 | tf_op jit(solution)/shard_map/ppermute | solution.py:593
  32.4 4.2 %shard_map.78 = (bf16[192,640]{1,0:T(8,128)(2,1)S(1)}, bf16[192,640]{1,0:T(8,128)(2,1)S(1)}, bf16[640,128]{1,0:T(8,128)(2,1)S(1)}, f32[2,384,128]{2,1,0:T(8,128)S(1)}) custom-call(f32[1,128]{1,0:T(1,128)S(1)} %get-tuple-element.34.info, bf16[3,384,1280]{2,1,0:T(8,128)(2,1)S(1)} %shard_map.76.local.refs_0_, ...), custom_call_target="tpu_custom_call" | custom-call | tf_op jit(solution)/shard_map/pallas_call | solution.py:511
  36.6 3.7 %collective-permute-start.10 = (bf16[640,128]{1,0:T(8,128)(2,1)S(1)}, bf16[640,128]{1,0:T(8,128)(2,1)S(1)}, u32[]{:S(2)}, u32[]{:S(2)}) collective-permute-start(bf16[640,128]{1,0:T(8,128)(2,1)S(1)} %get-tuple-element.57), channel_id=1, source_target_pairs={{0,16},{8,24},{16,0},{24,8},{1,17},{9,25},{17,1},{25,9},{2,18},{10... | collective-permute-start | bytes 491528 | tf_op jit(solution)/shard_map/ppermute | solution.py:623
  40.3 4.2 %shard_map.79 = (bf16[192,640]{1,0:T(8,128)(2,1)S(1)}, bf16[192,640]{1,0:T(8,128)(2,1)S(1)}) custom-call(f32[1,128]{1,0:T(1,128)S(1)} %get-tuple-element.34.info, bf16[3,384,1280]{2,1,0:T(8,128)(2,1)S(1)} %shard_map.76.local.refs_0_, bf16[2,96,1280]{2,1,0:T(8,128)(2,1)S(1)} %collective-permute-done.4.refs_1_, ...), custom_call_target="tpu_custom_call" | custom-call | tf_op jit(solution)/shard_map/pallas_call | solution.py:511
  44.6 0.5 %collective-permute-start.9 = (bf16[192,640]{1,0:T(8,128)(2,1)S(1)}, bf16[192,640]{1,0:T(8,128)(2,1)S(1)}, u32[]{:S(2)}, u32[]{:S(2)}) collective-permute-start(bf16[192,640]{1,0:T(8,128)(2,1)S(1)} %get-tuple-element.56), channel_id=1, source_target_pairs={{0,8},{8,0},{16,24},{24,16},{1,9},{9,1},{17,25},{25,17},{2,10},{10... | collective-permute-start | bytes 737288 | tf_op jit(solution)/shard_map/ppermute | solution.py:630
  45.2 0.1 collective-permute-start.11
  45.2 0.9 %collective-permute-done.8.flex_there = bf16[192,640]{1,0:T(8,128)(2,1)S(1)} collective-permute-done((bf16[192,640]{1,0:T(8,128)(2,1)S(1)}, bf16[192,640]{1,0:T(8,128)(2,1)S(1)}, u32[]{:S(2)}, u32[]{:S(2)}) %collective-permute-start.8) | collective-permute-done | bytes 245792 | tf_op jit(solution)/shard_map/ppermute | solution.py:629
  46.1 0.4 collective-permute-done.9.fixed_there
  46.5 0.2 collective-permute-done.11.back_there
  46.7 1.4 %shard_map.80 = bf16[192,2560]{1,0:T(8,128)(2,1)} custom-call(f32[1,128]{1,0:T(1,128)S(1)} %get-tuple-element.34.info, bf16[192,640]{1,0:T(8,128)(2,1)S(1)} %get-tuple-element.47.flex_here, bf16[192,640]{1,0:T(8,128)(2,1)S(1)} %get-tuple-element.52.fixed_here, bf16[192,640]{1,0:T(8,128)(2,1)S(1)} %collective-permute-done.8.flex_there, ...), custom_call_target="tpu_custom_call" | custom-call | tf_op jit(solution)/shard_map/pallas_call | solution.py:511
  (32 shorter events, 0.2 us)
Async XLA Ops:
  0.0 16.3 %copy-start.2 = (bf16[192,2560]{1,0:T(8,128)(2,1)S(1)}, bf16[192,2560]{1,0:T(8,128)(2,1)}, u32[]{:S(2)}) copy-start(bf16[192,2560]{1,0:T(8,128)(2,1)} %v_ref.5) | copy-start | bytes 2949124
  0.0 16.3 %copy-start.1 = (bf16[192,2560]{1,0:T(8,128)(2,1)S(1)}, bf16[192,2560]{1,0:T(8,128)(2,1)}, u32[]{:S(2)}) copy-start(bf16[192,2560]{1,0:T(8,128)(2,1)} %k_ref.5) | copy-start | bytes 2949124
  0.0 16.3 %copy-start = (bf16[192,2560]{1,0:T(8,128)(2,1)S(1)}, bf16[192,2560]{1,0:T(8,128)(2,1)}, u32[]{:S(2)}) copy-start(bf16[192,2560]{1,0:T(8,128)(2,1)} %q_ref.5) | copy-start | bytes 2949124
  3.8 12.5 %collective-permute-start = (bf16[3,192,1280]{2,1,0:T(8,128)(2,1)}, bf16[3,192,1280]{2,1,0:T(8,128)(2,1)S(1)}, u32[]{:S(2)}, u32[]{:S(2)}) collective-permute-start(bf16[3,192,1280]{2,1,0:T(8,128)(2,1)} %get-tuple-element.32), channel_id=1, source_target_pairs={{0,8},{8,0},{16,24},{24,16},{1,9},{9,1},{17,25},{25,17},{2,10},{10... | collective-permute-start | bytes 4423688 | tf_op jit(solution)/shard_map/ppermute | solution.py:574
  4.3 17.9 %copy-start.6 = (f32[3,192]{1,0:T(4,128)S(1)}, f32[3,192]{1,0:T(4,128)}, u32[]{:S(2)}) copy-start(f32[3,192]{1,0:T(4,128)} %get-tuple-element.38.sums) | copy-start | bytes 6916
  4.3 17.9 %collective-permute-start.4 = (bf16[2,96,1280]{2,1,0:T(8,128)(2,1)}, bf16[2,96,1280]{2,1,0:T(8,128)(2,1)S(1)}, u32[]{:S(2)}, u32[]{:S(2)}) collective-permute-start(bf16[2,96,1280]{2,1,0:T(8,128)(2,1)} %get-tuple-element.35), channel_id=1, source_target_pairs={{8,24},{16,0},{9,25},{17,1},{10,26},{18,2},{11,27},{19,3},{12,28},... | collective-permute-start | bytes 1474568 | tf_op jit(solution)/shard_map/ppermute | solution.py:572
  5.7 16.5 %collective-permute-start.5 = (bf16[2,96,1280]{2,1,0:T(8,128)(2,1)}, bf16[2,96,1280]{2,1,0:T(8,128)(2,1)}, u32[]{:S(2)}, u32[]{:S(2)}) collective-permute-start(bf16[2,96,1280]{2,1,0:T(8,128)(2,1)} %get-tuple-element.36), channel_id=1, source_target_pairs={{8,16},{16,8},{9,17},{17,9},{10,18},{18,10},{11,19},{19,11},{12,20... | collective-permute-start | bytes 1474568 | tf_op jit(solution)/shard_map/ppermute | solution.py:573
  7.2 13.6 %copy-start.11 = (s32[4,2]{0,1:T(2,128)S(1)}, s32[4,2]{0,1:T(2,128)}, u32[]{:S(2)}) copy-start(s32[4,2]{0,1:T(2,128)} %param.13) | copy-start | bytes 100
  7.2 6.8 %collective-permute-start.3 = (f32[3,192]{1,0:T(4,128)}, f32[3,192]{1,0:T(4,128)S(1)}, u32[]{:S(2)}, u32[]{:S(2)}) collective-permute-start(f32[3,192]{1,0:T(4,128)} %get-tuple-element.38.sums), channel_id=1, source_target_pairs={{0,12},{4,8},{8,4},{12,0},{16,28},{20,24},{24,20},{28,16},{1,13},{... | collective-permute-start | bytes 6920 | tf_op jit(solution)/shard_map/ppermute | solution.py:577
  12.5 3.8 %collective-permute-start.2 = (f32[3,192]{1,0:T(4,128)}, f32[3,192]{1,0:T(4,128)S(1)}, u32[]{:S(2)}, u32[]{:S(2)}) collective-permute-start(f32[3,192]{1,0:T(4,128)} %get-tuple-element.38.sums), channel_id=1, source_target_pairs={{0,4},{4,0},{1,5},{5,1},{2,6},{6,2},{3,7},{7,3},{8,12},{12,8},{9,1... | collective-permute-start | bytes 6920 | tf_op jit(solution)/shard_map/ppermute | solution.py:576
  14.0 2.3 %collective-permute-start.1 = (f32[3,192]{1,0:T(4,128)}, f32[3,192]{1,0:T(4,128)S(1)}, u32[]{:S(2)}, u32[]{:S(2)}) collective-permute-start(f32[3,192]{1,0:T(4,128)} %get-tuple-element.38.sums), channel_id=1, source_target_pairs={{0,8},{8,0},{16,24},{24,16},{1,9},{9,1},{17,25},{25,17},{2,10},{10... | collective-permute-start | bytes 6920 | tf_op jit(solution)/shard_map/ppermute | solution.py:575
  16.3 0.7 %copy-start.5 = (f32[3,192]{1,0:T(4,128)S(1)}, f32[3,192]{1,0:T(4,128)}, u32[]{:S(2)}) copy-start(f32[3,192]{1,0:T(4,128)} %get-tuple-element.38.sums) | copy-start | bytes 6916
  17.0 1.8 %copy-start.3 = (bf16[3,192,1280]{2,1,0:T(8,128)(2,1)}, bf16[3,192,1280]{2,1,0:T(8,128)(2,1)S(1)}, u32[]{:S(2)}) copy-start(bf16[3,192,1280]{2,1,0:T(8,128)(2,1)S(1)} %collective-permute-done.mate) | copy-start | bytes 4423684
  17.0 3.9 %copy-start.9 = (f32[2560]{0:T(1024)S(1)}, f32[2560]{0:T(1024)}, u32[]{:S(2)}) copy-start(f32[2560]{0:T(1024)} %param.10) | copy-start | bytes 30724
  17.0 3.9 %copy-start.10 = (f32[2560]{0:T(1024)S(1)}, f32[2560]{0:T(1024)}, u32[]{:S(2)}) copy-start(f32[2560]{0:T(1024)} %param.11) | copy-start | bytes 30724
  18.8 0.7 %copy-start.8 = (bf16[1600,128]{1,0:T(8,128)(2,1)}, bf16[1600,128]{1,0:T(8,128)(2,1)S(1)}, u32[]{:S(2)}) copy-start(bf16[1600,128]{1,0:T(8,128)(2,1)S(1)} %get-tuple-element.51) | copy-start | bytes 1228804
  19.6 12.9 %collective-permute-start.6 = (bf16[1632,128]{1,0:T(8,128)(2,1)}, bf16[1632,128]{1,0:T(8,128)(2,1)}, u32[]{:S(2)}, u32[]{:S(2)}) collective-permute-start(bf16[1632,128]{1,0:T(8,128)(2,1)} %get-tuple-element.37), channel_id=1, source_target_pairs={{0,16},{8,24},{16,0},{24,8},{1,17},{9,25},{17,1},{25,9},{2,18},{10... | collective-permute-start | bytes 1253384 | tf_op jit(solution)/shard_map/ppermute | solution.py:593
  20.9 19.4 %collective-permute-start.7 = (bf16[1600,128]{1,0:T(8,128)(2,1)}, bf16[1600,128]{1,0:T(8,128)(2,1)}, u32[]{:S(2)}, u32[]{:S(2)}) collective-permute-start(bf16[1600,128]{1,0:T(8,128)(2,1)} %copy-done.8), channel_id=1, source_target_pairs={{0,16},{8,24},{16,0},{24,8},{1,17},{9,25},{17,1},{25,9},{2,18},{10... | collective-permute-start | bytes 1228808 | tf_op jit(solution)/shard_map/ppermute | solution.py:594
  24.7 1.4 %copy-start.4 = (bf16[3,192,1280]{2,1,0:T(8,128)(2,1)S(1)}, bf16[3,192,1280]{2,1,0:T(8,128)(2,1)}, u32[]{:S(2)}) copy-start(bf16[3,192,1280]{2,1,0:T(8,128)(2,1)} %copy-done.3) | copy-start | bytes 4423684
  36.6 8.5 %collective-permute-start.10 = (bf16[640,128]{1,0:T(8,128)(2,1)S(1)}, bf16[640,128]{1,0:T(8,128)(2,1)S(1)}, u32[]{:S(2)}, u32[]{:S(2)}) collective-permute-start(bf16[640,128]{1,0:T(8,128)(2,1)S(1)} %get-tuple-element.57), channel_id=1, source_target_pairs={{0,16},{8,24},{16,0},{24,8},{1,17},{9,25},{17,1},{25,9},{2,18},{10... | collective-permute-start | bytes 491528 | tf_op jit(solution)/shard_map/ppermute | solution.py:623
  40.3 6.4 %copy-start.7 = (s32[192]{0:T(256)S(1)}, s32[192]{0:T(256)}, u32[]{:S(2)}) copy-start(s32[192]{0:T(256)} %param.12) | copy-start | bytes 2308
  44.6 1.6 %collective-permute-start.8 = (bf16[192,640]{1,0:T(8,128)(2,1)S(1)}, bf16[192,640]{1,0:T(8,128)(2,1)S(1)}, u32[]{:S(2)}, u32[]{:S(2)}) collective-permute-start(bf16[192,640]{1,0:T(8,128)(2,1)S(1)} %get-tuple-element.55), channel_id=1, source_target_pairs={{0,8},{8,0},{16,24},{24,16},{1,9},{9,1},{17,25},{25,17},{2,10},{10... | collective-permute-start | bytes 737288 | tf_op jit(solution)/shard_map/ppermute | solution.py:629
  44.6 1.9 %collective-permute-start.9 = (bf16[192,640]{1,0:T(8,128)(2,1)S(1)}, bf16[192,640]{1,0:T(8,128)(2,1)S(1)}, u32[]{:S(2)}, u32[]{:S(2)}) collective-permute-start(bf16[192,640]{1,0:T(8,128)(2,1)S(1)} %get-tuple-element.56), channel_id=1, source_target_pairs={{0,8},{8,0},{16,24},{24,16},{1,9},{9,1},{17,25},{25,17},{2,10},{10... | collective-permute-start | bytes 737288 | tf_op jit(solution)/shard_map/ppermute | solution.py:630
  45.2 1.6 %collective-permute-start.11 = (bf16[640,128]{1,0:T(8,128)(2,1)S(1)}, bf16[640,128]{1,0:T(8,128)(2,1)S(1)}, u32[]{:S(2)}, u32[]{:S(2)}) collective-permute-start(bf16[640,128]{1,0:T(8,128)(2,1)S(1)} %collective-permute-done.10.back_here), channel_id=1, source_target_pairs={{0,8},{8,0},{16,24},{24,16},{1,9},{9,1},{17,25},{25,17},{2,10},{10... | collective-permute-start | bytes 491528 | tf_op jit(solution)/shard_map/ppermute | solution.py:632

commit v10 on v9

--- a/solution.py
+++ b/solution.py
@@ -23,7 +23,7 @@
 REST = CHIP - NEAR
 HALF = 5
 WIDE = HALF * HD
-TILE = 192
+TILE = 128
 SHORT = 640
 FIRST_ROWS = 1600
 SECOND_ROWS = 1600

time: 48.1 us -> 48.7 us (1.012)
  waiting for transfers between devices: 7.2 us -> 8.91 us
  Pallas kernels: 21.6 us -> 20.8 us
  starting transfers between devices: 15.8 us -> 15.3 us
    ppermute x1, waiting for transfers between devices: 0.01 us -> 1.1 us  [on_device(): second_stream = lax.ppermute(second_send, 'ctx', ACROSS)]
    pallas_call x8, Pallas kernels: 21.6 us -> 20.8 us  [call(): pl.pallas_call(kernel, grid=(1,), out_shape=out_shape, in_specs=in_specs,...]
    ppermute x1, waiting for transfers between devices: 2.66 us -> 3.27 us  [on_device(): first_stream = lax.ppermute(first_send, 'ctx', ACROSS)]
    ppermute x1, starting transfers between devices: 3.67 us -> 3.11 us  [on_device(): back_here = lax.ppermute(back_send, 'ctx', ACROSS)]
  transfers between devices with their start and end apart: 12 -> 12, of which waited for: 6 -> 7; matrix products, arithmetic and copies ran while one was open for 1% -> 1% of each run, Pallas kernels for 34% -> 32%
where the time goes in v10:
time: 48.7 us; the launch traced here: 48.4 us
  Pallas kernels  20.8 us (43%)
  starting transfers between devices  15.3 us (31%)
  waiting for transfers between devices  8.91 us (18%)
  local copies, waits for them, and re-layouts  3.16 us (6%)
    pallas_call x8, Pallas kernels, call(): pl.pallas_call(kernel, grid=(1,), out_shape=out_shape, in_specs=in_specs,...  20.8 us
    ppermute x1, starting transfers between devices, on_device(): mate_row_sums = lax.ppermute(sums, ('ctx', 'row'), OPPOSITE)  5.3 us
    ppermute x1, waiting for transfers between devices, on_device(): first_stream = lax.ppermute(first_send, 'ctx', ACROSS)  3.27 us
    ppermute x1, starting transfers between devices, on_device(): back_here = lax.ppermute(back_send, 'ctx', ACROSS)  3.11 us
    unnamed x25, local copies, waits for them, and re-layouts  2.92 us
    ppermute x1, waiting for transfers between devices, on_device(): row_sums = lax.ppermute(sums, 'row', OTHER_ROW)  1.7 us
    ppermute x1, starting transfers between devices, on_device(): near_slanted = lax.ppermute(near_other, 'ctx', SLANTED)  1.48 us
    ppermute x1, starting transfers between devices, on_device(): near_straight = lax.ppermute(near_own, 'ctx', STRAIGHT)  1.41 us
  transfers between devices with their start and end apart: 12, of which 7 were waited for; matrix products, arithmetic and copies ran while one was open for 1% of the time, Pallas kernels for 32%

profile of v10, /device:TPU:0, one launch (start us, length us, event | category | flops | bytes accessed | tf_op | source)
XLA Modules:
  0.0 48.4 jit_solution(9022645443321154956)
XLA Ops:
  0.0 3.8 %shard_map.73 = (bf16[3,192,1280]{2,1,0:T(8,128)(2,1)}, bf16[2,96,1280]{2,1,0:T(8,128)(2,1)}, bf16[2,96,1280]{2,1,0:T(8,128)(2,1)}, f32[3,192]{1,0:T(4,128)}) custom-call(bf16[192,2560]{1,0:T(8,128)(2,1)} %q_ref.5, bf16[192,2560]{1,0:T(8,128)(2,1)} %k_ref.5, bf16[192,2560]{1,0:T(8,128)(2,1)} %v_ref.5, s32[1,192]{1,0:T(1,128)} %bitcast.1), custom_call_target="tpu_custom_call" | custom-call | tf_op jit(solution)/shard_map/pallas_call | solution.py:511
  3.8 0.5 collective-permute-start
  4.3 1.4 %collective-permute-start.4 = (bf16[2,96,1280]{2,1,0:T(8,128)(2,1)}, bf16[2,96,1280]{2,1,0:T(8,128)(2,1)S(1)}, u32[]{:S(2)}, u32[]{:S(2)}) collective-permute-start(bf16[2,96,1280]{2,1,0:T(8,128)(2,1)} %get-tuple-element.35), channel_id=1, source_target_pairs={{8,24},{16,0},{9,25},{17,1},{10,26},{18,2},{11,27},{19,3},{12,28},... | collective-permute-start | bytes 1474568 | tf_op jit(solution)/shard_map/ppermute | solution.py:572
  5.7 1.5 %collective-permute-start.5 = (bf16[2,96,1280]{2,1,0:T(8,128)(2,1)}, bf16[2,96,1280]{2,1,0:T(8,128)(2,1)}, u32[]{:S(2)}, u32[]{:S(2)}) collective-permute-start(bf16[2,96,1280]{2,1,0:T(8,128)(2,1)} %get-tuple-element.36), channel_id=1, source_target_pairs={{8,16},{16,8},{9,17},{17,9},{10,18},{18,10},{11,19},{19,11},{12,20... | collective-permute-start | bytes 1474568 | tf_op jit(solution)/shard_map/ppermute | solution.py:573
  7.2 5.3 %collective-permute-start.3 = (f32[3,192]{1,0:T(4,128)}, f32[3,192]{1,0:T(4,128)S(1)}, u32[]{:S(2)}, u32[]{:S(2)}) collective-permute-start(f32[3,192]{1,0:T(4,128)} %get-tuple-element.38.sums), channel_id=1, source_target_pairs={{0,12},{4,8},{8,4},{12,0},{16,28},{20,24},{24,20},{28,16},{1,13},{... | collective-permute-start | bytes 6920 | tf_op jit(solution)/shard_map/ppermute | solution.py:577
  12.5 0.2 collective-permute-start.2
  12.7 1.3 %collective-permute-done.3.mate_row_sums = f32[3,192]{1,0:T(4,128)S(1)} collective-permute-done((f32[3,192]{1,0:T(4,128)}, f32[3,192]{1,0:T(4,128)S(1)}, u32[]{:S(2)}, u32[]{:S(2)}) %collective-permute-start.3) | collective-permute-done | bytes 2336 | tf_op jit(solution)/shard_map/ppermute | solution.py:577
  14.0 0.6 %collective-permute-start.1 = (f32[3,192]{1,0:T(4,128)}, f32[3,192]{1,0:T(4,128)S(1)}, u32[]{:S(2)}, u32[]{:S(2)}) collective-permute-start(f32[3,192]{1,0:T(4,128)} %get-tuple-element.38.sums), channel_id=1, source_target_pairs={{0,8},{8,0},{16,24},{24,16},{1,9},{9,1},{17,25},{25,17},{2,10},{10... | collective-permute-start | bytes 6920 | tf_op jit(solution)/shard_map/ppermute | solution.py:575
  14.6 1.7 %collective-permute-done.2.row_sums = f32[3,192]{1,0:T(4,128)S(1)} collective-permute-done((f32[3,192]{1,0:T(4,128)}, f32[3,192]{1,0:T(4,128)S(1)}, u32[]{:S(2)}, u32[]{:S(2)}) %collective-permute-start.2) | collective-permute-done | bytes 2336 | tf_op jit(solution)/shard_map/ppermute | solution.py:576
  16.3 0.7 %copy-done.5 = f32[3,192]{1,0:T(4,128)S(1)} copy-done((f32[3,192]{1,0:T(4,128)S(1)}, f32[3,192]{1,0:T(4,128)}, u32[]{:S(2)}) %copy-start.5) | copy-done | bytes 2328
  17.0 1.7 %shard_map.74 = (bf16[1632,128]{1,0:T(8,128)(2,1)}, bf16[1600,128]{1,0:T(8,128)(2,1)S(1)}, f32[2,384]{1,0:T(2,128)S(1)}, f32[1,128]{1,0:T(1,128)S(1)}) custom-call(bf16[192,2560]{1,0:T(8,128)(2,1)S(1)} %copy-done, bf16[192,2560]{1,0:T(8,128)(2,1)S(1)} %copy-done.1, bf16[192,2560]{1,0:T(8,128)(2,1)S(1)} %copy-done.2, ...), custom_call_target="tpu_custom_call" | custom-call | tf_op jit(solution)/shard_map/pallas_call | solution.py:511
  18.7 0.7 %copy-done.8 = bf16[1600,128]{1,0:T(8,128)(2,1)} copy-done((bf16[1600,128]{1,0:T(8,128)(2,1)}, bf16[1600,128]{1,0:T(8,128)(2,1)S(1)}, u32[]{:S(2)}) %copy-start.8) | copy-done | bytes 409624
  19.4 1.2 %collective-permute-start.6 = (bf16[1632,128]{1,0:T(8,128)(2,1)}, bf16[1632,128]{1,0:T(8,128)(2,1)}, u32[]{:S(2)}, u32[]{:S(2)}) collective-permute-start(bf16[1632,128]{1,0:T(8,128)(2,1)} %get-tuple-element.37), channel_id=1, source_target_pairs={{0,16},{8,24},{16,0},{24,8},{1,17},{9,25},{17,1},{25,9},{2,18},{10... | collective-permute-start | bytes 1253384 | tf_op jit(solution)/shard_map/ppermute | solution.py:593
  20.7 0.1 copy.9.grid
  20.8 0.8 %collective-permute-start.7 = (bf16[1600,128]{1,0:T(8,128)(2,1)}, bf16[1600,128]{1,0:T(8,128)(2,1)}, u32[]{:S(2)}, u32[]{:S(2)}) collective-permute-start(bf16[1600,128]{1,0:T(8,128)(2,1)} %copy-done.8), channel_id=1, source_target_pairs={{0,16},{8,24},{16,0},{24,8},{1,17},{9,25},{17,1},{25,9},{2,18},{10... | collective-permute-start | bytes 1228808 | tf_op jit(solution)/shard_map/ppermute | solution.py:594
  21.7 0.1 pad_maximum_fusion
  21.8 0.2 broadcast_in_dim_reshape.3.freqs
  22.0 2.5 %shard_map.75 = (f32[768,128]{1,0:T(8,128)S(1)}, f32[768,128]{1,0:T(8,128)S(1)}, f32[1,768]{1,0:T(1,128)S(1)}) custom-call(s32[4,2]{1,0:T(4,128)S(1)} %copy.9.grid, f32[1,128]{1,0:T(1,128)S(1)} %get-tuple-element.34.info, f32[3,192]{1,0:T(4,128)S(1)} %copy-done.6, f32[3,192]{1,0:T(4,128)S(1)} %collective-permute-done.1.mate_sums, ...), custom_call_target="tpu_custom_call" | custom-call | tf_op jit(solution)/shard_map/pallas_call | solution.py:511
  24.6 1.4 %copy-done.4 = bf16[3,192,1280]{2,1,0:T(8,128)(2,1)S(1)} copy-done((bf16[3,192,1280]{2,1,0:T(8,128)(2,1)S(1)}, bf16[3,192,1280]{2,1,0:T(8,128)(2,1)}, u32[]{:S(2)}) %copy-start.4) | copy-done | bytes 1474584
  25.9 1.5 %shard_map.76.local.refs_0_ = bf16[3,384,1280]{2,1,0:T(8,128)(2,1)S(1)} custom-call(bf16[192,2560]{1,0:T(8,128)(2,1)S(1)} %copy-done, bf16[192,2560]{1,0:T(8,128)(2,1)S(1)} %copy-done.1, bf16[192,2560]{1,0:T(8,128)(2,1)S(1)} %copy-done.2, bf16[3,192,1280]{2,1,0:T(8,128)(2,1)S(1)} %copy-done.4, f32[768,128]{1,0:T(8,128)S(1)} %get-tuple-element.39.cosine.refs_6_, ...), custom_call_target="tpu_custom_call" | custom-call | tf_op jit(solution)/shard_map/pallas_call | solution.py:511
  27.5 1.6 %shard_map.77 = (f32[384,1280]{1,0:T(8,128)S(1)}, f32[384,640]{1,0:T(8,128)S(1)}) custom-call(bf16[3,384,1280]{2,1,0:T(8,128)(2,1)S(1)} %shard_map.76.local.refs_0_, f32[1,768]{1,0:T(1,128)S(1)} %get-tuple-element.44.ids.refs_5_), custom_call_target="tpu_custom_call" | custom-call | tf_op jit(solution)/shard_map/pallas_call | solution.py:511
  29.0 3.3 %collective-permute-done.6.refs_8_.refs_9_ = bf16[1632,128]{1,0:T(8,128)(2,1)} collective-permute-done((bf16[1632,128]{1,0:T(8,128)(2,1)}, bf16[1632,128]{1,0:T(8,128)(2,1)}, u32[]{:S(2)}, u32[]{:S(2)}) %collective-permute-start.6) | collective-permute-done | bytes 417824 | tf_op jit(solution)/shard_map/ppermute | solution.py:593
  32.3 4.0 %shard_map.78 = (bf16[192,640]{1,0:T(8,128)(2,1)S(1)}, bf16[192,640]{1,0:T(8,128)(2,1)S(1)}, bf16[640,128]{1,0:T(8,128)(2,1)S(1)}, f32[2,384,128]{2,1,0:T(8,128)S(1)}) custom-call(f32[1,128]{1,0:T(1,128)S(1)} %get-tuple-element.34.info, bf16[3,384,1280]{2,1,0:T(8,128)(2,1)S(1)} %shard_map.76.local.refs_0_, ...), custom_call_target="tpu_custom_call" | custom-call | tf_op jit(solution)/shard_map/pallas_call | solution.py:511
  36.3 3.1 %collective-permute-start.10 = (bf16[640,128]{1,0:T(8,128)(2,1)S(1)}, bf16[640,128]{1,0:T(8,128)(2,1)S(1)}, u32[]{:S(2)}, u32[]{:S(2)}) collective-permute-start(bf16[640,128]{1,0:T(8,128)(2,1)S(1)} %get-tuple-element.57), channel_id=1, source_target_pairs={{0,16},{8,24},{16,0},{24,8},{1,17},{9,25},{17,1},{25,9},{2,18},{10... | collective-permute-start | bytes 491528 | tf_op jit(solution)/shard_map/ppermute | solution.py:623
  39.4 1.1 %collective-permute-done.7.refs_10_ = bf16[1600,128]{1,0:T(8,128)(2,1)} collective-permute-done((bf16[1600,128]{1,0:T(8,128)(2,1)}, bf16[1600,128]{1,0:T(8,128)(2,1)}, u32[]{:S(2)}, u32[]{:S(2)}) %collective-permute-start.7) | collective-permute-done | bytes 409632 | tf_op jit(solution)/shard_map/ppermute | solution.py:594
  40.5 4.2 %shard_map.79 = (bf16[192,640]{1,0:T(8,128)(2,1)S(1)}, bf16[192,640]{1,0:T(8,128)(2,1)S(1)}) custom-call(f32[1,128]{1,0:T(1,128)S(1)} %get-tuple-element.34.info, bf16[3,384,1280]{2,1,0:T(8,128)(2,1)S(1)} %shard_map.76.local.refs_0_, bf16[2,96,1280]{2,1,0:T(8,128)(2,1)S(1)} %collective-permute-done.4.refs_1_, ...), custom_call_target="tpu_custom_call" | custom-call | tf_op jit(solution)/shard_map/pallas_call | solution.py:511
  44.9 0.5 %collective-permute-start.9 = (bf16[192,640]{1,0:T(8,128)(2,1)S(1)}, bf16[192,640]{1,0:T(8,128)(2,1)S(1)}, u32[]{:S(2)}, u32[]{:S(2)}) collective-permute-start(bf16[192,640]{1,0:T(8,128)(2,1)S(1)} %get-tuple-element.56), channel_id=1, source_target_pairs={{0,8},{8,0},{16,24},{24,16},{1,9},{9,1},{17,25},{25,17},{2,10},{10... | collective-permute-start | bytes 737288 | tf_op jit(solution)/shard_map/ppermute | solution.py:630
  45.4 0.1 collective-permute-start.11
  45.5 0.9 %collective-permute-done.8.flex_there = bf16[192,640]{1,0:T(8,128)(2,1)S(1)} collective-permute-done((bf16[192,640]{1,0:T(8,128)(2,1)S(1)}, bf16[192,640]{1,0:T(8,128)(2,1)S(1)}, u32[]{:S(2)}, u32[]{:S(2)}) %collective-permute-start.8) | collective-permute-done | bytes 245792 | tf_op jit(solution)/shard_map/ppermute | solution.py:629
  46.4 0.4 collective-permute-done.9.fixed_there
  46.7 0.2 collective-permute-done.11.back_there
  47.0 1.4 %shard_map.80 = bf16[192,2560]{1,0:T(8,128)(2,1)} custom-call(f32[1,128]{1,0:T(1,128)S(1)} %get-tuple-element.34.info, bf16[192,640]{1,0:T(8,128)(2,1)S(1)} %get-tuple-element.47.flex_here, bf16[192,640]{1,0:T(8,128)(2,1)S(1)} %get-tuple-element.52.fixed_here, bf16[192,640]{1,0:T(8,128)(2,1)S(1)} %collective-permute-done.8.flex_there, ...), custom_call_target="tpu_custom_call" | custom-call | tf_op jit(solution)/shard_map/pallas_call | solution.py:511
  (32 shorter events, 0.2 us)
Async XLA Ops:
  0.0 16.3 %copy-start.2 = (bf16[192,2560]{1,0:T(8,128)(2,1)S(1)}, bf16[192,2560]{1,0:T(8,128)(2,1)}, u32[]{:S(2)}) copy-start(bf16[192,2560]{1,0:T(8,128)(2,1)} %v_ref.5) | copy-start | bytes 2949124
  0.0 16.3 %copy-start.1 = (bf16[192,2560]{1,0:T(8,128)(2,1)S(1)}, bf16[192,2560]{1,0:T(8,128)(2,1)}, u32[]{:S(2)}) copy-start(bf16[192,2560]{1,0:T(8,128)(2,1)} %k_ref.5) | copy-start | bytes 2949124
  0.0 16.3 %copy-start = (bf16[192,2560]{1,0:T(8,128)(2,1)S(1)}, bf16[192,2560]{1,0:T(8,128)(2,1)}, u32[]{:S(2)}) copy-start(bf16[192,2560]{1,0:T(8,128)(2,1)} %q_ref.5) | copy-start | bytes 2949124
  3.8 12.5 %collective-permute-start = (bf16[3,192,1280]{2,1,0:T(8,128)(2,1)}, bf16[3,192,1280]{2,1,0:T(8,128)(2,1)S(1)}, u32[]{:S(2)}, u32[]{:S(2)}) collective-permute-start(bf16[3,192,1280]{2,1,0:T(8,128)(2,1)} %get-tuple-element.32), channel_id=1, source_target_pairs={{0,8},{8,0},{16,24},{24,16},{1,9},{9,1},{17,25},{25,17},{2,10},{10... | collective-permute-start | bytes 4423688 | tf_op jit(solution)/shard_map/ppermute | solution.py:574
  4.3 17.8 %copy-start.6 = (f32[3,192]{1,0:T(4,128)S(1)}, f32[3,192]{1,0:T(4,128)}, u32[]{:S(2)}) copy-start(f32[3,192]{1,0:T(4,128)} %get-tuple-element.38.sums) | copy-start | bytes 6916
  4.3 17.7 %collective-permute-start.4 = (bf16[2,96,1280]{2,1,0:T(8,128)(2,1)}, bf16[2,96,1280]{2,1,0:T(8,128)(2,1)S(1)}, u32[]{:S(2)}, u32[]{:S(2)}) collective-permute-start(bf16[2,96,1280]{2,1,0:T(8,128)(2,1)} %get-tuple-element.35), channel_id=1, source_target_pairs={{8,24},{16,0},{9,25},{17,1},{10,26},{18,2},{11,27},{19,3},{12,28},... | collective-permute-start | bytes 1474568 | tf_op jit(solution)/shard_map/ppermute | solution.py:572
  5.7 16.3 %collective-permute-start.5 = (bf16[2,96,1280]{2,1,0:T(8,128)(2,1)}, bf16[2,96,1280]{2,1,0:T(8,128)(2,1)}, u32[]{:S(2)}, u32[]{:S(2)}) collective-permute-start(bf16[2,96,1280]{2,1,0:T(8,128)(2,1)} %get-tuple-element.36), channel_id=1, source_target_pairs={{8,16},{16,8},{9,17},{17,9},{10,18},{18,10},{11,19},{19,11},{12,20... | collective-permute-start | bytes 1474568 | tf_op jit(solution)/shard_map/ppermute | solution.py:573
  7.2 13.5 %copy-start.11 = (s32[4,2]{0,1:T(2,128)S(1)}, s32[4,2]{0,1:T(2,128)}, u32[]{:S(2)}) copy-start(s32[4,2]{0,1:T(2,128)} %param.13) | copy-start | bytes 100
  7.2 6.8 %collective-permute-start.3 = (f32[3,192]{1,0:T(4,128)}, f32[3,192]{1,0:T(4,128)S(1)}, u32[]{:S(2)}, u32[]{:S(2)}) collective-permute-start(f32[3,192]{1,0:T(4,128)} %get-tuple-element.38.sums), channel_id=1, source_target_pairs={{0,12},{4,8},{8,4},{12,0},{16,28},{20,24},{24,20},{28,16},{1,13},{... | collective-permute-start | bytes 6920 | tf_op jit(solution)/shard_map/ppermute | solution.py:577
  12.5 3.8 %collective-permute-start.2 = (f32[3,192]{1,0:T(4,128)}, f32[3,192]{1,0:T(4,128)S(1)}, u32[]{:S(2)}, u32[]{:S(2)}) collective-permute-start(f32[3,192]{1,0:T(4,128)} %get-tuple-element.38.sums), channel_id=1, source_target_pairs={{0,4},{4,0},{1,5},{5,1},{2,6},{6,2},{3,7},{7,3},{8,12},{12,8},{9,1... | collective-permute-start | bytes 6920 | tf_op jit(solution)/shard_map/ppermute | solution.py:576
  14.0 2.3 %collective-permute-start.1 = (f32[3,192]{1,0:T(4,128)}, f32[3,192]{1,0:T(4,128)S(1)}, u32[]{:S(2)}, u32[]{:S(2)}) collective-permute-start(f32[3,192]{1,0:T(4,128)} %get-tuple-element.38.sums), channel_id=1, source_target_pairs={{0,8},{8,0},{16,24},{24,16},{1,9},{9,1},{17,25},{25,17},{2,10},{10... | collective-permute-start | bytes 6920 | tf_op jit(solution)/shard_map/ppermute | solution.py:575
  16.3 0.7 %copy-start.5 = (f32[3,192]{1,0:T(4,128)S(1)}, f32[3,192]{1,0:T(4,128)}, u32[]{:S(2)}) copy-start(f32[3,192]{1,0:T(4,128)} %get-tuple-element.38.sums) | copy-start | bytes 6916
  17.0 1.7 %copy-start.3 = (bf16[3,192,1280]{2,1,0:T(8,128)(2,1)}, bf16[3,192,1280]{2,1,0:T(8,128)(2,1)S(1)}, u32[]{:S(2)}) copy-start(bf16[3,192,1280]{2,1,0:T(8,128)(2,1)S(1)} %collective-permute-done.mate) | copy-start | bytes 4423684
  17.0 3.8 %copy-start.9 = (f32[2560]{0:T(1024)S(1)}, f32[2560]{0:T(1024)}, u32[]{:S(2)}) copy-start(f32[2560]{0:T(1024)} %param.10) | copy-start | bytes 30724
  17.0 3.8 %copy-start.10 = (f32[2560]{0:T(1024)S(1)}, f32[2560]{0:T(1024)}, u32[]{:S(2)}) copy-start(f32[2560]{0:T(1024)} %param.11) | copy-start | bytes 30724
  18.7 0.7 %copy-start.8 = (bf16[1600,128]{1,0:T(8,128)(2,1)}, bf16[1600,128]{1,0:T(8,128)(2,1)S(1)}, u32[]{:S(2)}) copy-start(bf16[1600,128]{1,0:T(8,128)(2,1)S(1)} %get-tuple-element.51) | copy-start | bytes 1228804
  19.4 12.9 %collective-permute-start.6 = (bf16[1632,128]{1,0:T(8,128)(2,1)}, bf16[1632,128]{1,0:T(8,128)(2,1)}, u32[]{:S(2)}, u32[]{:S(2)}) collective-permute-start(bf16[1632,128]{1,0:T(8,128)(2,1)} %get-tuple-element.37), channel_id=1, source_target_pairs={{0,16},{8,24},{16,0},{24,8},{1,17},{9,25},{17,1},{25,9},{2,18},{10... | collective-permute-start | bytes 1253384 | tf_op jit(solution)/shard_map/ppermute | solution.py:593
  20.8 19.7 %collective-permute-start.7 = (bf16[1600,128]{1,0:T(8,128)(2,1)}, bf16[1600,128]{1,0:T(8,128)(2,1)}, u32[]{:S(2)}, u32[]{:S(2)}) collective-permute-start(bf16[1600,128]{1,0:T(8,128)(2,1)} %copy-done.8), channel_id=1, source_target_pairs={{0,16},{8,24},{16,0},{24,8},{1,17},{9,25},{17,1},{25,9},{2,18},{10... | collective-permute-start | bytes 1228808 | tf_op jit(solution)/shard_map/ppermute | solution.py:594
  24.6 1.4 %copy-start.4 = (bf16[3,192,1280]{2,1,0:T(8,128)(2,1)S(1)}, bf16[3,192,1280]{2,1,0:T(8,128)(2,1)}, u32[]{:S(2)}) copy-start(bf16[3,192,1280]{2,1,0:T(8,128)(2,1)} %copy-done.3) | copy-start | bytes 4423684
  36.3 9.0 %collective-permute-start.10 = (bf16[640,128]{1,0:T(8,128)(2,1)S(1)}, bf16[640,128]{1,0:T(8,128)(2,1)S(1)}, u32[]{:S(2)}, u32[]{:S(2)}) collective-permute-start(bf16[640,128]{1,0:T(8,128)(2,1)S(1)} %get-tuple-element.57), channel_id=1, source_target_pairs={{0,16},{8,24},{16,0},{24,8},{1,17},{9,25},{17,1},{25,9},{2,18},{10... | collective-permute-start | bytes 491528 | tf_op jit(solution)/shard_map/ppermute | solution.py:623
  40.5 6.4 %copy-start.7 = (s32[192]{0:T(256)S(1)}, s32[192]{0:T(256)}, u32[]{:S(2)}) copy-start(s32[192]{0:T(256)} %param.12) | copy-start | bytes 2308
  44.8 1.6 %collective-permute-start.8 = (bf16[192,640]{1,0:T(8,128)(2,1)S(1)}, bf16[192,640]{1,0:T(8,128)(2,1)S(1)}, u32[]{:S(2)}, u32[]{:S(2)}) collective-permute-start(bf16[192,640]{1,0:T(8,128)(2,1)S(1)} %get-tuple-element.55), channel_id=1, source_target_pairs={{0,8},{8,0},{16,24},{24,16},{1,9},{9,1},{17,25},{25,17},{2,10},{10... | collective-permute-start | bytes 737288 | tf_op jit(solution)/shard_map/ppermute | solution.py:629
  44.9 1.9 %collective-permute-start.9 = (bf16[192,640]{1,0:T(8,128)(2,1)S(1)}, bf16[192,640]{1,0:T(8,128)(2,1)S(1)}, u32[]{:S(2)}, u32[]{:S(2)}) collective-permute-start(bf16[192,640]{1,0:T(8,128)(2,1)S(1)} %get-tuple-element.56), channel_id=1, source_target_pairs={{0,8},{8,0},{16,24},{24,16},{1,9},{9,1},{17,25},{25,17},{2,10},{10... | collective-permute-start | bytes 737288 | tf_op jit(solution)/shard_map/ppermute | solution.py:630
  45.4 1.6 %collective-permute-start.11 = (bf16[640,128]{1,0:T(8,128)(2,1)S(1)}, bf16[640,128]{1,0:T(8,128)(2,1)S(1)}, u32[]{:S(2)}, u32[]{:S(2)}) collective-permute-start(bf16[640,128]{1,0:T(8,128)(2,1)S(1)} %collective-permute-done.10.back_here), channel_id=1, source_target_pairs={{0,8},{8,0},{16,24},{24,16},{1,9},{9,1},{17,25},{25,17},{2,10},{10... | collective-permute-start | bytes 491528 | tf_op jit(solution)/shard_map/ppermute | solution.py:632
